TPU v7x, 512 devices: a whole 4x8x8 slice. The times are simulated.
512 devices in a mesh: replica: 16 (over z, y_lo), fsdp: 32 (over y_hi, x, core).
Axes of the slice: x: 4, y: 8 (y_hi: 4, y_lo: 2; y = y_hi * 2 + y_lo), z: 8, core: 2. Of those that a mesh axis runs over, the one named last changes fastest.
Arguments:
- inputs: bfloat16 [16, 12288, 4096], P('replica', 'fsdp'), may hold values from -6 to 6
- feature_gain: float32 [4096], replicated, may hold values from 0.7 to 14
- key_weight: bfloat16 [16, 4096, 512], P('replica', 'fsdp'), may hold values from -0.09375 to 0.09375
- teacher_keys: bfloat16 [16, 12288, 512], P('replica', 'fsdp'), may hold values from -40 to 40
- global_frag: bfloat16 [4194304], P('fsdp'), may hold values from -6 to 6
- local_frag: bfloat16 [16, 4194304], P('replica', 'fsdp'), may hold values from -6 to 6
- momentum: float32 [4194304], P(('fsdp', 'replica')), may hold values from -3 to 3
Outputs:
- clipped_grad: bfloat16 [16, 4096, 512], P('replica', 'fsdp')
- new_global: bfloat16 [4194304], P('fsdp')
- new_momentum: float32 [4194304], P(('fsdp', 'replica'))
All inputs are finite; a program needn't handle non-finite values.
Results may differ from a plain program's by a relative error of at most 0.027.
Values may be sent and summed in bfloat16 or wider, within the bound.
No kernel may reach another device: no remote copies, remote signals or barrier semaphores. Data moves between devices by JAX's collectives and lax.ppermute only.
A program may use at most 64 MiB of HBM per device.

v0:
```python
import jax
import jax.numpy as jnp
from jax import lax
from jax.sharding import PartitionSpec as P

QBLOCK = 128


outer_decay = 0.9
outer_rate = 0.7
clip_ratio = 2.0
epsilon = 1e-06


def encode(difference):
    blocks = difference.reshape(-1, QBLOCK)
    scales = (clip_ratio * jnp.sqrt(jnp.mean(blocks * blocks, axis=-1) + epsilon)).astype(
        jnp.bfloat16
    )
    block_codes = jnp.clip(blocks / scales.astype(jnp.float32)[:, None], -1.0, 1.0).astype(
        jnp.bfloat16
    )
    return (block_codes, scales)


def shards(inputs, feature_gain, key_weight, teacher_keys, global_frag, local_frag, momentum):
    scaled = (inputs[0].astype(jnp.float32) * feature_gain[None, :]).astype(jnp.bfloat16)
    weight_rows = key_weight[0]
    columns = scaled
    projected = jnp.dot(
        columns,
        lax.all_gather(weight_rows, "fsdp", axis=0, tiled=True),
        preferred_element_type=jnp.float32,
    )
    residual = (projected - teacher_keys[0].astype(jnp.float32)).astype(jnp.bfloat16)
    columns = scaled
    gradient = lax.psum_scatter(
        lax.dot_general(
            columns, residual, (((0,), (0,)), ((), ())), preferred_element_type=jnp.float32
        ).astype(jnp.bfloat16),
        "fsdp",
        scatter_dimension=0,
        tiled=True,
    ).astype(jnp.float32)
    entries = scaled.shape[1] * weight_rows.shape[1]
    square_sum = lax.psum(jnp.sum(gradient * gradient), "fsdp")
    factor = jnp.minimum(1.0, lax.rsqrt(square_sum / entries + epsilon))
    clipped_grad = (gradient * factor).astype(jnp.bfloat16)[None]
    global_values = global_frag.astype(jnp.float32)
    block_codes, scales = encode(global_values - local_frag[0].astype(jnp.float32))
    replicas = lax.axis_size("replica")
    share_size = global_frag.shape[0] // replicas
    offset = lax.axis_index("replica") * share_size
    decoded = (
        lax.all_gather(block_codes[None], "replica", axis=0, tiled=True).astype(jnp.float32)
        * lax.all_gather(scales[None], "replica", axis=0, tiled=True).astype(jnp.float32)[
            :, :, None
        ]
    )
    summed = jnp.sum(decoded, axis=0)
    pseudo = summed.reshape(-1) / replicas
    momentum_whole = lax.all_gather(
        momentum.astype(jnp.bfloat16), "replica", axis=0, tiled=True
    ).astype(momentum.dtype)
    momentum_next = outer_decay * momentum_whole + pseudo
    new_global = (global_values - outer_rate * (pseudo + outer_decay * momentum_next)).astype(
        jnp.bfloat16
    )
    new_momentum = lax.dynamic_slice_in_dim(momentum_next, offset, share_size)
    return (clipped_grad, new_global, new_momentum)


def solution(mesh):
    return jax.shard_map(
        shards,
        mesh=mesh,
        in_specs=(
            P("replica", "fsdp", None),
            P(),
            P("replica", "fsdp", None),
            P("replica", "fsdp", None),
            P("fsdp"),
            P("replica", "fsdp"),
            P(("fsdp", "replica")),
        ),
        out_specs=(P("replica", "fsdp", None), P("fsdp"), P(("fsdp", "replica"))),
        check_vma=False,
    )
```

profile of v0, /device:TPU:1, one launch (start us, length us, event | category | flops | bytes accessed | tf_op | source)
XLA Modules:
  0.0 383.2 jit_solution(16420352281111359904)
XLA Ops:
  7.2 0.0 all-gather.7.cloned.1.call-start
  7.2 0.7 all-gather.7.cloned.1.call-update
  7.9 0.0 all-gather.5.cloned.1.call-start
  7.9 1.6 convert_element_type.104
  9.5 1.2 bitcast_reduce_fusion
  10.7 1.9 fusion.18
  12.6 0.0 all-gather.5.cloned.1.call-update
  12.6 0.0 reduce-scatter.2.cloned.1.call-start
  12.7 70.0 %all-gather.7.cloned.1.call-done = bf16[1,4096,512]{2,1,0:T(8,128)(2,1)} async-done(((bf16[1,128,512]{2,1,0:T(8,128)(2,1)}), bf16[1,4096,512]{2,1,0:T(8,128)(2,1)}) %all-gather.7.cloned.1.call-update) | async-done | bytes 4194320 | tf_op jit(solution)/shard_map/all_gather | solution.py:32
  82.7 10.3 %convolution_convert_fusion = bf16[4096,512]{1,0:T(8,128)(2,1)} fusion(bf16[1,384,4096]{2,1,0:T(8,128)(2,1)} %param.7, f32[4096]{0:T(1024)} %param.8, bf16[1,4096,512]{2,1,0:T(8,128)(2,1)} %all-gather.7.cloned.1.call-done, bf16[1,384,512]{2,1,0:T(8,128)(2,1)} %param.10), kind=kOutput, calls=%fused_computation.3 | convolution fusion | flops 3233349632 | bytes 11943936 | tf_op jit(solution)/shard_map/dot_general | solution.py:38
  93.0 0.0 copy-start.1
  93.0 0.0 copy-start
  93.0 0.0 reduce-scatter.2.cloned.1.call-update
  93.0 0.7 copy-done.1
  93.8 27.7 %all-gather.1 = bf16[16384]{0:T(1024)(128)(2,1)S(1)} all-gather(bf16[1024]{0:T(1024)(128)(2,1)S(1)} %get-tuple-element.4), channel_id=3, replica_groups=mesh['replica'=16,'fsdp'=32] {'replica'}, dimensions={0}, use_global_device_ids=true | all-gather | bytes 34816 | tf_op jit(solution)/shard_map/all_gather | solution.py:56
  121.4 31.6 %all_gather.15 = bf16[131072]{0:T(1024)(128)(2,1)S(1)} all-gather(bf16[8192]{0:T(1024)(128)(2,1)S(1)} %convert_element_type.99), channel_id=1, replica_groups=mesh['replica'=16,'fsdp'=32] {'replica'}, dimensions={0}, use_global_device_ids=true | all-gather | bytes 278528 | tf_op jit(solution)/shard_map/all_gather | solution.py:62
  153.1 39.2 %all-gather.5.cloned.1.call-done = bf16[16,1024,128]{2,1,0:T(8,128)(2,1)} async-done(((bf16[1,1024,128]{2,1,0:T(8,128)(2,1)}), bf16[16,1024,128]{2,1,0:T(8,128)(2,1)}) %all-gather.5.cloned.1.call-update) | async-done | bytes 4194320 | tf_op jit(solution)/shard_map/all_gather | solution.py:55
  192.3 4.4 %multiply_reduce_fusion = f32[1024,128]{1,0:T(8,128)S(1)} fusion(bf16[16,1024,128]{2,1,0:T(8,128)(2,1)} %all-gather.5.cloned.1.call-done, f32[16,1024]{1,0:T(8,128)S(1)} %reshape.97), kind=kLoop, calls=%fused_computation | loop fusion | flops 6160384 | bytes 4784128 | tf_op jit(solution)/shard_map/reduce_sum | solution.py:60
  196.7 0.0 copy-done
  196.7 0.9 bitcast_add_fusion.1
  197.6 102.8 %reduce-scatter.2.cloned.1.call-done = bf16[128,512]{1,0:T(8,128)(2,1)} async-done(((bf16[4096,512]{1,0:T(8,128)(2,1)}), bf16[128,512]{1,0:T(8,128)(2,1)}) %reduce-scatter.2.cloned.1.call-update) | async-done | bytes 131088 | tf_op jit(solution)/shard_map/reduce_scatter | solution.py:37
  300.4 1.6 fusion.19
  302.0 0.6 dynamic_slice.3
  302.6 71.8 %psum.7 = f32[]{:T(128)} all-reduce(f32[]{:T(128)} %fusion.19), channel_id=1, replica_groups=mesh['replica'=16,'fsdp'=32] {'fsdp'}, use_global_device_ids=true, to_apply=%region_2.0 | all-reduce | flops 1 | bytes 8 | tf_op jit(solution)/shard_map/psum | solution.py:46
  375.1 1.6 fusion.21
  (3 shorter events, 0.0 us)
Async XLA Ops:
  7.2 75.5 %all-gather.7.cloned.1.call-start = ((), (), s32[]{:S(2)}) async-start(), calls=%async_computation.3 | async-start | bytes 4325376 | tf_op jit(solution)/shard_map/all_gather | solution.py:32
  7.9 184.4 %all-gather.5.cloned.1.call-start = ((), (), s32[]{:S(2)}) async-start(), calls=%async_computation.2 | async-start | bytes 4456448 | tf_op jit(solution)/shard_map/all_gather | solution.py:55
  12.6 287.8 %reduce-scatter.2.cloned.1.call-start = ((), (), s32[]{:S(2)}) async-start(), calls=%async_computation.1 | async-start | bytes 4325376 | tf_op jit(solution)/shard_map/reduce_scatter | solution.py:37
  93.0 0.8 copy-start.1
  93.0 103.7 %copy-start = (bf16[131072]{0:T(1024)(128)(2,1)S(1)}, bf16[131072]{0:T(1024)(128)(2,1)}, u32[]{:S(2)}) copy-start(bf16[131072]{0:T(1024)(128)(2,1)} %param.11) | copy-start | bytes 786436
Sparse Core Ops, SparseCore 0:
  11.1 71.5 all-gather.6
  85.3 106.8 all-gather.4
  196.8 103.5 reduce-scatter.1
where the time goes:
time: 384 us; the launch traced here: 383 us
  waiting for transfers between devices  213 us (55%)
  blocking collectives  131 us (34%)
  between operations  14.5 us (4%)
  other arithmetic  13.1 us (3%)
  matrix products  10.3 us (3%)
    reduce_scatter x1, waiting for transfers between devices, shards(): lax.psum_scatter(lax.dot_general(columns, residual, (((0,), (0,)), ((), (...  103 us
    psum x1, blocking collectives, shards(): square_sum = lax.psum(jnp.sum(gradient * gradient), 'fsdp')  71.8 us
    all_gather x1, waiting for transfers between devices, shards(): lax.all_gather(weight_rows, 'fsdp', axis=0, tiled=True)  70 us
    all_gather x1, waiting for transfers between devices, shards(): lax.all_gather(block_codes[None], 'replica', axis=0, tiled=True)  39.2 us
    all_gather x1, blocking collectives, shards(): lax.all_gather(momentum.astype(jnp.bfloat16), 'replica', axis=0, tiled=True)  31.6 us
    all_gather x1, blocking collectives, shards(): lax.all_gather(scales[None], 'replica', axis=0, tiled=True)  27.7 us
    dot_general x1, matrix products, shards(): lax.dot_general(columns, residual, (((0,), (0,)), ((), ())), preferred_el...  10.3 us
  transfers between devices with their start and end apart: 3, of which 3 were waited for; matrix products, arithmetic and copies ran while one was open for 5% of the time, Pallas kernels for 0%

commit v1 on v0

v1 whole, which is shorter than its diff:
```python
import jax
import jax.numpy as jnp
from jax import lax
from jax.sharding import Mesh
from jax.sharding import PartitionSpec as P

QBLOCK = 128


outer_decay = 0.9
outer_rate = 0.7
clip_ratio = 2.0
epsilon = 1e-06

AXES = {"z": 8, "y_lo": 2, "y_hi": 4, "x": 4, "core": 2}
REPLICA = ("z", "y_lo")
FSDP = ("y_hi", "x", "core")


def encode(difference):
    blocks = difference.reshape(-1, QBLOCK)
    scales = (clip_ratio * jnp.sqrt(jnp.mean(blocks * blocks, axis=-1) + epsilon)).astype(
        jnp.bfloat16
    )
    block_codes = jnp.clip(blocks / scales.astype(jnp.float32)[:, None], -1.0, 1.0).astype(
        jnp.bfloat16
    )
    return (block_codes, scales)


def exchange_sum(parts, axis):
    arrived = lax.all_to_all(parts, axis, split_axis=0, concat_axis=0, tiled=True)
    return jnp.sum(arrived.astype(jnp.float32), axis=0)


def fragment_update(global_frag, local_frag, momentum):
    global_values = global_frag.astype(jnp.float32)
    block_codes, scales = encode(global_values - local_frag[0].astype(jnp.float32))
    decoded = (
        block_codes.astype(jnp.float32) * scales.astype(jnp.float32)[:, None]
    ).astype(jnp.bfloat16)
    replicas = AXES["z"] * AXES["y_lo"]
    share = global_frag.shape[0] // replicas
    rows = share // QBLOCK
    pseudo = exchange_sum(decoded.reshape(replicas, rows, QBLOCK), REPLICA) / replicas
    new_momentum = outer_decay * momentum.reshape(rows, QBLOCK) + pseudo
    offset = lax.axis_index(REPLICA) * share
    own_global = lax.dynamic_slice_in_dim(global_frag, offset, share).reshape(rows, QBLOCK)
    own_next = (
        own_global.astype(jnp.float32) - outer_rate * (pseudo + outer_decay * new_momentum)
    ).astype(jnp.bfloat16)
    new_global = lax.all_to_all(
        jnp.broadcast_to(own_next[None], (replicas, rows, QBLOCK)),
        REPLICA,
        split_axis=0,
        concat_axis=0,
        tiled=True,
    )
    return new_global.reshape(-1), new_momentum.reshape(-1)


def shards(inputs, feature_gain, key_weight, teacher_keys, global_frag, local_frag, momentum):
    tokens, features = inputs.shape[1:]
    rows, width = key_weight.shape[1:]
    scaled = (inputs[0].astype(jnp.float32) * feature_gain[None, :]).astype(jnp.bfloat16)
    by_owner = lax.optimization_barrier(
        scaled.reshape(tokens, AXES["y_hi"], AXES["x"], AXES["core"], rows)
        .transpose(0, 3, 2, 1, 4)
        .reshape(tokens, features)
    )
    new_global, new_momentum = fragment_update(global_frag, local_frag, momentum)
    projected = jnp.dot(
        scaled,
        lax.all_gather(key_weight[0], FSDP, axis=0, tiled=True),
        preferred_element_type=jnp.float32,
    )
    residual = (projected - teacher_keys[0].astype(jnp.float32)).astype(jnp.bfloat16)
    partial = lax.dot_general(
        by_owner, residual, (((0,), (0,)), ((), ())), preferred_element_type=jnp.float32
    )
    for axis in ("core", "x", "y_hi"):
        partial = exchange_sum(
            partial.astype(jnp.bfloat16).reshape(AXES[axis], -1, width), axis
        )
    gradient = partial
    squares = jnp.sum(gradient * gradient)
    spread = lax.all_to_all(
        jnp.full((lax.axis_size(FSDP), 1), squares), FSDP, split_axis=0, concat_axis=0, tiled=True
    )
    factor = jnp.minimum(1.0, lax.rsqrt(jnp.sum(spread) / (features * width) + epsilon))
    clipped_grad = (gradient * factor).astype(jnp.bfloat16)[None]
    return (clipped_grad, new_global, new_momentum)


def solution(mesh):
    parted = Mesh(mesh.devices.reshape(tuple(AXES.values())), tuple(AXES))
    return jax.shard_map(
        shards,
        mesh=parted,
        in_specs=(
            P(REPLICA, FSDP, None),
            P(),
            P(REPLICA, FSDP, None),
            P(REPLICA, FSDP, None),
            P(FSDP),
            P(REPLICA, FSDP),
            P(FSDP + REPLICA),
        ),
        out_specs=(P(REPLICA, FSDP, None), P(FSDP), P(FSDP + REPLICA)),
        check_vma=False,
    )
```

time: 384 us -> 212 us (0.55)
  blocking collectives: 131 us -> 8.06 us
  waiting for transfers between devices: 213 us -> 128 us
  starting transfers between devices: 0.12 us -> 33.3 us
  local copies, waits for them, and re-layouts: 1.37 us -> 8.45 us
    reduce_scatter x1 -> x0, waiting for transfers between devices: 103 us -> none  [shards(): lax.psum_scatter(lax.dot_general(columns, residual, (((0,), (0,)), ((), (...]
    psum x1 -> x0, blocking collectives: 71.8 us -> none  [shards(): square_sum = lax.psum(jnp.sum(gradient * gradient), 'fsdp')]
    all_gather x2 -> x0, blocking collectives: 59.3 us -> none  [the longest x1 31.6 us: shards(): lax.all_gather(momentum.astype(jnp.bfloat16), 'replica', axis=0, tiled=True)]
    all_to_all x0 -> x5, waiting for transfers between devices: none -> 59.2 us  [the longest x3 42.4 us: exchange_sum(): lax.all_to_all(parts, axis, split_axis=0, concat_axis=0, tiled=True)]
    all_gather x2 -> x1, waiting for transfers between devices: 109 us -> 68.4 us  [shards(): lax.all_gather(key_weight[0], FSDP, axis=0, tiled=True)]
    all_to_all x0 -> x5, starting transfers between devices: none -> 33.3 us  [the longest x3 15.1 us: exchange_sum(): lax.all_to_all(parts, axis, split_axis=0, concat_axis=0, tiled=True)]
    all_to_all x0 -> x1, blocking collectives: none -> 8.06 us  [exchange_sum(): lax.all_to_all(parts, axis, split_axis=0, concat_axis=0, tiled=True)]
    dot_general x1 -> x2, matrix products: 10.3 us -> 7.31 us  [the longest x1 4.97 us: shards(): jnp.dot(scaled, lax.all_gather(key_weight[0], FSDP, axis=0, tiled=True),...]
  transfers between devices with their start and end apart: 3 -> 6, of which waited for: 3 -> 6; matrix products, arithmetic and copies ran while one was open for 5% -> 5% of each run, Pallas kernels for 0% -> 0%
where the time goes in v1:
time: 212 us
  waiting for transfers between devices  128 us (60%)
  starting transfers between devices  33.3 us (16%)
  between operations  14.9 us (7%)
  other arithmetic  11.3 us (5%)
  local copies, waits for them, and re-layouts  8.45 us (4%)
  blocking collectives  8.06 us (4%)
  matrix products  7.31 us (3%)
    all_gather x1, waiting for transfers between devices, shards(): lax.all_gather(key_weight[0], FSDP, axis=0, tiled=True)  68.4 us
    all_to_all x3, waiting for transfers between devices, exchange_sum(): lax.all_to_all(parts, axis, split_axis=0, concat_axis=0, tiled=True)  42.4 us
    all_to_all x3, starting transfers between devices, exchange_sum(): lax.all_to_all(parts, axis, split_axis=0, concat_axis=0, tiled=True)  15.1 us
    all_to_all x1, starting transfers between devices, fragment_update(): lax.all_to_all(jnp.broadcast_to(own_next[None], (replicas, rows, QBLOCK))...  10.6 us
    all_to_all x1, waiting for transfers between devices, shards(): lax.all_to_all(jnp.full((lax.axis_size(FSDP), 1), squares), FSDP, split_a...  8.69 us
    all_to_all x1, waiting for transfers between devices, fragment_update(): lax.all_to_all(jnp.broadcast_to(own_next[None], (replicas, rows, QBLOCK))...  8.18 us
    all_to_all x1, blocking collectives, exchange_sum(): lax.all_to_all(parts, axis, split_axis=0, concat_axis=0, tiled=True)  8.06 us
    all_to_all x1, starting transfers between devices, shards(): lax.all_to_all(jnp.full((lax.axis_size(FSDP), 1), squares), FSDP, split_a...  7.57 us
  transfers between devices with their start and end apart: 6, of which 6 were waited for; matrix products, arithmetic and copies ran while one was open for 5% of the time, Pallas kernels for 0%

profile of v1, /device:TPU:1, one launch (start us, length us, event | category | flops | bytes accessed | tf_op | source)
XLA Modules:
  0.0 211.6 jit_solution(12195371473950894367)
XLA Ops:
  7.2 0.0 all-gather.3.cloned.1.call-start
  7.2 0.7 all-gather.3.cloned.1.call-update
  7.9 0.0 copy-start.4
  7.9 3.4 %copy.14 = bf16[1,384,4096]{1,2,0:T(8,128)(2,1)S(1)} copy(bf16[1,384,4096]{2,1,0:T(8,128)(2,1)} %param.7) | data formatting | bytes 6291456 | tf_op args[0]
  11.3 0.0 copy-done.4
  11.4 0.7 fusion.3
  12.1 0.0 copy-start.5
  12.1 2.2 %copy.15 = bf16[384,2,4,4,128]{0,4,3,2,1:T(8,128)(2,1)} copy(bf16[384,2,4,4,128]{0,4,1,2,3:T(8,128)(2,1)S(1)} %fusion.3) | data formatting | bytes 6291456 | tf_op jit(solution)/shard_map/transpose | solution.py:68
  14.3 68.4 %all-gather.3.cloned.1.call-done = bf16[1,4096,512]{2,1,0:T(8,128)(2,1)} async-done(((bf16[1,128,512]{2,1,0:T(8,128)(2,1)}), bf16[1,4096,512]{2,1,0:T(8,128)(2,1)}) %all-gather.3.cloned.1.call-update) | async-done | bytes 4194320 | tf_op jit(solution)/shard_map/all_gather | solution.py:74
  82.7 0.0 copy-done.5
  82.7 0.0 copy-start
  82.7 5.0 %fusion.12 = bf16[384,512]{1,0:T(8,128)(2,1)S(1)} fusion(bf16[1,4096,512]{2,1,0:T(8,128)(2,1)} %all-gather.3.cloned.1.call-done, f32[4096]{0:T(1024)S(1)} %copy-done.4, bf16[1,384,4096]{1,2,0:T(8,128)(2,1)S(1)} %copy.14, bf16[1,384,512]{2,1,0:T(8,128)(2,1)S(1)} %copy-done.5), kind=kOutput, calls=%fused_computation.10 | convolution fusion | flops 1615921152 | bytes 8142848 | tf_op jit(solution)/shard_map/dot_general | solution.py:72
  87.7 0.0 copy-done
  87.7 2.3 %convolution_convert_fusion = bf16[4096,512]{1,0:T(8,128)(2,1)S(1)} fusion(bf16[384,4096]{0,1:T(8,128)(2,1)S(1)} %bitcast.54, bf16[384,512]{1,0:T(8,128)(2,1)S(1)} %fusion.12), kind=kOutput, calls=%fused_computation.3 | convolution fusion | flops 1612709888 | bytes 7733248 | tf_op jit(solution)/shard_map/dot_general | solution.py:78
  90.0 8.1 %all_to_all.31 = bf16[2,2048,512]{2,1,0:T(8,128)(2,1)} all-to-all(bf16[2,2048,512]{2,1,0:T(8,128)(2,1)S(1)} %bitcast.53), channel_id=1, replica_groups=mesh['z'=8,'y_lo'=2,'y_hi'=4,'x'=4,'core'=2] {'core'}, dimensions={0} | all-to-all | bytes 8388608 | tf_op jit(solution)/shard_map/all_to_all | solution.py:32
  98.1 4.9 %reduce_sum.69 = bf16[2048,512]{1,0:T(8,128)(2,1)} reduce(bf16[2,2048,512]{2,1,0:T(8,128)(2,1)} %all_to_all.31, bf16[]{:T(256)} %constant.9.clone.1), dimensions={0}, to_apply=%region_0.0 | reduce | flops 1048576 | bytes 6291458 | tf_op jit(solution)/shard_map/reduce_sum | solution.py:33
  103.0 0.0 copy-start.1
  103.0 0.0 copy-start.2
  103.0 3.8 %all-to-all-start.1 = ((bf16[4,512,512]{2,1,0:T(8,128)(2,1)}), bf16[4,512,512]{2,1,0:T(8,128)(2,1)S(1)}, u32[]{:S(2)}, u32[]{:S(2)}) async-start(bf16[4,512,512]{2,1,0:T(8,128)(2,1)} %bitcast.8), calls=%async_computation.1 | async-start | bytes 4194304 | tf_op jit(solution)/shard_map/all_to_all | solution.py:32
  106.8 0.0 copy-done.1
  106.9 0.5 convert_element_type.132
  107.4 0.0 copy-done.2
  107.4 0.0 copy-start.3
  107.4 0.2 bitcast_reduce_fusion
  107.6 0.1 reshape.126
  107.7 0.9 multiply_convert_fusion.1
  108.6 24.0 %all-to-all-done.1 = bf16[4,512,512]{2,1,0:T(8,128)(2,1)S(1)} async-done(((bf16[4,512,512]{2,1,0:T(8,128)(2,1)}), bf16[4,512,512]{2,1,0:T(8,128)(2,1)S(1)}, u32[]{:S(2)}, u32[]{:S(2)}) %all-to-all-start.1) | async-done | bytes 2097184 | tf_op jit(solution)/shard_map/all_to_all | solution.py:32
  132.6 7.4 %all-to-all-start.4 = ((bf16[16,64,128]{2,1,0:T(8,128)(2,1)}), bf16[16,64,128]{2,1,0:T(8,128)(2,1)S(1)}, u32[]{:S(2)}, u32[]{:S(2)}) async-start(bf16[16,64,128]{2,1,0:T(8,128)(2,1)} %multiply_convert_fusion.1), calls=%async_computation.4 | async-start | bytes 524288 | tf_op jit(solution)/shard_map/all_to_all | solution.py:32
  140.1 1.2 reduce_sum.70
  141.3 7.8 %all-to-all-done.4 = bf16[16,64,128]{2,1,0:T(8,128)(2,1)S(1)} async-done(((bf16[16,64,128]{2,1,0:T(8,128)(2,1)}), bf16[16,64,128]{2,1,0:T(8,128)(2,1)S(1)}, u32[]{:S(2)}, u32[]{:S(2)}) %all-to-all-start.4) | async-done | bytes 262176 | tf_op jit(solution)/shard_map/all_to_all | solution.py:32
  149.1 3.8 %all-to-all-start.2 = ((bf16[4,128,512]{2,1,0:T(8,128)(2,1)}), bf16[4,128,512]{2,1,0:T(8,128)(2,1)S(1)}, u32[]{:S(2)}, u32[]{:S(2)}) async-start(bf16[4,128,512]{2,1,0:T(8,128)(2,1)} %bitcast.9), calls=%async_computation.2 | async-start | bytes 1048576 | tf_op jit(solution)/shard_map/all_to_all | solution.py:32
  153.0 0.0 copy-done.3
  153.0 10.5 %all-to-all-done.2 = bf16[4,128,512]{2,1,0:T(8,128)(2,1)S(1)} async-done(((bf16[4,128,512]{2,1,0:T(8,128)(2,1)}), bf16[4,128,512]{2,1,0:T(8,128)(2,1)S(1)}, u32[]{:S(2)}, u32[]{:S(2)}) %all-to-all-start.2) | async-done | bytes 524320 | tf_op jit(solution)/shard_map/all_to_all | solution.py:32
  163.6 0.8 broadcast_in_dim.5
  164.3 10.6 %all-to-all-start.5 = ((bf16[16,64,128]{2,1,0:T(8,128)(2,1)}), bf16[16,64,128]{2,1,0:T(8,128)(2,1)S(1)}, u32[]{:S(2)}, u32[]{:S(2)}) async-start(bf16[16,64,128]{2,1,0:T(8,128)(2,1)} %broadcast_in_dim.5), calls=%async_computation.5 | async-start | bytes 524288 | tf_op jit(solution)/shard_map/all_to_all | solution.py:52
  174.9 0.1 convert_reduce_fusion
  175.0 0.7 multiply_reduce_fusion
  175.7 8.2 %all-to-all-done.5 = bf16[16,64,128]{2,1,0:T(8,128)(2,1)S(1)} async-done(((bf16[16,64,128]{2,1,0:T(8,128)(2,1)}), bf16[16,64,128]{2,1,0:T(8,128)(2,1)S(1)}, u32[]{:S(2)}, u32[]{:S(2)}) %all-to-all-start.5) | async-done | bytes 262176 | tf_op jit(solution)/shard_map/all_to_all | solution.py:52
  183.9 1.3 broadcast_in_dim.4
  185.1 7.6 %all-to-all-start.3 = ((f32[32,1,1]{2,1,0:T(1,128)}), f32[32,1,1]{2,1,0:T(1,128)S(1)}, u32[]{:S(2)}, u32[]{:S(2)}) async-start(f32[32,1,1]{2,1,0:T(1,128)} %broadcast_in_dim.4), calls=%async_computation.3 | async-start | bytes 32768 | tf_op jit(solution)/shard_map/all_to_all | solution.py:87
  192.7 0.6 bitcast_add_fusion
  193.3 8.7 %all-to-all-done.3 = f32[32,1,1]{2,1,0:T(1,128)S(1)} async-done(((f32[32,1,1]{2,1,0:T(1,128)}), f32[32,1,1]{2,1,0:T(1,128)S(1)}, u32[]{:S(2)}, u32[]{:S(2)}) %all-to-all-start.3) | async-done | bytes 160 | tf_op jit(solution)/shard_map/all_to_all | solution.py:87
  202.0 0.6 reduce_sum.73
  203.3 0.7 fusion.17
  204.0 0.7 copy.19
  (3 shorter events, 0.1 us)
Async XLA Ops:
  7.2 75.5 %all-gather.3.cloned.1.call-start = ((), (), s32[]{:S(2)}) async-start(), calls=%async_computation.6 | async-start | bytes 4325376 | tf_op jit(solution)/shard_map/all_gather | solution.py:74
  7.9 3.4 %copy-start.4 = (f32[4096]{0:T(1024)S(1)}, f32[4096]{0:T(1024)}, u32[]{:S(2)}) copy-start(f32[4096]{0:T(1024)} %param.8) | copy-start | bytes 49156
  12.1 70.6 %copy-start.5 = (bf16[1,384,512]{2,1,0:T(8,128)(2,1)S(1)}, bf16[1,384,512]{2,1,0:T(8,128)(2,1)}, u32[]{:S(2)}) copy-start(bf16[1,384,512]{2,1,0:T(8,128)(2,1)} %param.10) | copy-start | bytes 1179652
  82.7 5.0 %copy-start = (bf16[384,2,4,4,128]{0,4,3,2,1:T(8,128)(2,1)S(1)}, bf16[384,2,4,4,128]{0,4,3,2,1:T(8,128)(2,1)}, u32[]{:S(2)}) copy-start(bf16[384,2,4,4,128]{0,4,3,2,1:T(8,128)(2,1)} %copy.15) | copy-start | bytes 9437188
  103.0 3.9 %copy-start.1 = (bf16[1,131072]{1,0:T(2,128)(2,1)S(1)}, bf16[1,131072]{1,0:T(2,128)(2,1)}, u32[]{:S(2)}) copy-start(bf16[1,131072]{1,0:T(2,128)(2,1)} %param.12) | copy-start | bytes 786436
  103.0 4.4 %copy-start.2 = (bf16[131072]{0:T(1024)(128)(2,1)S(1)}, bf16[131072]{0:T(1024)(128)(2,1)}, u32[]{:S(2)}) copy-start(bf16[131072]{0:T(1024)(128)(2,1)} %param.11) | copy-start | bytes 786436
  103.0 29.6 %all-to-all-start.1 = ((bf16[4,512,512]{2,1,0:T(8,128)(2,1)}), bf16[4,512,512]{2,1,0:T(8,128)(2,1)S(1)}, u32[]{:S(2)}, u32[]{:S(2)}) async-start(bf16[4,512,512]{2,1,0:T(8,128)(2,1)} %bitcast.8), calls=%async_computation.1 | async-start | bytes 4194304 | tf_op jit(solution)/shard_map/all_to_all | solution.py:32
  107.4 45.6 %copy-start.3 = (f32[8192]{0:T(1024)S(1)}, f32[8192]{0:T(1024)}, u32[]{:S(2)}) copy-start(f32[8192]{0:T(1024)} %param.13) | copy-start | bytes 98308
  132.6 16.5 %all-to-all-start.4 = ((bf16[16,64,128]{2,1,0:T(8,128)(2,1)}), bf16[16,64,128]{2,1,0:T(8,128)(2,1)S(1)}, u32[]{:S(2)}, u32[]{:S(2)}) async-start(bf16[16,64,128]{2,1,0:T(8,128)(2,1)} %multiply_convert_fusion.1), calls=%async_computation.4 | async-start | bytes 524288 | tf_op jit(solution)/shard_map/all_to_all | solution.py:32
  149.1 14.4 %all-to-all-start.2 = ((bf16[4,128,512]{2,1,0:T(8,128)(2,1)}), bf16[4,128,512]{2,1,0:T(8,128)(2,1)S(1)}, u32[]{:S(2)}, u32[]{:S(2)}) async-start(bf16[4,128,512]{2,1,0:T(8,128)(2,1)} %bitcast.9), calls=%async_computation.2 | async-start | bytes 1048576 | tf_op jit(solution)/shard_map/all_to_all | solution.py:32
  164.3 19.6 %all-to-all-start.5 = ((bf16[16,64,128]{2,1,0:T(8,128)(2,1)}), bf16[16,64,128]{2,1,0:T(8,128)(2,1)S(1)}, u32[]{:S(2)}, u32[]{:S(2)}) async-start(bf16[16,64,128]{2,1,0:T(8,128)(2,1)} %broadcast_in_dim.5), calls=%async_computation.5 | async-start | bytes 524288 | tf_op jit(solution)/shard_map/all_to_all | solution.py:52
  185.1 16.9 %all-to-all-start.3 = ((f32[32,1,1]{2,1,0:T(1,128)}), f32[32,1,1]{2,1,0:T(1,128)S(1)}, u32[]{:S(2)}, u32[]{:S(2)}) async-start(f32[32,1,1]{2,1,0:T(1,128)} %broadcast_in_dim.4), calls=%async_computation.3 | async-start | bytes 32768 | tf_op jit(solution)/shard_map/all_to_all | solution.py:87
Sparse Core Ops, SparseCore 0:
  11.1 71.5 all-gather.2

commit v2 on v1

v2 whole, which is shorter than its diff:
```python
import functools

import jax
import jax.numpy as jnp
from jax import lax
from jax.experimental import pallas as pl
from jax.experimental.pallas import tpu as pltpu
from jax.sharding import Mesh
from jax.sharding import PartitionSpec as P

QBLOCK = 128
LANES = 128


outer_decay = 0.9
outer_rate = 0.7
clip_ratio = 2.0
epsilon = 1e-06

AXES = {"z": 8, "y_lo": 2, "y_hi": 4, "x": 4, "core": 2}
REPLICA = ("z", "y_lo")
FSDP = ("y_hi", "x", "core")
CHIPS = AXES["x"] * AXES["y_hi"]
X_FIRST = 384


def encode(difference):
    blocks = difference.reshape(-1, QBLOCK)
    scales = (clip_ratio * jnp.sqrt(jnp.mean(blocks * blocks, axis=-1) + epsilon)).astype(
        jnp.bfloat16
    )
    block_codes = jnp.clip(blocks / scales.astype(jnp.float32)[:, None], -1.0, 1.0).astype(
        jnp.bfloat16
    )
    return (block_codes, scales)


def send(value, axis, step):
    size = AXES[axis]
    return lax.ppermute(value, axis, [(i, (i + step) % size) for i in range(size)])


def tied(*values):
    return lax.optimization_barrier(values)


def arrange_kernel(order_ref, inputs_ref, gain_ref, own_ref, other_ref):
    for half, out_ref in enumerate((own_ref, other_ref)):
        for j in range(CHIPS):
            start = pl.multiple_of(order_ref[half * CHIPS + j] * LANES, LANES)
            columns = pl.ds(start, LANES)
            out_ref[:, j * LANES : (j + 1) * LANES] = (
                inputs_ref[:, columns].astype(jnp.float32) * gain_ref[:, columns]
            ).astype(jnp.bfloat16)


def arrange(inputs, feature_gain):
    tokens, features = inputs.shape
    x, y, core = (lax.axis_index(name) for name in ("x", "y_hi", "core"))
    rx, ry = jnp.arange(CHIPS) // AXES["y_hi"], jnp.arange(CHIPS) % AXES["y_hi"]
    chip = (y + ry) % AXES["y_hi"] * AXES["x"] + (x + rx) % AXES["x"]
    order = jnp.concatenate([chip * 2 + core, chip * 2 + 1 - core]).astype(jnp.int32)
    half = jax.ShapeDtypeStruct((tokens, features // 2), jnp.bfloat16)
    return pl.pallas_call(
        arrange_kernel,
        out_shape=(half, half),
        in_specs=[
            pl.BlockSpec(memory_space=pltpu.SMEM),
            pl.BlockSpec(memory_space=pltpu.VMEM),
            pl.BlockSpec(memory_space=pltpu.VMEM),
        ],
        out_specs=(pl.BlockSpec(memory_space=pltpu.VMEM),) * 2,
        compiler_params=pltpu.CompilerParams(vmem_limit_bytes=24 << 20),
        name="arrange",
    )(order, inputs, feature_gain[None, :])


def fragment_sum(global_frag, local_frag):
    difference = global_frag.astype(jnp.float32) - local_frag.astype(jnp.float32)
    block_codes, scales = encode(difference)
    decoded = (
        block_codes.astype(jnp.float32) * scales.astype(jnp.float32)[:, None]
    ).astype(jnp.bfloat16)
    replicas = AXES["z"] * AXES["y_lo"]
    arrived = lax.all_to_all(
        decoded.reshape(replicas, -1, QBLOCK), REPLICA, split_axis=0, concat_axis=0, tiled=True
    )
    return arrived


def fragment_update(arrived, global_frag, momentum):
    replicas, rows = arrived.shape[:2]
    share = rows * QBLOCK
    pseudo = jnp.sum(arrived.astype(jnp.float32), axis=0) / replicas
    new_momentum = outer_decay * momentum.reshape(rows, QBLOCK) + pseudo
    offset = lax.axis_index(REPLICA) * share
    own_global = lax.dynamic_slice_in_dim(global_frag, offset, share).reshape(rows, QBLOCK)
    own_next = (
        own_global.astype(jnp.float32) - outer_rate * (pseudo + outer_decay * new_momentum)
    ).astype(jnp.bfloat16)
    new_global = lax.all_to_all(
        jnp.broadcast_to(own_next[None], (replicas, rows, QBLOCK)),
        REPLICA,
        split_axis=0,
        concat_axis=0,
        tiled=True,
    )
    return new_global.reshape(-1), new_momentum.reshape(-1)


def total(values):
    return functools.reduce(jnp.add, [value.astype(jnp.float32) for value in values])


def shards(inputs, feature_gain, key_weight, teacher_keys, global_frag, local_frag, momentum):
    features = inputs.shape[2]
    rows, width = key_weight.shape[1:]
    steps = (2, 1, 3)

    weight = key_weight[0]
    parts = [weight[:, :X_FIRST], weight[:, X_FIRST:]]
    axes = [("y_hi", "x"), ("x", "y_hi")]
    near = [{0: part} | {k: send(part, a[0], -k) for k in steps} for part, a in zip(parts, axes)]
    own, other = arrange(inputs[0], feature_gain)
    scaled = jnp.concatenate([own, send(other, "core", 1)], axis=0)
    targets = jnp.concatenate([teacher_keys[0], send(teacher_keys[0], "core", 1)], axis=0)
    arrived = fragment_sum(global_frag, local_frag[0])
    near = [jnp.stack([n[k] for k in range(4)]) for n in near]
    far = [{0: n} | {k: send(n, a[1], -k) for k in steps} for n, a in zip(near, axes)]
    far = [jnp.stack([f[k] for k in range(4)]) for f in far]
    gathered = jnp.concatenate(
        [
            far[0].reshape(CHIPS * rows, X_FIRST),
            far[1].transpose(1, 0, 2, 3).reshape(CHIPS * rows, width - X_FIRST),
        ],
        axis=1,
    )
    gathered, arrived, scaled, targets = tied(gathered, arrived, scaled, targets)

    partial = jnp.dot(scaled, gathered, preferred_element_type=jnp.float32)
    tokens = inputs.shape[1]
    theirs = send(partial, "core", 1)
    projected = partial + jnp.concatenate([theirs[tokens:], theirs[:tokens]], axis=0)
    residual = (projected - targets.astype(jnp.float32)).astype(jnp.bfloat16)

    def product(columns, targets):
        return lax.dot_general(
            columns, targets, (((0,), (0,)), ((), ())), preferred_element_type=jnp.float32
        ).astype(jnp.bfloat16)

    by_y = (
        product(scaled, residual[:, X_FIRST:])
        .reshape(AXES["x"], AXES["y_hi"], rows, width - X_FIRST)
        .transpose(1, 0, 2, 3)
    )
    group = scaled.shape[1] // AXES["x"]
    by_x = [
        product(scaled[:, k * group : (k + 1) * group], residual[:, :X_FIRST]).reshape(
            AXES["y_hi"], rows, X_FIRST
        )
        for k in range(4)
    ]
    sums = []
    first_x = [by_x[0]] + [send(by_x[k], "x", k) for k in steps]
    first_y = [by_y[0]] + [send(by_y[k], "y_hi", k) for k in steps]
    arrived, first_x[0] = tied(arrived, first_x[0])
    new_global, new_momentum = fragment_update(arrived, global_frag, momentum)
    first_x, first_y, new_global = tied(first_x, first_y, new_global)
    second = [total(first_x).astype(jnp.bfloat16), total(first_y).astype(jnp.bfloat16)]
    for value, axis in zip(second, ("y_hi", "x")):
        sums.append(total([value[0]] + [send(value[k], axis, k) for k in steps]))
    gradient = jnp.concatenate(sums, axis=1)

    squares = jnp.sum(gradient * gradient)
    spread = lax.all_to_all(
        jnp.full((lax.axis_size(FSDP), 1), squares), FSDP, split_axis=0, concat_axis=0, tiled=True
    )
    factor = jnp.minimum(1.0, lax.rsqrt(jnp.sum(spread) / (features * width) + epsilon))
    clipped_grad = (gradient * factor).astype(jnp.bfloat16)[None]
    return (clipped_grad, new_global, new_momentum)


def solution(mesh):
    parted = Mesh(mesh.devices.reshape(tuple(AXES.values())), tuple(AXES))
    return jax.shard_map(
        shards,
        mesh=parted,
        in_specs=(
            P(REPLICA, FSDP, None),
            P(),
            P(REPLICA, FSDP, None),
            P(REPLICA, FSDP, None),
            P(FSDP),
            P(REPLICA, FSDP),
            P(FSDP + REPLICA),
        ),
        out_specs=(P(REPLICA, FSDP, None), P(FSDP), P(FSDP + REPLICA)),
        check_vma=False,
    )
```

time: 212 us -> 200 us (0.943)
  waiting for transfers between devices: 128 us -> 19.6 us
  starting transfers between devices: 33.3 us -> 135 us
  between operations: 14.9 us -> 1.93 us
  other arithmetic: 11.3 us -> 23.2 us
  blocking collectives: 8.06 us -> 0 us
  matrix products: 7.31 us -> 9.71 us
    ppermute x0 -> x27, starting transfers between devices: none -> 106 us  [send(): lax.ppermute(value, axis, [(i, (i + step) % size) for i in range(size)])]
    all_gather x1 -> x0, waiting for transfers between devices: 68.4 us -> none  [shards(): lax.all_gather(key_weight[0], FSDP, axis=0, tiled=True)]
    all_to_all x3 -> x1, waiting for transfers between devices: 42.4 us -> 0.01 us  [fragment_sum(): lax.all_to_all(decoded.reshape(replicas, -1, QBLOCK), REPLICA, split_axis...]
    ppermute x0 -> x27, waiting for transfers between devices: none -> 10.9 us  [send(): lax.ppermute(value, axis, [(i, (i + step) % size) for i in range(size)])]
    all_to_all x1, waiting for transfers between devices: 8.18 us -> 0.01 us  [fragment_update(): lax.all_to_all(jnp.broadcast_to(own_next[None], (replicas, rows, QBLOCK))...]
    all_to_all x1 -> x0, blocking collectives: 8.06 us -> none  [exchange_sum(): lax.all_to_all(parts, axis, split_axis=0, concat_axis=0, tiled=True)]
    concatenate x0 -> x4, other arithmetic: none -> 7.08 us  [the longest x1 3.43 us: shards(): scaled = jnp.concatenate([own, send(other, 'core', 1)], axis=0)]
    another operation x0 -> x4, other arithmetic: none -> 6.03 us  [shards(): far = [jnp.stack([f[k] for k in range(4)]) for f in far]]
  transfers between devices with their start and end apart: 6 -> 30, of which waited for: 6 -> 7; matrix products, arithmetic and copies ran while one was open for 5% -> 10% of each run, Pallas kernels for 0% -> 1%
where the time goes in v2:
time: 200 us; the launch traced here: 198 us
  starting transfers between devices  135 us (68%)
  other arithmetic  23.2 us (12%)
  waiting for transfers between devices  19.6 us (10%)
  matrix products  9.71 us (5%)
  local copies, waits for them, and re-layouts  7.54 us (4%)
    ppermute x27, starting transfers between devices, send(): lax.ppermute(value, axis, [(i, (i + step) % size) for i in range(size)])  106 us
    ppermute x27, waiting for transfers between devices, send(): lax.ppermute(value, axis, [(i, (i + step) % size) for i in range(size)])  10.9 us
    all_to_all x1, starting transfers between devices, fragment_sum(): lax.all_to_all(decoded.reshape(replicas, -1, QBLOCK), REPLICA, split_axis...  10.6 us
    all_to_all x1, starting transfers between devices, shards(): lax.all_to_all(jnp.full((lax.axis_size(FSDP), 1), squares), FSDP, split_a...  10 us
    all_to_all x1, waiting for transfers between devices, shards(): lax.all_to_all(jnp.full((lax.axis_size(FSDP), 1), squares), FSDP, split_a...  8.79 us
    all_to_all x1, starting transfers between devices, fragment_update(): lax.all_to_all(jnp.broadcast_to(own_next[None], (replicas, rows, QBLOCK))...  7.92 us
    another operation x4, other arithmetic, shards(): far = [jnp.stack([f[k] for k in range(4)]) for f in far]  6.03 us
    dot_general x1, matrix products, shards(): partial = jnp.dot(scaled, gathered, preferred_element_type=jnp.float32)  5.49 us
  transfers between devices with their start and end apart: 30, of which 7 were waited for; matrix products, arithmetic and copies ran while one was open for 10% of the time, Pallas kernels for 1%

profile of v2, /device:TPU:1, one launch (start us, length us, event | category | flops | bytes accessed | tf_op | source)
XLA Modules:
  0.0 198.4 jit_solution(2582127812934782011)
XLA Ops:
  0.6 0.8 slice_bitcast_fusion.12
  1.5 5.2 %collective-permute-start.6 = (bf16[128,128]{1,0:T(8,128)(2,1)S(1)}, bf16[128,128]{1,0:T(8,128)(2,1)S(1)}, u32[]{:S(2)}, u32[]{:S(2)}) collective-permute-start(bf16[128,128]{1,0:T(8,128)(2,1)S(1)} %get-tuple-element.58), channel_id=1, source_target_pairs={{0,6},{2,0},{4,2},{6,4},{1,7},{3,1},{5,3},{7,5},{8,14},{10,8},{12,... | collective-permute-start | bytes 98312 | tf_op jit(solution)/shard_map/ppermute | solution.py:40
  6.7 2.4 %collective-permute-start.7 = (bf16[128,128]{1,0:T(8,128)(2,1)S(1)}, bf16[128,128]{1,0:T(8,128)(2,1)}, u32[]{:S(2)}, u32[]{:S(2)}) collective-permute-start(bf16[128,128]{1,0:T(8,128)(2,1)S(1)} %get-tuple-element.58), channel_id=1, source_target_pairs={{0,4},{2,6},{4,0},{6,2},{1,5},{3,7},{5,1},{7,3},{8,12},{10,14},{12... | collective-permute-start | bytes 98312 | tf_op jit(solution)/shard_map/ppermute | solution.py:40
  9.1 2.5 %collective-permute-start.8 = (bf16[128,128]{1,0:T(8,128)(2,1)S(1)}, bf16[128,128]{1,0:T(8,128)(2,1)}, u32[]{:S(2)}, u32[]{:S(2)}) collective-permute-start(bf16[128,128]{1,0:T(8,128)(2,1)S(1)} %get-tuple-element.58), channel_id=1, source_target_pairs={{0,2},{2,4},{4,6},{6,0},{1,3},{3,5},{5,7},{7,1},{8,10},{10,12},{12... | collective-permute-start | bytes 98312 | tf_op jit(solution)/shard_map/ppermute | solution.py:40
  11.8 1.9 copy-done
  13.7 0.7 copy-done.1
  14.4 1.4 arrange.1
  15.8 6.4 %collective-permute-start.12 = (bf16[384,2048]{1,0:T(8,128)(2,1)S(1)}, bf16[384,2048]{1,0:T(8,128)(2,1)}, u32[]{:S(2)}, u32[]{:S(2)}) collective-permute-start(bf16[384,2048]{1,0:T(8,128)(2,1)S(1)} %get-tuple-element.21), channel_id=1, source_target_pairs={{0,1},{1,0},{2,3},{3,2},{4,5},{5,4},{6,7},{7,6},{8,9},{9,8},{10,11... | collective-permute-start | bytes 4718600 | tf_op jit(solution)/shard_map/ppermute | solution.py:40
  22.2 0.7 slice_bitcast_fusion.13
  22.9 2.9 %collective-permute-start = (bf16[128,384]{1,0:T(8,128)(2,1)}, bf16[128,384]{1,0:T(8,128)(2,1)S(1)}, u32[]{:S(2)}, u32[]{:S(2)}) collective-permute-start(bf16[128,384]{1,0:T(8,128)(2,1)} %get-tuple-element.54), channel_id=1, source_target_pairs={{0,24},{8,0},{16,8},{24,16},{1,25},{9,1},{17,9},{25,17},{2,26},{10... | collective-permute-start | bytes 294920 | tf_op jit(solution)/shard_map/ppermute | solution.py:40
  26.4 0.9 bitcast_reduce_fusion
  27.3 3.5 %collective-permute-start.1 = (bf16[128,384]{1,0:T(8,128)(2,1)}, bf16[128,384]{1,0:T(8,128)(2,1)S(1)}, u32[]{:S(2)}, u32[]{:S(2)}) collective-permute-start(bf16[128,384]{1,0:T(8,128)(2,1)} %get-tuple-element.54), channel_id=1, source_target_pairs={{0,16},{8,24},{16,0},{24,8},{1,17},{9,25},{17,1},{25,9},{2,18},{10... | collective-permute-start | bytes 294920 | tf_op jit(solution)/shard_map/ppermute | solution.py:40
  30.8 4.2 %collective-permute-start.2 = (bf16[128,384]{1,0:T(8,128)(2,1)}, bf16[128,384]{1,0:T(8,128)(2,1)S(1)}, u32[]{:S(2)}, u32[]{:S(2)}) collective-permute-start(bf16[128,384]{1,0:T(8,128)(2,1)} %get-tuple-element.54), channel_id=1, source_target_pairs={{0,8},{8,16},{16,24},{24,0},{1,9},{9,17},{17,25},{25,1},{2,10},{10... | collective-permute-start | bytes 294920 | tf_op jit(solution)/shard_map/ppermute | solution.py:40
  35.0 1.5 fusion.29
  36.5 3.2 %collective-permute-start.9 = (bf16[4,128,128]{2,1,0:T(8,128)(2,1)}, bf16[4,128,128]{2,1,0:T(8,128)(2,1)}, u32[]{:S(2)}, u32[]{:S(2)}) collective-permute-start(bf16[4,128,128]{2,1,0:T(8,128)(2,1)} %get-tuple-element.56), channel_id=1, source_target_pairs={{0,24},{8,0},{16,8},{24,16},{1,25},{9,1},{17,9},{25,17},{2,26},{10... | collective-permute-start | bytes 393224 | tf_op jit(solution)/shard_map/ppermute | solution.py:40
  39.7 5.7 %collective-permute-start.10 = (bf16[4,128,128]{2,1,0:T(8,128)(2,1)}, bf16[4,128,128]{2,1,0:T(8,128)(2,1)}, u32[]{:S(2)}, u32[]{:S(2)}) collective-permute-start(bf16[4,128,128]{2,1,0:T(8,128)(2,1)} %get-tuple-element.56), channel_id=1, source_target_pairs={{0,16},{8,24},{16,0},{24,8},{1,17},{9,25},{17,1},{25,9},{2,18},{10... | collective-permute-start | bytes 393224 | tf_op jit(solution)/shard_map/ppermute | solution.py:40
  45.4 2.1 %collective-permute-start.11 = (bf16[4,128,128]{2,1,0:T(8,128)(2,1)}, bf16[4,128,128]{2,1,0:T(8,128)(2,1)}, u32[]{:S(2)}, u32[]{:S(2)}) collective-permute-start(bf16[4,128,128]{2,1,0:T(8,128)(2,1)} %get-tuple-element.56), channel_id=1, source_target_pairs={{0,8},{8,16},{16,24},{24,0},{1,9},{9,17},{17,25},{25,1},{2,10},{10... | collective-permute-start | bytes 393224 | tf_op jit(solution)/shard_map/ppermute | solution.py:40
  47.6 3.6 %collective-permute-start.13 = (bf16[384,512]{1,0:T(8,128)(2,1)}, bf16[384,512]{1,0:T(8,128)(2,1)}, u32[]{:S(2)}, u32[]{:S(2)}) collective-permute-start(bf16[384,512]{1,0:T(8,128)(2,1)} %bitcast.28), channel_id=1, source_target_pairs={{0,1},{1,0},{2,3},{3,2},{4,5},{5,4},{6,7},{7,6},{8,9},{9,8},{10,11... | collective-permute-start | bytes 1179656 | tf_op jit(solution)/shard_map/ppermute | solution.py:40
  51.2 1.9 fusion.30
  53.1 4.3 %collective-permute-start.3 = (bf16[4,128,384]{2,1,0:T(8,128)(2,1)}, bf16[4,128,384]{2,1,0:T(8,128)(2,1)}, u32[]{:S(2)}, u32[]{:S(2)}) collective-permute-start(bf16[4,128,384]{2,1,0:T(8,128)(2,1)} %get-tuple-element.49), channel_id=1, source_target_pairs={{0,6},{2,0},{4,2},{6,4},{1,7},{3,1},{5,3},{7,5},{8,14},{10,8},{12,... | collective-permute-start | bytes 1179656 | tf_op jit(solution)/shard_map/ppermute | solution.py:40
  57.4 3.4 %collective-permute-start.4 = (bf16[4,128,384]{2,1,0:T(8,128)(2,1)}, bf16[4,128,384]{2,1,0:T(8,128)(2,1)}, u32[]{:S(2)}, u32[]{:S(2)}) collective-permute-start(bf16[4,128,384]{2,1,0:T(8,128)(2,1)} %get-tuple-element.49), channel_id=1, source_target_pairs={{0,4},{2,6},{4,0},{6,2},{1,5},{3,7},{5,1},{7,3},{8,12},{10,14},{12... | collective-permute-start | bytes 1179656 | tf_op jit(solution)/shard_map/ppermute | solution.py:40
  60.8 2.8 %collective-permute-start.5 = (bf16[4,128,384]{2,1,0:T(8,128)(2,1)}, bf16[4,128,384]{2,1,0:T(8,128)(2,1)}, u32[]{:S(2)}, u32[]{:S(2)}) collective-permute-start(bf16[4,128,384]{2,1,0:T(8,128)(2,1)} %get-tuple-element.49), channel_id=1, source_target_pairs={{0,2},{2,4},{4,6},{6,0},{1,3},{3,5},{5,7},{7,1},{8,10},{10,12},{12... | collective-permute-start | bytes 1179656 | tf_op jit(solution)/shard_map/ppermute | solution.py:40
  63.6 2.0 multiply_convert_fusion
  65.5 10.6 %all-to-all-start = ((bf16[16,64,128]{2,1,0:T(8,128)(2,1)}), bf16[16,64,128]{2,1,0:T(8,128)(2,1)}, u32[]{:S(2)}, u32[]{:S(2)}) async-start(bf16[16,64,128]{2,1,0:T(8,128)(2,1)} %multiply_convert_fusion), calls=%async_computation | async-start | bytes 524288 | tf_op jit(solution)/shard_map/all_to_all | solution.py:85
  76.1 1.2 pad_maximum_fusion.4
  77.3 2.1 %pad_maximum_fusion.3 = bf16[768,512]{1,0:T(8,128)(2,1)} fusion(bf16[384,512]{1,0:T(8,128)(2,1)} %collective-permute-done.13, bf16[384,512]{1,0:T(8,128)(2,1)} %bitcast.28), kind=kLoop, calls=%fused_computation.11 | loop fusion | flops 1572864 | bytes 1572864 | tf_op jit(solution)/shard_map/concatenate | solution.py:126
  79.3 1.3 collective-permute-done.5
  80.6 1.5 pad_maximum_fusion.2
  82.1 1.5 pad_maximum_fusion.1
  83.6 3.4 %pad_maximum_fusion = bf16[768,2048]{1,0:T(8,128)(2,1)} fusion(bf16[384,2048]{1,0:T(8,128)(2,1)} %collective-permute-done.12, bf16[384,2048]{1,0:T(8,128)(2,1)S(1)} %get-tuple-element.20), kind=kLoop, calls=%fused_computation | loop fusion | flops 6291456 | bytes 6291456 | tf_op jit(solution)/shard_map/concatenate | solution.py:125
  87.0 5.5 %fusion.32 = f32[768,512]{1,0:T(8,128)} fusion(bf16[768,2048]{1,0:T(8,128)(2,1)} %pad_maximum_fusion, bf16[2048,512]{1,0:T(8,128)(2,1)} %pad_maximum_fusion.1), kind=kOutput, calls=%fused_computation.88 | convolution fusion | flops 1610612736 | bytes 6815744 | tf_op jit(solution)/shard_map/dot_general | solution.py:140
  92.5 3.6 %collective-permute-start.14 = (f32[768,512]{1,0:T(8,128)}, f32[768,512]{1,0:T(8,128)S(1)}, u32[]{:S(2)}, u32[]{:S(2)}) collective-permute-start(f32[768,512]{1,0:T(8,128)} %fusion.32), channel_id=1, source_target_pairs={{0,1},{1,0},{2,3},{3,2},{4,5},{5,4},{6,7},{7,6},{8,9},{9,8},{10,11... | collective-permute-start | bytes 4718600 | tf_op jit(solution)/shard_map/ppermute | solution.py:40
  96.2 3.2 %collective-permute-done.14 = f32[768,512]{1,0:T(8,128)S(1)} collective-permute-done((f32[768,512]{1,0:T(8,128)}, f32[768,512]{1,0:T(8,128)S(1)}, u32[]{:S(2)}, u32[]{:S(2)}) %collective-permute-start.14) | collective-permute-done | bytes 1572896 | tf_op jit(solution)/shard_map/ppermute | solution.py:40
  99.5 2.0 %fusion.1 = bf16[768,512]{1,0:T(8,128)(2,1)S(1)} fusion(f32[768,512]{1,0:T(8,128)} %fusion.32, f32[384,512]{1,0:T(8,128)S(1)} %get-tuple-element.40, f32[384,512]{1,0:T(8,128)S(1)} %get-tuple-element.39, bf16[768,512]{1,0:T(8,128)(2,1)S(1)} %copy-done.3), kind=kLoop, calls=%fused_computation.6 | loop fusion | flops 1966080 | bytes 4718592 | tf_op jit(solution)/shard_map/convert_element_type | solution.py:144
  101.9 1.0 convolution_convert_fusion
  102.9 1.3 convolution_convert_fusion.1
  104.9 0.6 convolution_convert_fusion.3
  105.5 0.6 convolution_convert_fusion.4
  106.2 3.1 %collective-permute-start.17 = (bf16[4,128,384]{2,1,0:T(8,128)(2,1)}, bf16[4,128,384]{2,1,0:T(8,128)(2,1)S(1)}, u32[]{:S(2)}, u32[]{:S(2)}) collective-permute-start(bf16[4,128,384]{2,1,0:T(8,128)(2,1)} %bitcast.32), channel_id=1, source_target_pairs={{0,6},{2,0},{4,2},{6,4},{1,7},{3,1},{5,3},{7,5},{8,14},{10,8},{12,... | collective-permute-start | bytes 1179656 | tf_op jit(solution)/shard_map/ppermute | solution.py:40
  109.2 2.2 %collective-permute-start.16 = (bf16[4,128,384]{2,1,0:T(8,128)(2,1)S(1)}, bf16[4,128,384]{2,1,0:T(8,128)(2,1)S(1)}, u32[]{:S(2)}, u32[]{:S(2)}) collective-permute-start(bf16[4,128,384]{2,1,0:T(8,128)(2,1)S(1)} %bitcast.116), channel_id=1, source_target_pairs={{0,2},{2,4},{4,6},{6,0},{1,3},{3,5},{5,7},{7,1},{8,10},{10,12},{12... | collective-permute-start | bytes 1179656 | tf_op jit(solution)/shard_map/ppermute | solution.py:40
  111.5 3.6 %collective-permute-start.15 = (bf16[4,128,384]{2,1,0:T(8,128)(2,1)S(1)}, bf16[4,128,384]{2,1,0:T(8,128)(2,1)S(1)}, u32[]{:S(2)}, u32[]{:S(2)}) collective-permute-start(bf16[4,128,384]{2,1,0:T(8,128)(2,1)S(1)} %bitcast.115), channel_id=1, source_target_pairs={{0,4},{2,6},{4,0},{6,2},{1,5},{3,7},{5,1},{7,3},{8,12},{10,14},{12... | collective-permute-start | bytes 1179656 | tf_op jit(solution)/shard_map/ppermute | solution.py:40
  115.1 1.0 convert_reduce_fusion
  116.1 0.7 fusion.17
  116.9 0.8 broadcast_in_dim.7
  117.6 7.9 %all-to-all-start.1 = ((bf16[16,64,128]{2,1,0:T(8,128)(2,1)}), bf16[16,64,128]{2,1,0:T(8,128)(2,1)S(1)}, u32[]{:S(2)}, u32[]{:S(2)}) async-start(bf16[16,64,128]{2,1,0:T(8,128)(2,1)} %broadcast_in_dim.7), calls=%async_computation.1 | async-start | bytes 524288 | tf_op jit(solution)/shard_map/all_to_all | solution.py:101
  125.6 4.9 %collective-permute-start.18 = (bf16[4,128,128]{2,1,0:T(8,128)(2,1)S(1)}, bf16[4,128,128]{2,1,0:T(8,128)(2,1)S(1)}, u32[]{:S(2)}, u32[]{:S(2)}) collective-permute-start(bf16[4,128,128]{2,1,0:T(8,128)(2,1)S(1)} %get-tuple-element.43), channel_id=1, source_target_pairs={{0,16},{8,24},{16,0},{24,8},{1,17},{9,25},{17,1},{25,9},{2,18},{10... | collective-permute-start | bytes 393224 | tf_op jit(solution)/shard_map/ppermute | solution.py:40
  130.5 4.8 %collective-permute-start.19 = (bf16[4,128,128]{2,1,0:T(8,128)(2,1)S(1)}, bf16[4,128,128]{2,1,0:T(8,128)(2,1)S(1)}, u32[]{:S(2)}, u32[]{:S(2)}) collective-permute-start(bf16[4,128,128]{2,1,0:T(8,128)(2,1)S(1)} %get-tuple-element.42), channel_id=1, source_target_pairs={{0,8},{8,16},{16,24},{24,0},{1,9},{9,17},{17,25},{25,1},{2,10},{10... | collective-permute-start | bytes 393224 | tf_op jit(solution)/shard_map/ppermute | solution.py:40
  135.5 8.4 %collective-permute-start.20 = (bf16[4,128,128]{2,1,0:T(8,128)(2,1)S(1)}, bf16[4,128,128]{2,1,0:T(8,128)(2,1)S(1)}, u32[]{:S(2)}, u32[]{:S(2)}) collective-permute-start(bf16[4,128,128]{2,1,0:T(8,128)(2,1)S(1)} %get-tuple-element.41), channel_id=1, source_target_pairs={{0,24},{8,0},{16,8},{24,16},{1,25},{9,1},{17,9},{25,17},{2,26},{10... | collective-permute-start | bytes 393224 | tf_op jit(solution)/shard_map/ppermute | solution.py:40
  143.9 2.8 %collective-permute-done.20 = bf16[4,128,128]{2,1,0:T(8,128)(2,1)S(1)} collective-permute-done((bf16[4,128,128]{2,1,0:T(8,128)(2,1)S(1)}, bf16[4,128,128]{2,1,0:T(8,128)(2,1)S(1)}, u32[]{:S(2)}, u32[]{:S(2)}) %collective-permute-start.20) | collective-permute-done | bytes 131104 | tf_op jit(solution)/shard_map/ppermute | solution.py:40
  146.9 3.6 %collective-permute-start.24 = (bf16[128,128]{1,0:T(8,128)(2,1)S(1)}, bf16[128,128]{1,0:T(8,128)(2,1)S(1)}, u32[]{:S(2)}, u32[]{:S(2)}) collective-permute-start(bf16[128,128]{1,0:T(8,128)(2,1)S(1)} %get-tuple-element.50), channel_id=1, source_target_pairs={{0,4},{2,6},{4,0},{6,2},{1,5},{3,7},{5,1},{7,3},{8,12},{10,14},{12... | collective-permute-start | bytes 98312 | tf_op jit(solution)/shard_map/ppermute | solution.py:40
  150.5 2.9 %collective-permute-start.25 = (bf16[128,128]{1,0:T(8,128)(2,1)S(1)}, bf16[128,128]{1,0:T(8,128)(2,1)S(1)}, u32[]{:S(2)}, u32[]{:S(2)}) collective-permute-start(bf16[128,128]{1,0:T(8,128)(2,1)S(1)} %get-tuple-element.52), channel_id=1, source_target_pairs={{0,2},{2,4},{4,6},{6,0},{1,3},{3,5},{5,7},{7,1},{8,10},{10,12},{12... | collective-permute-start | bytes 98312 | tf_op jit(solution)/shard_map/ppermute | solution.py:40
  153.4 3.6 %collective-permute-start.26 = (bf16[128,128]{1,0:T(8,128)(2,1)S(1)}, bf16[128,128]{1,0:T(8,128)(2,1)S(1)}, u32[]{:S(2)}, u32[]{:S(2)}) collective-permute-start(bf16[128,128]{1,0:T(8,128)(2,1)S(1)} %get-tuple-element.51), channel_id=1, source_target_pairs={{0,6},{2,0},{4,2},{6,4},{1,7},{3,1},{5,3},{7,5},{8,14},{10,8},{12,... | collective-permute-start | bytes 98312 | tf_op jit(solution)/shard_map/ppermute | solution.py:40
  157.3 6.1 %collective-permute-start.21 = (bf16[128,384]{1,0:T(8,128)(2,1)S(1)}, bf16[128,384]{1,0:T(8,128)(2,1)S(1)}, u32[]{:S(2)}, u32[]{:S(2)}) collective-permute-start(bf16[128,384]{1,0:T(8,128)(2,1)S(1)} %get-tuple-element.45), channel_id=1, source_target_pairs={{0,16},{8,24},{16,0},{24,8},{1,17},{9,25},{17,1},{25,9},{2,18},{10... | collective-permute-start | bytes 294920 | tf_op jit(solution)/shard_map/ppermute | solution.py:40
  163.4 3.8 %collective-permute-start.22 = (bf16[128,384]{1,0:T(8,128)(2,1)S(1)}, bf16[128,384]{1,0:T(8,128)(2,1)S(1)}, u32[]{:S(2)}, u32[]{:S(2)}) collective-permute-start(bf16[128,384]{1,0:T(8,128)(2,1)S(1)} %get-tuple-element.47), channel_id=1, source_target_pairs={{0,8},{8,16},{16,24},{24,0},{1,9},{9,17},{17,25},{25,1},{2,10},{10... | collective-permute-start | bytes 294920 | tf_op jit(solution)/shard_map/ppermute | solution.py:40
  167.3 3.6 %collective-permute-start.23 = (bf16[128,384]{1,0:T(8,128)(2,1)S(1)}, bf16[128,384]{1,0:T(8,128)(2,1)S(1)}, u32[]{:S(2)}, u32[]{:S(2)}) collective-permute-start(bf16[128,384]{1,0:T(8,128)(2,1)S(1)} %get-tuple-element.46), channel_id=1, source_target_pairs={{0,24},{8,0},{16,8},{24,16},{1,25},{9,1},{17,9},{25,17},{2,26},{10... | collective-permute-start | bytes 294920 | tf_op jit(solution)/shard_map/ppermute | solution.py:40
  171.3 3.0 %collective-permute-done.23 = bf16[128,384]{1,0:T(8,128)(2,1)S(1)} collective-permute-done((bf16[128,384]{1,0:T(8,128)(2,1)S(1)}, bf16[128,384]{1,0:T(8,128)(2,1)S(1)}, u32[]{:S(2)}, u32[]{:S(2)}) %collective-permute-start.23) | collective-permute-done | bytes 98336 | tf_op jit(solution)/shard_map/ppermute | solution.py:40
  174.3 0.7 fusion.11
  175.0 1.3 broadcast_in_dim.8
  176.3 10.0 %all-to-all-start.2 = ((f32[32,1,1]{2,1,0:T(1,128)}), f32[32,1,1]{2,1,0:T(1,128)S(1)}, u32[]{:S(2)}, u32[]{:S(2)}) async-start(f32[32,1,1]{2,1,0:T(1,128)} %broadcast_in_dim.8), calls=%async_computation.2 | async-start | bytes 32768 | tf_op jit(solution)/shard_map/all_to_all | solution.py:175
  186.3 0.6 bitcast_add_fusion
  186.9 8.8 %all-to-all-done.2 = f32[32,1,1]{2,1,0:T(1,128)S(1)} async-done(((f32[32,1,1]{2,1,0:T(1,128)}), f32[32,1,1]{2,1,0:T(1,128)S(1)}, u32[]{:S(2)}, u32[]{:S(2)}) %all-to-all-start.2) | async-done | bytes 160 | tf_op jit(solution)/shard_map/all_to_all | solution.py:175
  195.7 0.6 reduce_sum.39
  197.0 0.7 fusion.10
  197.7 0.7 copy.28
  (60 shorter events, 2.9 us)
Async XLA Ops:
  0.6 21.6 %copy-start.7 = (bf16[1,128,512]{2,1,0:T(8,128)(2,1)S(1)}, bf16[1,128,512]{2,1,0:T(8,128)(2,1)}, u32[]{:S(2)}) copy-start(bf16[1,128,512]{2,1,0:T(8,128)(2,1)} %param.9) | copy-start | bytes 393220
  1.5 25.8 %collective-permute-start.6 = (bf16[128,128]{1,0:T(8,128)(2,1)S(1)}, bf16[128,128]{1,0:T(8,128)(2,1)S(1)}, u32[]{:S(2)}, u32[]{:S(2)}) collective-permute-start(bf16[128,128]{1,0:T(8,128)(2,1)S(1)} %get-tuple-element.58), channel_id=1, source_target_pairs={{0,6},{2,0},{4,2},{6,4},{1,7},{3,1},{5,3},{7,5},{8,14},{10,8},{12,... | collective-permute-start | bytes 98312 | tf_op jit(solution)/shard_map/ppermute | solution.py:40
  6.7 24.1 %collective-permute-start.7 = (bf16[128,128]{1,0:T(8,128)(2,1)S(1)}, bf16[128,128]{1,0:T(8,128)(2,1)}, u32[]{:S(2)}, u32[]{:S(2)}) collective-permute-start(bf16[128,128]{1,0:T(8,128)(2,1)S(1)} %get-tuple-element.58), channel_id=1, source_target_pairs={{0,4},{2,6},{4,0},{6,2},{1,5},{3,7},{5,1},{7,3},{8,12},{10,14},{12... | collective-permute-start | bytes 98312 | tf_op jit(solution)/shard_map/ppermute | solution.py:40
  9.1 25.9 %collective-permute-start.8 = (bf16[128,128]{1,0:T(8,128)(2,1)S(1)}, bf16[128,128]{1,0:T(8,128)(2,1)}, u32[]{:S(2)}, u32[]{:S(2)}) collective-permute-start(bf16[128,128]{1,0:T(8,128)(2,1)S(1)} %get-tuple-element.58), channel_id=1, source_target_pairs={{0,2},{2,4},{4,6},{6,0},{1,3},{3,5},{5,7},{7,1},{8,10},{10,12},{12... | collective-permute-start | bytes 98312 | tf_op jit(solution)/shard_map/ppermute | solution.py:40
  11.8 1.9 copy-start
  13.7 0.7 copy-start.1
  14.4 11.5 %copy-start.4 = (bf16[1,131072]{1,0:T(2,128)(2,1)S(1)}, bf16[1,131072]{1,0:T(2,128)(2,1)}, u32[]{:S(2)}) copy-start(bf16[1,131072]{1,0:T(2,128)(2,1)} %param.12) | copy-start | bytes 786436
  14.4 12.0 %copy-start.5 = (bf16[131072]{0:T(1024)(128)(2,1)S(1)}, bf16[131072]{0:T(1024)(128)(2,1)}, u32[]{:S(2)}) copy-start(bf16[131072]{0:T(1024)(128)(2,1)} %param.11) | copy-start | bytes 786436
  15.8 67.8 %collective-permute-start.12 = (bf16[384,2048]{1,0:T(8,128)(2,1)S(1)}, bf16[384,2048]{1,0:T(8,128)(2,1)}, u32[]{:S(2)}, u32[]{:S(2)}) collective-permute-start(bf16[384,2048]{1,0:T(8,128)(2,1)S(1)} %get-tuple-element.21), channel_id=1, source_target_pairs={{0,1},{1,0},{2,3},{3,2},{4,5},{5,4},{6,7},{7,6},{8,9},{9,8},{10,11... | collective-permute-start | bytes 4718600 | tf_op jit(solution)/shard_map/ppermute | solution.py:40
  22.9 16.8 %collective-permute-start = (bf16[128,384]{1,0:T(8,128)(2,1)}, bf16[128,384]{1,0:T(8,128)(2,1)S(1)}, u32[]{:S(2)}, u32[]{:S(2)}) collective-permute-start(bf16[128,384]{1,0:T(8,128)(2,1)} %get-tuple-element.54), channel_id=1, source_target_pairs={{0,24},{8,0},{16,8},{24,16},{1,25},{9,1},{17,9},{25,17},{2,26},{10... | collective-permute-start | bytes 294920 | tf_op jit(solution)/shard_map/ppermute | solution.py:40
  27.3 18.1 %collective-permute-start.1 = (bf16[128,384]{1,0:T(8,128)(2,1)}, bf16[128,384]{1,0:T(8,128)(2,1)S(1)}, u32[]{:S(2)}, u32[]{:S(2)}) collective-permute-start(bf16[128,384]{1,0:T(8,128)(2,1)} %get-tuple-element.54), channel_id=1, source_target_pairs={{0,16},{8,24},{16,0},{24,8},{1,17},{9,25},{17,1},{25,9},{2,18},{10... | collective-permute-start | bytes 294920 | tf_op jit(solution)/shard_map/ppermute | solution.py:40
  30.8 16.8 %collective-permute-start.2 = (bf16[128,384]{1,0:T(8,128)(2,1)}, bf16[128,384]{1,0:T(8,128)(2,1)S(1)}, u32[]{:S(2)}, u32[]{:S(2)}) collective-permute-start(bf16[128,384]{1,0:T(8,128)(2,1)} %get-tuple-element.54), channel_id=1, source_target_pairs={{0,8},{8,16},{16,24},{24,0},{1,9},{9,17},{17,25},{25,1},{2,10},{10... | collective-permute-start | bytes 294920 | tf_op jit(solution)/shard_map/ppermute | solution.py:40
  36.5 16.6 %collective-permute-start.9 = (bf16[4,128,128]{2,1,0:T(8,128)(2,1)}, bf16[4,128,128]{2,1,0:T(8,128)(2,1)}, u32[]{:S(2)}, u32[]{:S(2)}) collective-permute-start(bf16[4,128,128]{2,1,0:T(8,128)(2,1)} %get-tuple-element.56), channel_id=1, source_target_pairs={{0,24},{8,0},{16,8},{24,16},{1,25},{9,1},{17,9},{25,17},{2,26},{10... | collective-permute-start | bytes 393224 | tf_op jit(solution)/shard_map/ppermute | solution.py:40
  39.7 11.5 %copy-start.8 = (bf16[128,384]{1,0:T(8,128)(2,1)}, bf16[128,384]{1,0:T(8,128)(2,1)S(1)}, u32[]{:S(2)}) copy-start(bf16[128,384]{1,0:T(8,128)(2,1)S(1)} %collective-permute-done) | copy-start | bytes 294916
  39.7 17.7 %collective-permute-start.10 = (bf16[4,128,128]{2,1,0:T(8,128)(2,1)}, bf16[4,128,128]{2,1,0:T(8,128)(2,1)}, u32[]{:S(2)}, u32[]{:S(2)}) collective-permute-start(bf16[4,128,128]{2,1,0:T(8,128)(2,1)} %get-tuple-element.56), channel_id=1, source_target_pairs={{0,16},{8,24},{16,0},{24,8},{1,17},{9,25},{17,1},{25,9},{2,18},{10... | collective-permute-start | bytes 393224 | tf_op jit(solution)/shard_map/ppermute | solution.py:40
  45.4 5.8 %copy-start.9 = (bf16[128,384]{1,0:T(8,128)(2,1)}, bf16[128,384]{1,0:T(8,128)(2,1)S(1)}, u32[]{:S(2)}) copy-start(bf16[128,384]{1,0:T(8,128)(2,1)S(1)} %collective-permute-done.1) | copy-start | bytes 294916
  45.4 15.4 %collective-permute-start.11 = (bf16[4,128,128]{2,1,0:T(8,128)(2,1)}, bf16[4,128,128]{2,1,0:T(8,128)(2,1)}, u32[]{:S(2)}, u32[]{:S(2)}) collective-permute-start(bf16[4,128,128]{2,1,0:T(8,128)(2,1)} %get-tuple-element.56), channel_id=1, source_target_pairs={{0,8},{8,16},{16,24},{24,0},{1,9},{9,17},{17,25},{25,1},{2,10},{10... | collective-permute-start | bytes 393224 | tf_op jit(solution)/shard_map/ppermute | solution.py:40
  47.6 3.6 %copy-start.10 = (bf16[128,384]{1,0:T(8,128)(2,1)}, bf16[128,384]{1,0:T(8,128)(2,1)S(1)}, u32[]{:S(2)}) copy-start(bf16[128,384]{1,0:T(8,128)(2,1)S(1)} %collective-permute-done.2) | copy-start | bytes 294916
  47.6 29.7 %collective-permute-start.13 = (bf16[384,512]{1,0:T(8,128)(2,1)}, bf16[384,512]{1,0:T(8,128)(2,1)}, u32[]{:S(2)}, u32[]{:S(2)}) collective-permute-start(bf16[384,512]{1,0:T(8,128)(2,1)} %bitcast.28), channel_id=1, source_target_pairs={{0,1},{1,0},{2,3},{3,2},{4,5},{5,4},{6,7},{7,6},{8,9},{9,8},{10,11... | collective-permute-start | bytes 1179656 | tf_op jit(solution)/shard_map/ppermute | solution.py:40
  53.1 26.2 %collective-permute-start.3 = (bf16[4,128,384]{2,1,0:T(8,128)(2,1)}, bf16[4,128,384]{2,1,0:T(8,128)(2,1)}, u32[]{:S(2)}, u32[]{:S(2)}) collective-permute-start(bf16[4,128,384]{2,1,0:T(8,128)(2,1)} %get-tuple-element.49), channel_id=1, source_target_pairs={{0,6},{2,0},{4,2},{6,4},{1,7},{3,1},{5,3},{7,5},{8,14},{10,8},{12,... | collective-permute-start | bytes 1179656 | tf_op jit(solution)/shard_map/ppermute | solution.py:40
  57.4 21.9 %collective-permute-start.4 = (bf16[4,128,384]{2,1,0:T(8,128)(2,1)}, bf16[4,128,384]{2,1,0:T(8,128)(2,1)}, u32[]{:S(2)}, u32[]{:S(2)}) collective-permute-start(bf16[4,128,384]{2,1,0:T(8,128)(2,1)} %get-tuple-element.49), channel_id=1, source_target_pairs={{0,4},{2,6},{4,0},{6,2},{1,5},{3,7},{5,1},{7,3},{8,12},{10,14},{12... | collective-permute-start | bytes 1179656 | tf_op jit(solution)/shard_map/ppermute | solution.py:40
  60.8 19.8 %collective-permute-start.5 = (bf16[4,128,384]{2,1,0:T(8,128)(2,1)}, bf16[4,128,384]{2,1,0:T(8,128)(2,1)}, u32[]{:S(2)}, u32[]{:S(2)}) collective-permute-start(bf16[4,128,384]{2,1,0:T(8,128)(2,1)} %get-tuple-element.49), channel_id=1, source_target_pairs={{0,2},{2,4},{4,6},{6,0},{1,3},{3,5},{5,7},{7,1},{8,10},{10,12},{12... | collective-permute-start | bytes 1179656 | tf_op jit(solution)/shard_map/ppermute | solution.py:40
  65.5 21.5 %all-to-all-start = ((bf16[16,64,128]{2,1,0:T(8,128)(2,1)}), bf16[16,64,128]{2,1,0:T(8,128)(2,1)}, u32[]{:S(2)}, u32[]{:S(2)}) async-start(bf16[16,64,128]{2,1,0:T(8,128)(2,1)} %multiply_convert_fusion), calls=%async_computation | async-start | bytes 524288 | tf_op jit(solution)/shard_map/all_to_all | solution.py:85
  92.5 7.0 %copy-start.3 = (bf16[768,512]{1,0:T(8,128)(2,1)S(1)}, bf16[768,512]{1,0:T(8,128)(2,1)}, u32[]{:S(2)}) copy-start(bf16[768,512]{1,0:T(8,128)(2,1)} %pad_maximum_fusion.3) | copy-start | bytes 2359300
  92.5 6.9 %collective-permute-start.14 = (f32[768,512]{1,0:T(8,128)}, f32[768,512]{1,0:T(8,128)S(1)}, u32[]{:S(2)}, u32[]{:S(2)}) collective-permute-start(f32[768,512]{1,0:T(8,128)} %fusion.32), channel_id=1, source_target_pairs={{0,1},{1,0},{2,3},{3,2},{4,5},{5,4},{6,7},{7,6},{8,9},{9,8},{10,11... | collective-permute-start | bytes 4718600 | tf_op jit(solution)/shard_map/ppermute | solution.py:40
  99.5 2.4 %copy-start.2 = (bf16[768,2048]{1,0:T(8,128)(2,1)S(1)}, bf16[768,2048]{1,0:T(8,128)(2,1)}, u32[]{:S(2)}) copy-start(bf16[768,2048]{1,0:T(8,128)(2,1)} %pad_maximum_fusion) | copy-start | bytes 9437188
  105.5 10.6 %copy-start.6 = (f32[8192]{0:T(1024)S(1)}, f32[8192]{0:T(1024)}, u32[]{:S(2)}) copy-start(f32[8192]{0:T(1024)} %param.13) | copy-start | bytes 98308
  106.2 40.6 %collective-permute-start.17 = (bf16[4,128,384]{2,1,0:T(8,128)(2,1)}, bf16[4,128,384]{2,1,0:T(8,128)(2,1)S(1)}, u32[]{:S(2)}, u32[]{:S(2)}) collective-permute-start(bf16[4,128,384]{2,1,0:T(8,128)(2,1)} %bitcast.32), channel_id=1, source_target_pairs={{0,6},{2,0},{4,2},{6,4},{1,7},{3,1},{5,3},{7,5},{8,14},{10,8},{12,... | collective-permute-start | bytes 1179656 | tf_op jit(solution)/shard_map/ppermute | solution.py:40
  109.2 37.5 %collective-permute-start.16 = (bf16[4,128,384]{2,1,0:T(8,128)(2,1)S(1)}, bf16[4,128,384]{2,1,0:T(8,128)(2,1)S(1)}, u32[]{:S(2)}, u32[]{:S(2)}) collective-permute-start(bf16[4,128,384]{2,1,0:T(8,128)(2,1)S(1)} %bitcast.116), channel_id=1, source_target_pairs={{0,2},{2,4},{4,6},{6,0},{1,3},{3,5},{5,7},{7,1},{8,10},{10,12},{12... | collective-permute-start | bytes 1179656 | tf_op jit(solution)/shard_map/ppermute | solution.py:40
  111.5 35.3 %collective-permute-start.15 = (bf16[4,128,384]{2,1,0:T(8,128)(2,1)S(1)}, bf16[4,128,384]{2,1,0:T(8,128)(2,1)S(1)}, u32[]{:S(2)}, u32[]{:S(2)}) collective-permute-start(bf16[4,128,384]{2,1,0:T(8,128)(2,1)S(1)} %bitcast.115), channel_id=1, source_target_pairs={{0,4},{2,6},{4,0},{6,2},{1,5},{3,7},{5,1},{7,3},{8,12},{10,14},{12... | collective-permute-start | bytes 1179656 | tf_op jit(solution)/shard_map/ppermute | solution.py:40
  117.6 29.1 %all-to-all-start.1 = ((bf16[16,64,128]{2,1,0:T(8,128)(2,1)}), bf16[16,64,128]{2,1,0:T(8,128)(2,1)S(1)}, u32[]{:S(2)}, u32[]{:S(2)}) async-start(bf16[16,64,128]{2,1,0:T(8,128)(2,1)} %broadcast_in_dim.7), calls=%async_computation.1 | async-start | bytes 524288 | tf_op jit(solution)/shard_map/all_to_all | solution.py:101
  125.6 9.9 %collective-permute-start.18 = (bf16[4,128,128]{2,1,0:T(8,128)(2,1)S(1)}, bf16[4,128,128]{2,1,0:T(8,128)(2,1)S(1)}, u32[]{:S(2)}, u32[]{:S(2)}) collective-permute-start(bf16[4,128,128]{2,1,0:T(8,128)(2,1)S(1)} %get-tuple-element.43), channel_id=1, source_target_pairs={{0,16},{8,24},{16,0},{24,8},{1,17},{9,25},{17,1},{25,9},{2,18},{10... | collective-permute-start | bytes 393224 | tf_op jit(solution)/shard_map/ppermute | solution.py:40
  130.5 13.4 %collective-permute-start.19 = (bf16[4,128,128]{2,1,0:T(8,128)(2,1)S(1)}, bf16[4,128,128]{2,1,0:T(8,128)(2,1)S(1)}, u32[]{:S(2)}, u32[]{:S(2)}) collective-permute-start(bf16[4,128,128]{2,1,0:T(8,128)(2,1)S(1)} %get-tuple-element.42), channel_id=1, source_target_pairs={{0,8},{8,16},{16,24},{24,0},{1,9},{9,17},{17,25},{25,1},{2,10},{10... | collective-permute-start | bytes 393224 | tf_op jit(solution)/shard_map/ppermute | solution.py:40
  135.5 11.2 %collective-permute-start.20 = (bf16[4,128,128]{2,1,0:T(8,128)(2,1)S(1)}, bf16[4,128,128]{2,1,0:T(8,128)(2,1)S(1)}, u32[]{:S(2)}, u32[]{:S(2)}) collective-permute-start(bf16[4,128,128]{2,1,0:T(8,128)(2,1)S(1)} %get-tuple-element.41), channel_id=1, source_target_pairs={{0,24},{8,0},{16,8},{24,16},{1,25},{9,1},{17,9},{25,17},{2,26},{10... | collective-permute-start | bytes 393224 | tf_op jit(solution)/shard_map/ppermute | solution.py:40
  146.9 20.4 %collective-permute-start.24 = (bf16[128,128]{1,0:T(8,128)(2,1)S(1)}, bf16[128,128]{1,0:T(8,128)(2,1)S(1)}, u32[]{:S(2)}, u32[]{:S(2)}) collective-permute-start(bf16[128,128]{1,0:T(8,128)(2,1)S(1)} %get-tuple-element.50), channel_id=1, source_target_pairs={{0,4},{2,6},{4,0},{6,2},{1,5},{3,7},{5,1},{7,3},{8,12},{10,14},{12... | collective-permute-start | bytes 98312 | tf_op jit(solution)/shard_map/ppermute | solution.py:40
  150.5 20.3 %collective-permute-start.25 = (bf16[128,128]{1,0:T(8,128)(2,1)S(1)}, bf16[128,128]{1,0:T(8,128)(2,1)S(1)}, u32[]{:S(2)}, u32[]{:S(2)}) collective-permute-start(bf16[128,128]{1,0:T(8,128)(2,1)S(1)} %get-tuple-element.52), channel_id=1, source_target_pairs={{0,2},{2,4},{4,6},{6,0},{1,3},{3,5},{5,7},{7,1},{8,10},{10,12},{12... | collective-permute-start | bytes 98312 | tf_op jit(solution)/shard_map/ppermute | solution.py:40
  153.4 17.4 %collective-permute-start.26 = (bf16[128,128]{1,0:T(8,128)(2,1)S(1)}, bf16[128,128]{1,0:T(8,128)(2,1)S(1)}, u32[]{:S(2)}, u32[]{:S(2)}) collective-permute-start(bf16[128,128]{1,0:T(8,128)(2,1)S(1)} %get-tuple-element.51), channel_id=1, source_target_pairs={{0,6},{2,0},{4,2},{6,4},{1,7},{3,1},{5,3},{7,5},{8,14},{10,8},{12,... | collective-permute-start | bytes 98312 | tf_op jit(solution)/shard_map/ppermute | solution.py:40
  157.3 13.6 %collective-permute-start.21 = (bf16[128,384]{1,0:T(8,128)(2,1)S(1)}, bf16[128,384]{1,0:T(8,128)(2,1)S(1)}, u32[]{:S(2)}, u32[]{:S(2)}) collective-permute-start(bf16[128,384]{1,0:T(8,128)(2,1)S(1)} %get-tuple-element.45), channel_id=1, source_target_pairs={{0,16},{8,24},{16,0},{24,8},{1,17},{9,25},{17,1},{25,9},{2,18},{10... | collective-permute-start | bytes 294920 | tf_op jit(solution)/shard_map/ppermute | solution.py:40
  163.4 7.9 %collective-permute-start.22 = (bf16[128,384]{1,0:T(8,128)(2,1)S(1)}, bf16[128,384]{1,0:T(8,128)(2,1)S(1)}, u32[]{:S(2)}, u32[]{:S(2)}) collective-permute-start(bf16[128,384]{1,0:T(8,128)(2,1)S(1)} %get-tuple-element.47), channel_id=1, source_target_pairs={{0,8},{8,16},{16,24},{24,0},{1,9},{9,17},{17,25},{25,1},{2,10},{10... | collective-permute-start | bytes 294920 | tf_op jit(solution)/shard_map/ppermute | solution.py:40
  167.3 7.0 %collective-permute-start.23 = (bf16[128,384]{1,0:T(8,128)(2,1)S(1)}, bf16[128,384]{1,0:T(8,128)(2,1)S(1)}, u32[]{:S(2)}, u32[]{:S(2)}) collective-permute-start(bf16[128,384]{1,0:T(8,128)(2,1)S(1)} %get-tuple-element.46), channel_id=1, source_target_pairs={{0,24},{8,0},{16,8},{24,16},{1,25},{9,1},{17,9},{25,17},{2,26},{10... | collective-permute-start | bytes 294920 | tf_op jit(solution)/shard_map/ppermute | solution.py:40
  176.3 19.4 %all-to-all-start.2 = ((f32[32,1,1]{2,1,0:T(1,128)}), f32[32,1,1]{2,1,0:T(1,128)S(1)}, u32[]{:S(2)}, u32[]{:S(2)}) async-start(f32[32,1,1]{2,1,0:T(1,128)} %broadcast_in_dim.8), calls=%async_computation.2 | async-start | bytes 32768 | tf_op jit(solution)/shard_map/all_to_all | solution.py:175

commit v3 on v2

v3 whole, which is shorter than its diff:
```python
import jax
import jax.numpy as jnp
from jax import lax
from jax.experimental import pallas as pl
from jax.experimental.pallas import tpu as pltpu
from jax.sharding import Mesh
from jax.sharding import PartitionSpec as P

QBLOCK = 128
LANES = 128


outer_decay = 0.9
outer_rate = 0.7
clip_ratio = 2.0
epsilon = 1e-06

AXES = {"z": 8, "y_lo": 2, "y_hi": 4, "x": 4, "core": 2}
REPLICA = ("z", "y_lo")
FSDP = ("y_hi", "x", "core")
CHIPS = AXES["x"] * AXES["y_hi"]


def encode(difference):
    blocks = difference.reshape(-1, QBLOCK)
    scales = (clip_ratio * jnp.sqrt(jnp.mean(blocks * blocks, axis=-1) + epsilon)).astype(
        jnp.bfloat16
    )
    block_codes = jnp.clip(blocks / scales.astype(jnp.float32)[:, None], -1.0, 1.0).astype(
        jnp.bfloat16
    )
    return (block_codes, scales)


def send(value, axis, step):
    size = AXES[axis]
    return lax.ppermute(value, axis, [(i, (i + step) % size) for i in range(size)])


def tied(*values):
    return lax.optimization_barrier(values)


def arrange_kernel(order_ref, inputs_ref, gain_ref, own_ref, other_ref):
    for half, out_ref in enumerate((own_ref, other_ref)):
        for j in range(CHIPS):
            start = pl.multiple_of(order_ref[half * CHIPS + j] * LANES, LANES)
            columns = pl.ds(start, LANES)
            out_ref[:, j * LANES : (j + 1) * LANES] = (
                inputs_ref[:, columns].astype(jnp.float32) * gain_ref[:, columns]
            ).astype(jnp.bfloat16)


def arrange(inputs, feature_gain):
    tokens, features = inputs.shape
    core = lax.axis_index("core")
    chip = jnp.arange(CHIPS) % AXES["y_hi"] * AXES["x"] + jnp.arange(CHIPS) // AXES["y_hi"]
    order = jnp.concatenate([chip * 2 + core, chip * 2 + 1 - core]).astype(jnp.int32)
    half = jax.ShapeDtypeStruct((tokens, features // 2), jnp.bfloat16)
    return pl.pallas_call(
        arrange_kernel,
        out_shape=(half, half),
        in_specs=[
            pl.BlockSpec(memory_space=pltpu.SMEM),
            pl.BlockSpec(memory_space=pltpu.VMEM),
            pl.BlockSpec(memory_space=pltpu.VMEM),
        ],
        out_specs=(pl.BlockSpec(memory_space=pltpu.VMEM),) * 2,
        compiler_params=pltpu.CompilerParams(vmem_limit_bytes=24 << 20),
        name="arrange",
    )(order, inputs, feature_gain[None, :])


def exchange(parts, axis):
    return lax.all_to_all(parts, axis, split_axis=0, concat_axis=0, tiled=True)


def spread(value, axis):
    return exchange(jnp.broadcast_to(value[None], (lax.axis_size(axis), *value.shape)), axis)


def total(arrived):
    return jnp.sum(arrived.astype(jnp.float32), axis=0)


def fragment_codes(global_frag, local_frag):
    difference = global_frag.astype(jnp.float32) - local_frag.astype(jnp.float32)
    block_codes, scales = encode(difference)
    decoded = block_codes.astype(jnp.float32) * scales.astype(jnp.float32)[:, None]
    return decoded.astype(jnp.bfloat16).reshape(lax.axis_size(REPLICA), -1, QBLOCK)


def fragment_update(decoded, global_frag, momentum):
    replicas, rows = decoded.shape[:2]
    share = rows * QBLOCK
    pseudo = total(exchange(decoded, REPLICA)) / replicas
    new_momentum = outer_decay * momentum.reshape(rows, QBLOCK) + pseudo
    offset = lax.axis_index(REPLICA) * share
    own_global = lax.dynamic_slice_in_dim(global_frag, offset, share).reshape(rows, QBLOCK)
    own_next = (
        own_global.astype(jnp.float32) - outer_rate * (pseudo + outer_decay * new_momentum)
    ).astype(jnp.bfloat16)
    return spread(own_next, REPLICA).reshape(-1), new_momentum.reshape(-1)


def shards(inputs, feature_gain, key_weight, teacher_keys, global_frag, local_frag, momentum):
    tokens, features = inputs.shape[1:]
    rows, width = key_weight.shape[1:]

    column = spread(key_weight[0], "y_hi")
    own, other = arrange(inputs[0], feature_gain)
    decoded = fragment_codes(global_frag, local_frag[0])
    column, own, other, decoded = tied(column, own, other, decoded)
    gathered = lax.all_gather(
        column.reshape(AXES["y_hi"] * rows, width), "x", axis=0, tiled=True
    )
    scaled = jnp.concatenate([own, send(other, "core", 1)], axis=0)
    targets = jnp.concatenate([teacher_keys[0], send(teacher_keys[0], "core", 1)], axis=0)
    new_global, new_momentum = fragment_update(decoded, global_frag, momentum)
    gathered, new_global, scaled, targets = tied(gathered, new_global, scaled, targets)

    partial = jnp.dot(scaled, gathered, preferred_element_type=jnp.float32)
    theirs = send(partial, "core", 1)
    projected = partial + jnp.concatenate([theirs[tokens:], theirs[:tokens]], axis=0)
    residual = (projected - targets.astype(jnp.float32)).astype(jnp.bfloat16)
    gradient = lax.dot_general(
        scaled, residual, (((0,), (0,)), ((), ())), preferred_element_type=jnp.float32
    )
    for axis in ("x", "y_hi"):
        gradient = total(
            exchange(gradient.astype(jnp.bfloat16).reshape(AXES[axis], -1, width), axis)
        )

    squares = jnp.sum(gradient * gradient)
    mean_square = jnp.sum(spread(squares[None], FSDP)) / (features * width)
    factor = jnp.minimum(1.0, lax.rsqrt(mean_square + epsilon))
    clipped_grad = (gradient * factor).astype(jnp.bfloat16)[None]
    return (clipped_grad, new_global, new_momentum)


def solution(mesh):
    parted = Mesh(mesh.devices.reshape(tuple(AXES.values())), tuple(AXES))
    return jax.shard_map(
        shards,
        mesh=parted,
        in_specs=(
            P(REPLICA, FSDP, None),
            P(),
            P(REPLICA, FSDP, None),
            P(REPLICA, FSDP, None),
            P(FSDP),
            P(REPLICA, FSDP),
            P(FSDP + REPLICA),
        ),
        out_specs=(P(REPLICA, FSDP, None), P(FSDP), P(FSDP + REPLICA)),
        check_vma=False,
    )
```

time: 200 us -> 162 us (0.81)
  starting transfers between devices: 135 us -> 42.1 us
  blocking collectives: 0 us -> 46.8 us
  between operations: 1.93 us -> 14.9 us
  waiting for transfers between devices: 19.6 us -> 31.6 us
  other arithmetic: 23.2 us -> 11.5 us
  matrix products: 9.71 us -> 6.3 us
    ppermute x27 -> x3, starting transfers between devices: 106 us -> 12.7 us  [send(): lax.ppermute(value, axis, [(i, (i + step) % size) for i in range(size)])]
    all_to_all x0 -> x2, blocking collectives: none -> 46.8 us  [exchange(): return lax.all_to_all(parts, axis, split_axis=0, concat_axis=0, tiled=True)]
    all_to_all x3 -> x4, waiting for transfers between devices: 8.79 us -> 28.6 us  [exchange(): return lax.all_to_all(parts, axis, split_axis=0, concat_axis=0, tiled=True)]
    ppermute x27 -> x3, waiting for transfers between devices: 10.9 us -> 3.02 us  [send(): lax.ppermute(value, axis, [(i, (i + step) % size) for i in range(size)])]
    another operation x4 -> x0, other arithmetic: 6.03 us -> none  [shards(): far = [jnp.stack([f[k] for k in range(4)]) for f in far]]
    dot_general x5 -> x1, matrix products: 4.21 us -> 1.9 us  [shards(): lax.dot_general(scaled, residual, (((0,), (0,)), ((), ())), preferred_ele...]
    convert_element_type x5 -> x2, other arithmetic: 4.8 us -> 2.49 us  [the longest x1 1.58 us: fragment_codes(): local_frag.astype(jnp.float32)]
    all_to_all x3 -> x4, starting transfers between devices: 28.5 us -> 29.4 us  [exchange(): return lax.all_to_all(parts, axis, split_axis=0, concat_axis=0, tiled=True)]
  transfers between devices with their start and end apart: 30 -> 8, of which waited for: 7 -> 5; matrix products, arithmetic and copies ran while one was open for 10% -> 6% of each run, Pallas kernels for 1% -> 1%
where the time goes in v3:
time: 162 us
  blocking collectives  46.8 us (29%)
  starting transfers between devices  42.1 us (26%)
  waiting for transfers between devices  31.6 us (20%)
  between operations  14.9 us (9%)
  other arithmetic  11.5 us (7%)
  local copies, waits for them, and re-layouts  7.16 us (4%)
  matrix products  6.3 us (4%)
    all_to_all x2, blocking collectives, exchange(): return lax.all_to_all(parts, axis, split_axis=0, concat_axis=0, tiled=True)  46.8 us
    all_to_all x4, starting transfers between devices, exchange(): return lax.all_to_all(parts, axis, split_axis=0, concat_axis=0, tiled=True)  29.4 us
    all_to_all x4, waiting for transfers between devices, exchange(): return lax.all_to_all(parts, axis, split_axis=0, concat_axis=0, tiled=True)  28.6 us
    ppermute x3, starting transfers between devices, send(): lax.ppermute(value, axis, [(i, (i + step) % size) for i in range(size)])  12.7 us
    dot_general x1, matrix products, shards(): partial = jnp.dot(scaled, gathered, preferred_element_type=jnp.float32)  4.4 us
    broadcast_in_dim x3, local copies, waits for them, and re-layouts, spread(): jnp.broadcast_to(value[None], (lax.axis_size(axis), *value.shape))  3.92 us
  transfers between devices with their start and end apart: 8, of which 5 were waited for; matrix products, arithmetic and copies ran while one was open for 6% of the time, Pallas kernels for 1%

profile of v3, /device:TPU:1, one launch (start us, length us, event | category | flops | bytes accessed | tf_op | source)
XLA Modules:
  0.0 161.8 jit_solution(18376618645804506872)
XLA Ops:
  7.2 0.0 copy-start.8
  7.2 0.0 copy-start.3
  7.2 0.0 copy-start
  7.2 1.9 %broadcast_in_dim.11 = bf16[4,128,512]{2,1,0:T(8,128)(2,1)} broadcast(bf16[128,512]{1,0:T(8,128)(2,1)} %bitcast.41), dimensions={1,2} | broadcast | bytes 655360 | tf_op jit(solution)/shard_map/broadcast_in_dim | solution.py:79
  9.1 7.6 %all-to-all-start = ((bf16[4,128,512]{2,1,0:T(8,128)(2,1)}), bf16[4,128,512]{2,1,0:T(8,128)(2,1)}, u32[]{:S(2)}, u32[]{:S(2)}) async-start(bf16[4,128,512]{2,1,0:T(8,128)(2,1)} %broadcast_in_dim.11), calls=%async_computation | async-start | bytes 1048576 | tf_op jit(solution)/shard_map/all_to_all | solution.py:75
  16.7 0.0 all-gather.2.cloned.1.call-start
  16.7 1.6 convert_element_type.98
  18.3 0.0 copy-done.8
  18.3 0.9 bitcast_reduce_fusion
  19.2 0.1 reshape.107
  19.3 0.0 copy-start.6
  19.3 0.1 pad_add_fusion.order_ref
  19.4 0.0 copy-done.3
  19.4 0.0 copy-done
  19.4 0.0 copy-start.9
  19.4 1.4 arrange.1
  20.8 0.0 copy-start.1
  20.8 1.1 copy-done.1
  22.0 0.0 copy-start.4
  22.0 1.2 copy-done.4
  23.1 0.0 copy-done.6
  23.1 0.9 multiply_convert_fusion
  24.0 0.0 copy-start.2
  24.0 6.7 %all-to-all-done = bf16[4,128,512]{2,1,0:T(8,128)(2,1)} async-done(((bf16[4,128,512]{2,1,0:T(8,128)(2,1)}), bf16[4,128,512]{2,1,0:T(8,128)(2,1)}, u32[]{:S(2)}, u32[]{:S(2)}) %all-to-all-start) | async-done | bytes 524320 | tf_op jit(solution)/shard_map/all_to_all | solution.py:75
  30.7 0.0 all-gather.2.cloned.1.call-update
  30.7 4.7 %collective-permute-start = (bf16[384,2048]{1,0:T(8,128)(2,1)}, bf16[384,2048]{1,0:T(8,128)(2,1)S(1)}, u32[]{:S(2)}, u32[]{:S(2)}) collective-permute-start(bf16[384,2048]{1,0:T(8,128)(2,1)} %copy-done.4), channel_id=1, source_target_pairs={{0,1},{1,0},{2,3},{3,2},{4,5},{5,4},{6,7},{7,6},{8,9},{9,8},{10,11... | collective-permute-start | bytes 4718600 | tf_op jit(solution)/shard_map/ppermute | solution.py:37
  35.5 9.8 %all-to-all-start.1 = ((bf16[16,64,128]{2,1,0:T(8,128)(2,1)}), bf16[16,64,128]{2,1,0:T(8,128)(2,1)S(1)}, u32[]{:S(2)}, u32[]{:S(2)}) async-start(bf16[16,64,128]{2,1,0:T(8,128)(2,1)} %multiply_convert_fusion), calls=%async_computation.1 | async-start | bytes 524288 | tf_op jit(solution)/shard_map/all_to_all | solution.py:75
  45.3 2.2 %collective-permute-start.1 = (bf16[384,512]{1,0:T(8,128)(2,1)}, bf16[384,512]{1,0:T(8,128)(2,1)}, u32[]{:S(2)}, u32[]{:S(2)}) collective-permute-start(bf16[384,512]{1,0:T(8,128)(2,1)} %bitcast.39), channel_id=1, source_target_pairs={{0,1},{1,0},{2,3},{3,2},{4,5},{5,4},{6,7},{7,6},{8,9},{9,8},{10,11... | collective-permute-start | bytes 1179656 | tf_op jit(solution)/shard_map/ppermute | solution.py:37
  47.5 8.1 %all-to-all-done.1 = bf16[16,64,128]{2,1,0:T(8,128)(2,1)S(1)} async-done(((bf16[16,64,128]{2,1,0:T(8,128)(2,1)}), bf16[16,64,128]{2,1,0:T(8,128)(2,1)S(1)}, u32[]{:S(2)}, u32[]{:S(2)}) %all-to-all-start.1) | async-done | bytes 262176 | tf_op jit(solution)/shard_map/all_to_all | solution.py:75
  55.7 0.0 copy-done.9
  55.7 0.7 fusion.4
  56.5 0.8 broadcast_in_dim.13
  57.2 4.5 %all-to-all-start.2 = ((bf16[16,64,128]{2,1,0:T(8,128)(2,1)}), bf16[16,64,128]{2,1,0:T(8,128)(2,1)S(1)}, u32[]{:S(2)}, u32[]{:S(2)}) async-start(bf16[16,64,128]{2,1,0:T(8,128)(2,1)} %broadcast_in_dim.13), calls=%async_computation.2 | async-start | bytes 524288 | tf_op jit(solution)/shard_map/all_to_all | solution.py:75
  61.7 0.0 collective-permute-done.1
  61.7 2.1 %pad_maximum_fusion.1 = bf16[768,512]{1,0:T(8,128)(2,1)} fusion(bf16[384,512]{1,0:T(8,128)(2,1)} %collective-permute-done.1, bf16[384,512]{1,0:T(8,128)(2,1)} %bitcast.40), kind=kLoop, calls=%fused_computation.6 | loop fusion | flops 1572864 | bytes 1572864 | tf_op jit(solution)/shard_map/concatenate | solution.py:118
  63.8 0.0 collective-permute-done
  63.8 0.0 copy-done.2
  63.8 1.9 %pad_maximum_fusion = bf16[768,2048]{1,0:T(8,128)(2,1)} fusion(bf16[384,2048]{1,0:T(8,128)(2,1)S(1)} %collective-permute-done, bf16[384,2048]{1,0:T(8,128)(2,1)S(1)} %copy-done.2), kind=kLoop, calls=%fused_computation | loop fusion | flops 6291456 | bytes 6291456 | tf_op jit(solution)/shard_map/concatenate | solution.py:117
  65.7 5.0 %all-to-all-done.2 = bf16[16,64,128]{2,1,0:T(8,128)(2,1)S(1)} async-done(((bf16[16,64,128]{2,1,0:T(8,128)(2,1)}), bf16[16,64,128]{2,1,0:T(8,128)(2,1)S(1)}, u32[]{:S(2)}, u32[]{:S(2)}) %all-to-all-start.2) | async-done | bytes 262176 | tf_op jit(solution)/shard_map/all_to_all | solution.py:75
  70.6 0.0 all-gather.2.cloned.1.call-done
  70.6 0.0 copy-start.7
  70.6 4.4 %fusion.14 = f32[768,512]{1,0:T(8,128)S(1)} fusion(bf16[768,2048]{1,0:T(8,128)(2,1)} %pad_maximum_fusion, bf16[2048,512]{1,0:T(8,128)(2,1)} %all-gather.2.cloned.1.call-done), kind=kOutput, calls=%fused_computation.36 | convolution fusion | flops 1610612736 | bytes 6815744 | tf_op jit(solution)/shard_map/dot_general | solution.py:122
  75.0 0.0 copy-start.5
  75.1 5.7 %collective-permute-start.2 = (f32[768,512]{1,0:T(8,128)S(1)}, f32[768,512]{1,0:T(8,128)S(1)}, u32[]{:S(2)}, u32[]{:S(2)}) collective-permute-start(f32[768,512]{1,0:T(8,128)S(1)} %fusion.14), channel_id=1, source_target_pairs={{0,1},{1,0},{2,3},{3,2},{4,5},{5,4},{6,7},{7,6},{8,9},{9,8},{10,11... | collective-permute-start | bytes 4718600 | tf_op jit(solution)/shard_map/ppermute | solution.py:37
  80.8 3.0 %collective-permute-done.2 = f32[768,512]{1,0:T(8,128)S(1)} collective-permute-done((f32[768,512]{1,0:T(8,128)S(1)}, f32[768,512]{1,0:T(8,128)S(1)}, u32[]{:S(2)}, u32[]{:S(2)}) %collective-permute-start.2) | collective-permute-done | bytes 1572896 | tf_op jit(solution)/shard_map/ppermute | solution.py:37
  83.8 0.1 fusion.13
  83.9 0.0 copy-done.7
  83.9 0.0 copy-done.5
  83.9 1.9 %convolution_convert_fusion = bf16[2048,512]{1,0:T(8,128)(2,1)S(1)} fusion(bf16[768,2048]{1,0:T(8,128)(2,1)S(1)} %copy-done.5, f32[768,512]{1,0:T(8,128)S(1)} %fusion.14, f32[384,512]{1,0:T(8,128)S(1)} %get-tuple-element.26, f32[384,512]{1,0:T(8,128)S(1)} %get-tuple-element.25, bf16[768,512]{1,0:T(8,128)(2,1)S(1)} %copy-done.7), kind=kOutput, calls=%fused_computation.1 | convolution fusion | flops 1613627392 | bytes 9175040 | tf_op jit(solution)/shard_map/dot_general | solution.py:126
  85.8 29.4 %all_to_all.31 = bf16[4,512,512]{2,1,0:T(8,128)(2,1)S(1)} all-to-all(bf16[4,512,512]{2,1,0:T(8,128)(2,1)S(1)} %bitcast.34), channel_id=1, replica_groups=mesh['z'=8,'y_lo'=2,'y_hi'=4,'x'=4,'core'=2] {'x'}, dimensions={0} | all-to-all | bytes 4194304 | tf_op jit(solution)/shard_map/all_to_all | solution.py:75
  115.2 0.6 reduce_sum.59
  115.9 17.5 %all_to_all.32 = bf16[4,128,512]{2,1,0:T(8,128)(2,1)S(1)} all-to-all(bf16[4,128,512]{2,1,0:T(8,128)(2,1)S(1)} %bitcast.37), channel_id=1, replica_groups=mesh['z'=8,'y_lo'=2,'y_hi'=4,'x'=4,'core'=2] {'y_hi'}, dimensions={0} | all-to-all | bytes 1048576 | tf_op jit(solution)/shard_map/all_to_all | solution.py:75
  133.3 0.1 convert_reduce_fusion
  133.4 0.7 multiply_reduce_fusion
  134.1 1.3 broadcast_in_dim.28
  135.3 7.5 %all-to-all-start.5 = ((f32[32,1,1]{2,1,0:T(1,128)}), f32[32,1,1]{2,1,0:T(1,128)S(1)}, u32[]{:S(2)}, u32[]{:S(2)}) async-start(f32[32,1,1]{2,1,0:T(1,128)} %broadcast_in_dim.28), calls=%async_computation.5 | async-start | bytes 32768 | tf_op jit(solution)/shard_map/all_to_all | solution.py:75
  142.8 0.6 bitcast_add_fusion
  143.4 8.8 %all-to-all-done.5 = f32[32,1,1]{2,1,0:T(1,128)S(1)} async-done(((f32[32,1,1]{2,1,0:T(1,128)}), f32[32,1,1]{2,1,0:T(1,128)S(1)}, u32[]{:S(2)}, u32[]{:S(2)}) %all-to-all-start.5) | async-done | bytes 160 | tf_op jit(solution)/shard_map/all_to_all | solution.py:75
  152.2 0.6 reduce_sum.62
  153.5 0.7 fusion.3
  154.2 0.7 copy.13
  (3 shorter events, 0.1 us)
Async XLA Ops:
  7.2 11.2 %copy-start.8 = (bf16[131072]{0:T(1024)(128)(2,1)S(1)}, bf16[131072]{0:T(1024)(128)(2,1)}, u32[]{:S(2)}) copy-start(bf16[131072]{0:T(1024)(128)(2,1)} %param.11) | copy-start | bytes 786436
  7.2 12.2 %copy-start.3 = (f32[4096]{0:T(1024)S(1)}, f32[4096]{0:T(1024)}, u32[]{:S(2)}) copy-start(f32[4096]{0:T(1024)} %param.8) | copy-start | bytes 49156
  7.2 12.2 %copy-start = (bf16[1,384,4096]{2,1,0:T(8,128)(2,1)S(1)}, bf16[1,384,4096]{2,1,0:T(8,128)(2,1)}, u32[]{:S(2)}) copy-start(bf16[1,384,4096]{2,1,0:T(8,128)(2,1)} %param.7) | copy-start | bytes 9437188
  9.1 21.6 %all-to-all-start = ((bf16[4,128,512]{2,1,0:T(8,128)(2,1)}), bf16[4,128,512]{2,1,0:T(8,128)(2,1)}, u32[]{:S(2)}, u32[]{:S(2)}) async-start(bf16[4,128,512]{2,1,0:T(8,128)(2,1)} %broadcast_in_dim.11), calls=%async_computation | async-start | bytes 1048576 | tf_op jit(solution)/shard_map/all_to_all | solution.py:75
  16.7 53.9 %all-gather.2.cloned.1.call-start = ((), (), s32[]{:S(2)}) async-start(), calls=%async_computation.6 | async-start | bytes 2621440 | tf_op jit(solution)/shard_map/all_gather | solution.py:114
  19.3 3.8 %copy-start.6 = (f32[131072]{0:T(1024)S(1)}, f32[131072]{0:T(1024)}, u32[]{:S(2)}) copy-start(f32[131072]{0:T(1024)} %get-tuple-element.24) | copy-start | bytes 1572868
  19.4 36.3 %copy-start.9 = (f32[8192]{0:T(1024)S(1)}, f32[8192]{0:T(1024)}, u32[]{:S(2)}) copy-start(f32[8192]{0:T(1024)} %param.13) | copy-start | bytes 98308
  20.8 1.2 copy-start.1
  22.0 1.2 copy-start.4
  24.0 39.8 %copy-start.2 = (bf16[384,2048]{1,0:T(8,128)(2,1)S(1)}, bf16[384,2048]{1,0:T(8,128)(2,1)}, u32[]{:S(2)}) copy-start(bf16[384,2048]{1,0:T(8,128)(2,1)} %copy-done.1) | copy-start | bytes 4718596
  30.7 33.1 %collective-permute-start = (bf16[384,2048]{1,0:T(8,128)(2,1)}, bf16[384,2048]{1,0:T(8,128)(2,1)S(1)}, u32[]{:S(2)}, u32[]{:S(2)}) collective-permute-start(bf16[384,2048]{1,0:T(8,128)(2,1)} %copy-done.4), channel_id=1, source_target_pairs={{0,1},{1,0},{2,3},{3,2},{4,5},{5,4},{6,7},{7,6},{8,9},{9,8},{10,11... | collective-permute-start | bytes 4718600 | tf_op jit(solution)/shard_map/ppermute | solution.py:37
  35.5 20.2 %all-to-all-start.1 = ((bf16[16,64,128]{2,1,0:T(8,128)(2,1)}), bf16[16,64,128]{2,1,0:T(8,128)(2,1)S(1)}, u32[]{:S(2)}, u32[]{:S(2)}) async-start(bf16[16,64,128]{2,1,0:T(8,128)(2,1)} %multiply_convert_fusion), calls=%async_computation.1 | async-start | bytes 524288 | tf_op jit(solution)/shard_map/all_to_all | solution.py:75
  45.3 16.4 %collective-permute-start.1 = (bf16[384,512]{1,0:T(8,128)(2,1)}, bf16[384,512]{1,0:T(8,128)(2,1)}, u32[]{:S(2)}, u32[]{:S(2)}) collective-permute-start(bf16[384,512]{1,0:T(8,128)(2,1)} %bitcast.39), channel_id=1, source_target_pairs={{0,1},{1,0},{2,3},{3,2},{4,5},{5,4},{6,7},{7,6},{8,9},{9,8},{10,11... | collective-permute-start | bytes 1179656 | tf_op jit(solution)/shard_map/ppermute | solution.py:37
  57.2 13.4 %all-to-all-start.2 = ((bf16[16,64,128]{2,1,0:T(8,128)(2,1)}), bf16[16,64,128]{2,1,0:T(8,128)(2,1)S(1)}, u32[]{:S(2)}, u32[]{:S(2)}) async-start(bf16[16,64,128]{2,1,0:T(8,128)(2,1)} %broadcast_in_dim.13), calls=%async_computation.2 | async-start | bytes 524288 | tf_op jit(solution)/shard_map/all_to_all | solution.py:75
  70.6 13.3 %copy-start.7 = (bf16[768,512]{1,0:T(8,128)(2,1)S(1)}, bf16[768,512]{1,0:T(8,128)(2,1)}, u32[]{:S(2)}) copy-start(bf16[768,512]{1,0:T(8,128)(2,1)} %pad_maximum_fusion.1) | copy-start | bytes 2359300
  75.0 8.9 %copy-start.5 = (bf16[768,2048]{1,0:T(8,128)(2,1)S(1)}, bf16[768,2048]{1,0:T(8,128)(2,1)}, u32[]{:S(2)}) copy-start(bf16[768,2048]{1,0:T(8,128)(2,1)} %pad_maximum_fusion) | copy-start | bytes 9437188
  75.1 8.7 %collective-permute-start.2 = (f32[768,512]{1,0:T(8,128)S(1)}, f32[768,512]{1,0:T(8,128)S(1)}, u32[]{:S(2)}, u32[]{:S(2)}) collective-permute-start(f32[768,512]{1,0:T(8,128)S(1)} %fusion.14), channel_id=1, source_target_pairs={{0,1},{1,0},{2,3},{3,2},{4,5},{5,4},{6,7},{7,6},{8,9},{9,8},{10,11... | collective-permute-start | bytes 4718600 | tf_op jit(solution)/shard_map/ppermute | solution.py:37
  135.3 16.9 %all-to-all-start.5 = ((f32[32,1,1]{2,1,0:T(1,128)}), f32[32,1,1]{2,1,0:T(1,128)S(1)}, u32[]{:S(2)}, u32[]{:S(2)}) async-start(f32[32,1,1]{2,1,0:T(1,128)} %broadcast_in_dim.28), calls=%async_computation.5 | async-start | bytes 32768 | tf_op jit(solution)/shard_map/all_to_all | solution.py:75
Sparse Core Ops, SparseCore 0:
  30.8 39.5 all-gather.1

commit v4 on v3

--- a/solution.py
+++ b/solution.py
@@ -1,3 +1,5 @@
+import functools
+
 import jax
 import jax.numpy as jnp
 from jax import lax
@@ -19,6 +21,7 @@
 REPLICA = ("z", "y_lo")
 FSDP = ("y_hi", "x", "core")
 CHIPS = AXES["x"] * AXES["y_hi"]
+STEPS = (2, 1, 3)
 
 
 def encode(difference):
@@ -53,8 +56,9 @@
 
 def arrange(inputs, feature_gain):
     tokens, features = inputs.shape
-    core = lax.axis_index("core")
-    chip = jnp.arange(CHIPS) % AXES["y_hi"] * AXES["x"] + jnp.arange(CHIPS) // AXES["y_hi"]
+    x, y, core = (lax.axis_index(name) for name in ("x", "y_hi", "core"))
+    rx, ry = jnp.arange(CHIPS) // AXES["y_hi"], jnp.arange(CHIPS) % AXES["y_hi"]
+    chip = (y + ry) % AXES["y_hi"] * AXES["x"] + (x + rx) % AXES["x"]
     order = jnp.concatenate([chip * 2 + core, chip * 2 + 1 - core]).astype(jnp.int32)
     half = jax.ShapeDtypeStruct((tokens, features // 2), jnp.bfloat16)
     return pl.pallas_call(
@@ -79,8 +83,8 @@
     return exchange(jnp.broadcast_to(value[None], (lax.axis_size(axis), *value.shape)), axis)
 
 
-def total(arrived):
-    return jnp.sum(arrived.astype(jnp.float32), axis=0)
+def total(values):
+    return functools.reduce(jnp.add, [value.astype(jnp.float32) for value in values])
 
 
 def fragment_codes(global_frag, local_frag):
@@ -90,10 +94,10 @@
     return decoded.astype(jnp.bfloat16).reshape(lax.axis_size(REPLICA), -1, QBLOCK)
 
 
-def fragment_update(decoded, global_frag, momentum):
-    replicas, rows = decoded.shape[:2]
+def fragment_update(arrived, global_frag, momentum):
+    replicas, rows = arrived.shape[:2]
     share = rows * QBLOCK
-    pseudo = total(exchange(decoded, REPLICA)) / replicas
+    pseudo = jnp.sum(arrived.astype(jnp.float32), axis=0) / replicas
     new_momentum = outer_decay * momentum.reshape(rows, QBLOCK) + pseudo
     offset = lax.axis_index(REPLICA) * share
     own_global = lax.dynamic_slice_in_dim(global_frag, offset, share).reshape(rows, QBLOCK)
@@ -107,29 +111,38 @@
     tokens, features = inputs.shape[1:]
     rows, width = key_weight.shape[1:]
 
-    column = spread(key_weight[0], "y_hi")
+    weight = key_weight[0]
+    near = [weight] + [None] * 3
+    for k in STEPS:
+        near[k] = send(weight, "y_hi", -k)
+    arrived = exchange(fragment_codes(global_frag, local_frag[0]), REPLICA)
+    column = jnp.concatenate(near, axis=0)
     own, other = arrange(inputs[0], feature_gain)
-    decoded = fragment_codes(global_frag, local_frag[0])
-    column, own, other, decoded = tied(column, own, other, decoded)
-    gathered = lax.all_gather(
-        column.reshape(AXES["y_hi"] * rows, width), "x", axis=0, tiled=True
-    )
+    column, arrived, own, other = tied(column, arrived, own, other)
+    far = {k: send(column, "x", -k) for k in STEPS}
     scaled = jnp.concatenate([own, send(other, "core", 1)], axis=0)
     targets = jnp.concatenate([teacher_keys[0], send(teacher_keys[0], "core", 1)], axis=0)
-    new_global, new_momentum = fragment_update(decoded, global_frag, momentum)
-    gathered, new_global, scaled, targets = tied(gathered, new_global, scaled, targets)
+    scaled, targets = tied(scaled, targets)
+    group = scaled.shape[1] // AXES["x"]
+    blocks = [scaled[:, k * group : (k + 1) * group] for k in range(AXES["x"])]
+    partial = jnp.dot(blocks[0], column, preferred_element_type=jnp.float32)
+    new_global, new_momentum = fragment_update(arrived, global_frag, momentum)
+    for k in STEPS:
+        partial += jnp.dot(blocks[k], far[k], preferred_element_type=jnp.float32)
+    partial, new_global = tied(partial, new_global)
 
-    partial = jnp.dot(scaled, gathered, preferred_element_type=jnp.float32)
     theirs = send(partial, "core", 1)
     projected = partial + jnp.concatenate([theirs[tokens:], theirs[:tokens]], axis=0)
     residual = (projected - targets.astype(jnp.float32)).astype(jnp.bfloat16)
-    gradient = lax.dot_general(
-        scaled, residual, (((0,), (0,)), ((), ())), preferred_element_type=jnp.float32
-    )
-    for axis in ("x", "y_hi"):
-        gradient = total(
-            exchange(gradient.astype(jnp.bfloat16).reshape(AXES[axis], -1, width), axis)
-        )
+    gradient = [
+        lax.dot_general(
+            block, residual, (((0,), (0,)), ((), ())), preferred_element_type=jnp.float32
+        ).astype(jnp.bfloat16)
+        for block in blocks
+    ]
+    mine = total([gradient[0]] + [send(gradient[k], "x", k) for k in STEPS])
+    mine = mine.astype(jnp.bfloat16).reshape(AXES["y_hi"], rows, width)
+    gradient = total([mine[0]] + [send(mine[k], "y_hi", k) for k in STEPS])
 
     squares = jnp.sum(gradient * gradient)
     mean_square = jnp.sum(spread(squares[None], FSDP)) / (features * width)

time: 162 us -> 163 us (level)
  blocking collectives: 46.8 us -> 0 us
  starting transfers between devices: 42.1 us -> 88.3 us
  between operations: 14.9 us -> 1.71 us
  waiting for transfers between devices: 31.6 us -> 42 us
  other arithmetic: 11.5 us -> 13.6 us
  matrix products: 6.3 us -> 8.33 us
    all_to_all x2 -> x0, blocking collectives: 46.8 us -> none  [exchange(): return lax.all_to_all(parts, axis, split_axis=0, concat_axis=0, tiled=True)]
    ppermute x3 -> x15, starting transfers between devices: 12.7 us -> 56.3 us  [send(): lax.ppermute(value, axis, [(i, (i + step) % size) for i in range(size)])]
    ppermute x3 -> x15, waiting for transfers between devices: 3.02 us -> 33.3 us  [send(): lax.ppermute(value, axis, [(i, (i + step) % size) for i in range(size)])]
    all_to_all x4 -> x3, waiting for transfers between devices: 28.6 us -> 8.7 us  [exchange(): return lax.all_to_all(parts, axis, split_axis=0, concat_axis=0, tiled=True)]
    all_to_all x4 -> x3, starting transfers between devices: 29.4 us -> 32 us  [exchange(): return lax.all_to_all(parts, axis, split_axis=0, concat_axis=0, tiled=True)]
    dot_general x2 -> x8, matrix products: 6.3 us -> 8.33 us  [the longest x3 5.24 us: shards(): partial += jnp.dot(blocks[k], far[k], preferred_element_type=jnp.float32)]
    broadcast_in_dim x3 -> x2, local copies, waits for them, and re-layouts: 3.92 us -> 2.01 us  [spread(): jnp.broadcast_to(value[None], (lax.axis_size(axis), *value.shape))]
    unnamed x21 -> x17, local copies, waits for them, and re-layouts: 3.05 us -> 4.46 us
  transfers between devices with their start and end apart: 8 -> 18, of which waited for: 5 -> 9; matrix products, arithmetic and copies ran while one was open for 6% -> 7% of each run, Pallas kernels for 1% -> 1%
where the time goes in v4:
time: 163 us; the launch traced here: 162 us
  starting transfers between devices  88.3 us (54%)
  waiting for transfers between devices  42 us (26%)
  other arithmetic  13.6 us (8%)
  matrix products  8.33 us (5%)
  local copies, waits for them, and re-layouts  6.69 us (4%)
  between operations  1.71 us (1%)
    ppermute x15, starting transfers between devices, send(): lax.ppermute(value, axis, [(i, (i + step) % size) for i in range(size)])  56.3 us
    ppermute x15, waiting for transfers between devices, send(): lax.ppermute(value, axis, [(i, (i + step) % size) for i in range(size)])  33.3 us
    all_to_all x3, starting transfers between devices, exchange(): return lax.all_to_all(parts, axis, split_axis=0, concat_axis=0, tiled=True)  32 us
    all_to_all x3, waiting for transfers between devices, exchange(): return lax.all_to_all(parts, axis, split_axis=0, concat_axis=0, tiled=True)  8.7 us
    dot_general x3, matrix products, shards(): partial += jnp.dot(blocks[k], far[k], preferred_element_type=jnp.float32)  5.24 us
    unnamed x17, local copies, waits for them, and re-layouts  4.46 us
  transfers between devices with their start and end apart: 18, of which 9 were waited for; matrix products, arithmetic and copies ran while one was open for 7% of the time, Pallas kernels for 1%

profile of v4, /device:TPU:1, one launch (start us, length us, event | category | flops | bytes accessed | tf_op | source)
XLA Modules:
  0.0 162.0 jit_solution(11845026166629451060)
XLA Ops:
  0.6 1.7 %convert_element_type.129 = f32[1,131072]{1,0:T(1,128)S(1)} convert(bf16[1,131072]{1,0:T(2,128)(2,1)} %param.12) | non-fusion elementwise | flops 131072 | bytes 786432 | tf_op jit(solution)/shard_map/convert_element_type | solution.py:91
  2.4 0.0 copy-start.3
  2.4 1.8 %bitcast_reduce_fusion = (f32[1024]{0:T(1024)S(1)}, f32[131072]{0:T(1024)}) fusion(f32[131072]{0:T(1024)S(1)} %bitcast.37, bf16[131072]{0:T(1024)(128)(2,1)} %param.11), kind=kLoop, calls=%fused_computation.28 | loop fusion | flops 523264 | bytes 1314816 | tf_op jit(solution)/shard_map/reduce_sum | solution.py:29
  4.2 0.1 reshape.91
  4.3 2.0 %multiply_convert_fusion = bf16[16,64,128]{2,1,0:T(8,128)(2,1)} fusion(f32[16,64]{1,0:T(8,128)S(1)} %reshape.91, f32[16,64,128]{2,1,0:T(8,128)} %bitcast.36), kind=kLoop, calls=%fused_computation.30 | loop fusion | flops 786432 | bytes 790528 | tf_op jit(solution)/shard_map/convert_element_type | solution.py:94
  6.3 12.0 %all-to-all-start = ((bf16[16,64,128]{2,1,0:T(8,128)(2,1)}), bf16[16,64,128]{2,1,0:T(8,128)(2,1)S(1)}, u32[]{:S(2)}, u32[]{:S(2)}) async-start(bf16[16,64,128]{2,1,0:T(8,128)(2,1)} %multiply_convert_fusion), calls=%async_computation | async-start | bytes 524288 | tf_op jit(solution)/shard_map/all_to_all | solution.py:79
  18.2 5.0 %collective-permute-start = (bf16[128,512]{1,0:T(8,128)(2,1)}, bf16[128,512]{1,0:T(8,128)(2,1)}, u32[]{:S(2)}, u32[]{:S(2)}) collective-permute-start(bf16[128,512]{1,0:T(8,128)(2,1)} %bitcast), channel_id=1, source_target_pairs={{0,24},{8,0},{16,8},{24,16},{1,25},{9,1},{17,9},{25,17},{2,26},{10... | collective-permute-start | bytes 393224 | tf_op jit(solution)/shard_map/ppermute | solution.py:40
  23.2 4.4 %collective-permute-start.1 = (bf16[128,512]{1,0:T(8,128)(2,1)}, bf16[128,512]{1,0:T(8,128)(2,1)}, u32[]{:S(2)}, u32[]{:S(2)}) collective-permute-start(bf16[128,512]{1,0:T(8,128)(2,1)} %bitcast), channel_id=1, source_target_pairs={{0,16},{8,24},{16,0},{24,8},{1,17},{9,25},{17,1},{25,9},{2,18},{10... | collective-permute-start | bytes 393224 | tf_op jit(solution)/shard_map/ppermute | solution.py:40
  27.7 3.3 %collective-permute-start.2 = (bf16[128,512]{1,0:T(8,128)(2,1)}, bf16[128,512]{1,0:T(8,128)(2,1)}, u32[]{:S(2)}, u32[]{:S(2)}) collective-permute-start(bf16[128,512]{1,0:T(8,128)(2,1)} %bitcast), channel_id=1, source_target_pairs={{0,8},{8,16},{16,24},{24,0},{1,9},{9,17},{17,25},{25,1},{2,10},{10... | collective-permute-start | bytes 393224 | tf_op jit(solution)/shard_map/ppermute | solution.py:40
  31.0 0.1 pad_add_fusion.order_ref
  31.1 1.4 arrange.1
  32.6 1.2 copy-done.1
  33.7 1.1 copy-done.4
  34.9 0.0 collective-permute-done
  34.9 0.0 collective-permute-done.1
  34.9 1.9 %collective-permute-done.2 = bf16[128,512]{1,0:T(8,128)(2,1)} collective-permute-done((bf16[128,512]{1,0:T(8,128)(2,1)}, bf16[128,512]{1,0:T(8,128)(2,1)}, u32[]{:S(2)}, u32[]{:S(2)}) %collective-permute-start.2) | collective-permute-done | bytes 131104 | tf_op jit(solution)/shard_map/ppermute | solution.py:40
  36.8 1.1 pad_maximum_fusion.2
  37.9 0.0 all-to-all-done
  37.9 5.0 %collective-permute-start.3 = (bf16[384,2048]{1,0:T(8,128)(2,1)}, bf16[384,2048]{1,0:T(8,128)(2,1)}, u32[]{:S(2)}, u32[]{:S(2)}) collective-permute-start(bf16[384,2048]{1,0:T(8,128)(2,1)} %copy-done.4), channel_id=1, source_target_pairs={{0,1},{1,0},{2,3},{3,2},{4,5},{5,4},{6,7},{7,6},{8,9},{9,8},{10,11... | collective-permute-start | bytes 4718600 | tf_op jit(solution)/shard_map/ppermute | solution.py:40
  42.9 1.9 %collective-permute-start.4 = (bf16[384,512]{1,0:T(8,128)(2,1)}, bf16[384,512]{1,0:T(8,128)(2,1)}, u32[]{:S(2)}, u32[]{:S(2)}) collective-permute-start(bf16[384,512]{1,0:T(8,128)(2,1)} %bitcast.39), channel_id=1, source_target_pairs={{0,1},{1,0},{2,3},{3,2},{4,5},{5,4},{6,7},{7,6},{8,9},{9,8},{10,11... | collective-permute-start | bytes 1179656 | tf_op jit(solution)/shard_map/ppermute | solution.py:40
  44.9 2.0 %collective-permute-done.4 = bf16[384,512]{1,0:T(8,128)(2,1)} collective-permute-done((bf16[384,512]{1,0:T(8,128)(2,1)}, bf16[384,512]{1,0:T(8,128)(2,1)}, u32[]{:S(2)}, u32[]{:S(2)}) %collective-permute-start.4) | collective-permute-done | bytes 393248 | tf_op jit(solution)/shard_map/ppermute | solution.py:40
  46.9 1.2 pad_maximum_fusion.1
  48.1 4.7 %collective-permute-start.5 = (bf16[512,512]{1,0:T(8,128)(2,1)S(1)}, bf16[512,512]{1,0:T(8,128)(2,1)}, u32[]{:S(2)}, u32[]{:S(2)}) collective-permute-start(bf16[512,512]{1,0:T(8,128)(2,1)S(1)} %pad_maximum_fusion.2), channel_id=1, source_target_pairs={{0,4},{2,6},{4,0},{6,2},{1,5},{3,7},{5,1},{7,3},{8,12},{10,14},{12... | collective-permute-start | bytes 1572872 | tf_op jit(solution)/shard_map/ppermute | solution.py:40
  52.7 2.8 %collective-permute-start.6 = (bf16[512,512]{1,0:T(8,128)(2,1)S(1)}, bf16[512,512]{1,0:T(8,128)(2,1)}, u32[]{:S(2)}, u32[]{:S(2)}) collective-permute-start(bf16[512,512]{1,0:T(8,128)(2,1)S(1)} %pad_maximum_fusion.2), channel_id=1, source_target_pairs={{0,6},{2,0},{4,2},{6,4},{1,7},{3,1},{5,3},{7,5},{8,14},{10,8},{12,... | collective-permute-start | bytes 1572872 | tf_op jit(solution)/shard_map/ppermute | solution.py:40
  55.5 2.5 %collective-permute-start.7 = (bf16[512,512]{1,0:T(8,128)(2,1)S(1)}, bf16[512,512]{1,0:T(8,128)(2,1)}, u32[]{:S(2)}, u32[]{:S(2)}) collective-permute-start(bf16[512,512]{1,0:T(8,128)(2,1)S(1)} %pad_maximum_fusion.2), channel_id=1, source_target_pairs={{0,2},{2,4},{4,6},{6,0},{1,3},{3,5},{5,7},{7,1},{8,10},{10,12},{12... | collective-permute-start | bytes 1572872 | tf_op jit(solution)/shard_map/ppermute | solution.py:40
  58.1 0.7 fusion.22
  58.8 0.8 broadcast_in_dim.9
  59.6 9.9 %all-to-all-start.1 = ((bf16[16,64,128]{2,1,0:T(8,128)(2,1)}), bf16[16,64,128]{2,1,0:T(8,128)(2,1)S(1)}, u32[]{:S(2)}, u32[]{:S(2)}) async-start(bf16[16,64,128]{2,1,0:T(8,128)(2,1)} %broadcast_in_dim.9), calls=%async_computation.1 | async-start | bytes 524288 | tf_op jit(solution)/shard_map/all_to_all | solution.py:79
  69.5 1.8 %pad_maximum_fusion = bf16[768,2048]{1,0:T(8,128)(2,1)S(1)} fusion(bf16[384,2048]{1,0:T(8,128)(2,1)} %collective-permute-done.3, bf16[384,2048]{1,0:T(8,128)(2,1)S(1)} %copy-done.2), kind=kLoop, calls=%fused_computation | loop fusion | flops 6291456 | bytes 6291456 | tf_op jit(solution)/shard_map/concatenate | solution.py:123
  71.3 0.6 fusion.19
  71.9 2.0 %fusion.16 = f32[768,512]{1,0:T(8,128)S(1)} fusion(bf16[512,512]{1,0:T(8,128)(2,1)} %collective-permute-done.5, bf16[768,2048]{1,0:T(8,128)(2,1)S(1)} %pad_maximum_fusion), kind=kOutput, calls=%fused_computation.22 | convolution fusion | flops 402653184 | bytes 2883584 | tf_op jit(solution)/shard_map/dot_general | solution.py:131
  73.9 2.2 %collective-permute-done.6 = bf16[512,512]{1,0:T(8,128)(2,1)} collective-permute-done((bf16[512,512]{1,0:T(8,128)(2,1)S(1)}, bf16[512,512]{1,0:T(8,128)(2,1)}, u32[]{:S(2)}, u32[]{:S(2)}) %collective-permute-start.6) | collective-permute-done | bytes 524320 | tf_op jit(solution)/shard_map/ppermute | solution.py:40
  76.1 1.6 fusion.13
  77.7 0.0 collective-permute-done.7
  77.8 1.6 %add_add_fusion = f32[768,512]{1,0:T(8,128)S(1)} fusion(f32[768,512]{1,0:T(8,128)S(1)} %fusion.13, f32[768,512]{1,0:T(8,128)S(1)} %fusion.19, f32[768,512]{1,0:T(8,128)S(1)} %fusion.16, bf16[512,512]{1,0:T(8,128)(2,1)} %collective-permute-done.7, bf16[768,2048]{1,0:T(8,128)(2,1)S(1)} %pad_maximum_fusion), kind=kOutput, calls=%fused_computation.4 | convolution fusion | flops 403832832 | bytes 7602176 | tf_op jit(solution)/shard_map/dot_general | solution.py:131
  79.4 0.0 all-to-all-done.1
  79.4 4.5 %collective-permute-start.8 = (f32[768,512]{1,0:T(8,128)S(1)}, f32[768,512]{1,0:T(8,128)S(1)}, u32[]{:S(2)}, u32[]{:S(2)}) collective-permute-start(f32[768,512]{1,0:T(8,128)S(1)} %add_add_fusion), channel_id=1, source_target_pairs={{0,1},{1,0},{2,3},{3,2},{4,5},{5,4},{6,7},{7,6},{8,9},{9,8},{10,11... | collective-permute-start | bytes 4718600 | tf_op jit(solution)/shard_map/ppermute | solution.py:40
  83.9 3.0 %collective-permute-done.8 = f32[768,512]{1,0:T(8,128)S(1)} collective-permute-done((f32[768,512]{1,0:T(8,128)S(1)}, f32[768,512]{1,0:T(8,128)S(1)}, u32[]{:S(2)}, u32[]{:S(2)}) %collective-permute-start.8) | collective-permute-done | bytes 1572896 | tf_op jit(solution)/shard_map/ppermute | solution.py:40
  86.9 0.1 fusion.34
  87.0 0.5 fusion.1
  87.5 1.4 copy-done.6
  88.9 0.6 convolution_convert_fusion.2
  89.5 0.6 convolution_convert_fusion.1
  90.1 0.6 convolution_convert_fusion
  90.8 2.6 %collective-permute-start.9 = (bf16[512,512]{1,0:T(8,128)(2,1)S(1)}, bf16[512,512]{1,0:T(8,128)(2,1)S(1)}, u32[]{:S(2)}, u32[]{:S(2)}) collective-permute-start(bf16[512,512]{1,0:T(8,128)(2,1)S(1)} %convolution_convert_fusion.2), channel_id=1, source_target_pairs={{0,4},{2,6},{4,0},{6,2},{1,5},{3,7},{5,1},{7,3},{8,12},{10,14},{12... | collective-permute-start | bytes 1572872 | tf_op jit(solution)/shard_map/ppermute | solution.py:40
  93.3 3.9 %collective-permute-start.10 = (bf16[512,512]{1,0:T(8,128)(2,1)S(1)}, bf16[512,512]{1,0:T(8,128)(2,1)S(1)}, u32[]{:S(2)}, u32[]{:S(2)}) collective-permute-start(bf16[512,512]{1,0:T(8,128)(2,1)S(1)} %convolution_convert_fusion.1), channel_id=1, source_target_pairs={{0,2},{2,4},{4,6},{6,0},{1,3},{3,5},{5,7},{7,1},{8,10},{10,12},{12... | collective-permute-start | bytes 1572872 | tf_op jit(solution)/shard_map/ppermute | solution.py:40
  97.2 2.6 %collective-permute-start.11 = (bf16[512,512]{1,0:T(8,128)(2,1)S(1)}, bf16[512,512]{1,0:T(8,128)(2,1)S(1)}, u32[]{:S(2)}, u32[]{:S(2)}) collective-permute-start(bf16[512,512]{1,0:T(8,128)(2,1)S(1)} %convolution_convert_fusion), channel_id=1, source_target_pairs={{0,6},{2,0},{4,2},{6,4},{1,7},{3,1},{5,3},{7,5},{8,14},{10,8},{12,... | collective-permute-start | bytes 1572872 | tf_op jit(solution)/shard_map/ppermute | solution.py:40
  99.8 7.5 %collective-permute-done.9 = bf16[512,512]{1,0:T(8,128)(2,1)S(1)} collective-permute-done((bf16[512,512]{1,0:T(8,128)(2,1)S(1)}, bf16[512,512]{1,0:T(8,128)(2,1)S(1)}, u32[]{:S(2)}, u32[]{:S(2)}) %collective-permute-start.9) | collective-permute-done | bytes 524320 | tf_op jit(solution)/shard_map/ppermute | solution.py:40
  107.3 11.9 %collective-permute-done.10 = bf16[512,512]{1,0:T(8,128)(2,1)S(1)} collective-permute-done((bf16[512,512]{1,0:T(8,128)(2,1)S(1)}, bf16[512,512]{1,0:T(8,128)(2,1)S(1)}, u32[]{:S(2)}, u32[]{:S(2)}) %collective-permute-start.10) | collective-permute-done | bytes 524320 | tf_op jit(solution)/shard_map/ppermute | solution.py:40
  119.2 0.0 collective-permute-done.11
  119.2 0.7 fusion.6
  120.0 5.8 %collective-permute-start.12 = (bf16[128,512]{1,0:T(8,128)(2,1)S(1)}, bf16[128,512]{1,0:T(8,128)(2,1)S(1)}, u32[]{:S(2)}, u32[]{:S(2)}) collective-permute-start(bf16[128,512]{1,0:T(8,128)(2,1)S(1)} %get-tuple-element.27), channel_id=1, source_target_pairs={{0,16},{8,24},{16,0},{24,8},{1,17},{9,25},{17,1},{25,9},{2,18},{10... | collective-permute-start | bytes 393224 | tf_op jit(solution)/shard_map/ppermute | solution.py:40
  125.8 2.1 %collective-permute-start.13 = (bf16[128,512]{1,0:T(8,128)(2,1)S(1)}, bf16[128,512]{1,0:T(8,128)(2,1)S(1)}, u32[]{:S(2)}, u32[]{:S(2)}) collective-permute-start(bf16[128,512]{1,0:T(8,128)(2,1)S(1)} %get-tuple-element.29), channel_id=1, source_target_pairs={{0,8},{8,16},{16,24},{24,0},{1,9},{9,17},{17,25},{25,1},{2,10},{10... | collective-permute-start | bytes 393224 | tf_op jit(solution)/shard_map/ppermute | solution.py:40
  127.9 5.3 %collective-permute-start.14 = (bf16[128,512]{1,0:T(8,128)(2,1)S(1)}, bf16[128,512]{1,0:T(8,128)(2,1)S(1)}, u32[]{:S(2)}, u32[]{:S(2)}) collective-permute-start(bf16[128,512]{1,0:T(8,128)(2,1)S(1)} %get-tuple-element.28), channel_id=1, source_target_pairs={{0,24},{8,0},{16,8},{24,16},{1,25},{9,1},{17,9},{25,17},{2,26},{10... | collective-permute-start | bytes 393224 | tf_op jit(solution)/shard_map/ppermute | solution.py:40
  133.2 2.1 %collective-permute-done.13 = bf16[128,512]{1,0:T(8,128)(2,1)S(1)} collective-permute-done((bf16[128,512]{1,0:T(8,128)(2,1)S(1)}, bf16[128,512]{1,0:T(8,128)(2,1)S(1)}, u32[]{:S(2)}, u32[]{:S(2)}) %collective-permute-start.13) | collective-permute-done | bytes 131104 | tf_op jit(solution)/shard_map/ppermute | solution.py:40
  135.4 2.5 %collective-permute-done.14 = bf16[128,512]{1,0:T(8,128)(2,1)S(1)} collective-permute-done((bf16[128,512]{1,0:T(8,128)(2,1)S(1)}, bf16[128,512]{1,0:T(8,128)(2,1)S(1)}, u32[]{:S(2)}, u32[]{:S(2)}) %collective-permute-start.14) | collective-permute-done | bytes 131104 | tf_op jit(solution)/shard_map/ppermute | solution.py:40
  137.9 0.7 multiply_reduce_fusion
  138.6 1.3 broadcast_in_dim.10
  139.8 10.1 %all-to-all-start.2 = ((f32[32,1,1]{2,1,0:T(1,128)}), f32[32,1,1]{2,1,0:T(1,128)S(1)}, u32[]{:S(2)}, u32[]{:S(2)}) async-start(f32[32,1,1]{2,1,0:T(1,128)} %broadcast_in_dim.10), calls=%async_computation.2 | async-start | bytes 32768 | tf_op jit(solution)/shard_map/all_to_all | solution.py:79
  149.9 0.6 bitcast_add_fusion
  150.6 8.7 %all-to-all-done.2 = f32[32,1,1]{2,1,0:T(1,128)S(1)} async-done(((f32[32,1,1]{2,1,0:T(1,128)}), f32[32,1,1]{2,1,0:T(1,128)S(1)}, u32[]{:S(2)}, u32[]{:S(2)}) %all-to-all-start.2) | async-done | bytes 160 | tf_op jit(solution)/shard_map/all_to_all | solution.py:79
  159.3 0.6 reduce_sum.39
  160.6 0.7 fusion.21
  161.3 0.7 copy.13
  (19 shorter events, 0.1 us)
Async XLA Ops:
  0.6 30.5 %copy-start = (bf16[1,384,4096]{2,1,0:T(8,128)(2,1)S(1)}, bf16[1,384,4096]{2,1,0:T(8,128)(2,1)}, u32[]{:S(2)}) copy-start(bf16[1,384,4096]{2,1,0:T(8,128)(2,1)} %param.7) | copy-start | bytes 9437188
  2.4 28.8 %copy-start.3 = (f32[4096]{0:T(1024)S(1)}, f32[4096]{0:T(1024)}, u32[]{:S(2)}) copy-start(f32[4096]{0:T(1024)} %param.8) | copy-start | bytes 49156
  6.3 31.7 %all-to-all-start = ((bf16[16,64,128]{2,1,0:T(8,128)(2,1)}), bf16[16,64,128]{2,1,0:T(8,128)(2,1)S(1)}, u32[]{:S(2)}, u32[]{:S(2)}) async-start(bf16[16,64,128]{2,1,0:T(8,128)(2,1)} %multiply_convert_fusion), calls=%async_computation | async-start | bytes 524288 | tf_op jit(solution)/shard_map/all_to_all | solution.py:79
  18.2 16.6 %collective-permute-start = (bf16[128,512]{1,0:T(8,128)(2,1)}, bf16[128,512]{1,0:T(8,128)(2,1)}, u32[]{:S(2)}, u32[]{:S(2)}) collective-permute-start(bf16[128,512]{1,0:T(8,128)(2,1)} %bitcast), channel_id=1, source_target_pairs={{0,24},{8,0},{16,8},{24,16},{1,25},{9,1},{17,9},{25,17},{2,26},{10... | collective-permute-start | bytes 393224 | tf_op jit(solution)/shard_map/ppermute | solution.py:40
  23.2 11.6 %collective-permute-start.1 = (bf16[128,512]{1,0:T(8,128)(2,1)}, bf16[128,512]{1,0:T(8,128)(2,1)}, u32[]{:S(2)}, u32[]{:S(2)}) collective-permute-start(bf16[128,512]{1,0:T(8,128)(2,1)} %bitcast), channel_id=1, source_target_pairs={{0,16},{8,24},{16,0},{24,8},{1,17},{9,25},{17,1},{25,9},{2,18},{10... | collective-permute-start | bytes 393224 | tf_op jit(solution)/shard_map/ppermute | solution.py:40
  27.7 9.1 %collective-permute-start.2 = (bf16[128,512]{1,0:T(8,128)(2,1)}, bf16[128,512]{1,0:T(8,128)(2,1)}, u32[]{:S(2)}, u32[]{:S(2)}) collective-permute-start(bf16[128,512]{1,0:T(8,128)(2,1)} %bitcast), channel_id=1, source_target_pairs={{0,8},{8,16},{16,24},{24,0},{1,9},{9,17},{17,25},{25,1},{2,10},{10... | collective-permute-start | bytes 393224 | tf_op jit(solution)/shard_map/ppermute | solution.py:40
  32.6 1.2 copy-start.1
  33.7 1.1 copy-start.4
  34.9 23.2 %copy-start.7 = (f32[8192]{0:T(1024)S(1)}, f32[8192]{0:T(1024)}, u32[]{:S(2)}) copy-start(f32[8192]{0:T(1024)} %param.13) | copy-start | bytes 98308
  37.9 31.6 %copy-start.2 = (bf16[384,2048]{1,0:T(8,128)(2,1)S(1)}, bf16[384,2048]{1,0:T(8,128)(2,1)}, u32[]{:S(2)}) copy-start(bf16[384,2048]{1,0:T(8,128)(2,1)} %copy-done.1) | copy-start | bytes 4718596
  37.9 31.6 %collective-permute-start.3 = (bf16[384,2048]{1,0:T(8,128)(2,1)}, bf16[384,2048]{1,0:T(8,128)(2,1)}, u32[]{:S(2)}, u32[]{:S(2)}) collective-permute-start(bf16[384,2048]{1,0:T(8,128)(2,1)} %copy-done.4), channel_id=1, source_target_pairs={{0,1},{1,0},{2,3},{3,2},{4,5},{5,4},{6,7},{7,6},{8,9},{9,8},{10,11... | collective-permute-start | bytes 4718600 | tf_op jit(solution)/shard_map/ppermute | solution.py:40
  42.9 4.0 %collective-permute-start.4 = (bf16[384,512]{1,0:T(8,128)(2,1)}, bf16[384,512]{1,0:T(8,128)(2,1)}, u32[]{:S(2)}, u32[]{:S(2)}) collective-permute-start(bf16[384,512]{1,0:T(8,128)(2,1)} %bitcast.39), channel_id=1, source_target_pairs={{0,1},{1,0},{2,3},{3,2},{4,5},{5,4},{6,7},{7,6},{8,9},{9,8},{10,11... | collective-permute-start | bytes 1179656 | tf_op jit(solution)/shard_map/ppermute | solution.py:40
  48.1 23.8 %collective-permute-start.5 = (bf16[512,512]{1,0:T(8,128)(2,1)S(1)}, bf16[512,512]{1,0:T(8,128)(2,1)}, u32[]{:S(2)}, u32[]{:S(2)}) collective-permute-start(bf16[512,512]{1,0:T(8,128)(2,1)S(1)} %pad_maximum_fusion.2), channel_id=1, source_target_pairs={{0,4},{2,6},{4,0},{6,2},{1,5},{3,7},{5,1},{7,3},{8,12},{10,14},{12... | collective-permute-start | bytes 1572872 | tf_op jit(solution)/shard_map/ppermute | solution.py:40
  52.7 23.4 %collective-permute-start.6 = (bf16[512,512]{1,0:T(8,128)(2,1)S(1)}, bf16[512,512]{1,0:T(8,128)(2,1)}, u32[]{:S(2)}, u32[]{:S(2)}) collective-permute-start(bf16[512,512]{1,0:T(8,128)(2,1)S(1)} %pad_maximum_fusion.2), channel_id=1, source_target_pairs={{0,6},{2,0},{4,2},{6,4},{1,7},{3,1},{5,3},{7,5},{8,14},{10,8},{12,... | collective-permute-start | bytes 1572872 | tf_op jit(solution)/shard_map/ppermute | solution.py:40
  55.5 22.2 %collective-permute-start.7 = (bf16[512,512]{1,0:T(8,128)(2,1)S(1)}, bf16[512,512]{1,0:T(8,128)(2,1)}, u32[]{:S(2)}, u32[]{:S(2)}) collective-permute-start(bf16[512,512]{1,0:T(8,128)(2,1)S(1)} %pad_maximum_fusion.2), channel_id=1, source_target_pairs={{0,2},{2,4},{4,6},{6,0},{1,3},{3,5},{5,7},{7,1},{8,10},{10,12},{12... | collective-permute-start | bytes 1572872 | tf_op jit(solution)/shard_map/ppermute | solution.py:40
  59.6 19.8 %all-to-all-start.1 = ((bf16[16,64,128]{2,1,0:T(8,128)(2,1)}), bf16[16,64,128]{2,1,0:T(8,128)(2,1)S(1)}, u32[]{:S(2)}, u32[]{:S(2)}) async-start(bf16[16,64,128]{2,1,0:T(8,128)(2,1)} %broadcast_in_dim.9), calls=%async_computation.1 | async-start | bytes 524288 | tf_op jit(solution)/shard_map/all_to_all | solution.py:79
  71.3 6.5 %copy-start.5 = (bf16[768,2048]{1,0:T(8,128)(2,1)}, bf16[768,2048]{1,0:T(8,128)(2,1)S(1)}, u32[]{:S(2)}) copy-start(bf16[768,2048]{1,0:T(8,128)(2,1)S(1)} %pad_maximum_fusion) | copy-start | bytes 9437188
  79.4 7.5 %collective-permute-start.8 = (f32[768,512]{1,0:T(8,128)S(1)}, f32[768,512]{1,0:T(8,128)S(1)}, u32[]{:S(2)}, u32[]{:S(2)}) collective-permute-start(f32[768,512]{1,0:T(8,128)S(1)} %add_add_fusion), channel_id=1, source_target_pairs={{0,1},{1,0},{2,3},{3,2},{4,5},{5,4},{6,7},{7,6},{8,9},{9,8},{10,11... | collective-permute-start | bytes 4718600 | tf_op jit(solution)/shard_map/ppermute | solution.py:40
  87.0 1.9 %copy-start.6 = (bf16[768,2048]{1,0:T(8,128)(2,1)S(1)}, bf16[768,2048]{1,0:T(8,128)(2,1)}, u32[]{:S(2)}) copy-start(bf16[768,2048]{1,0:T(8,128)(2,1)} %copy-done.5) | copy-start | bytes 9437188
  90.8 16.6 %collective-permute-start.9 = (bf16[512,512]{1,0:T(8,128)(2,1)S(1)}, bf16[512,512]{1,0:T(8,128)(2,1)S(1)}, u32[]{:S(2)}, u32[]{:S(2)}) collective-permute-start(bf16[512,512]{1,0:T(8,128)(2,1)S(1)} %convolution_convert_fusion.2), channel_id=1, source_target_pairs={{0,4},{2,6},{4,0},{6,2},{1,5},{3,7},{5,1},{7,3},{8,12},{10,14},{12... | collective-permute-start | bytes 1572872 | tf_op jit(solution)/shard_map/ppermute | solution.py:40
  93.3 25.9 %collective-permute-start.10 = (bf16[512,512]{1,0:T(8,128)(2,1)S(1)}, bf16[512,512]{1,0:T(8,128)(2,1)S(1)}, u32[]{:S(2)}, u32[]{:S(2)}) collective-permute-start(bf16[512,512]{1,0:T(8,128)(2,1)S(1)} %convolution_convert_fusion.1), channel_id=1, source_target_pairs={{0,2},{2,4},{4,6},{6,0},{1,3},{3,5},{5,7},{7,1},{8,10},{10,12},{12... | collective-permute-start | bytes 1572872 | tf_op jit(solution)/shard_map/ppermute | solution.py:40
  97.2 22.0 %collective-permute-start.11 = (bf16[512,512]{1,0:T(8,128)(2,1)S(1)}, bf16[512,512]{1,0:T(8,128)(2,1)S(1)}, u32[]{:S(2)}, u32[]{:S(2)}) collective-permute-start(bf16[512,512]{1,0:T(8,128)(2,1)S(1)} %convolution_convert_fusion), channel_id=1, source_target_pairs={{0,6},{2,0},{4,2},{6,4},{1,7},{3,1},{5,3},{7,5},{8,14},{10,8},{12,... | collective-permute-start | bytes 1572872 | tf_op jit(solution)/shard_map/ppermute | solution.py:40
  120.0 13.2 %collective-permute-start.12 = (bf16[128,512]{1,0:T(8,128)(2,1)S(1)}, bf16[128,512]{1,0:T(8,128)(2,1)S(1)}, u32[]{:S(2)}, u32[]{:S(2)}) collective-permute-start(bf16[128,512]{1,0:T(8,128)(2,1)S(1)} %get-tuple-element.27), channel_id=1, source_target_pairs={{0,16},{8,24},{16,0},{24,8},{1,17},{9,25},{17,1},{25,9},{2,18},{10... | collective-permute-start | bytes 393224 | tf_op jit(solution)/shard_map/ppermute | solution.py:40
  125.8 9.6 %collective-permute-start.13 = (bf16[128,512]{1,0:T(8,128)(2,1)S(1)}, bf16[128,512]{1,0:T(8,128)(2,1)S(1)}, u32[]{:S(2)}, u32[]{:S(2)}) collective-permute-start(bf16[128,512]{1,0:T(8,128)(2,1)S(1)} %get-tuple-element.29), channel_id=1, source_target_pairs={{0,8},{8,16},{16,24},{24,0},{1,9},{9,17},{17,25},{25,1},{2,10},{10... | collective-permute-start | bytes 393224 | tf_op jit(solution)/shard_map/ppermute | solution.py:40
  127.9 9.9 %collective-permute-start.14 = (bf16[128,512]{1,0:T(8,128)(2,1)S(1)}, bf16[128,512]{1,0:T(8,128)(2,1)S(1)}, u32[]{:S(2)}, u32[]{:S(2)}) collective-permute-start(bf16[128,512]{1,0:T(8,128)(2,1)S(1)} %get-tuple-element.28), channel_id=1, source_target_pairs={{0,24},{8,0},{16,8},{24,16},{1,25},{9,1},{17,9},{25,17},{2,26},{10... | collective-permute-start | bytes 393224 | tf_op jit(solution)/shard_map/ppermute | solution.py:40
  139.8 19.4 %all-to-all-start.2 = ((f32[32,1,1]{2,1,0:T(1,128)}), f32[32,1,1]{2,1,0:T(1,128)S(1)}, u32[]{:S(2)}, u32[]{:S(2)}) async-start(f32[32,1,1]{2,1,0:T(1,128)} %broadcast_in_dim.10), calls=%async_computation.2 | async-start | bytes 32768 | tf_op jit(solution)/shard_map/all_to_all | solution.py:79

commit v5 on v4

--- a/solution.py
+++ b/solution.py
@@ -44,35 +44,33 @@
     return lax.optimization_barrier(values)
 
 
-def arrange_kernel(order_ref, inputs_ref, gain_ref, own_ref, other_ref):
-    for half, out_ref in enumerate((own_ref, other_ref)):
-        for j in range(CHIPS):
-            start = pl.multiple_of(order_ref[half * CHIPS + j] * LANES, LANES)
-            columns = pl.ds(start, LANES)
-            out_ref[:, j * LANES : (j + 1) * LANES] = (
-                inputs_ref[:, columns].astype(jnp.float32) * gain_ref[:, columns]
+def arrange_kernel(order_ref, inputs_ref, theirs_ref, gain_ref, scaled_ref):
+    tokens = inputs_ref.shape[0]
+    for j in range(CHIPS):
+        start = pl.multiple_of(order_ref[j] * LANES, LANES)
+        columns = pl.ds(start, LANES)
+        place = slice(j * LANES, (j + 1) * LANES)
+        for row, ref in ((0, inputs_ref), (tokens, theirs_ref)):
+            scaled_ref[row : row + tokens, place] = (
+                ref[:, columns].astype(jnp.float32) * gain_ref[:, columns]
             ).astype(jnp.bfloat16)
 
 
-def arrange(inputs, feature_gain):
+def arrange(inputs, theirs, feature_gain):
     tokens, features = inputs.shape
     x, y, core = (lax.axis_index(name) for name in ("x", "y_hi", "core"))
     rx, ry = jnp.arange(CHIPS) // AXES["y_hi"], jnp.arange(CHIPS) % AXES["y_hi"]
     chip = (y + ry) % AXES["y_hi"] * AXES["x"] + (x + rx) % AXES["x"]
-    order = jnp.concatenate([chip * 2 + core, chip * 2 + 1 - core]).astype(jnp.int32)
-    half = jax.ShapeDtypeStruct((tokens, features // 2), jnp.bfloat16)
+    order = (chip * 2 + core).astype(jnp.int32)
+    in_vmem = pl.BlockSpec(memory_space=pltpu.VMEM)
     return pl.pallas_call(
         arrange_kernel,
-        out_shape=(half, half),
-        in_specs=[
-            pl.BlockSpec(memory_space=pltpu.SMEM),
-            pl.BlockSpec(memory_space=pltpu.VMEM),
-            pl.BlockSpec(memory_space=pltpu.VMEM),
-        ],
-        out_specs=(pl.BlockSpec(memory_space=pltpu.VMEM),) * 2,
+        out_shape=jax.ShapeDtypeStruct((2 * tokens, features // 2), jnp.bfloat16),
+        in_specs=[pl.BlockSpec(memory_space=pltpu.SMEM)] + [in_vmem] * 3,
+        out_specs=in_vmem,
         compiler_params=pltpu.CompilerParams(vmem_limit_bytes=24 << 20),
         name="arrange",
-    )(order, inputs, feature_gain[None, :])
+    )(order, inputs, theirs, feature_gain[None, :])
 
 
 def exchange(parts, axis):
@@ -115,32 +113,40 @@
     near = [weight] + [None] * 3
     for k in STEPS:
         near[k] = send(weight, "y_hi", -k)
+    raw = send(inputs[0], "core", 1)
+    targets = [teacher_keys[0], send(teacher_keys[0], "core", 1)]
+    column = jnp.concatenate(near, axis=0)
+    column, global_frag, local_frag = tied(column, global_frag, local_frag)
+    far = {k: send(column, "x", -k) for k in STEPS}
     arrived = exchange(fragment_codes(global_frag, local_frag[0]), REPLICA)
-    column = jnp.concatenate(near, axis=0)
-    own, other = arrange(inputs[0], feature_gain)
-    column, arrived, own, other = tied(column, arrived, own, other)
-    far = {k: send(column, "x", -k) for k in STEPS}
-    scaled = jnp.concatenate([own, send(other, "core", 1)], axis=0)
-    targets = jnp.concatenate([teacher_keys[0], send(teacher_keys[0], "core", 1)], axis=0)
-    scaled, targets = tied(scaled, targets)
+    scaled = arrange(inputs[0], raw, feature_gain)
     group = scaled.shape[1] // AXES["x"]
     blocks = [scaled[:, k * group : (k + 1) * group] for k in range(AXES["x"])]
     partial = jnp.dot(blocks[0], column, preferred_element_type=jnp.float32)
-    new_global, new_momentum = fragment_update(arrived, global_frag, momentum)
     for k in STEPS:
+        if k == STEPS[-1]:
+            partial, arrived, targets = tied(partial, arrived, targets)
         partial += jnp.dot(blocks[k], far[k], preferred_element_type=jnp.float32)
-    partial, new_global = tied(partial, new_global)
 
     theirs = send(partial, "core", 1)
-    projected = partial + jnp.concatenate([theirs[tokens:], theirs[:tokens]], axis=0)
-    residual = (projected - targets.astype(jnp.float32)).astype(jnp.bfloat16)
+    residual = [
+        (mine + other - target.astype(jnp.float32)).astype(jnp.bfloat16)
+        for mine, other, target in zip(
+            (partial[:tokens], partial[tokens:]), (theirs[tokens:], theirs[:tokens]), targets
+        )
+    ]
+    residual = jnp.concatenate(residual, axis=0)
     gradient = [
         lax.dot_general(
             block, residual, (((0,), (0,)), ((), ())), preferred_element_type=jnp.float32
         ).astype(jnp.bfloat16)
         for block in blocks
     ]
-    mine = total([gradient[0]] + [send(gradient[k], "x", k) for k in STEPS])
+    gradient[0], arrived = tied(gradient[0], arrived)
+    new_global, new_momentum = fragment_update(arrived, global_frag, momentum)
+    arrivals = [send(gradient[k], "x", k) for k in STEPS]
+    arrivals, new_global = tied(arrivals, new_global)
+    mine = total([gradient[0]] + arrivals)
     mine = mine.astype(jnp.bfloat16).reshape(AXES["y_hi"], rows, width)
     gradient = total([mine[0]] + [send(mine[k], "y_hi", k) for k in STEPS])
 

time: 163 us -> 157 us (0.963)
  blocking collectives: 0 us -> 16.4 us
  starting transfers between devices: 88.3 us -> 73.5 us
  waiting for transfers between devices: 42 us -> 30.9 us
  matrix products: 8.33 us -> 10.2 us
    all_to_all x0 -> x1, blocking collectives: none -> 16.4 us  [exchange(): return lax.all_to_all(parts, axis, split_axis=0, concat_axis=0, tiled=True)]
    all_to_all x3 -> x2, starting transfers between devices: 32 us -> 20.1 us  [exchange(): return lax.all_to_all(parts, axis, split_axis=0, concat_axis=0, tiled=True)]
    ppermute x15, waiting for transfers between devices: 33.3 us -> 22.2 us  [send(): lax.ppermute(value, axis, [(i, (i + step) % size) for i in range(size)])]
    concatenate x3 -> x0, other arithmetic: 3 us -> none  [the longest x1 1.76 us: shards(): scaled = jnp.concatenate([own, send(other, 'core', 1)], axis=0)]
    ppermute x15, starting transfers between devices: 56.3 us -> 53.4 us  [send(): lax.ppermute(value, axis, [(i, (i + step) % size) for i in range(size)])]
    convert_element_type x1 -> x2, other arithmetic: 0.46 us -> 2.78 us  [the longest x1 2.51 us: shards(): (mine + other - target.astype(jnp.float32)).astype(jnp.bfloat16)]
    unnamed x17 -> x15, local copies, waits for them, and re-layouts: 4.46 us -> 6.16 us
    all_to_all x3 -> x2, waiting for transfers between devices: 8.7 us -> 8.69 us  [exchange(): return lax.all_to_all(parts, axis, split_axis=0, concat_axis=0, tiled=True)]
  transfers between devices with their start and end apart: 18 -> 17, of which waited for: 9 -> 7; matrix products, arithmetic and copies ran while one was open for 7% -> 9% of each run, Pallas kernels for 1% -> 1%
where the time goes in v5:
time: 157 us; the launch traced here: 156 us
  starting transfers between devices  73.5 us (47%)
  waiting for transfers between devices  30.9 us (20%)
  blocking collectives  16.4 us (10%)
  other arithmetic  14 us (9%)
  matrix products  10.2 us (6%)
  local copies, waits for them, and re-layouts  7.57 us (5%)
  between operations  1.67 us (1%)
    ppermute x15, starting transfers between devices, send(): lax.ppermute(value, axis, [(i, (i + step) % size) for i in range(size)])  53.4 us
    ppermute x15, waiting for transfers between devices, send(): lax.ppermute(value, axis, [(i, (i + step) % size) for i in range(size)])  22.2 us
    all_to_all x2, starting transfers between devices, exchange(): return lax.all_to_all(parts, axis, split_axis=0, concat_axis=0, tiled=True)  20.1 us
    all_to_all x1, blocking collectives, exchange(): return lax.all_to_all(parts, axis, split_axis=0, concat_axis=0, tiled=True)  16.4 us
    all_to_all x2, waiting for transfers between devices, exchange(): return lax.all_to_all(parts, axis, split_axis=0, concat_axis=0, tiled=True)  8.69 us
    unnamed x15, local copies, waits for them, and re-layouts  6.16 us
    dot_general x3, matrix products, shards(): partial += jnp.dot(blocks[k], far[k], preferred_element_type=jnp.float32)  6.13 us
  transfers between devices with their start and end apart: 17, of which 7 were waited for; matrix products, arithmetic and copies ran while one was open for 9% of the time, Pallas kernels for 1%

profile of v5, /device:TPU:1, one launch (start us, length us, event | category | flops | bytes accessed | tf_op | source)
XLA Modules:
  0.0 155.7 jit_solution(17062834456143285801)
XLA Ops:
  0.6 0.0 copy-start.5
  0.6 8.9 %collective-permute-start = (bf16[384,4096]{1,0:T(8,128)(2,1)}, bf16[384,4096]{1,0:T(8,128)(2,1)S(1)}, u32[]{:S(2)}, u32[]{:S(2)}) collective-permute-start(bf16[384,4096]{1,0:T(8,128)(2,1)} %bitcast.30), channel_id=1, source_target_pairs={{0,1},{1,0},{2,3},{3,2},{4,5},{5,4},{6,7},{7,6},{8,9},{9,8},{10,11... | collective-permute-start | bytes 9437192 | tf_op jit(solution)/shard_map/ppermute | solution.py:40
  9.6 1.9 %collective-permute-start.1 = (bf16[128,512]{1,0:T(8,128)(2,1)}, bf16[128,512]{1,0:T(8,128)(2,1)S(1)}, u32[]{:S(2)}, u32[]{:S(2)}) collective-permute-start(bf16[128,512]{1,0:T(8,128)(2,1)} %bitcast.38), channel_id=1, source_target_pairs={{0,24},{8,0},{16,8},{24,16},{1,25},{9,1},{17,9},{25,17},{2,26},{10... | collective-permute-start | bytes 393224 | tf_op jit(solution)/shard_map/ppermute | solution.py:40
  11.5 2.1 %collective-permute-start.2 = (bf16[128,512]{1,0:T(8,128)(2,1)}, bf16[128,512]{1,0:T(8,128)(2,1)}, u32[]{:S(2)}, u32[]{:S(2)}) collective-permute-start(bf16[128,512]{1,0:T(8,128)(2,1)} %bitcast.39), channel_id=1, source_target_pairs={{0,16},{8,24},{16,0},{24,8},{1,17},{9,25},{17,1},{25,9},{2,18},{10... | collective-permute-start | bytes 393224 | tf_op jit(solution)/shard_map/ppermute | solution.py:40
  13.6 4.2 %collective-permute-start.3 = (bf16[128,512]{1,0:T(8,128)(2,1)}, bf16[128,512]{1,0:T(8,128)(2,1)}, u32[]{:S(2)}, u32[]{:S(2)}) collective-permute-start(bf16[128,512]{1,0:T(8,128)(2,1)} %bitcast.40), channel_id=1, source_target_pairs={{0,8},{8,16},{16,24},{24,0},{1,9},{9,17},{17,25},{25,1},{2,10},{10... | collective-permute-start | bytes 393224 | tf_op jit(solution)/shard_map/ppermute | solution.py:40
  17.9 2.8 %collective-permute-start.6 = (bf16[384,512]{1,0:T(8,128)(2,1)}, bf16[384,512]{1,0:T(8,128)(2,1)}, u32[]{:S(2)}, u32[]{:S(2)}) collective-permute-start(bf16[384,512]{1,0:T(8,128)(2,1)} %bitcast.36), channel_id=1, source_target_pairs={{0,1},{1,0},{2,3},{3,2},{4,5},{5,4},{6,7},{7,6},{8,9},{9,8},{10,11... | collective-permute-start | bytes 1179656 | tf_op jit(solution)/shard_map/ppermute | solution.py:40
  20.7 0.0 collective-permute-done.1
  20.7 2.2 %collective-permute-done.2 = bf16[128,512]{1,0:T(8,128)(2,1)} collective-permute-done((bf16[128,512]{1,0:T(8,128)(2,1)}, bf16[128,512]{1,0:T(8,128)(2,1)}, u32[]{:S(2)}, u32[]{:S(2)}) %collective-permute-start.2) | collective-permute-done | bytes 131104 | tf_op jit(solution)/shard_map/ppermute | solution.py:40
  22.9 8.4 %collective-permute-done.3 = bf16[128,512]{1,0:T(8,128)(2,1)} collective-permute-done((bf16[128,512]{1,0:T(8,128)(2,1)}, bf16[128,512]{1,0:T(8,128)(2,1)}, u32[]{:S(2)}, u32[]{:S(2)}) %collective-permute-start.3) | collective-permute-done | bytes 131104 | tf_op jit(solution)/shard_map/ppermute | solution.py:40
  31.3 1.9 %pad_maximum_fusion.1 = bf16[512,512]{1,0:T(8,128)(2,1)} fusion(bf16[128,512]{1,0:T(8,128)(2,1)} %collective-permute-done.3, bf16[128,512]{1,0:T(8,128)(2,1)} %collective-permute-done.2, bf16[128,512]{1,0:T(8,128)(2,1)S(1)} %collective-permute-done.1, bf16[128,512]{1,0:T(8,128)(2,1)} %bitcast.41), kind=kLoop, calls=%fused_computation.25 | loop fusion | flops 2097152 | bytes 1048576 | tf_op jit(solution)/shard_map/concatenate | solution.py:118
  33.1 1.9 %collective-permute-start.4 = (bf16[512,512]{1,0:T(8,128)(2,1)}, bf16[512,512]{1,0:T(8,128)(2,1)}, u32[]{:S(2)}, u32[]{:S(2)}) collective-permute-start(bf16[512,512]{1,0:T(8,128)(2,1)} %pad_maximum_fusion.1), channel_id=1, source_target_pairs={{0,4},{2,6},{4,0},{6,2},{1,5},{3,7},{5,1},{7,3},{8,12},{10,14},{12... | collective-permute-start | bytes 1572872 | tf_op jit(solution)/shard_map/ppermute | solution.py:40
  35.0 1.9 %collective-permute-start.5 = (bf16[512,512]{1,0:T(8,128)(2,1)}, bf16[512,512]{1,0:T(8,128)(2,1)}, u32[]{:S(2)}, u32[]{:S(2)}) collective-permute-start(bf16[512,512]{1,0:T(8,128)(2,1)} %pad_maximum_fusion.1), channel_id=1, source_target_pairs={{0,6},{2,0},{4,2},{6,4},{1,7},{3,1},{5,3},{7,5},{8,14},{10,8},{12,... | collective-permute-start | bytes 1572872 | tf_op jit(solution)/shard_map/ppermute | solution.py:40
  37.0 3.4 %collective-permute-start.7 = (bf16[512,512]{1,0:T(8,128)(2,1)}, bf16[512,512]{1,0:T(8,128)(2,1)}, u32[]{:S(2)}, u32[]{:S(2)}) collective-permute-start(bf16[512,512]{1,0:T(8,128)(2,1)} %pad_maximum_fusion.1), channel_id=1, source_target_pairs={{0,2},{2,4},{4,6},{6,0},{1,3},{3,5},{5,7},{7,1},{8,10},{10,12},{12... | collective-permute-start | bytes 1572872 | tf_op jit(solution)/shard_map/ppermute | solution.py:40
  40.3 1.6 %convert_element_type.137 = f32[1,131072]{1,0:T(1,128)S(1)} convert(bf16[1,131072]{1,0:T(2,128)(2,1)} %param.12) | non-fusion elementwise | flops 131072 | bytes 786432 | tf_op jit(solution)/shard_map/convert_element_type | solution.py:89
  41.9 0.0 copy-start.3
  42.0 0.9 bitcast_reduce_fusion
  42.8 0.1 reshape.91
  42.9 2.0 %multiply_convert_fusion = bf16[16,64,128]{2,1,0:T(8,128)(2,1)} fusion(f32[16,64]{1,0:T(8,128)S(1)} %reshape.91, f32[16,64,128]{2,1,0:T(8,128)} %bitcast.33), kind=kLoop, calls=%fused_computation.28 | loop fusion | flops 786432 | bytes 790528 | tf_op jit(solution)/shard_map/convert_element_type | solution.py:92
  44.9 9.8 %all-to-all-start = ((bf16[16,64,128]{2,1,0:T(8,128)(2,1)}), bf16[16,64,128]{2,1,0:T(8,128)(2,1)S(1)}, u32[]{:S(2)}, u32[]{:S(2)}) async-start(bf16[16,64,128]{2,1,0:T(8,128)(2,1)} %multiply_convert_fusion), calls=%async_computation | async-start | bytes 524288 | tf_op jit(solution)/shard_map/all_to_all | solution.py:77
  54.7 0.0 collective-permute-done.theirs_ref
  54.7 1.6 %copy-done.1 = bf16[384,4096]{1,0:T(8,128)(2,1)} copy-done((bf16[384,4096]{1,0:T(8,128)(2,1)}, bf16[384,4096]{1,0:T(8,128)(2,1)S(1)}, u32[]{:S(2)}) %copy-start.1) | copy-done | bytes 3145752
  56.4 1.9 %copy-done = bf16[1,384,4096]{2,1,0:T(8,128)(2,1)S(1)} copy-done((bf16[1,384,4096]{2,1,0:T(8,128)(2,1)S(1)}, bf16[1,384,4096]{2,1,0:T(8,128)(2,1)}, u32[]{:S(2)}) %copy-start) | copy-done | bytes 3145752
  58.3 1.9 %copy-done.2 = bf16[384,4096]{1,0:T(8,128)(2,1)S(1)} copy-done((bf16[384,4096]{1,0:T(8,128)(2,1)S(1)}, bf16[384,4096]{1,0:T(8,128)(2,1)}, u32[]{:S(2)}) %copy-start.2) | copy-done | bytes 3145752
  60.2 1.4 arrange.1
  61.6 1.6 %fusion.16 = f32[768,512]{1,0:T(8,128)S(1)} fusion(bf16[512,512]{1,0:T(8,128)(2,1)} %pad_maximum_fusion.1, bf16[768,2048]{1,0:T(8,128)(2,1)S(1)} %arrange.1), kind=kOutput, calls=%fused_computation.23 | convolution fusion | flops 402653184 | bytes 2883584 | tf_op jit(solution)/shard_map/dot_general | solution.py:125
  63.2 0.0 collective-permute-done.4
  63.2 1.6 %fusion.13 = f32[768,512]{1,0:T(8,128)S(1)} fusion(bf16[512,512]{1,0:T(8,128)(2,1)} %collective-permute-done.4, bf16[768,2048]{1,0:T(8,128)(2,1)S(1)} %arrange.1), kind=kOutput, calls=%fused_computation.20 | convolution fusion | flops 402653184 | bytes 2883584 | tf_op jit(solution)/shard_map/dot_general | solution.py:129
  64.8 0.0 collective-permute-done.5
  64.8 2.8 %add_add_fusion = f32[768,512]{1,0:T(8,128)} fusion(f32[768,512]{1,0:T(8,128)S(1)} %fusion.16, f32[768,512]{1,0:T(8,128)S(1)} %fusion.13, bf16[512,512]{1,0:T(8,128)(2,1)} %collective-permute-done.5, bf16[768,2048]{1,0:T(8,128)(2,1)S(1)} %arrange.1), kind=kOutput, calls=%fused_computation | convolution fusion | flops 403439616 | bytes 6029312 | tf_op jit(solution)/shard_map/dot_general | solution.py:129
  67.6 0.0 collective-permute-done.6
  67.6 0.0 all-to-all-done
  67.6 0.0 collective-permute-done.7
  67.6 1.7 %fusion.5 = f32[768,512]{1,0:T(8,128)S(1)} fusion(bf16[512,512]{1,0:T(8,128)(2,1)} %collective-permute-done.7, bf16[768,2048]{1,0:T(8,128)(2,1)S(1)} %arrange.1), kind=kOutput, calls=%fused_computation.14 | convolution fusion | flops 402653184 | bytes 2883584 | tf_op jit(solution)/shard_map/dot_general | solution.py:129
  69.4 1.5 add.120
  70.9 3.5 %collective-permute-start.8 = (f32[768,512]{1,0:T(8,128)}, f32[768,512]{1,0:T(8,128)}, u32[]{:S(2)}, u32[]{:S(2)}) collective-permute-start(f32[768,512]{1,0:T(8,128)} %add.120), channel_id=1, source_target_pairs={{0,1},{1,0},{2,3},{3,2},{4,5},{5,4},{6,7},{7,6},{8,9},{9,8},{10,11... | collective-permute-start | bytes 4718600 | tf_op jit(solution)/shard_map/ppermute | solution.py:40
  74.4 3.4 %collective-permute-done.8 = f32[768,512]{1,0:T(8,128)} collective-permute-done((f32[768,512]{1,0:T(8,128)}, f32[768,512]{1,0:T(8,128)}, u32[]{:S(2)}, u32[]{:S(2)}) %collective-permute-start.8) | collective-permute-done | bytes 1572896 | tf_op jit(solution)/shard_map/ppermute | solution.py:40
  77.8 2.5 %fusion.3 = (bf16[384,512]{1,0:T(8,128)(2,1)S(1)}, bf16[384,512]{1,0:T(8,128)(2,1)S(1)}) fusion(f32[768,512]{1,0:T(8,128)} %collective-permute-done.8, f32[768,512]{1,0:T(8,128)} %add.120, bf16[384,512]{1,0:T(8,128)(2,1)} %bitcast.37, bf16[384,512]{1,0:T(8,128)(2,1)} %collective-permute-done.6), kind=kLoop, calls=%fused_computation.11 | loop fusion | flops 1572864 | bytes 4718592 | tf_op jit(solution)/shard_map/convert_element_type | solution.py:133
  80.3 0.6 convolution_convert_fusion.3
  80.9 0.6 convolution_convert_fusion
  81.5 0.6 convolution_convert_fusion.1
  82.1 0.0 copy-start.6
  82.1 0.6 convolution_convert_fusion.2
  82.8 4.0 %collective-permute-start.11 = (bf16[512,512]{1,0:T(8,128)(2,1)S(1)}, bf16[512,512]{1,0:T(8,128)(2,1)S(1)}, u32[]{:S(2)}, u32[]{:S(2)}) collective-permute-start(bf16[512,512]{1,0:T(8,128)(2,1)S(1)} %convolution_convert_fusion), channel_id=1, source_target_pairs={{0,6},{2,0},{4,2},{6,4},{1,7},{3,1},{5,3},{7,5},{8,14},{10,8},{12,... | collective-permute-start | bytes 1572872 | tf_op jit(solution)/shard_map/ppermute | solution.py:40
  86.8 1.9 %collective-permute-start.10 = (bf16[512,512]{1,0:T(8,128)(2,1)S(1)}, bf16[512,512]{1,0:T(8,128)(2,1)S(1)}, u32[]{:S(2)}, u32[]{:S(2)}) collective-permute-start(bf16[512,512]{1,0:T(8,128)(2,1)S(1)} %convolution_convert_fusion.1), channel_id=1, source_target_pairs={{0,2},{2,4},{4,6},{6,0},{1,3},{3,5},{5,7},{7,1},{8,10},{10,12},{12... | collective-permute-start | bytes 1572872 | tf_op jit(solution)/shard_map/ppermute | solution.py:40
  88.8 3.1 %collective-permute-start.9 = (bf16[512,512]{1,0:T(8,128)(2,1)S(1)}, bf16[512,512]{1,0:T(8,128)(2,1)S(1)}, u32[]{:S(2)}, u32[]{:S(2)}) collective-permute-start(bf16[512,512]{1,0:T(8,128)(2,1)S(1)} %convolution_convert_fusion.2), channel_id=1, source_target_pairs={{0,4},{2,6},{4,0},{6,2},{1,5},{3,7},{5,1},{7,3},{8,12},{10,14},{12... | collective-permute-start | bytes 1572872 | tf_op jit(solution)/shard_map/ppermute | solution.py:40
  91.9 0.7 fusion.19
  92.7 16.4 %all_to_all.16 = bf16[16,64,128]{2,1,0:T(8,128)(2,1)S(1)} all-to-all(bf16[16,64,128]{2,1,0:T(8,128)(2,1)S(1)} %broadcast_in_dim.9), channel_id=1, replica_groups=mesh['z'=8,'y_lo'=2,'y_hi'=4,'x'=4,'core'=2] {'z','y_lo'}, dimensions={0} | all-to-all | bytes 524288 | tf_op jit(solution)/shard_map/all_to_all | solution.py:77
  109.1 0.0 collective-permute-done.11
  109.1 4.9 %collective-permute-done.10 = bf16[512,512]{1,0:T(8,128)(2,1)S(1)} collective-permute-done((bf16[512,512]{1,0:T(8,128)(2,1)S(1)}, bf16[512,512]{1,0:T(8,128)(2,1)S(1)}, u32[]{:S(2)}, u32[]{:S(2)}) %collective-permute-start.10) | collective-permute-done | bytes 524320 | tf_op jit(solution)/shard_map/ppermute | solution.py:40
  114.0 0.0 collective-permute-done.9
  114.0 0.3 add_convert_fusion
  114.3 6.3 %collective-permute-start.12 = (bf16[128,512]{1,0:T(8,128)(2,1)S(1)}, bf16[128,512]{1,0:T(8,128)(2,1)S(1)}, u32[]{:S(2)}, u32[]{:S(2)}) collective-permute-start(bf16[128,512]{1,0:T(8,128)(2,1)S(1)} %get-tuple-element.33), channel_id=1, source_target_pairs={{0,16},{8,24},{16,0},{24,8},{1,17},{9,25},{17,1},{25,9},{2,18},{10... | collective-permute-start | bytes 393224 | tf_op jit(solution)/shard_map/ppermute | solution.py:40
  120.7 2.5 %collective-permute-start.13 = (bf16[128,512]{1,0:T(8,128)(2,1)S(1)}, bf16[128,512]{1,0:T(8,128)(2,1)S(1)}, u32[]{:S(2)}, u32[]{:S(2)}) collective-permute-start(bf16[128,512]{1,0:T(8,128)(2,1)S(1)} %get-tuple-element.35), channel_id=1, source_target_pairs={{0,8},{8,16},{16,24},{24,0},{1,9},{9,17},{17,25},{25,1},{2,10},{10... | collective-permute-start | bytes 393224 | tf_op jit(solution)/shard_map/ppermute | solution.py:40
  123.2 4.9 %collective-permute-start.14 = (bf16[128,512]{1,0:T(8,128)(2,1)S(1)}, bf16[128,512]{1,0:T(8,128)(2,1)S(1)}, u32[]{:S(2)}, u32[]{:S(2)}) collective-permute-start(bf16[128,512]{1,0:T(8,128)(2,1)S(1)} %get-tuple-element.34), channel_id=1, source_target_pairs={{0,24},{8,0},{16,8},{24,16},{1,25},{9,1},{17,9},{25,17},{2,26},{10... | collective-permute-start | bytes 393224 | tf_op jit(solution)/shard_map/ppermute | solution.py:40
  128.1 1.0 collective-permute-done.13
  129.1 2.4 %collective-permute-done.14 = bf16[128,512]{1,0:T(8,128)(2,1)S(1)} collective-permute-done((bf16[128,512]{1,0:T(8,128)(2,1)S(1)}, bf16[128,512]{1,0:T(8,128)(2,1)S(1)}, u32[]{:S(2)}, u32[]{:S(2)}) %collective-permute-start.14) | collective-permute-done | bytes 131104 | tf_op jit(solution)/shard_map/ppermute | solution.py:40
  131.4 0.7 multiply_reduce_fusion
  132.1 1.3 broadcast_in_dim.10
  133.4 10.2 %all-to-all-start.2 = ((f32[32,1,1]{2,1,0:T(1,128)}), f32[32,1,1]{2,1,0:T(1,128)S(1)}, u32[]{:S(2)}, u32[]{:S(2)}) async-start(f32[32,1,1]{2,1,0:T(1,128)} %broadcast_in_dim.10), calls=%async_computation.2 | async-start | bytes 32768 | tf_op jit(solution)/shard_map/all_to_all | solution.py:77
  143.6 0.6 bitcast_add_fusion
  144.2 8.7 %all-to-all-done.2 = f32[32,1,1]{2,1,0:T(1,128)S(1)} async-done(((f32[32,1,1]{2,1,0:T(1,128)}), f32[32,1,1]{2,1,0:T(1,128)S(1)}, u32[]{:S(2)}, u32[]{:S(2)}) %all-to-all-start.2) | async-done | bytes 160 | tf_op jit(solution)/shard_map/all_to_all | solution.py:77
  152.9 0.6 reduce_sum.39
  154.2 0.7 fusion.18
  155.0 0.7 copy.13
  (14 shorter events, 0.2 us)
Async XLA Ops:
  0.6 41.3 %copy-start.5 = (bf16[131072]{0:T(1024)(128)(2,1)S(1)}, bf16[131072]{0:T(1024)(128)(2,1)}, u32[]{:S(2)}) copy-start(bf16[131072]{0:T(1024)(128)(2,1)} %param.11) | copy-start | bytes 786436
  0.6 54.1 %collective-permute-start = (bf16[384,4096]{1,0:T(8,128)(2,1)}, bf16[384,4096]{1,0:T(8,128)(2,1)S(1)}, u32[]{:S(2)}, u32[]{:S(2)}) collective-permute-start(bf16[384,4096]{1,0:T(8,128)(2,1)} %bitcast.30), channel_id=1, source_target_pairs={{0,1},{1,0},{2,3},{3,2},{4,5},{5,4},{6,7},{7,6},{8,9},{9,8},{10,11... | collective-permute-start | bytes 9437192 | tf_op jit(solution)/shard_map/ppermute | solution.py:40
  9.6 11.1 %collective-permute-start.1 = (bf16[128,512]{1,0:T(8,128)(2,1)}, bf16[128,512]{1,0:T(8,128)(2,1)S(1)}, u32[]{:S(2)}, u32[]{:S(2)}) collective-permute-start(bf16[128,512]{1,0:T(8,128)(2,1)} %bitcast.38), channel_id=1, source_target_pairs={{0,24},{8,0},{16,8},{24,16},{1,25},{9,1},{17,9},{25,17},{2,26},{10... | collective-permute-start | bytes 393224 | tf_op jit(solution)/shard_map/ppermute | solution.py:40
  11.5 11.4 %collective-permute-start.2 = (bf16[128,512]{1,0:T(8,128)(2,1)}, bf16[128,512]{1,0:T(8,128)(2,1)}, u32[]{:S(2)}, u32[]{:S(2)}) collective-permute-start(bf16[128,512]{1,0:T(8,128)(2,1)} %bitcast.39), channel_id=1, source_target_pairs={{0,16},{8,24},{16,0},{24,8},{1,17},{9,25},{17,1},{25,9},{2,18},{10... | collective-permute-start | bytes 393224 | tf_op jit(solution)/shard_map/ppermute | solution.py:40
  13.6 17.6 %collective-permute-start.3 = (bf16[128,512]{1,0:T(8,128)(2,1)}, bf16[128,512]{1,0:T(8,128)(2,1)}, u32[]{:S(2)}, u32[]{:S(2)}) collective-permute-start(bf16[128,512]{1,0:T(8,128)(2,1)} %bitcast.40), channel_id=1, source_target_pairs={{0,8},{8,16},{16,24},{24,0},{1,9},{9,17},{17,25},{25,1},{2,10},{10... | collective-permute-start | bytes 393224 | tf_op jit(solution)/shard_map/ppermute | solution.py:40
  17.9 49.8 %collective-permute-start.6 = (bf16[384,512]{1,0:T(8,128)(2,1)}, bf16[384,512]{1,0:T(8,128)(2,1)}, u32[]{:S(2)}, u32[]{:S(2)}) collective-permute-start(bf16[384,512]{1,0:T(8,128)(2,1)} %bitcast.36), channel_id=1, source_target_pairs={{0,1},{1,0},{2,3},{3,2},{4,5},{5,4},{6,7},{7,6},{8,9},{9,8},{10,11... | collective-permute-start | bytes 1179656 | tf_op jit(solution)/shard_map/ppermute | solution.py:40
  33.1 30.1 %collective-permute-start.4 = (bf16[512,512]{1,0:T(8,128)(2,1)}, bf16[512,512]{1,0:T(8,128)(2,1)}, u32[]{:S(2)}, u32[]{:S(2)}) collective-permute-start(bf16[512,512]{1,0:T(8,128)(2,1)} %pad_maximum_fusion.1), channel_id=1, source_target_pairs={{0,4},{2,6},{4,0},{6,2},{1,5},{3,7},{5,1},{7,3},{8,12},{10,14},{12... | collective-permute-start | bytes 1572872 | tf_op jit(solution)/shard_map/ppermute | solution.py:40
  35.0 29.8 %collective-permute-start.5 = (bf16[512,512]{1,0:T(8,128)(2,1)}, bf16[512,512]{1,0:T(8,128)(2,1)}, u32[]{:S(2)}, u32[]{:S(2)}) collective-permute-start(bf16[512,512]{1,0:T(8,128)(2,1)} %pad_maximum_fusion.1), channel_id=1, source_target_pairs={{0,6},{2,0},{4,2},{6,4},{1,7},{3,1},{5,3},{7,5},{8,14},{10,8},{12,... | collective-permute-start | bytes 1572872 | tf_op jit(solution)/shard_map/ppermute | solution.py:40
  37.0 30.7 %collective-permute-start.7 = (bf16[512,512]{1,0:T(8,128)(2,1)}, bf16[512,512]{1,0:T(8,128)(2,1)}, u32[]{:S(2)}, u32[]{:S(2)}) collective-permute-start(bf16[512,512]{1,0:T(8,128)(2,1)} %pad_maximum_fusion.1), channel_id=1, source_target_pairs={{0,2},{2,4},{4,6},{6,0},{1,3},{3,5},{5,7},{7,1},{8,10},{10,12},{12... | collective-permute-start | bytes 1572872 | tf_op jit(solution)/shard_map/ppermute | solution.py:40
  41.9 14.4 %copy-start.3 = (f32[4096]{0:T(1024)S(1)}, f32[4096]{0:T(1024)}, u32[]{:S(2)}) copy-start(f32[4096]{0:T(1024)} %param.8) | copy-start | bytes 49156
  44.9 22.8 %all-to-all-start = ((bf16[16,64,128]{2,1,0:T(8,128)(2,1)}), bf16[16,64,128]{2,1,0:T(8,128)(2,1)S(1)}, u32[]{:S(2)}, u32[]{:S(2)}) async-start(bf16[16,64,128]{2,1,0:T(8,128)(2,1)} %multiply_convert_fusion), calls=%async_computation | async-start | bytes 524288 | tf_op jit(solution)/shard_map/all_to_all | solution.py:77
  54.7 1.7 %copy-start.1 = (bf16[384,4096]{1,0:T(8,128)(2,1)}, bf16[384,4096]{1,0:T(8,128)(2,1)S(1)}, u32[]{:S(2)}) copy-start(bf16[384,4096]{1,0:T(8,128)(2,1)S(1)} %collective-permute-done.theirs_ref) | copy-start | bytes 9437188
  56.4 1.9 %copy-start = (bf16[1,384,4096]{2,1,0:T(8,128)(2,1)S(1)}, bf16[1,384,4096]{2,1,0:T(8,128)(2,1)}, u32[]{:S(2)}) copy-start(bf16[1,384,4096]{2,1,0:T(8,128)(2,1)} %param.7) | copy-start | bytes 9437188
  58.3 1.9 %copy-start.2 = (bf16[384,4096]{1,0:T(8,128)(2,1)S(1)}, bf16[384,4096]{1,0:T(8,128)(2,1)}, u32[]{:S(2)}) copy-start(bf16[384,4096]{1,0:T(8,128)(2,1)} %copy-done.1) | copy-start | bytes 9437188
  67.6 1.7 %copy-start.4 = (f32[768,512]{1,0:T(8,128)S(1)}, f32[768,512]{1,0:T(8,128)}, u32[]{:S(2)}) copy-start(f32[768,512]{1,0:T(8,128)} %add_add_fusion) | copy-start | bytes 4718596
  70.9 6.9 %collective-permute-start.8 = (f32[768,512]{1,0:T(8,128)}, f32[768,512]{1,0:T(8,128)}, u32[]{:S(2)}, u32[]{:S(2)}) collective-permute-start(f32[768,512]{1,0:T(8,128)} %add.120), channel_id=1, source_target_pairs={{0,1},{1,0},{2,3},{3,2},{4,5},{5,4},{6,7},{7,6},{8,9},{9,8},{10,11... | collective-permute-start | bytes 4718600 | tf_op jit(solution)/shard_map/ppermute | solution.py:40
  82.1 9.7 %copy-start.6 = (f32[8192]{0:T(1024)S(1)}, f32[8192]{0:T(1024)}, u32[]{:S(2)}) copy-start(f32[8192]{0:T(1024)} %param.13) | copy-start | bytes 98308
  82.8 26.3 %collective-permute-start.11 = (bf16[512,512]{1,0:T(8,128)(2,1)S(1)}, bf16[512,512]{1,0:T(8,128)(2,1)S(1)}, u32[]{:S(2)}, u32[]{:S(2)}) collective-permute-start(bf16[512,512]{1,0:T(8,128)(2,1)S(1)} %convolution_convert_fusion), channel_id=1, source_target_pairs={{0,6},{2,0},{4,2},{6,4},{1,7},{3,1},{5,3},{7,5},{8,14},{10,8},{12,... | collective-permute-start | bytes 1572872 | tf_op jit(solution)/shard_map/ppermute | solution.py:40
  86.8 27.2 %collective-permute-start.10 = (bf16[512,512]{1,0:T(8,128)(2,1)S(1)}, bf16[512,512]{1,0:T(8,128)(2,1)S(1)}, u32[]{:S(2)}, u32[]{:S(2)}) collective-permute-start(bf16[512,512]{1,0:T(8,128)(2,1)S(1)} %convolution_convert_fusion.1), channel_id=1, source_target_pairs={{0,2},{2,4},{4,6},{6,0},{1,3},{3,5},{5,7},{7,1},{8,10},{10,12},{12... | collective-permute-start | bytes 1572872 | tf_op jit(solution)/shard_map/ppermute | solution.py:40
  88.8 25.2 %collective-permute-start.9 = (bf16[512,512]{1,0:T(8,128)(2,1)S(1)}, bf16[512,512]{1,0:T(8,128)(2,1)S(1)}, u32[]{:S(2)}, u32[]{:S(2)}) collective-permute-start(bf16[512,512]{1,0:T(8,128)(2,1)S(1)} %convolution_convert_fusion.2), channel_id=1, source_target_pairs={{0,4},{2,6},{4,0},{6,2},{1,5},{3,7},{5,1},{7,3},{8,12},{10,14},{12... | collective-permute-start | bytes 1572872 | tf_op jit(solution)/shard_map/ppermute | solution.py:40
  114.3 13.7 %collective-permute-start.12 = (bf16[128,512]{1,0:T(8,128)(2,1)S(1)}, bf16[128,512]{1,0:T(8,128)(2,1)S(1)}, u32[]{:S(2)}, u32[]{:S(2)}) collective-permute-start(bf16[128,512]{1,0:T(8,128)(2,1)S(1)} %get-tuple-element.33), channel_id=1, source_target_pairs={{0,16},{8,24},{16,0},{24,8},{1,17},{9,25},{17,1},{25,9},{2,18},{10... | collective-permute-start | bytes 393224 | tf_op jit(solution)/shard_map/ppermute | solution.py:40
  120.7 8.4 %collective-permute-start.13 = (bf16[128,512]{1,0:T(8,128)(2,1)S(1)}, bf16[128,512]{1,0:T(8,128)(2,1)S(1)}, u32[]{:S(2)}, u32[]{:S(2)}) collective-permute-start(bf16[128,512]{1,0:T(8,128)(2,1)S(1)} %get-tuple-element.35), channel_id=1, source_target_pairs={{0,8},{8,16},{16,24},{24,0},{1,9},{9,17},{17,25},{25,1},{2,10},{10... | collective-permute-start | bytes 393224 | tf_op jit(solution)/shard_map/ppermute | solution.py:40
  123.2 8.3 %collective-permute-start.14 = (bf16[128,512]{1,0:T(8,128)(2,1)S(1)}, bf16[128,512]{1,0:T(8,128)(2,1)S(1)}, u32[]{:S(2)}, u32[]{:S(2)}) collective-permute-start(bf16[128,512]{1,0:T(8,128)(2,1)S(1)} %get-tuple-element.34), channel_id=1, source_target_pairs={{0,24},{8,0},{16,8},{24,16},{1,25},{9,1},{17,9},{25,17},{2,26},{10... | collective-permute-start | bytes 393224 | tf_op jit(solution)/shard_map/ppermute | solution.py:40
  133.4 19.5 %all-to-all-start.2 = ((f32[32,1,1]{2,1,0:T(1,128)}), f32[32,1,1]{2,1,0:T(1,128)S(1)}, u32[]{:S(2)}, u32[]{:S(2)}) async-start(f32[32,1,1]{2,1,0:T(1,128)} %broadcast_in_dim.10), calls=%async_computation.2 | async-start | bytes 32768 | tf_op jit(solution)/shard_map/all_to_all | solution.py:77

commit v6 on v4

--- a/solution.py
+++ b/solution.py
@@ -44,35 +44,40 @@
     return lax.optimization_barrier(values)
 
 
-def arrange_kernel(order_ref, inputs_ref, gain_ref, own_ref, other_ref):
-    for half, out_ref in enumerate((own_ref, other_ref)):
-        for j in range(CHIPS):
-            start = pl.multiple_of(order_ref[half * CHIPS + j] * LANES, LANES)
-            columns = pl.ds(start, LANES)
-            out_ref[:, j * LANES : (j + 1) * LANES] = (
-                inputs_ref[:, columns].astype(jnp.float32) * gain_ref[:, columns]
+def arrange_kernel(order_ref, inputs_ref, theirs_ref, gain_ref, scaled_ref):
+    for j in range(CHIPS):
+        start = pl.multiple_of(order_ref[j] * LANES, LANES)
+        columns = pl.ds(start, LANES)
+        gain = gain_ref[:, columns]
+        for half, ref in enumerate((inputs_ref, theirs_ref)):
+            scaled_ref[half, :, j * LANES : (j + 1) * LANES] = (
+                ref[:, columns].astype(jnp.float32) * gain
             ).astype(jnp.bfloat16)
 
 
-def arrange(inputs, feature_gain):
+def arrange(inputs, theirs, feature_gain):
     tokens, features = inputs.shape
     x, y, core = (lax.axis_index(name) for name in ("x", "y_hi", "core"))
     rx, ry = jnp.arange(CHIPS) // AXES["y_hi"], jnp.arange(CHIPS) % AXES["y_hi"]
     chip = (y + ry) % AXES["y_hi"] * AXES["x"] + (x + rx) % AXES["x"]
-    order = jnp.concatenate([chip * 2 + core, chip * 2 + 1 - core]).astype(jnp.int32)
-    half = jax.ShapeDtypeStruct((tokens, features // 2), jnp.bfloat16)
-    return pl.pallas_call(
+    order = (chip * 2 + core).astype(jnp.int32)
+    step = 96
+    block = pl.BlockSpec((step, features), lambda i: (i, 0))
+    scaled = pl.pallas_call(
         arrange_kernel,
-        out_shape=(half, half),
+        grid=(tokens // step,),
+        out_shape=jax.ShapeDtypeStruct((2, tokens, features // 2), jnp.bfloat16),
         in_specs=[
             pl.BlockSpec(memory_space=pltpu.SMEM),
-            pl.BlockSpec(memory_space=pltpu.VMEM),
-            pl.BlockSpec(memory_space=pltpu.VMEM),
+            block,
+            block,
+            pl.BlockSpec((1, features), lambda i: (0, 0)),
         ],
-        out_specs=(pl.BlockSpec(memory_space=pltpu.VMEM),) * 2,
+        out_specs=pl.BlockSpec((2, step, features // 2), lambda i: (0, i, 0)),
         compiler_params=pltpu.CompilerParams(vmem_limit_bytes=24 << 20),
         name="arrange",
-    )(order, inputs, feature_gain[None, :])
+    )(order, inputs, theirs, feature_gain[None, :])
+    return scaled.reshape(2 * tokens, features // 2)
 
 
 def exchange(parts, axis):
@@ -115,21 +120,24 @@
     near = [weight] + [None] * 3
     for k in STEPS:
         near[k] = send(weight, "y_hi", -k)
+    near[1], inputs, teacher_keys, global_frag, local_frag = tied(
+        near[1], inputs, teacher_keys, global_frag, local_frag
+    )
+    raw = send(inputs[0], "core", 1)
+    their_targets = send(teacher_keys[0], "core", 1)
     arrived = exchange(fragment_codes(global_frag, local_frag[0]), REPLICA)
     column = jnp.concatenate(near, axis=0)
-    own, other = arrange(inputs[0], feature_gain)
-    column, arrived, own, other = tied(column, arrived, own, other)
     far = {k: send(column, "x", -k) for k in STEPS}
-    scaled = jnp.concatenate([own, send(other, "core", 1)], axis=0)
-    targets = jnp.concatenate([teacher_keys[0], send(teacher_keys[0], "core", 1)], axis=0)
-    scaled, targets = tied(scaled, targets)
+    new_global, new_momentum = fragment_update(arrived, global_frag, momentum)
+    targets = jnp.concatenate([teacher_keys[0], their_targets], axis=0)
+    scaled = arrange(inputs[0], raw, feature_gain)
     group = scaled.shape[1] // AXES["x"]
     blocks = [scaled[:, k * group : (k + 1) * group] for k in range(AXES["x"])]
     partial = jnp.dot(blocks[0], column, preferred_element_type=jnp.float32)
-    new_global, new_momentum = fragment_update(arrived, global_frag, momentum)
+    last = STEPS[-1]
+    far[last], new_global, targets = tied(far[last], new_global, targets)
     for k in STEPS:
         partial += jnp.dot(blocks[k], far[k], preferred_element_type=jnp.float32)
-    partial, new_global = tied(partial, new_global)
 
     theirs = send(partial, "core", 1)
     projected = partial + jnp.concatenate([theirs[tokens:], theirs[:tokens]], axis=0)

time: 163 us -> 176 us (1.080)
  waiting for transfers between devices: 42 us -> 53 us
  starting transfers between devices: 88.3 us -> 92.8 us
  local copies, waits for them, and re-layouts: 6.69 us -> 3.64 us
  Pallas kernels: 1.42 us -> 3.3 us
  other arithmetic: 13.6 us -> 11.8 us
    ppermute x15, starting transfers between devices: 56.3 us -> 68.9 us  [send(): lax.ppermute(value, axis, [(i, (i + step) % size) for i in range(size)])]
    ppermute x15, waiting for transfers between devices: 33.3 us -> 44.2 us  [send(): lax.ppermute(value, axis, [(i, (i + step) % size) for i in range(size)])]
    all_to_all x3, starting transfers between devices: 32 us -> 24 us  [exchange(): return lax.all_to_all(parts, axis, split_axis=0, concat_axis=0, tiled=True)]
    unnamed x17 -> x21, local copies, waits for them, and re-layouts: 4.46 us -> 1.41 us
    pallas_call x1, Pallas kernels: 1.42 us -> 3.3 us  [arrange(): pl.pallas_call(arrange_kernel, grid=(tokens // step,), out_shape=jax.Shap...]
  transfers between devices with their start and end apart: 18 -> 18, of which waited for: 9 -> 10; matrix products, arithmetic and copies ran while one was open for 7% -> 8% of each run, Pallas kernels for 1% -> 2%
where the time goes in v6:
time: 176 us; the launch traced here: 175 us
  starting transfers between devices  92.8 us (53%)
  waiting for transfers between devices  53 us (30%)
  other arithmetic  11.8 us (7%)
  matrix products  8.91 us (5%)
  local copies, waits for them, and re-layouts  3.64 us (2%)
  Pallas kernels  3.3 us (2%)
    ppermute x15, starting transfers between devices, send(): lax.ppermute(value, axis, [(i, (i + step) % size) for i in range(size)])  68.9 us
    ppermute x15, waiting for transfers between devices, send(): lax.ppermute(value, axis, [(i, (i + step) % size) for i in range(size)])  44.2 us
    all_to_all x3, starting transfers between devices, exchange(): return lax.all_to_all(parts, axis, split_axis=0, concat_axis=0, tiled=True)  24 us
    all_to_all x3, waiting for transfers between devices, exchange(): return lax.all_to_all(parts, axis, split_axis=0, concat_axis=0, tiled=True)  8.83 us
    dot_general x3, matrix products, shards(): partial += jnp.dot(blocks[k], far[k], preferred_element_type=jnp.float32)  4.92 us
  transfers between devices with their start and end apart: 18, of which 10 were waited for; matrix products, arithmetic and copies ran while one was open for 8% of the time, Pallas kernels for 2%

profile of v6, /device:TPU:1, one launch (start us, length us, event | category | flops | bytes accessed | tf_op | source)
XLA Modules:
  0.0 175.2 jit_solution(8351814707222650507)
XLA Ops:
  0.6 6.7 %collective-permute-start = (bf16[128,512]{1,0:T(8,128)(2,1)}, bf16[128,512]{1,0:T(8,128)(2,1)S(1)}, u32[]{:S(2)}, u32[]{:S(2)}) collective-permute-start(bf16[128,512]{1,0:T(8,128)(2,1)} %bitcast.48), channel_id=1, source_target_pairs={{0,24},{8,0},{16,8},{24,16},{1,25},{9,1},{17,9},{25,17},{2,26},{10... | collective-permute-start | bytes 393224 | tf_op jit(solution)/shard_map/ppermute | solution.py:40
  7.4 5.9 %collective-permute-done = bf16[128,512]{1,0:T(8,128)(2,1)S(1)} collective-permute-done((bf16[128,512]{1,0:T(8,128)(2,1)}, bf16[128,512]{1,0:T(8,128)(2,1)S(1)}, u32[]{:S(2)}, u32[]{:S(2)}) %collective-permute-start) | collective-permute-done | bytes 131104 | tf_op jit(solution)/shard_map/ppermute | solution.py:40
  13.3 4.1 %collective-permute-start.1 = (bf16[384,4096]{1,0:T(8,128)(2,1)}, bf16[384,4096]{1,0:T(8,128)(2,1)}, u32[]{:S(2)}, u32[]{:S(2)}) collective-permute-start(bf16[384,4096]{1,0:T(8,128)(2,1)} %bitcast.42), channel_id=1, source_target_pairs={{0,1},{1,0},{2,3},{3,2},{4,5},{5,4},{6,7},{7,6},{8,9},{9,8},{10,11... | collective-permute-start | bytes 9437192 | tf_op jit(solution)/shard_map/ppermute | solution.py:40
  17.4 1.6 convert_element_type.130
  19.0 0.0 copy-start.4
  19.0 1.2 bitcast_reduce_fusion
  20.2 0.0 copy-start.3
  20.2 0.1 reshape.96
  20.3 0.9 multiply_convert_fusion
  21.2 8.9 %all-to-all-start = ((bf16[16,64,128]{2,1,0:T(8,128)(2,1)}), bf16[16,64,128]{2,1,0:T(8,128)(2,1)S(1)}, u32[]{:S(2)}, u32[]{:S(2)}) async-start(bf16[16,64,128]{2,1,0:T(8,128)(2,1)} %multiply_convert_fusion), calls=%async_computation | async-start | bytes 524288 | tf_op jit(solution)/shard_map/all_to_all | solution.py:84
  30.1 4.4 %collective-permute-start.3 = (bf16[128,512]{1,0:T(8,128)(2,1)S(1)}, bf16[128,512]{1,0:T(8,128)(2,1)S(1)}, u32[]{:S(2)}, u32[]{:S(2)}) collective-permute-start(bf16[128,512]{1,0:T(8,128)(2,1)S(1)} %bitcast.50), channel_id=1, source_target_pairs={{0,8},{8,16},{16,24},{24,0},{1,9},{9,17},{17,25},{25,1},{2,10},{10... | collective-permute-start | bytes 393224 | tf_op jit(solution)/shard_map/ppermute | solution.py:40
  34.5 5.7 %collective-permute-start.2 = (bf16[128,512]{1,0:T(8,128)(2,1)S(1)}, bf16[128,512]{1,0:T(8,128)(2,1)}, u32[]{:S(2)}, u32[]{:S(2)}) collective-permute-start(bf16[128,512]{1,0:T(8,128)(2,1)S(1)} %bitcast.51), channel_id=1, source_target_pairs={{0,16},{8,24},{16,0},{24,8},{1,17},{9,25},{17,1},{25,9},{2,18},{10... | collective-permute-start | bytes 393224 | tf_op jit(solution)/shard_map/ppermute | solution.py:40
  40.2 2.8 %collective-permute-start.7 = (bf16[384,512]{1,0:T(8,128)(2,1)}, bf16[384,512]{1,0:T(8,128)(2,1)}, u32[]{:S(2)}, u32[]{:S(2)}) collective-permute-start(bf16[384,512]{1,0:T(8,128)(2,1)} %bitcast.10), channel_id=1, source_target_pairs={{0,1},{1,0},{2,3},{3,2},{4,5},{5,4},{6,7},{7,6},{8,9},{9,8},{10,11... | collective-permute-start | bytes 1179656 | tf_op jit(solution)/shard_map/ppermute | solution.py:40
  43.0 0.0 collective-permute-done.3
  43.0 0.0 copy-start.8
  43.0 0.6 copy-done.8
  43.6 5.7 %collective-permute-done.2 = bf16[128,512]{1,0:T(8,128)(2,1)} collective-permute-done((bf16[128,512]{1,0:T(8,128)(2,1)S(1)}, bf16[128,512]{1,0:T(8,128)(2,1)}, u32[]{:S(2)}, u32[]{:S(2)}) %collective-permute-start.2) | collective-permute-done | bytes 131104 | tf_op jit(solution)/shard_map/ppermute | solution.py:40
  49.3 2.1 %pad_maximum_fusion.1 = bf16[512,512]{1,0:T(8,128)(2,1)} fusion(bf16[128,512]{1,0:T(8,128)(2,1)} %copy-done.8, bf16[128,512]{1,0:T(8,128)(2,1)} %collective-permute-done.2, bf16[128,512]{1,0:T(8,128)(2,1)} %copy-done.6, bf16[128,512]{1,0:T(8,128)(2,1)} %bitcast.49), kind=kLoop, calls=%fused_computation.26 | loop fusion | flops 2097152 | bytes 1048576 | tf_op jit(solution)/shard_map/concatenate | solution.py:129
  51.4 3.2 %collective-permute-start.6 = (bf16[512,512]{1,0:T(8,128)(2,1)}, bf16[512,512]{1,0:T(8,128)(2,1)}, u32[]{:S(2)}, u32[]{:S(2)}) collective-permute-start(bf16[512,512]{1,0:T(8,128)(2,1)} %pad_maximum_fusion.1), channel_id=1, source_target_pairs={{0,2},{2,4},{4,6},{6,0},{1,3},{3,5},{5,7},{7,1},{8,10},{10,12},{12... | collective-permute-start | bytes 1572872 | tf_op jit(solution)/shard_map/ppermute | solution.py:40
  54.6 0.0 all-to-all-done
  54.7 0.7 fusion.22
  55.4 0.8 broadcast_in_dim.9
  56.2 6.1 %all-to-all-start.1 = ((bf16[16,64,128]{2,1,0:T(8,128)(2,1)}), bf16[16,64,128]{2,1,0:T(8,128)(2,1)S(1)}, u32[]{:S(2)}, u32[]{:S(2)}) async-start(bf16[16,64,128]{2,1,0:T(8,128)(2,1)} %broadcast_in_dim.9), calls=%async_computation.1 | async-start | bytes 524288 | tf_op jit(solution)/shard_map/all_to_all | solution.py:84
  62.3 3.4 %collective-permute-start.5 = (bf16[512,512]{1,0:T(8,128)(2,1)}, bf16[512,512]{1,0:T(8,128)(2,1)}, u32[]{:S(2)}, u32[]{:S(2)}) collective-permute-start(bf16[512,512]{1,0:T(8,128)(2,1)} %pad_maximum_fusion.1), channel_id=1, source_target_pairs={{0,6},{2,0},{4,2},{6,4},{1,7},{3,1},{5,3},{7,5},{8,14},{10,8},{12,... | collective-permute-start | bytes 1572872 | tf_op jit(solution)/shard_map/ppermute | solution.py:40
  65.7 3.4 %collective-permute-start.4 = (bf16[512,512]{1,0:T(8,128)(2,1)}, bf16[512,512]{1,0:T(8,128)(2,1)}, u32[]{:S(2)}, u32[]{:S(2)}) collective-permute-start(bf16[512,512]{1,0:T(8,128)(2,1)} %pad_maximum_fusion.1), channel_id=1, source_target_pairs={{0,4},{2,6},{4,0},{6,2},{1,5},{3,7},{5,1},{7,3},{8,12},{10,14},{12... | collective-permute-start | bytes 1572872 | tf_op jit(solution)/shard_map/ppermute | solution.py:40
  69.1 0.0 collective-permute-done.7
  69.1 2.1 %pad_maximum_fusion = bf16[768,512]{1,0:T(8,128)(2,1)} fusion(bf16[384,512]{1,0:T(8,128)(2,1)} %collective-permute-done.7, bf16[384,512]{1,0:T(8,128)(2,1)} %bitcast.10), kind=kLoop, calls=%fused_computation.13 | loop fusion | flops 1572864 | bytes 1572864 | tf_op jit(solution)/shard_map/concatenate | solution.py:132
  71.2 0.0 collective-permute-done.6
  71.2 0.1 all-to-all-done.1
  71.3 0.0 collective-permute-done.1.theirs_ref
  71.4 0.0 copy-start.5
  71.4 0.0 copy-start.9
  71.4 3.3 %arrange.1 = bf16[2,384,2048]{2,1,0:T(8,128)(2,1)S(1)} custom-call(s32[16]{0:T(128)S(1)} %fusion.34.order_ref, bf16[384,4096]{1,0:T(8,128)(2,1)S(1)} %bitcast.43, bf16[384,4096]{1,0:T(8,128)(2,1)} %collective-permute-done.1.theirs_ref, f32[1,4096]{1,0:T(1,128)S(1)} %bitcast.44), custom_call_target="tpu_custom_call" | custom-call | tf_op jit(solution)/shard_map/arrange/pallas_call | solution.py:66
  74.7 1.5 fusion.19
  76.2 1.6 fusion.13
  77.8 2.8 %collective-permute-done.4 = bf16[512,512]{1,0:T(8,128)(2,1)} collective-permute-done((bf16[512,512]{1,0:T(8,128)(2,1)}, bf16[512,512]{1,0:T(8,128)(2,1)}, u32[]{:S(2)}, u32[]{:S(2)}) %collective-permute-start.4) | collective-permute-done | bytes 524320 | tf_op jit(solution)/shard_map/ppermute | solution.py:40
  80.6 1.6 fusion.16
  82.3 1.7 add_add_fusion
  84.0 12.4 %collective-permute-start.8 = (f32[768,512]{1,0:T(8,128)S(1)}, f32[768,512]{1,0:T(8,128)S(1)}, u32[]{:S(2)}, u32[]{:S(2)}) collective-permute-start(f32[768,512]{1,0:T(8,128)S(1)} %add_add_fusion), channel_id=1, source_target_pairs={{0,1},{1,0},{2,3},{3,2},{4,5},{5,4},{6,7},{7,6},{8,9},{9,8},{10,11... | collective-permute-start | bytes 4718600 | tf_op jit(solution)/shard_map/ppermute | solution.py:40
  96.4 3.0 %collective-permute-done.8 = f32[768,512]{1,0:T(8,128)S(1)} collective-permute-done((f32[768,512]{1,0:T(8,128)S(1)}, f32[768,512]{1,0:T(8,128)S(1)}, u32[]{:S(2)}, u32[]{:S(2)}) %collective-permute-start.8) | collective-permute-done | bytes 1572896 | tf_op jit(solution)/shard_map/ppermute | solution.py:40
  99.4 0.1 fusion.35
  99.5 0.5 fusion.1
  100.0 0.6 convolution_convert_fusion
  100.6 0.6 convolution_convert_fusion.1
  101.2 0.6 convolution_convert_fusion.2
  101.8 1.9 %collective-permute-start.9 = (bf16[512,512]{1,0:T(8,128)(2,1)S(1)}, bf16[512,512]{1,0:T(8,128)(2,1)S(1)}, u32[]{:S(2)}, u32[]{:S(2)}) collective-permute-start(bf16[512,512]{1,0:T(8,128)(2,1)S(1)} %convolution_convert_fusion.2), channel_id=1, source_target_pairs={{0,4},{2,6},{4,0},{6,2},{1,5},{3,7},{5,1},{7,3},{8,12},{10,14},{12... | collective-permute-start | bytes 1572872 | tf_op jit(solution)/shard_map/ppermute | solution.py:40
  103.7 5.8 %collective-permute-start.10 = (bf16[512,512]{1,0:T(8,128)(2,1)S(1)}, bf16[512,512]{1,0:T(8,128)(2,1)S(1)}, u32[]{:S(2)}, u32[]{:S(2)}) collective-permute-start(bf16[512,512]{1,0:T(8,128)(2,1)S(1)} %convolution_convert_fusion.1), channel_id=1, source_target_pairs={{0,2},{2,4},{4,6},{6,0},{1,3},{3,5},{5,7},{7,1},{8,10},{10,12},{12... | collective-permute-start | bytes 1572872 | tf_op jit(solution)/shard_map/ppermute | solution.py:40
  109.6 1.9 %collective-permute-start.11 = (bf16[512,512]{1,0:T(8,128)(2,1)S(1)}, bf16[512,512]{1,0:T(8,128)(2,1)S(1)}, u32[]{:S(2)}, u32[]{:S(2)}) collective-permute-start(bf16[512,512]{1,0:T(8,128)(2,1)S(1)} %convolution_convert_fusion), channel_id=1, source_target_pairs={{0,6},{2,0},{4,2},{6,4},{1,7},{3,1},{5,3},{7,5},{8,14},{10,8},{12,... | collective-permute-start | bytes 1572872 | tf_op jit(solution)/shard_map/ppermute | solution.py:40
  111.5 6.9 %collective-permute-done.9 = bf16[512,512]{1,0:T(8,128)(2,1)S(1)} collective-permute-done((bf16[512,512]{1,0:T(8,128)(2,1)S(1)}, bf16[512,512]{1,0:T(8,128)(2,1)S(1)}, u32[]{:S(2)}, u32[]{:S(2)}) %collective-permute-start.9) | collective-permute-done | bytes 524320 | tf_op jit(solution)/shard_map/ppermute | solution.py:40
  118.4 11.9 %collective-permute-done.10 = bf16[512,512]{1,0:T(8,128)(2,1)S(1)} collective-permute-done((bf16[512,512]{1,0:T(8,128)(2,1)S(1)}, bf16[512,512]{1,0:T(8,128)(2,1)S(1)}, u32[]{:S(2)}, u32[]{:S(2)}) %collective-permute-start.10) | collective-permute-done | bytes 524320 | tf_op jit(solution)/shard_map/ppermute | solution.py:40
  130.3 0.3 collective-permute-done.11
  130.6 0.7 fusion.6
  131.3 6.2 %collective-permute-start.12 = (bf16[128,512]{1,0:T(8,128)(2,1)S(1)}, bf16[128,512]{1,0:T(8,128)(2,1)S(1)}, u32[]{:S(2)}, u32[]{:S(2)}) collective-permute-start(bf16[128,512]{1,0:T(8,128)(2,1)S(1)} %get-tuple-element.23), channel_id=1, source_target_pairs={{0,16},{8,24},{16,0},{24,8},{1,17},{9,25},{17,1},{25,9},{2,18},{10... | collective-permute-start | bytes 393224 | tf_op jit(solution)/shard_map/ppermute | solution.py:40
  137.6 5.0 %collective-permute-start.14 = (bf16[128,512]{1,0:T(8,128)(2,1)S(1)}, bf16[128,512]{1,0:T(8,128)(2,1)S(1)}, u32[]{:S(2)}, u32[]{:S(2)}) collective-permute-start(bf16[128,512]{1,0:T(8,128)(2,1)S(1)} %get-tuple-element.24), channel_id=1, source_target_pairs={{0,24},{8,0},{16,8},{24,16},{1,25},{9,1},{17,9},{25,17},{2,26},{10... | collective-permute-start | bytes 393224 | tf_op jit(solution)/shard_map/ppermute | solution.py:40
  142.6 1.9 %collective-permute-start.13 = (bf16[128,512]{1,0:T(8,128)(2,1)S(1)}, bf16[128,512]{1,0:T(8,128)(2,1)S(1)}, u32[]{:S(2)}, u32[]{:S(2)}) collective-permute-start(bf16[128,512]{1,0:T(8,128)(2,1)S(1)} %get-tuple-element.25), channel_id=1, source_target_pairs={{0,8},{8,16},{16,24},{24,0},{1,9},{9,17},{17,25},{25,1},{2,10},{10... | collective-permute-start | bytes 393224 | tf_op jit(solution)/shard_map/ppermute | solution.py:40
  144.5 7.6 %collective-permute-done.14 = bf16[128,512]{1,0:T(8,128)(2,1)S(1)} collective-permute-done((bf16[128,512]{1,0:T(8,128)(2,1)S(1)}, bf16[128,512]{1,0:T(8,128)(2,1)S(1)}, u32[]{:S(2)}, u32[]{:S(2)}) %collective-permute-start.14) | collective-permute-done | bytes 131104 | tf_op jit(solution)/shard_map/ppermute | solution.py:40
  152.2 0.7 multiply_reduce_fusion
  152.8 1.3 broadcast_in_dim.10
  154.1 9.0 %all-to-all-start.2 = ((f32[32,1,1]{2,1,0:T(1,128)}), f32[32,1,1]{2,1,0:T(1,128)S(1)}, u32[]{:S(2)}, u32[]{:S(2)}) async-start(f32[32,1,1]{2,1,0:T(1,128)} %broadcast_in_dim.10), calls=%async_computation.2 | async-start | bytes 32768 | tf_op jit(solution)/shard_map/all_to_all | solution.py:84
  163.1 0.6 bitcast_add_fusion
  163.7 8.7 %all-to-all-done.2 = f32[32,1,1]{2,1,0:T(1,128)S(1)} async-done(((f32[32,1,1]{2,1,0:T(1,128)}), f32[32,1,1]{2,1,0:T(1,128)S(1)}, u32[]{:S(2)}, u32[]{:S(2)}) %all-to-all-start.2) | async-done | bytes 160 | tf_op jit(solution)/shard_map/all_to_all | solution.py:84
  172.4 0.6 reduce_sum.39
  173.8 0.7 fusion.21
  174.5 0.7 copy.13
  (21 shorter events, 0.1 us)
Async XLA Ops:
  0.6 12.7 %collective-permute-start = (bf16[128,512]{1,0:T(8,128)(2,1)}, bf16[128,512]{1,0:T(8,128)(2,1)S(1)}, u32[]{:S(2)}, u32[]{:S(2)}) collective-permute-start(bf16[128,512]{1,0:T(8,128)(2,1)} %bitcast.48), channel_id=1, source_target_pairs={{0,24},{8,0},{16,8},{24,16},{1,25},{9,1},{17,9},{25,17},{2,26},{10... | collective-permute-start | bytes 393224 | tf_op jit(solution)/shard_map/ppermute | solution.py:40
  13.3 5.7 %copy-start.6 = (bf16[128,512]{1,0:T(8,128)(2,1)}, bf16[128,512]{1,0:T(8,128)(2,1)S(1)}, u32[]{:S(2)}) copy-start(bf16[128,512]{1,0:T(8,128)(2,1)S(1)} %collective-permute-done) | copy-start | bytes 393220
  13.3 58.0 %collective-permute-start.1 = (bf16[384,4096]{1,0:T(8,128)(2,1)}, bf16[384,4096]{1,0:T(8,128)(2,1)}, u32[]{:S(2)}, u32[]{:S(2)}) collective-permute-start(bf16[384,4096]{1,0:T(8,128)(2,1)} %bitcast.42), channel_id=1, source_target_pairs={{0,1},{1,0},{2,3},{3,2},{4,5},{5,4},{6,7},{7,6},{8,9},{9,8},{10,11... | collective-permute-start | bytes 9437192 | tf_op jit(solution)/shard_map/ppermute | solution.py:40
  19.0 11.1 %copy-start.4 = (bf16[1,128,512]{2,1,0:T(8,128)(2,1)S(1)}, bf16[1,128,512]{2,1,0:T(8,128)(2,1)}, u32[]{:S(2)}) copy-start(bf16[1,128,512]{2,1,0:T(8,128)(2,1)} %param.9) | copy-start | bytes 393220
  20.2 34.5 %copy-start.3 = (f32[8192]{0:T(1024)S(1)}, f32[8192]{0:T(1024)}, u32[]{:S(2)}) copy-start(f32[8192]{0:T(1024)} %param.13) | copy-start | bytes 98308
  21.2 33.4 %all-to-all-start = ((bf16[16,64,128]{2,1,0:T(8,128)(2,1)}), bf16[16,64,128]{2,1,0:T(8,128)(2,1)S(1)}, u32[]{:S(2)}, u32[]{:S(2)}) async-start(bf16[16,64,128]{2,1,0:T(8,128)(2,1)} %multiply_convert_fusion), calls=%async_computation | async-start | bytes 524288 | tf_op jit(solution)/shard_map/all_to_all | solution.py:84
  30.1 12.9 %collective-permute-start.3 = (bf16[128,512]{1,0:T(8,128)(2,1)S(1)}, bf16[128,512]{1,0:T(8,128)(2,1)S(1)}, u32[]{:S(2)}, u32[]{:S(2)}) collective-permute-start(bf16[128,512]{1,0:T(8,128)(2,1)S(1)} %bitcast.50), channel_id=1, source_target_pairs={{0,8},{8,16},{16,24},{24,0},{1,9},{9,17},{17,25},{25,1},{2,10},{10... | collective-permute-start | bytes 393224 | tf_op jit(solution)/shard_map/ppermute | solution.py:40
  34.5 14.8 %collective-permute-start.2 = (bf16[128,512]{1,0:T(8,128)(2,1)S(1)}, bf16[128,512]{1,0:T(8,128)(2,1)}, u32[]{:S(2)}, u32[]{:S(2)}) collective-permute-start(bf16[128,512]{1,0:T(8,128)(2,1)S(1)} %bitcast.51), channel_id=1, source_target_pairs={{0,16},{8,24},{16,0},{24,8},{1,17},{9,25},{17,1},{25,9},{2,18},{10... | collective-permute-start | bytes 393224 | tf_op jit(solution)/shard_map/ppermute | solution.py:40
  40.2 28.9 %collective-permute-start.7 = (bf16[384,512]{1,0:T(8,128)(2,1)}, bf16[384,512]{1,0:T(8,128)(2,1)}, u32[]{:S(2)}, u32[]{:S(2)}) collective-permute-start(bf16[384,512]{1,0:T(8,128)(2,1)} %bitcast.10), channel_id=1, source_target_pairs={{0,1},{1,0},{2,3},{3,2},{4,5},{5,4},{6,7},{7,6},{8,9},{9,8},{10,11... | collective-permute-start | bytes 1179656 | tf_op jit(solution)/shard_map/ppermute | solution.py:40
  43.0 0.7 copy-start.8
  49.3 22.1 %copy-start = (bf16[1,384,4096]{2,1,0:T(8,128)(2,1)S(1)}, bf16[1,384,4096]{2,1,0:T(8,128)(2,1)}, u32[]{:S(2)}) copy-start(bf16[1,384,4096]{2,1,0:T(8,128)(2,1)} %param.7) | copy-start | bytes 9437188
  51.4 20.0 %copy-start.1 = (f32[4096]{0:T(1024)S(1)}, f32[4096]{0:T(1024)}, u32[]{:S(2)}) copy-start(f32[4096]{0:T(1024)} %param.8) | copy-start | bytes 49156
  51.4 19.8 %collective-permute-start.6 = (bf16[512,512]{1,0:T(8,128)(2,1)}, bf16[512,512]{1,0:T(8,128)(2,1)}, u32[]{:S(2)}, u32[]{:S(2)}) collective-permute-start(bf16[512,512]{1,0:T(8,128)(2,1)} %pad_maximum_fusion.1), channel_id=1, source_target_pairs={{0,2},{2,4},{4,6},{6,0},{1,3},{3,5},{5,7},{7,1},{8,10},{10,12},{12... | collective-permute-start | bytes 1572872 | tf_op jit(solution)/shard_map/ppermute | solution.py:40
  56.2 15.2 %all-to-all-start.1 = ((bf16[16,64,128]{2,1,0:T(8,128)(2,1)}), bf16[16,64,128]{2,1,0:T(8,128)(2,1)S(1)}, u32[]{:S(2)}, u32[]{:S(2)}) async-start(bf16[16,64,128]{2,1,0:T(8,128)(2,1)} %broadcast_in_dim.9), calls=%async_computation.1 | async-start | bytes 524288 | tf_op jit(solution)/shard_map/all_to_all | solution.py:84
  62.3 13.9 %collective-permute-start.5 = (bf16[512,512]{1,0:T(8,128)(2,1)}, bf16[512,512]{1,0:T(8,128)(2,1)}, u32[]{:S(2)}, u32[]{:S(2)}) collective-permute-start(bf16[512,512]{1,0:T(8,128)(2,1)} %pad_maximum_fusion.1), channel_id=1, source_target_pairs={{0,6},{2,0},{4,2},{6,4},{1,7},{3,1},{5,3},{7,5},{8,14},{10,8},{12,... | collective-permute-start | bytes 1572872 | tf_op jit(solution)/shard_map/ppermute | solution.py:40
  65.7 15.0 %collective-permute-start.4 = (bf16[512,512]{1,0:T(8,128)(2,1)}, bf16[512,512]{1,0:T(8,128)(2,1)}, u32[]{:S(2)}, u32[]{:S(2)}) collective-permute-start(bf16[512,512]{1,0:T(8,128)(2,1)} %pad_maximum_fusion.1), channel_id=1, source_target_pairs={{0,4},{2,6},{4,0},{6,2},{1,5},{3,7},{5,1},{7,3},{8,12},{10,14},{12... | collective-permute-start | bytes 1572872 | tf_op jit(solution)/shard_map/ppermute | solution.py:40
  71.4 3.3 %copy-start.5 = (bf16[1,128,512]{2,1,0:T(8,128)(2,1)S(1)}, bf16[1,128,512]{2,1,0:T(8,128)(2,1)}, u32[]{:S(2)}) copy-start(bf16[1,128,512]{2,1,0:T(8,128)(2,1)} %param.9) | copy-start | bytes 393220
  71.4 3.3 %copy-start.7 = (bf16[128,512]{1,0:T(8,128)(2,1)S(1)}, bf16[128,512]{1,0:T(8,128)(2,1)}, u32[]{:S(2)}) copy-start(bf16[128,512]{1,0:T(8,128)(2,1)} %copy-done.6) | copy-start | bytes 393220
  71.4 3.3 %copy-start.9 = (bf16[128,512]{1,0:T(8,128)(2,1)S(1)}, bf16[128,512]{1,0:T(8,128)(2,1)}, u32[]{:S(2)}) copy-start(bf16[128,512]{1,0:T(8,128)(2,1)} %copy-done.8) | copy-start | bytes 393220
  84.0 15.5 %copy-start.2 = (bf16[768,512]{1,0:T(8,128)(2,1)S(1)}, bf16[768,512]{1,0:T(8,128)(2,1)}, u32[]{:S(2)}) copy-start(bf16[768,512]{1,0:T(8,128)(2,1)} %pad_maximum_fusion) | copy-start | bytes 2359300
  84.0 15.4 %collective-permute-start.8 = (f32[768,512]{1,0:T(8,128)S(1)}, f32[768,512]{1,0:T(8,128)S(1)}, u32[]{:S(2)}, u32[]{:S(2)}) collective-permute-start(f32[768,512]{1,0:T(8,128)S(1)} %add_add_fusion), channel_id=1, source_target_pairs={{0,1},{1,0},{2,3},{3,2},{4,5},{5,4},{6,7},{7,6},{8,9},{9,8},{10,11... | collective-permute-start | bytes 4718600 | tf_op jit(solution)/shard_map/ppermute | solution.py:40
  101.8 16.6 %collective-permute-start.9 = (bf16[512,512]{1,0:T(8,128)(2,1)S(1)}, bf16[512,512]{1,0:T(8,128)(2,1)S(1)}, u32[]{:S(2)}, u32[]{:S(2)}) collective-permute-start(bf16[512,512]{1,0:T(8,128)(2,1)S(1)} %convolution_convert_fusion.2), channel_id=1, source_target_pairs={{0,4},{2,6},{4,0},{6,2},{1,5},{3,7},{5,1},{7,3},{8,12},{10,14},{12... | collective-permute-start | bytes 1572872 | tf_op jit(solution)/shard_map/ppermute | solution.py:40
  103.7 26.6 %collective-permute-start.10 = (bf16[512,512]{1,0:T(8,128)(2,1)S(1)}, bf16[512,512]{1,0:T(8,128)(2,1)S(1)}, u32[]{:S(2)}, u32[]{:S(2)}) collective-permute-start(bf16[512,512]{1,0:T(8,128)(2,1)S(1)} %convolution_convert_fusion.1), channel_id=1, source_target_pairs={{0,2},{2,4},{4,6},{6,0},{1,3},{3,5},{5,7},{7,1},{8,10},{10,12},{12... | collective-permute-start | bytes 1572872 | tf_op jit(solution)/shard_map/ppermute | solution.py:40
  109.6 21.0 %collective-permute-start.11 = (bf16[512,512]{1,0:T(8,128)(2,1)S(1)}, bf16[512,512]{1,0:T(8,128)(2,1)S(1)}, u32[]{:S(2)}, u32[]{:S(2)}) collective-permute-start(bf16[512,512]{1,0:T(8,128)(2,1)S(1)} %convolution_convert_fusion), channel_id=1, source_target_pairs={{0,6},{2,0},{4,2},{6,4},{1,7},{3,1},{5,3},{7,5},{8,14},{10,8},{12,... | collective-permute-start | bytes 1572872 | tf_op jit(solution)/shard_map/ppermute | solution.py:40
  131.3 13.2 %collective-permute-start.12 = (bf16[128,512]{1,0:T(8,128)(2,1)S(1)}, bf16[128,512]{1,0:T(8,128)(2,1)S(1)}, u32[]{:S(2)}, u32[]{:S(2)}) collective-permute-start(bf16[128,512]{1,0:T(8,128)(2,1)S(1)} %get-tuple-element.23), channel_id=1, source_target_pairs={{0,16},{8,24},{16,0},{24,8},{1,17},{9,25},{17,1},{25,9},{2,18},{10... | collective-permute-start | bytes 393224 | tf_op jit(solution)/shard_map/ppermute | solution.py:40
  137.6 14.6 %collective-permute-start.14 = (bf16[128,512]{1,0:T(8,128)(2,1)S(1)}, bf16[128,512]{1,0:T(8,128)(2,1)S(1)}, u32[]{:S(2)}, u32[]{:S(2)}) collective-permute-start(bf16[128,512]{1,0:T(8,128)(2,1)S(1)} %get-tuple-element.24), channel_id=1, source_target_pairs={{0,24},{8,0},{16,8},{24,16},{1,25},{9,1},{17,9},{25,17},{2,26},{10... | collective-permute-start | bytes 393224 | tf_op jit(solution)/shard_map/ppermute | solution.py:40
  142.6 9.6 %collective-permute-start.13 = (bf16[128,512]{1,0:T(8,128)(2,1)S(1)}, bf16[128,512]{1,0:T(8,128)(2,1)S(1)}, u32[]{:S(2)}, u32[]{:S(2)}) collective-permute-start(bf16[128,512]{1,0:T(8,128)(2,1)S(1)} %get-tuple-element.25), channel_id=1, source_target_pairs={{0,8},{8,16},{16,24},{24,0},{1,9},{9,17},{17,25},{25,1},{2,10},{10... | collective-permute-start | bytes 393224 | tf_op jit(solution)/shard_map/ppermute | solution.py:40
  154.1 18.3 %all-to-all-start.2 = ((f32[32,1,1]{2,1,0:T(1,128)}), f32[32,1,1]{2,1,0:T(1,128)S(1)}, u32[]{:S(2)}, u32[]{:S(2)}) async-start(f32[32,1,1]{2,1,0:T(1,128)} %broadcast_in_dim.10), calls=%async_computation.2 | async-start | bytes 32768 | tf_op jit(solution)/shard_map/all_to_all | solution.py:84

commit v7 on v6

--- a/solution.py
+++ b/solution.py
@@ -57,9 +57,9 @@
 
 def arrange(inputs, theirs, feature_gain):
     tokens, features = inputs.shape
-    x, y, core = (lax.axis_index(name) for name in ("x", "y_hi", "core"))
-    rx, ry = jnp.arange(CHIPS) // AXES["y_hi"], jnp.arange(CHIPS) % AXES["y_hi"]
-    chip = (y + ry) % AXES["y_hi"] * AXES["x"] + (x + rx) % AXES["x"]
+    x, core = lax.axis_index("x"), lax.axis_index("core")
+    rx, y = jnp.arange(CHIPS) // AXES["y_hi"], jnp.arange(CHIPS) % AXES["y_hi"]
+    chip = y * AXES["x"] + (x + rx) % AXES["x"]
     order = (chip * 2 + core).astype(jnp.int32)
     step = 96
     block = pl.BlockSpec((step, features), lambda i: (i, 0))
@@ -112,30 +112,66 @@
     return spread(own_next, REPLICA).reshape(-1), new_momentum.reshape(-1)
 
 
+def collect_kernel(arrived_ref, gradient_ref, squares_ref):
+    gradient = total([arrived_ref[k] for k in range(arrived_ref.shape[0])])
+    gradient_ref[...] = gradient
+    squares = jnp.sum(gradient * gradient, axis=0, keepdims=True)
+    squares_ref[...] = jnp.broadcast_to(
+        jnp.sum(squares, axis=1, keepdims=True), squares_ref.shape
+    )
+
+
+def collect(arrived):
+    in_vmem = pl.BlockSpec(memory_space=pltpu.VMEM)
+    return pl.pallas_call(
+        collect_kernel,
+        out_shape=(
+            jax.ShapeDtypeStruct(arrived.shape[1:], jnp.float32),
+            jax.ShapeDtypeStruct((CHIPS * AXES["core"], LANES), jnp.float32),
+        ),
+        in_specs=[in_vmem],
+        out_specs=(in_vmem, in_vmem),
+        name="collect",
+    )(arrived)
+
+
+def clip_kernel(entries, squares_ref, gradient_ref, clipped_ref):
+    mean_square = jnp.sum(squares_ref[...], axis=0, keepdims=True) / entries
+    factor = jnp.minimum(1.0, lax.rsqrt(mean_square + epsilon))
+    for j in range(gradient_ref.shape[1] // LANES):
+        columns = slice(j * LANES, (j + 1) * LANES)
+        clipped_ref[:, columns] = (gradient_ref[:, columns] * factor).astype(jnp.bfloat16)
+
+
+def clip(squares, gradient, entries):
+    in_vmem = pl.BlockSpec(memory_space=pltpu.VMEM)
+    return pl.pallas_call(
+        functools.partial(clip_kernel, entries),
+        out_shape=jax.ShapeDtypeStruct(gradient.shape, jnp.bfloat16),
+        in_specs=[in_vmem, in_vmem],
+        out_specs=in_vmem,
+        name="clip",
+    )(squares, gradient)
+
+
 def shards(inputs, feature_gain, key_weight, teacher_keys, global_frag, local_frag, momentum):
     tokens, features = inputs.shape[1:]
     rows, width = key_weight.shape[1:]
 
-    weight = key_weight[0]
-    near = [weight] + [None] * 3
-    for k in STEPS:
-        near[k] = send(weight, "y_hi", -k)
-    near[1], inputs, teacher_keys, global_frag, local_frag = tied(
-        near[1], inputs, teacher_keys, global_frag, local_frag
-    )
+    column = spread(key_weight[0], "y_hi").reshape(AXES["y_hi"] * rows, width)
     raw = send(inputs[0], "core", 1)
     their_targets = send(teacher_keys[0], "core", 1)
-    arrived = exchange(fragment_codes(global_frag, local_frag[0]), REPLICA)
-    column = jnp.concatenate(near, axis=0)
+    decoded = fragment_codes(global_frag, local_frag[0])
+    column, decoded = tied(column, decoded)
     far = {k: send(column, "x", -k) for k in STEPS}
-    new_global, new_momentum = fragment_update(arrived, global_frag, momentum)
+    arrived = exchange(decoded, REPLICA)
     targets = jnp.concatenate([teacher_keys[0], their_targets], axis=0)
     scaled = arrange(inputs[0], raw, feature_gain)
     group = scaled.shape[1] // AXES["x"]
     blocks = [scaled[:, k * group : (k + 1) * group] for k in range(AXES["x"])]
     partial = jnp.dot(blocks[0], column, preferred_element_type=jnp.float32)
     last = STEPS[-1]
-    far[last], new_global, targets = tied(far[last], new_global, targets)
+    far[last], arrived, targets = tied(far[last], arrived, targets)
     for k in STEPS:
         partial += jnp.dot(blocks[k], far[k], preferred_element_type=jnp.float32)
 
@@ -148,14 +184,13 @@
         ).astype(jnp.bfloat16)
         for block in blocks
     ]
+    gradient[0], arrived = tied(gradient[0], arrived)
+    new_global, new_momentum = fragment_update(arrived, global_frag, momentum)
     mine = total([gradient[0]] + [send(gradient[k], "x", k) for k in STEPS])
-    mine = mine.astype(jnp.bfloat16).reshape(AXES["y_hi"], rows, width)
-    gradient = total([mine[0]] + [send(mine[k], "y_hi", k) for k in STEPS])
-
-    squares = jnp.sum(gradient * gradient)
-    mean_square = jnp.sum(spread(squares[None], FSDP)) / (features * width)
-    factor = jnp.minimum(1.0, lax.rsqrt(mean_square + epsilon))
-    clipped_grad = (gradient * factor).astype(jnp.bfloat16)[None]
+    mine, new_global = tied(mine.astype(jnp.bfloat16), new_global)
+    gradient, squares = collect(exchange(mine.reshape(AXES["y_hi"], rows, width), "y_hi"))
+
+    clipped_grad = clip(exchange(squares, FSDP), gradient, features * width)[None]
     return (clipped_grad, new_global, new_momentum)
 
 

time: 176 us -> 161 us (0.915)
  starting transfers between devices: 92.8 us -> 66.7 us
  waiting for transfers between devices: 53 us -> 36.1 us
  blocking collectives: 0 us -> 15.3 us
  local copies, waits for them, and re-layouts: 3.64 us -> 10.8 us
  matrix products: 8.91 us -> 13.3 us
  Pallas kernels: 3.3 us -> 5.27 us
    ppermute x15 -> x9, starting transfers between devices: 68.9 us -> 34.8 us  [send(): lax.ppermute(value, axis, [(i, (i + step) % size) for i in range(size)])]
    ppermute x15 -> x9, waiting for transfers between devices: 44.2 us -> 18.9 us  [send(): lax.ppermute(value, axis, [(i, (i + step) % size) for i in range(size)])]
    all_to_all x0 -> x1, blocking collectives: none -> 15.3 us  [exchange(): return lax.all_to_all(parts, axis, split_axis=0, concat_axis=0, tiled=True)]
    all_to_all x3 -> x4, waiting for transfers between devices: 8.83 us -> 17.2 us  [exchange(): return lax.all_to_all(parts, axis, split_axis=0, concat_axis=0, tiled=True)]
    all_to_all x3 -> x4, starting transfers between devices: 24 us -> 31.9 us  [exchange(): return lax.all_to_all(parts, axis, split_axis=0, concat_axis=0, tiled=True)]
    unnamed x21 -> x17, local copies, waits for them, and re-layouts: 1.41 us -> 6.75 us
    pallas_call x0 -> x2, Pallas kernels: none -> 3.51 us  [the longest x1 1.85 us: collect(): pl.pallas_call(collect_kernel, out_shape=(jax.ShapeDtypeStruct(arrived.sh...]
    dot_general x4, matrix products: 2.52 us -> 5.66 us  [shards(): lax.dot_general(block, residual, (((0,), (0,)), ((), ())), preferred_elem...]
  transfers between devices with their start and end apart: 18 -> 13, of which waited for: 10 -> 5; matrix products, arithmetic and copies ran while one was open for 8% -> 9% of each run, Pallas kernels for 2% -> 1%
where the time goes in v7:
time: 161 us; the launch traced here: 159 us
  starting transfers between devices  66.7 us (41%)
  waiting for transfers between devices  36.1 us (22%)
  blocking collectives  15.3 us (10%)
  matrix products  13.3 us (8%)
  other arithmetic  11.1 us (7%)
  local copies, waits for them, and re-layouts  10.8 us (7%)
  Pallas kernels  5.27 us (3%)
    ppermute x9, starting transfers between devices, send(): lax.ppermute(value, axis, [(i, (i + step) % size) for i in range(size)])  34.8 us
    all_to_all x4, starting transfers between devices, exchange(): return lax.all_to_all(parts, axis, split_axis=0, concat_axis=0, tiled=True)  31.9 us
    ppermute x9, waiting for transfers between devices, send(): lax.ppermute(value, axis, [(i, (i + step) % size) for i in range(size)])  18.9 us
    all_to_all x4, waiting for transfers between devices, exchange(): return lax.all_to_all(parts, axis, split_axis=0, concat_axis=0, tiled=True)  17.2 us
    all_to_all x1, blocking collectives, exchange(): return lax.all_to_all(parts, axis, split_axis=0, concat_axis=0, tiled=True)  15.3 us
    unnamed x17, local copies, waits for them, and re-layouts  6.75 us
    dot_general x3, matrix products, shards(): partial += jnp.dot(blocks[k], far[k], preferred_element_type=jnp.float32)  6.03 us
    dot_general x4, matrix products, shards(): lax.dot_general(block, residual, (((0,), (0,)), ((), ())), preferred_elem...  5.66 us
  transfers between devices with their start and end apart: 13, of which 5 were waited for; matrix products, arithmetic and copies ran while one was open for 9% of the time, Pallas kernels for 1%

profile of v7, /device:TPU:1, one launch (start us, length us, event | category | flops | bytes accessed | tf_op | source)
XLA Modules:
  0.0 159.5 jit_solution(9299478552279120034)
XLA Ops:
  0.6 0.0 copy-start.5
  0.6 8.9 %collective-permute-start = (bf16[384,4096]{1,0:T(8,128)(2,1)}, bf16[384,4096]{1,0:T(8,128)(2,1)S(1)}, u32[]{:S(2)}, u32[]{:S(2)}) collective-permute-start(bf16[384,4096]{1,0:T(8,128)(2,1)} %bitcast.48), channel_id=1, source_target_pairs={{0,1},{1,0},{2,3},{3,2},{4,5},{5,4},{6,7},{7,6},{8,9},{9,8},{10,11... | collective-permute-start | bytes 9437192 | tf_op jit(solution)/shard_map/ppermute | solution.py:40
  9.6 1.8 %broadcast_in_dim.23 = bf16[4,128,512]{2,1,0:T(8,128)(2,1)} broadcast(bf16[128,512]{1,0:T(8,128)(2,1)} %bitcast.57), dimensions={1,2} | broadcast | bytes 655360 | tf_op jit(solution)/shard_map/broadcast_in_dim | solution.py:88
  11.3 4.1 %all-to-all-start = ((bf16[4,128,512]{2,1,0:T(8,128)(2,1)}), bf16[4,128,512]{2,1,0:T(8,128)(2,1)}, u32[]{:S(2)}, u32[]{:S(2)}) async-start(bf16[4,128,512]{2,1,0:T(8,128)(2,1)} %broadcast_in_dim.23), calls=%async_computation | async-start | bytes 1048576 | tf_op jit(solution)/shard_map/all_to_all | solution.py:84
  15.5 1.9 %collective-permute-start.4 = (bf16[384,512]{1,0:T(8,128)(2,1)}, bf16[384,512]{1,0:T(8,128)(2,1)}, u32[]{:S(2)}, u32[]{:S(2)}) collective-permute-start(bf16[384,512]{1,0:T(8,128)(2,1)} %bitcast.55), channel_id=1, source_target_pairs={{0,1},{1,0},{2,3},{3,2},{4,5},{5,4},{6,7},{7,6},{8,9},{9,8},{10,11... | collective-permute-start | bytes 1179656 | tf_op jit(solution)/shard_map/ppermute | solution.py:40
  17.4 1.6 convert_element_type.109
  19.0 0.0 copy-done.5
  19.0 0.9 bitcast_reduce_fusion
  19.9 0.0 copy-start.3
  19.9 0.1 reshape.90
  19.9 2.0 %multiply_convert_fusion = bf16[16,64,128]{2,1,0:T(8,128)(2,1)} fusion(f32[16,64]{1,0:T(8,128)S(1)} %reshape.90, f32[16,64,128]{2,1,0:T(8,128)} %bitcast.52), kind=kLoop, calls=%fused_computation.24 | loop fusion | flops 786432 | bytes 790528 | tf_op jit(solution)/shard_map/convert_element_type | solution.py:99
  21.9 8.5 %all-to-all-done = bf16[4,128,512]{2,1,0:T(8,128)(2,1)} async-done(((bf16[4,128,512]{2,1,0:T(8,128)(2,1)}), bf16[4,128,512]{2,1,0:T(8,128)(2,1)}, u32[]{:S(2)}, u32[]{:S(2)}) %all-to-all-start) | async-done | bytes 524320 | tf_op jit(solution)/shard_map/all_to_all | solution.py:84
  30.4 1.9 %collective-permute-start.3 = (bf16[512,512]{1,0:T(8,128)(2,1)}, bf16[512,512]{1,0:T(8,128)(2,1)}, u32[]{:S(2)}, u32[]{:S(2)}) collective-permute-start(bf16[512,512]{1,0:T(8,128)(2,1)} %bitcast.4), channel_id=1, source_target_pairs={{0,2},{2,4},{4,6},{6,0},{1,3},{3,5},{5,7},{7,1},{8,10},{10,12},{12... | collective-permute-start | bytes 1572872 | tf_op jit(solution)/shard_map/ppermute | solution.py:40
  32.3 8.8 %all-to-all-start.1 = ((bf16[16,64,128]{2,1,0:T(8,128)(2,1)}), bf16[16,64,128]{2,1,0:T(8,128)(2,1)S(1)}, u32[]{:S(2)}, u32[]{:S(2)}) async-start(bf16[16,64,128]{2,1,0:T(8,128)(2,1)} %multiply_convert_fusion), calls=%async_computation.1 | async-start | bytes 524288 | tf_op jit(solution)/shard_map/all_to_all | solution.py:84
  41.1 4.4 %collective-permute-start.1 = (bf16[512,512]{1,0:T(8,128)(2,1)}, bf16[512,512]{1,0:T(8,128)(2,1)}, u32[]{:S(2)}, u32[]{:S(2)}) collective-permute-start(bf16[512,512]{1,0:T(8,128)(2,1)} %bitcast.4), channel_id=1, source_target_pairs={{0,4},{2,6},{4,0},{6,2},{1,5},{3,7},{5,1},{7,3},{8,12},{10,14},{12... | collective-permute-start | bytes 1572872 | tf_op jit(solution)/shard_map/ppermute | solution.py:40
  45.5 0.0 collective-permute-done.4
  45.5 2.1 %pad_maximum_fusion = bf16[768,512]{1,0:T(8,128)(2,1)} fusion(bf16[384,512]{1,0:T(8,128)(2,1)} %collective-permute-done.4, bf16[384,512]{1,0:T(8,128)(2,1)} %bitcast.56), kind=kLoop, calls=%fused_computation.9 | loop fusion | flops 1572864 | bytes 1572864 | tf_op jit(solution)/shard_map/concatenate | solution.py:168
  47.6 3.1 %collective-permute-start.2 = (bf16[512,512]{1,0:T(8,128)(2,1)}, bf16[512,512]{1,0:T(8,128)(2,1)}, u32[]{:S(2)}, u32[]{:S(2)}) collective-permute-start(bf16[512,512]{1,0:T(8,128)(2,1)} %bitcast.4), channel_id=1, source_target_pairs={{0,6},{2,0},{4,2},{6,4},{1,7},{3,1},{5,3},{7,5},{8,14},{10,8},{12,... | collective-permute-start | bytes 1572872 | tf_op jit(solution)/shard_map/ppermute | solution.py:40
  50.6 0.0 all-to-all-done.1
  50.6 0.0 collective-permute-done.3
  50.6 0.0 collective-permute-done.theirs_ref
  50.7 0.0 copy-start.1
  50.7 1.6 %copy-done.1 = bf16[384,4096]{1,0:T(8,128)(2,1)} copy-done((bf16[384,4096]{1,0:T(8,128)(2,1)}, bf16[384,4096]{1,0:T(8,128)(2,1)S(1)}, u32[]{:S(2)}) %copy-start.1) | copy-done | bytes 3145752
  52.3 0.0 copy-done.3
  52.3 0.0 copy-start
  52.3 1.9 %copy-done = bf16[1,384,4096]{2,1,0:T(8,128)(2,1)S(1)} copy-done((bf16[1,384,4096]{2,1,0:T(8,128)(2,1)S(1)}, bf16[1,384,4096]{2,1,0:T(8,128)(2,1)}, u32[]{:S(2)}) %copy-start) | copy-done | bytes 3145752
  54.2 1.9 %copy-done.2 = bf16[384,4096]{1,0:T(8,128)(2,1)S(1)} copy-done((bf16[384,4096]{1,0:T(8,128)(2,1)S(1)}, bf16[384,4096]{1,0:T(8,128)(2,1)}, u32[]{:S(2)}) %copy-start.2) | copy-done | bytes 3145752
  56.1 1.8 %arrange.1 = bf16[2,384,2048]{2,1,0:T(8,128)(2,1)S(1)} custom-call(s32[16]{0:T(128)S(1)} %fusion.26.order_ref, bf16[384,4096]{1,0:T(8,128)(2,1)S(1)} %bitcast.49, bf16[384,4096]{1,0:T(8,128)(2,1)S(1)} %copy-done.2, f32[1,4096]{1,0:T(1,128)S(1)} %bitcast.50), custom_call_target="tpu_custom_call" | custom-call | tf_op jit(solution)/shard_map/arrange/pallas_call | solution.py:66
  57.8 1.6 %fusion.14 = f32[768,512]{1,0:T(8,128)S(1)} fusion(bf16[512,512]{1,0:T(8,128)(2,1)} %bitcast.4, bf16[768,2048]{1,0:T(8,128)(2,1)S(1)} %bitcast.40), kind=kOutput, calls=%fused_computation.20 | convolution fusion | flops 402653184 | bytes 2883584 | tf_op jit(solution)/shard_map/dot_general | solution.py:172
  59.5 0.0 collective-permute-done.1
  59.5 1.6 %fusion.11 = f32[768,512]{1,0:T(8,128)S(1)} fusion(bf16[512,512]{1,0:T(8,128)(2,1)} %collective-permute-done.1, bf16[768,2048]{1,0:T(8,128)(2,1)S(1)} %bitcast.41), kind=kOutput, calls=%fused_computation.17 | convolution fusion | flops 402653184 | bytes 2883584 | tf_op jit(solution)/shard_map/dot_general | solution.py:176
  61.1 6.9 %collective-permute-done.2 = bf16[512,512]{1,0:T(8,128)(2,1)} collective-permute-done((bf16[512,512]{1,0:T(8,128)(2,1)}, bf16[512,512]{1,0:T(8,128)(2,1)}, u32[]{:S(2)}, u32[]{:S(2)}) %collective-permute-start.2) | collective-permute-done | bytes 524320 | tf_op jit(solution)/shard_map/ppermute | solution.py:40
  68.0 1.6 %fusion.8 = f32[768,512]{1,0:T(8,128)S(1)} fusion(bf16[512,512]{1,0:T(8,128)(2,1)} %collective-permute-done.2, bf16[768,2048]{1,0:T(8,128)(2,1)S(1)} %bitcast.42), kind=kOutput, calls=%fused_computation.14 | convolution fusion | flops 402653184 | bytes 2883584 | tf_op jit(solution)/shard_map/dot_general | solution.py:176
  69.6 2.8 %add_add_fusion = f32[768,512]{1,0:T(8,128)} fusion(f32[768,512]{1,0:T(8,128)S(1)} %fusion.8, f32[768,512]{1,0:T(8,128)S(1)} %fusion.14, f32[768,512]{1,0:T(8,128)S(1)} %fusion.11, bf16[512,512]{1,0:T(8,128)(2,1)} %collective-permute-done.3, bf16[768,2048]{1,0:T(8,128)(2,1)S(1)} %bitcast.43), kind=kOutput, calls=%fused_computation.3 | convolution fusion | flops 403832832 | bytes 7602176 | tf_op jit(solution)/shard_map/dot_general | solution.py:176
  72.4 3.7 %collective-permute-start.5 = (f32[768,512]{1,0:T(8,128)}, f32[768,512]{1,0:T(8,128)}, u32[]{:S(2)}, u32[]{:S(2)}) collective-permute-start(f32[768,512]{1,0:T(8,128)} %add_add_fusion), channel_id=1, source_target_pairs={{0,1},{1,0},{2,3},{3,2},{4,5},{5,4},{6,7},{7,6},{8,9},{9,8},{10,11... | collective-permute-start | bytes 4718600 | tf_op jit(solution)/shard_map/ppermute | solution.py:40
  76.1 0.0 copy-start.4
  76.1 3.3 %collective-permute-done.5 = f32[768,512]{1,0:T(8,128)} collective-permute-done((f32[768,512]{1,0:T(8,128)}, f32[768,512]{1,0:T(8,128)}, u32[]{:S(2)}, u32[]{:S(2)}) %collective-permute-start.5) | collective-permute-done | bytes 1572896 | tf_op jit(solution)/shard_map/ppermute | solution.py:40
  79.5 1.5 fusion.27
  81.0 0.0 copy-done.4
  81.0 1.9 %fusion.1 = bf16[768,512]{1,0:T(8,128)(2,1)S(1)} fusion(f32[768,512]{1,0:T(8,128)} %add_add_fusion, f32[384,512]{1,0:T(8,128)S(1)} %get-tuple-element.28, f32[384,512]{1,0:T(8,128)S(1)} %get-tuple-element.27, bf16[768,512]{1,0:T(8,128)(2,1)S(1)} %copy-done.4), kind=kLoop, calls=%fused_computation.2 | loop fusion | flops 1966080 | bytes 4718592 | tf_op jit(solution)/shard_map/convert_element_type | solution.py:180
  82.9 1.4 convolution_convert_fusion.3
  84.3 1.4 convolution_convert_fusion.2
  85.7 1.4 convolution_convert_fusion.1
  87.1 1.4 convolution_convert_fusion
  88.5 4.4 %collective-permute-start.6 = (bf16[512,512]{1,0:T(8,128)(2,1)}, bf16[512,512]{1,0:T(8,128)(2,1)S(1)}, u32[]{:S(2)}, u32[]{:S(2)}) collective-permute-start(bf16[512,512]{1,0:T(8,128)(2,1)} %convolution_convert_fusion.2), channel_id=1, source_target_pairs={{0,4},{2,6},{4,0},{6,2},{1,5},{3,7},{5,1},{7,3},{8,12},{10,14},{12... | collective-permute-start | bytes 1572872 | tf_op jit(solution)/shard_map/ppermute | solution.py:40
  92.9 2.1 %collective-permute-start.7 = (bf16[512,512]{1,0:T(8,128)(2,1)}, bf16[512,512]{1,0:T(8,128)(2,1)S(1)}, u32[]{:S(2)}, u32[]{:S(2)}) collective-permute-start(bf16[512,512]{1,0:T(8,128)(2,1)} %convolution_convert_fusion.1), channel_id=1, source_target_pairs={{0,2},{2,4},{4,6},{6,0},{1,3},{3,5},{5,7},{7,1},{8,10},{10,12},{12... | collective-permute-start | bytes 1572872 | tf_op jit(solution)/shard_map/ppermute | solution.py:40
  95.0 4.4 %collective-permute-start.8 = (bf16[512,512]{1,0:T(8,128)(2,1)}, bf16[512,512]{1,0:T(8,128)(2,1)S(1)}, u32[]{:S(2)}, u32[]{:S(2)}) collective-permute-start(bf16[512,512]{1,0:T(8,128)(2,1)} %convolution_convert_fusion), channel_id=1, source_target_pairs={{0,6},{2,0},{4,2},{6,4},{1,7},{3,1},{5,3},{7,5},{8,14},{10,8},{12,... | collective-permute-start | bytes 1572872 | tf_op jit(solution)/shard_map/ppermute | solution.py:40
  99.4 0.0 copy-done.6
  99.5 0.7 fusion.16
  100.2 0.8 broadcast_in_dim.24
  100.9 7.5 %all-to-all-start.2 = ((bf16[16,64,128]{2,1,0:T(8,128)(2,1)}), bf16[16,64,128]{2,1,0:T(8,128)(2,1)S(1)}, u32[]{:S(2)}, u32[]{:S(2)}) async-start(bf16[16,64,128]{2,1,0:T(8,128)(2,1)} %broadcast_in_dim.24), calls=%async_computation.2 | async-start | bytes 524288 | tf_op jit(solution)/shard_map/all_to_all | solution.py:84
  108.5 0.0 collective-permute-done.6
  108.5 8.7 %collective-permute-done.7 = bf16[512,512]{1,0:T(8,128)(2,1)S(1)} collective-permute-done((bf16[512,512]{1,0:T(8,128)(2,1)}, bf16[512,512]{1,0:T(8,128)(2,1)S(1)}, u32[]{:S(2)}, u32[]{:S(2)}) %collective-permute-start.7) | collective-permute-done | bytes 524320 | tf_op jit(solution)/shard_map/ppermute | solution.py:40
  117.2 0.0 collective-permute-done.8
  117.2 1.3 add_convert_fusion
  118.5 0.0 all-to-all-done.2
  118.5 15.3 %all_to_all.31.arrived_ref = bf16[4,128,512]{2,1,0:T(8,128)(2,1)} all-to-all(bf16[4,128,512]{2,1,0:T(8,128)(2,1)S(1)} %bitcast.51), channel_id=1, replica_groups=mesh['z'=8,'y_lo'=2,'y_hi'=4,'x'=4,'core'=2] {'y_hi'}, dimensions={0} | all-to-all | bytes 1048576 | tf_op jit(solution)/shard_map/all_to_all | solution.py:84
  133.8 1.8 %collect.1 = (f32[128,512]{1,0:T(8,128)}, f32[32,128]{1,0:T(8,128)}) custom-call(bf16[4,128,512]{2,1,0:T(8,128)(2,1)} %all_to_all.31.arrived_ref), custom_call_target="tpu_custom_call" | custom-call | tf_op jit(solution)/shard_map/collect/pallas_call | solution.py:126
  135.6 11.5 %all-to-all-start.4 = ((f32[32,1,128]{2,1,0:T(1,128)}), f32[32,1,128]{2,1,0:T(1,128)S(1)}, u32[]{:S(2)}, u32[]{:S(2)}) async-start(f32[32,1,128]{2,1,0:T(1,128)} %bitcast.60), calls=%async_computation.4 | async-start | bytes 32768 | tf_op jit(solution)/shard_map/all_to_all | solution.py:84
  147.1 0.6 bitcast_add_fusion
  147.8 8.7 %all-to-all-done.4 = f32[32,1,128]{2,1,0:T(1,128)S(1)} async-done(((f32[32,1,128]{2,1,0:T(1,128)}), f32[32,1,128]{2,1,0:T(1,128)S(1)}, u32[]{:S(2)}, u32[]{:S(2)}) %all-to-all-start.4) | async-done | bytes 16416 | tf_op jit(solution)/shard_map/all_to_all | solution.py:84
  156.5 0.6 copy-done.7
  157.1 1.7 %clip.1 = bf16[128,512]{1,0:T(8,128)(2,1)} custom-call(f32[32,128]{1,0:T(8,128)} %bitcast.59, f32[128,512]{1,0:T(8,128)} %get-tuple-element.23.gradient_ref), custom_call_target="tpu_custom_call" | custom-call | tf_op jit(solution)/shard_map/clip/pallas_call | solution.py:148
  158.7 0.7 copy.13
  (6 shorter events, 0.1 us)
Async XLA Ops:
  0.6 18.4 %copy-start.5 = (bf16[131072]{0:T(1024)(128)(2,1)S(1)}, bf16[131072]{0:T(1024)(128)(2,1)}, u32[]{:S(2)}) copy-start(bf16[131072]{0:T(1024)(128)(2,1)} %param.11) | copy-start | bytes 786436
  0.6 50.0 %collective-permute-start = (bf16[384,4096]{1,0:T(8,128)(2,1)}, bf16[384,4096]{1,0:T(8,128)(2,1)S(1)}, u32[]{:S(2)}, u32[]{:S(2)}) collective-permute-start(bf16[384,4096]{1,0:T(8,128)(2,1)} %bitcast.48), channel_id=1, source_target_pairs={{0,1},{1,0},{2,3},{3,2},{4,5},{5,4},{6,7},{7,6},{8,9},{9,8},{10,11... | collective-permute-start | bytes 9437192 | tf_op jit(solution)/shard_map/ppermute | solution.py:40
  11.3 19.0 %all-to-all-start = ((bf16[4,128,512]{2,1,0:T(8,128)(2,1)}), bf16[4,128,512]{2,1,0:T(8,128)(2,1)}, u32[]{:S(2)}, u32[]{:S(2)}) async-start(bf16[4,128,512]{2,1,0:T(8,128)(2,1)} %broadcast_in_dim.23), calls=%async_computation | async-start | bytes 1048576 | tf_op jit(solution)/shard_map/all_to_all | solution.py:84
  15.5 30.0 %collective-permute-start.4 = (bf16[384,512]{1,0:T(8,128)(2,1)}, bf16[384,512]{1,0:T(8,128)(2,1)}, u32[]{:S(2)}, u32[]{:S(2)}) collective-permute-start(bf16[384,512]{1,0:T(8,128)(2,1)} %bitcast.55), channel_id=1, source_target_pairs={{0,1},{1,0},{2,3},{3,2},{4,5},{5,4},{6,7},{7,6},{8,9},{9,8},{10,11... | collective-permute-start | bytes 1179656 | tf_op jit(solution)/shard_map/ppermute | solution.py:40
  19.9 32.4 %copy-start.3 = (f32[4096]{0:T(1024)S(1)}, f32[4096]{0:T(1024)}, u32[]{:S(2)}) copy-start(f32[4096]{0:T(1024)} %param.8) | copy-start | bytes 49156
  30.4 20.3 %collective-permute-start.3 = (bf16[512,512]{1,0:T(8,128)(2,1)}, bf16[512,512]{1,0:T(8,128)(2,1)}, u32[]{:S(2)}, u32[]{:S(2)}) collective-permute-start(bf16[512,512]{1,0:T(8,128)(2,1)} %bitcast.4), channel_id=1, source_target_pairs={{0,2},{2,4},{4,6},{6,0},{1,3},{3,5},{5,7},{7,1},{8,10},{10,12},{12... | collective-permute-start | bytes 1572872 | tf_op jit(solution)/shard_map/ppermute | solution.py:40
  32.3 18.3 %all-to-all-start.1 = ((bf16[16,64,128]{2,1,0:T(8,128)(2,1)}), bf16[16,64,128]{2,1,0:T(8,128)(2,1)S(1)}, u32[]{:S(2)}, u32[]{:S(2)}) async-start(bf16[16,64,128]{2,1,0:T(8,128)(2,1)} %multiply_convert_fusion), calls=%async_computation.1 | async-start | bytes 524288 | tf_op jit(solution)/shard_map/all_to_all | solution.py:84
  41.1 18.4 %collective-permute-start.1 = (bf16[512,512]{1,0:T(8,128)(2,1)}, bf16[512,512]{1,0:T(8,128)(2,1)}, u32[]{:S(2)}, u32[]{:S(2)}) collective-permute-start(bf16[512,512]{1,0:T(8,128)(2,1)} %bitcast.4), channel_id=1, source_target_pairs={{0,4},{2,6},{4,0},{6,2},{1,5},{3,7},{5,1},{7,3},{8,12},{10,14},{12... | collective-permute-start | bytes 1572872 | tf_op jit(solution)/shard_map/ppermute | solution.py:40
  47.6 20.4 %collective-permute-start.2 = (bf16[512,512]{1,0:T(8,128)(2,1)}, bf16[512,512]{1,0:T(8,128)(2,1)}, u32[]{:S(2)}, u32[]{:S(2)}) collective-permute-start(bf16[512,512]{1,0:T(8,128)(2,1)} %bitcast.4), channel_id=1, source_target_pairs={{0,6},{2,0},{4,2},{6,4},{1,7},{3,1},{5,3},{7,5},{8,14},{10,8},{12,... | collective-permute-start | bytes 1572872 | tf_op jit(solution)/shard_map/ppermute | solution.py:40
  50.7 1.6 %copy-start.1 = (bf16[384,4096]{1,0:T(8,128)(2,1)}, bf16[384,4096]{1,0:T(8,128)(2,1)S(1)}, u32[]{:S(2)}) copy-start(bf16[384,4096]{1,0:T(8,128)(2,1)S(1)} %collective-permute-done.theirs_ref) | copy-start | bytes 9437188
  52.3 1.9 %copy-start = (bf16[1,384,4096]{2,1,0:T(8,128)(2,1)S(1)}, bf16[1,384,4096]{2,1,0:T(8,128)(2,1)}, u32[]{:S(2)}) copy-start(bf16[1,384,4096]{2,1,0:T(8,128)(2,1)} %param.7) | copy-start | bytes 9437188
  54.2 1.9 %copy-start.2 = (bf16[384,4096]{1,0:T(8,128)(2,1)S(1)}, bf16[384,4096]{1,0:T(8,128)(2,1)}, u32[]{:S(2)}) copy-start(bf16[384,4096]{1,0:T(8,128)(2,1)} %copy-done.1) | copy-start | bytes 9437188
  72.4 7.1 %collective-permute-start.5 = (f32[768,512]{1,0:T(8,128)}, f32[768,512]{1,0:T(8,128)}, u32[]{:S(2)}, u32[]{:S(2)}) collective-permute-start(f32[768,512]{1,0:T(8,128)} %add_add_fusion), channel_id=1, source_target_pairs={{0,1},{1,0},{2,3},{3,2},{4,5},{5,4},{6,7},{7,6},{8,9},{9,8},{10,11... | collective-permute-start | bytes 4718600 | tf_op jit(solution)/shard_map/ppermute | solution.py:40
  76.1 4.8 %copy-start.4 = (bf16[768,512]{1,0:T(8,128)(2,1)S(1)}, bf16[768,512]{1,0:T(8,128)(2,1)}, u32[]{:S(2)}) copy-start(bf16[768,512]{1,0:T(8,128)(2,1)} %pad_maximum_fusion) | copy-start | bytes 2359300
  87.1 12.3 %copy-start.6 = (f32[8192]{0:T(1024)S(1)}, f32[8192]{0:T(1024)}, u32[]{:S(2)}) copy-start(f32[8192]{0:T(1024)} %param.13) | copy-start | bytes 98308
  88.5 20.0 %collective-permute-start.6 = (bf16[512,512]{1,0:T(8,128)(2,1)}, bf16[512,512]{1,0:T(8,128)(2,1)S(1)}, u32[]{:S(2)}, u32[]{:S(2)}) collective-permute-start(bf16[512,512]{1,0:T(8,128)(2,1)} %convolution_convert_fusion.2), channel_id=1, source_target_pairs={{0,4},{2,6},{4,0},{6,2},{1,5},{3,7},{5,1},{7,3},{8,12},{10,14},{12... | collective-permute-start | bytes 1572872 | tf_op jit(solution)/shard_map/ppermute | solution.py:40
  92.9 24.3 %collective-permute-start.7 = (bf16[512,512]{1,0:T(8,128)(2,1)}, bf16[512,512]{1,0:T(8,128)(2,1)S(1)}, u32[]{:S(2)}, u32[]{:S(2)}) collective-permute-start(bf16[512,512]{1,0:T(8,128)(2,1)} %convolution_convert_fusion.1), channel_id=1, source_target_pairs={{0,2},{2,4},{4,6},{6,0},{1,3},{3,5},{5,7},{7,1},{8,10},{10,12},{12... | collective-permute-start | bytes 1572872 | tf_op jit(solution)/shard_map/ppermute | solution.py:40
  95.0 22.2 %collective-permute-start.8 = (bf16[512,512]{1,0:T(8,128)(2,1)}, bf16[512,512]{1,0:T(8,128)(2,1)S(1)}, u32[]{:S(2)}, u32[]{:S(2)}) collective-permute-start(bf16[512,512]{1,0:T(8,128)(2,1)} %convolution_convert_fusion), channel_id=1, source_target_pairs={{0,6},{2,0},{4,2},{6,4},{1,7},{3,1},{5,3},{7,5},{8,14},{10,8},{12,... | collective-permute-start | bytes 1572872 | tf_op jit(solution)/shard_map/ppermute | solution.py:40
  100.9 17.6 %all-to-all-start.2 = ((bf16[16,64,128]{2,1,0:T(8,128)(2,1)}), bf16[16,64,128]{2,1,0:T(8,128)(2,1)S(1)}, u32[]{:S(2)}, u32[]{:S(2)}) async-start(bf16[16,64,128]{2,1,0:T(8,128)(2,1)} %broadcast_in_dim.24), calls=%async_computation.2 | async-start | bytes 524288 | tf_op jit(solution)/shard_map/all_to_all | solution.py:84
  135.6 20.9 %all-to-all-start.4 = ((f32[32,1,128]{2,1,0:T(1,128)}), f32[32,1,128]{2,1,0:T(1,128)S(1)}, u32[]{:S(2)}, u32[]{:S(2)}) async-start(f32[32,1,128]{2,1,0:T(1,128)} %bitcast.60), calls=%async_computation.4 | async-start | bytes 32768 | tf_op jit(solution)/shard_map/all_to_all | solution.py:84
  156.5 0.6 copy-start.7

commit v8 on v7

--- a/solution.py
+++ b/solution.py
@@ -10,6 +10,7 @@
 
 QBLOCK = 128
 LANES = 128
+VMEM_LIMIT = 8 << 20
 
 
 outer_decay = 0.9
@@ -61,7 +62,7 @@
     rx, y = jnp.arange(CHIPS) // AXES["y_hi"], jnp.arange(CHIPS) % AXES["y_hi"]
     chip = y * AXES["x"] + (x + rx) % AXES["x"]
     order = (chip * 2 + core).astype(jnp.int32)
-    step = 96
+    step = 32
     block = pl.BlockSpec((step, features), lambda i: (i, 0))
     scaled = pl.pallas_call(
         arrange_kernel,
@@ -74,7 +75,7 @@
             pl.BlockSpec((1, features), lambda i: (0, 0)),
         ],
         out_specs=pl.BlockSpec((2, step, features // 2), lambda i: (0, i, 0)),
-        compiler_params=pltpu.CompilerParams(vmem_limit_bytes=24 << 20),
+        compiler_params=pltpu.CompilerParams(vmem_limit_bytes=VMEM_LIMIT),
         name="arrange",
     )(order, inputs, theirs, feature_gain[None, :])
     return scaled.reshape(2 * tokens, features // 2)
@@ -131,6 +132,7 @@
         ),
         in_specs=[in_vmem],
         out_specs=(in_vmem, in_vmem),
+        compiler_params=pltpu.CompilerParams(vmem_limit_bytes=VMEM_LIMIT),
         name="collect",
     )(arrived)
 
@@ -150,6 +152,7 @@
         out_shape=jax.ShapeDtypeStruct(gradient.shape, jnp.bfloat16),
         in_specs=[in_vmem, in_vmem],
         out_specs=in_vmem,
+        compiler_params=pltpu.CompilerParams(vmem_limit_bytes=VMEM_LIMIT),
         name="clip",
     )(squares, gradient)
 
@@ -161,17 +164,18 @@
     column = spread(key_weight[0], "y_hi").reshape(AXES["y_hi"] * rows, width)
     raw = send(inputs[0], "core", 1)
     their_targets = send(teacher_keys[0], "core", 1)
-    decoded = fragment_codes(global_frag, local_frag[0])
-    column, decoded = tied(column, decoded)
-    far = {k: send(column, "x", -k) for k in STEPS}
-    arrived = exchange(decoded, REPLICA)
     targets = jnp.concatenate([teacher_keys[0], their_targets], axis=0)
     scaled = arrange(inputs[0], raw, feature_gain)
+    column, scaled, targets, global_frag, local_frag = tied(
+        column, scaled, targets, global_frag, local_frag
+    )
+    far = {k: send(column, "x", -k) for k in STEPS}
+    arrived = exchange(fragment_codes(global_frag, local_frag[0]), REPLICA)
     group = scaled.shape[1] // AXES["x"]
     blocks = [scaled[:, k * group : (k + 1) * group] for k in range(AXES["x"])]
     partial = jnp.dot(blocks[0], column, preferred_element_type=jnp.float32)
     last = STEPS[-1]
-    far[last], arrived, targets = tied(far[last], arrived, targets)
+    far[last], arrived = tied(far[last], arrived)
     for k in STEPS:
         partial += jnp.dot(blocks[k], far[k], preferred_element_type=jnp.float32)
 

time: 161 us -> 155 us (0.963)
  waiting for transfers between devices: 36.1 us -> 31.8 us
  blocking collectives: 15.3 us -> 17.7 us
  starting transfers between devices: 66.7 us -> 64.6 us
  Pallas kernels: 5.27 us -> 3.49 us
    all_to_all x4, waiting for transfers between devices: 17.2 us -> 13.4 us  [exchange(): return lax.all_to_all(parts, axis, split_axis=0, concat_axis=0, tiled=True)]
    all_to_all x1, blocking collectives: 15.3 us -> 17.7 us  [exchange(): return lax.all_to_all(parts, axis, split_axis=0, concat_axis=0, tiled=True)]
    ppermute x9, starting transfers between devices: 34.8 us -> 32.4 us  [send(): lax.ppermute(value, axis, [(i, (i + step) % size) for i in range(size)])]
    unnamed x17 -> x19, local copies, waits for them, and re-layouts: 6.75 us -> 6.16 us
  transfers between devices with their start and end apart: 13 -> 13, of which waited for: 5 -> 7; matrix products, arithmetic and copies ran while one was open for 9% -> 10% of each run, Pallas kernels for 1% -> 1%
where the time goes in v8:
time: 155 us; the launch traced here: 154 us
  starting transfers between devices  64.6 us (42%)
  waiting for transfers between devices  31.8 us (21%)
  blocking collectives  17.7 us (11%)
  matrix products  14.5 us (9%)
  other arithmetic  10.9 us (7%)
  local copies, waits for them, and re-layouts  10.2 us (7%)
  Pallas kernels  3.49 us (2%)
    ppermute x9, starting transfers between devices, send(): lax.ppermute(value, axis, [(i, (i + step) % size) for i in range(size)])  32.4 us
    all_to_all x4, starting transfers between devices, exchange(): return lax.all_to_all(parts, axis, split_axis=0, concat_axis=0, tiled=True)  32.2 us
    ppermute x9, waiting for transfers between devices, send(): lax.ppermute(value, axis, [(i, (i + step) % size) for i in range(size)])  18.5 us
    all_to_all x1, blocking collectives, exchange(): return lax.all_to_all(parts, axis, split_axis=0, concat_axis=0, tiled=True)  17.7 us
    all_to_all x4, waiting for transfers between devices, exchange(): return lax.all_to_all(parts, axis, split_axis=0, concat_axis=0, tiled=True)  13.4 us
    unnamed x19, local copies, waits for them, and re-layouts  6.16 us
    dot_general x3, matrix products, shards(): partial += jnp.dot(blocks[k], far[k], preferred_element_type=jnp.float32)  6.03 us
    dot_general x4, matrix products, shards(): lax.dot_general(block, residual, (((0,), (0,)), ((), ())), preferred_elem...  5.66 us
  transfers between devices with their start and end apart: 13, of which 7 were waited for; matrix products, arithmetic and copies ran while one was open for 10% of the time, Pallas kernels for 1%

profile of v8, /device:TPU:1, one launch (start us, length us, event | category | flops | bytes accessed | tf_op | source)
XLA Modules:
  0.0 154.2 jit_solution(6912059530920730314)
XLA Ops:
  0.6 0.0 copy-start.6
  0.6 8.9 %collective-permute-start = (bf16[384,4096]{1,0:T(8,128)(2,1)}, bf16[384,4096]{1,0:T(8,128)(2,1)S(1)}, u32[]{:S(2)}, u32[]{:S(2)}) collective-permute-start(bf16[384,4096]{1,0:T(8,128)(2,1)} %bitcast.48), channel_id=1, source_target_pairs={{0,1},{1,0},{2,3},{3,2},{4,5},{5,4},{6,7},{7,6},{8,9},{9,8},{10,11... | collective-permute-start | bytes 9437192 | tf_op jit(solution)/shard_map/ppermute | solution.py:41
  9.6 0.0 copy-start.3
  9.6 1.7 %broadcast_in_dim.22 = bf16[4,128,512]{2,1,0:T(8,128)(2,1)} broadcast(bf16[128,512]{1,0:T(8,128)(2,1)} %bitcast.58), dimensions={1,2} | broadcast | bytes 655360 | tf_op jit(solution)/shard_map/broadcast_in_dim | solution.py:89
  11.3 4.1 %all-to-all-start = ((bf16[4,128,512]{2,1,0:T(8,128)(2,1)}), bf16[4,128,512]{2,1,0:T(8,128)(2,1)}, u32[]{:S(2)}, u32[]{:S(2)}) async-start(bf16[4,128,512]{2,1,0:T(8,128)(2,1)} %broadcast_in_dim.22), calls=%async_computation | async-start | bytes 1048576 | tf_op jit(solution)/shard_map/all_to_all | solution.py:85
  15.5 0.0 copy-done.6
  15.5 1.9 %collective-permute-start.1 = (bf16[384,512]{1,0:T(8,128)(2,1)S(1)}, bf16[384,512]{1,0:T(8,128)(2,1)}, u32[]{:S(2)}, u32[]{:S(2)}) collective-permute-start(bf16[384,512]{1,0:T(8,128)(2,1)S(1)} %bitcast.56), channel_id=1, source_target_pairs={{0,1},{1,0},{2,3},{3,2},{4,5},{5,4},{6,7},{7,6},{8,9},{9,8},{10,11... | collective-permute-start | bytes 1179656 | tf_op jit(solution)/shard_map/ppermute | solution.py:41
  17.4 1.8 %collective-permute-done.1 = bf16[384,512]{1,0:T(8,128)(2,1)} collective-permute-done((bf16[384,512]{1,0:T(8,128)(2,1)S(1)}, bf16[384,512]{1,0:T(8,128)(2,1)}, u32[]{:S(2)}, u32[]{:S(2)}) %collective-permute-start.1) | collective-permute-done | bytes 393248 | tf_op jit(solution)/shard_map/ppermute | solution.py:41
  19.2 1.9 %pad_maximum_fusion = bf16[768,512]{1,0:T(8,128)(2,1)} fusion(bf16[384,512]{1,0:T(8,128)(2,1)} %collective-permute-done.1, bf16[384,512]{1,0:T(8,128)(2,1)S(1)} %bitcast.57), kind=kLoop, calls=%fused_computation.9 | loop fusion | flops 1572864 | bytes 1572864 | tf_op jit(solution)/shard_map/concatenate | solution.py:167
  21.1 0.0 collective-permute-done.theirs_ref
  21.2 1.6 %copy-done.1 = bf16[384,4096]{1,0:T(8,128)(2,1)} copy-done((bf16[384,4096]{1,0:T(8,128)(2,1)}, bf16[384,4096]{1,0:T(8,128)(2,1)S(1)}, u32[]{:S(2)}) %copy-start.1) | copy-done | bytes 3145752
  22.8 0.0 copy-done.3
  22.8 1.9 %copy-done = bf16[1,384,4096]{2,1,0:T(8,128)(2,1)S(1)} copy-done((bf16[1,384,4096]{2,1,0:T(8,128)(2,1)S(1)}, bf16[1,384,4096]{2,1,0:T(8,128)(2,1)}, u32[]{:S(2)}) %copy-start) | copy-done | bytes 3145752
  24.7 1.9 %copy-done.2 = bf16[384,4096]{1,0:T(8,128)(2,1)S(1)} copy-done((bf16[384,4096]{1,0:T(8,128)(2,1)S(1)}, bf16[384,4096]{1,0:T(8,128)(2,1)}, u32[]{:S(2)}) %copy-start.2) | copy-done | bytes 3145752
  26.6 2.0 %arrange.1 = bf16[2,384,2048]{2,1,0:T(8,128)(2,1)S(1)} custom-call(s32[16]{0:T(128)S(1)} %fusion.26.order_ref, bf16[384,4096]{1,0:T(8,128)(2,1)S(1)} %bitcast.49, bf16[384,4096]{1,0:T(8,128)(2,1)S(1)} %copy-done.2, f32[1,4096]{1,0:T(1,128)S(1)} %bitcast.51), custom_call_target="tpu_custom_call" | custom-call | tf_op jit(solution)/shard_map/arrange/pallas_call | solution.py:67
  28.6 1.8 %all-to-all-done = bf16[4,128,512]{2,1,0:T(8,128)(2,1)} async-done(((bf16[4,128,512]{2,1,0:T(8,128)(2,1)}), bf16[4,128,512]{2,1,0:T(8,128)(2,1)}, u32[]{:S(2)}, u32[]{:S(2)}) %all-to-all-start) | async-done | bytes 524320 | tf_op jit(solution)/shard_map/all_to_all | solution.py:85
  30.4 1.9 %collective-permute-start.4 = (bf16[512,512]{1,0:T(8,128)(2,1)}, bf16[512,512]{1,0:T(8,128)(2,1)}, u32[]{:S(2)}, u32[]{:S(2)}) collective-permute-start(bf16[512,512]{1,0:T(8,128)(2,1)} %bitcast.1), channel_id=1, source_target_pairs={{0,2},{2,4},{4,6},{6,0},{1,3},{3,5},{5,7},{7,1},{8,10},{10,12},{12... | collective-permute-start | bytes 1572872 | tf_op jit(solution)/shard_map/ppermute | solution.py:41
  32.3 2.3 %collective-permute-start.2 = (bf16[512,512]{1,0:T(8,128)(2,1)}, bf16[512,512]{1,0:T(8,128)(2,1)}, u32[]{:S(2)}, u32[]{:S(2)}) collective-permute-start(bf16[512,512]{1,0:T(8,128)(2,1)} %bitcast.1), channel_id=1, source_target_pairs={{0,4},{2,6},{4,0},{6,2},{1,5},{3,7},{5,1},{7,3},{8,12},{10,14},{12... | collective-permute-start | bytes 1572872 | tf_op jit(solution)/shard_map/ppermute | solution.py:41
  34.5 1.6 %convert_element_type.109 = f32[1,131072]{1,0:T(1,128)S(1)} convert(bf16[1,131072]{1,0:T(2,128)(2,1)} %param.12) | non-fusion elementwise | flops 131072 | bytes 786432 | tf_op jit(solution)/shard_map/convert_element_type | solution.py:97
  36.1 0.0 copy-done.7
  36.1 0.9 bitcast_reduce_fusion
  37.0 0.1 reshape.90
  37.1 2.0 %multiply_convert_fusion = bf16[16,64,128]{2,1,0:T(8,128)(2,1)} fusion(f32[16,64]{1,0:T(8,128)S(1)} %reshape.90, f32[16,64,128]{2,1,0:T(8,128)} %bitcast.53), kind=kLoop, calls=%fused_computation.24 | loop fusion | flops 786432 | bytes 790528 | tf_op jit(solution)/shard_map/convert_element_type | solution.py:100
  39.0 10.9 %all-to-all-start.1 = ((bf16[16,64,128]{2,1,0:T(8,128)(2,1)}), bf16[16,64,128]{2,1,0:T(8,128)(2,1)S(1)}, u32[]{:S(2)}, u32[]{:S(2)}) async-start(bf16[16,64,128]{2,1,0:T(8,128)(2,1)} %multiply_convert_fusion), calls=%async_computation.1 | async-start | bytes 524288 | tf_op jit(solution)/shard_map/all_to_all | solution.py:85
  49.9 3.1 %collective-permute-start.3 = (bf16[512,512]{1,0:T(8,128)(2,1)}, bf16[512,512]{1,0:T(8,128)(2,1)}, u32[]{:S(2)}, u32[]{:S(2)}) collective-permute-start(bf16[512,512]{1,0:T(8,128)(2,1)} %bitcast.1), channel_id=1, source_target_pairs={{0,6},{2,0},{4,2},{6,4},{1,7},{3,1},{5,3},{7,5},{8,14},{10,8},{12,... | collective-permute-start | bytes 1572872 | tf_op jit(solution)/shard_map/ppermute | solution.py:41
  53.0 2.8 %fusion.14 = f32[768,512]{1,0:T(8,128)} fusion(bf16[512,512]{1,0:T(8,128)(2,1)} %bitcast.1, bf16[768,2048]{1,0:T(8,128)(2,1)S(1)} %bitcast.40), kind=kOutput, calls=%fused_computation.20 | convolution fusion | flops 402653184 | bytes 2883584 | tf_op jit(solution)/shard_map/dot_general | solution.py:176
  55.8 2.8 %all-to-all-done.1 = bf16[16,64,128]{2,1,0:T(8,128)(2,1)S(1)} async-done(((bf16[16,64,128]{2,1,0:T(8,128)(2,1)}), bf16[16,64,128]{2,1,0:T(8,128)(2,1)S(1)}, u32[]{:S(2)}, u32[]{:S(2)}) %all-to-all-start.1) | async-done | bytes 262176 | tf_op jit(solution)/shard_map/all_to_all | solution.py:85
  58.6 0.0 collective-permute-done.4
  58.7 0.0 collective-permute-done.2
  58.7 1.6 %fusion.11 = f32[768,512]{1,0:T(8,128)S(1)} fusion(bf16[512,512]{1,0:T(8,128)(2,1)} %collective-permute-done.2, bf16[768,2048]{1,0:T(8,128)(2,1)S(1)} %bitcast.41), kind=kOutput, calls=%fused_computation.17 | convolution fusion | flops 402653184 | bytes 2883584 | tf_op jit(solution)/shard_map/dot_general | solution.py:180
  60.3 0.0 copy-start.4
  60.3 3.0 %collective-permute-done.3 = bf16[512,512]{1,0:T(8,128)(2,1)} collective-permute-done((bf16[512,512]{1,0:T(8,128)(2,1)}, bf16[512,512]{1,0:T(8,128)(2,1)}, u32[]{:S(2)}, u32[]{:S(2)}) %collective-permute-start.3) | collective-permute-done | bytes 524320 | tf_op jit(solution)/shard_map/ppermute | solution.py:41
  63.3 1.6 %fusion.8 = f32[768,512]{1,0:T(8,128)S(1)} fusion(bf16[512,512]{1,0:T(8,128)(2,1)} %collective-permute-done.3, bf16[768,2048]{1,0:T(8,128)(2,1)S(1)} %bitcast.42), kind=kOutput, calls=%fused_computation.14 | convolution fusion | flops 402653184 | bytes 2883584 | tf_op jit(solution)/shard_map/dot_general | solution.py:180
  64.9 0.0 copy-done.4
  64.9 2.8 %add_add_fusion = f32[768,512]{1,0:T(8,128)} fusion(f32[768,512]{1,0:T(8,128)S(1)} %fusion.8, f32[768,512]{1,0:T(8,128)S(1)} %copy-done.4, f32[768,512]{1,0:T(8,128)S(1)} %fusion.11, bf16[512,512]{1,0:T(8,128)(2,1)} %collective-permute-done.4, bf16[768,2048]{1,0:T(8,128)(2,1)S(1)} %bitcast.43), kind=kOutput, calls=%fused_computation.3 | convolution fusion | flops 403832832 | bytes 7602176 | tf_op jit(solution)/shard_map/dot_general | solution.py:180
  67.8 5.1 %collective-permute-start.5 = (f32[768,512]{1,0:T(8,128)}, f32[768,512]{1,0:T(8,128)}, u32[]{:S(2)}, u32[]{:S(2)}) collective-permute-start(f32[768,512]{1,0:T(8,128)} %add_add_fusion), channel_id=1, source_target_pairs={{0,1},{1,0},{2,3},{3,2},{4,5},{5,4},{6,7},{7,6},{8,9},{9,8},{10,11... | collective-permute-start | bytes 4718600 | tf_op jit(solution)/shard_map/ppermute | solution.py:41
  72.9 0.0 copy-start.5
  72.9 3.3 %collective-permute-done.5 = f32[768,512]{1,0:T(8,128)} collective-permute-done((f32[768,512]{1,0:T(8,128)}, f32[768,512]{1,0:T(8,128)}, u32[]{:S(2)}, u32[]{:S(2)}) %collective-permute-start.5) | collective-permute-done | bytes 1572896 | tf_op jit(solution)/shard_map/ppermute | solution.py:41
  76.2 1.5 fusion.27
  77.7 0.0 copy-done.5
  77.7 1.9 %fusion.1 = bf16[768,512]{1,0:T(8,128)(2,1)S(1)} fusion(f32[768,512]{1,0:T(8,128)} %add_add_fusion, f32[384,512]{1,0:T(8,128)S(1)} %get-tuple-element.32, f32[384,512]{1,0:T(8,128)S(1)} %get-tuple-element.31, bf16[768,512]{1,0:T(8,128)(2,1)S(1)} %copy-done.5), kind=kLoop, calls=%fused_computation.2 | loop fusion | flops 1966080 | bytes 4718592 | tf_op jit(solution)/shard_map/convert_element_type | solution.py:184
  79.6 1.4 convolution_convert_fusion
  81.0 1.4 convolution_convert_fusion.1
  82.4 1.4 convolution_convert_fusion.2
  83.8 1.4 convolution_convert_fusion.3
  85.3 2.8 %collective-permute-start.6 = (bf16[512,512]{1,0:T(8,128)(2,1)}, bf16[512,512]{1,0:T(8,128)(2,1)S(1)}, u32[]{:S(2)}, u32[]{:S(2)}) collective-permute-start(bf16[512,512]{1,0:T(8,128)(2,1)} %convolution_convert_fusion.2), channel_id=1, source_target_pairs={{0,4},{2,6},{4,0},{6,2},{1,5},{3,7},{5,1},{7,3},{8,12},{10,14},{12... | collective-permute-start | bytes 1572872 | tf_op jit(solution)/shard_map/ppermute | solution.py:41
  88.0 4.0 %collective-permute-start.7 = (bf16[512,512]{1,0:T(8,128)(2,1)}, bf16[512,512]{1,0:T(8,128)(2,1)S(1)}, u32[]{:S(2)}, u32[]{:S(2)}) collective-permute-start(bf16[512,512]{1,0:T(8,128)(2,1)} %convolution_convert_fusion.1), channel_id=1, source_target_pairs={{0,2},{2,4},{4,6},{6,0},{1,3},{3,5},{5,7},{7,1},{8,10},{10,12},{12... | collective-permute-start | bytes 1572872 | tf_op jit(solution)/shard_map/ppermute | solution.py:41
  92.0 2.5 %collective-permute-start.8 = (bf16[512,512]{1,0:T(8,128)(2,1)}, bf16[512,512]{1,0:T(8,128)(2,1)S(1)}, u32[]{:S(2)}, u32[]{:S(2)}) collective-permute-start(bf16[512,512]{1,0:T(8,128)(2,1)} %convolution_convert_fusion), channel_id=1, source_target_pairs={{0,6},{2,0},{4,2},{6,4},{1,7},{3,1},{5,3},{7,5},{8,14},{10,8},{12,... | collective-permute-start | bytes 1572872 | tf_op jit(solution)/shard_map/ppermute | solution.py:41
  94.6 0.0 copy-done.8
  94.6 0.7 fusion.16
  95.3 0.8 broadcast_in_dim.24
  96.1 7.5 %all-to-all-start.2 = ((bf16[16,64,128]{2,1,0:T(8,128)(2,1)}), bf16[16,64,128]{2,1,0:T(8,128)(2,1)S(1)}, u32[]{:S(2)}, u32[]{:S(2)}) async-start(bf16[16,64,128]{2,1,0:T(8,128)(2,1)} %broadcast_in_dim.24), calls=%async_computation.2 | async-start | bytes 524288 | tf_op jit(solution)/shard_map/all_to_all | solution.py:85
  103.6 0.0 collective-permute-done.6
  103.6 10.3 %collective-permute-done.7 = bf16[512,512]{1,0:T(8,128)(2,1)S(1)} collective-permute-done((bf16[512,512]{1,0:T(8,128)(2,1)}, bf16[512,512]{1,0:T(8,128)(2,1)S(1)}, u32[]{:S(2)}, u32[]{:S(2)}) %collective-permute-start.7) | collective-permute-done | bytes 524320 | tf_op jit(solution)/shard_map/ppermute | solution.py:41
  113.9 0.0 collective-permute-done.8
  113.9 1.3 add_convert_fusion
  115.2 0.0 all-to-all-done.2
  115.3 17.7 %all_to_all.31.arrived_ref = bf16[4,128,512]{2,1,0:T(8,128)(2,1)S(1)} all-to-all(bf16[4,128,512]{2,1,0:T(8,128)(2,1)S(1)} %bitcast.52), channel_id=1, replica_groups=mesh['z'=8,'y_lo'=2,'y_hi'=4,'x'=4,'core'=2] {'y_hi'}, dimensions={0} | all-to-all | bytes 1048576 | tf_op jit(solution)/shard_map/all_to_all | solution.py:85
  132.9 0.8 collect.1
  133.7 9.6 %all-to-all-start.4 = ((f32[32,1,128]{2,1,0:T(1,128)}), f32[32,1,128]{2,1,0:T(1,128)S(1)}, u32[]{:S(2)}, u32[]{:S(2)}) async-start(f32[32,1,128]{2,1,0:T(1,128)} %bitcast.14), calls=%async_computation.4 | async-start | bytes 32768 | tf_op jit(solution)/shard_map/all_to_all | solution.py:85
  143.4 0.6 bitcast_add_fusion
  144.0 8.7 %all-to-all-done.4 = f32[32,1,128]{2,1,0:T(1,128)S(1)} async-done(((f32[32,1,128]{2,1,0:T(1,128)}), f32[32,1,128]{2,1,0:T(1,128)S(1)}, u32[]{:S(2)}, u32[]{:S(2)}) %all-to-all-start.4) | async-done | bytes 16416 | tf_op jit(solution)/shard_map/all_to_all | solution.py:85
  152.7 0.7 clip.1
  153.4 0.7 copy.13
  (8 shorter events, 0.1 us)
Async XLA Ops:
  0.6 14.8 %copy-start.6 = (bf16[1,384,512]{2,1,0:T(8,128)(2,1)S(1)}, bf16[1,384,512]{2,1,0:T(8,128)(2,1)}, u32[]{:S(2)}) copy-start(bf16[1,384,512]{2,1,0:T(8,128)(2,1)} %param.10) | copy-start | bytes 1179652
  0.6 20.5 %collective-permute-start = (bf16[384,4096]{1,0:T(8,128)(2,1)}, bf16[384,4096]{1,0:T(8,128)(2,1)S(1)}, u32[]{:S(2)}, u32[]{:S(2)}) collective-permute-start(bf16[384,4096]{1,0:T(8,128)(2,1)} %bitcast.48), channel_id=1, source_target_pairs={{0,1},{1,0},{2,3},{3,2},{4,5},{5,4},{6,7},{7,6},{8,9},{9,8},{10,11... | collective-permute-start | bytes 9437192 | tf_op jit(solution)/shard_map/ppermute | solution.py:41
  9.6 13.2 %copy-start.3 = (f32[4096]{0:T(1024)S(1)}, f32[4096]{0:T(1024)}, u32[]{:S(2)}) copy-start(f32[4096]{0:T(1024)} %param.8) | copy-start | bytes 49156
  11.3 19.0 %all-to-all-start = ((bf16[4,128,512]{2,1,0:T(8,128)(2,1)}), bf16[4,128,512]{2,1,0:T(8,128)(2,1)}, u32[]{:S(2)}, u32[]{:S(2)}) async-start(bf16[4,128,512]{2,1,0:T(8,128)(2,1)} %broadcast_in_dim.22), calls=%async_computation | async-start | bytes 1048576 | tf_op jit(solution)/shard_map/all_to_all | solution.py:85
  15.5 3.7 %collective-permute-start.1 = (bf16[384,512]{1,0:T(8,128)(2,1)S(1)}, bf16[384,512]{1,0:T(8,128)(2,1)}, u32[]{:S(2)}, u32[]{:S(2)}) collective-permute-start(bf16[384,512]{1,0:T(8,128)(2,1)S(1)} %bitcast.56), channel_id=1, source_target_pairs={{0,1},{1,0},{2,3},{3,2},{4,5},{5,4},{6,7},{7,6},{8,9},{9,8},{10,11... | collective-permute-start | bytes 1179656 | tf_op jit(solution)/shard_map/ppermute | solution.py:41
  21.2 1.6 %copy-start.1 = (bf16[384,4096]{1,0:T(8,128)(2,1)}, bf16[384,4096]{1,0:T(8,128)(2,1)S(1)}, u32[]{:S(2)}) copy-start(bf16[384,4096]{1,0:T(8,128)(2,1)S(1)} %collective-permute-done.theirs_ref) | copy-start | bytes 9437188
  22.8 1.9 %copy-start = (bf16[1,384,4096]{2,1,0:T(8,128)(2,1)S(1)}, bf16[1,384,4096]{2,1,0:T(8,128)(2,1)}, u32[]{:S(2)}) copy-start(bf16[1,384,4096]{2,1,0:T(8,128)(2,1)} %param.7) | copy-start | bytes 9437188
  24.7 1.9 %copy-start.2 = (bf16[384,4096]{1,0:T(8,128)(2,1)S(1)}, bf16[384,4096]{1,0:T(8,128)(2,1)}, u32[]{:S(2)}) copy-start(bf16[384,4096]{1,0:T(8,128)(2,1)} %copy-done.1) | copy-start | bytes 9437188
  26.6 9.6 %copy-start.7 = (bf16[131072]{0:T(1024)(128)(2,1)S(1)}, bf16[131072]{0:T(1024)(128)(2,1)}, u32[]{:S(2)}) copy-start(bf16[131072]{0:T(1024)(128)(2,1)} %param.11) | copy-start | bytes 786436
  30.4 28.3 %collective-permute-start.4 = (bf16[512,512]{1,0:T(8,128)(2,1)}, bf16[512,512]{1,0:T(8,128)(2,1)}, u32[]{:S(2)}, u32[]{:S(2)}) collective-permute-start(bf16[512,512]{1,0:T(8,128)(2,1)} %bitcast.1), channel_id=1, source_target_pairs={{0,2},{2,4},{4,6},{6,0},{1,3},{3,5},{5,7},{7,1},{8,10},{10,12},{12... | collective-permute-start | bytes 1572872 | tf_op jit(solution)/shard_map/ppermute | solution.py:41
  32.3 26.4 %collective-permute-start.2 = (bf16[512,512]{1,0:T(8,128)(2,1)}, bf16[512,512]{1,0:T(8,128)(2,1)}, u32[]{:S(2)}, u32[]{:S(2)}) collective-permute-start(bf16[512,512]{1,0:T(8,128)(2,1)} %bitcast.1), channel_id=1, source_target_pairs={{0,4},{2,6},{4,0},{6,2},{1,5},{3,7},{5,1},{7,3},{8,12},{10,14},{12... | collective-permute-start | bytes 1572872 | tf_op jit(solution)/shard_map/ppermute | solution.py:41
  39.0 19.6 %all-to-all-start.1 = ((bf16[16,64,128]{2,1,0:T(8,128)(2,1)}), bf16[16,64,128]{2,1,0:T(8,128)(2,1)S(1)}, u32[]{:S(2)}, u32[]{:S(2)}) async-start(bf16[16,64,128]{2,1,0:T(8,128)(2,1)} %multiply_convert_fusion), calls=%async_computation.1 | async-start | bytes 524288 | tf_op jit(solution)/shard_map/all_to_all | solution.py:85
  49.9 13.4 %collective-permute-start.3 = (bf16[512,512]{1,0:T(8,128)(2,1)}, bf16[512,512]{1,0:T(8,128)(2,1)}, u32[]{:S(2)}, u32[]{:S(2)}) collective-permute-start(bf16[512,512]{1,0:T(8,128)(2,1)} %bitcast.1), channel_id=1, source_target_pairs={{0,6},{2,0},{4,2},{6,4},{1,7},{3,1},{5,3},{7,5},{8,14},{10,8},{12,... | collective-permute-start | bytes 1572872 | tf_op jit(solution)/shard_map/ppermute | solution.py:41
  60.3 4.7 %copy-start.4 = (f32[768,512]{1,0:T(8,128)S(1)}, f32[768,512]{1,0:T(8,128)}, u32[]{:S(2)}) copy-start(f32[768,512]{1,0:T(8,128)} %fusion.14) | copy-start | bytes 4718596
  67.8 8.5 %collective-permute-start.5 = (f32[768,512]{1,0:T(8,128)}, f32[768,512]{1,0:T(8,128)}, u32[]{:S(2)}, u32[]{:S(2)}) collective-permute-start(f32[768,512]{1,0:T(8,128)} %add_add_fusion), channel_id=1, source_target_pairs={{0,1},{1,0},{2,3},{3,2},{4,5},{5,4},{6,7},{7,6},{8,9},{9,8},{10,11... | collective-permute-start | bytes 4718600 | tf_op jit(solution)/shard_map/ppermute | solution.py:41
  72.9 4.8 %copy-start.5 = (bf16[768,512]{1,0:T(8,128)(2,1)S(1)}, bf16[768,512]{1,0:T(8,128)(2,1)}, u32[]{:S(2)}) copy-start(bf16[768,512]{1,0:T(8,128)(2,1)} %pad_maximum_fusion) | copy-start | bytes 2359300
  83.8 10.7 %copy-start.8 = (f32[8192]{0:T(1024)S(1)}, f32[8192]{0:T(1024)}, u32[]{:S(2)}) copy-start(f32[8192]{0:T(1024)} %param.13) | copy-start | bytes 98308
  85.3 18.4 %collective-permute-start.6 = (bf16[512,512]{1,0:T(8,128)(2,1)}, bf16[512,512]{1,0:T(8,128)(2,1)S(1)}, u32[]{:S(2)}, u32[]{:S(2)}) collective-permute-start(bf16[512,512]{1,0:T(8,128)(2,1)} %convolution_convert_fusion.2), channel_id=1, source_target_pairs={{0,4},{2,6},{4,0},{6,2},{1,5},{3,7},{5,1},{7,3},{8,12},{10,14},{12... | collective-permute-start | bytes 1572872 | tf_op jit(solution)/shard_map/ppermute | solution.py:41
  88.0 25.9 %collective-permute-start.7 = (bf16[512,512]{1,0:T(8,128)(2,1)}, bf16[512,512]{1,0:T(8,128)(2,1)S(1)}, u32[]{:S(2)}, u32[]{:S(2)}) collective-permute-start(bf16[512,512]{1,0:T(8,128)(2,1)} %convolution_convert_fusion.1), channel_id=1, source_target_pairs={{0,2},{2,4},{4,6},{6,0},{1,3},{3,5},{5,7},{7,1},{8,10},{10,12},{12... | collective-permute-start | bytes 1572872 | tf_op jit(solution)/shard_map/ppermute | solution.py:41
  92.0 21.9 %collective-permute-start.8 = (bf16[512,512]{1,0:T(8,128)(2,1)}, bf16[512,512]{1,0:T(8,128)(2,1)S(1)}, u32[]{:S(2)}, u32[]{:S(2)}) collective-permute-start(bf16[512,512]{1,0:T(8,128)(2,1)} %convolution_convert_fusion), channel_id=1, source_target_pairs={{0,6},{2,0},{4,2},{6,4},{1,7},{3,1},{5,3},{7,5},{8,14},{10,8},{12,... | collective-permute-start | bytes 1572872 | tf_op jit(solution)/shard_map/ppermute | solution.py:41
  96.1 19.2 %all-to-all-start.2 = ((bf16[16,64,128]{2,1,0:T(8,128)(2,1)}), bf16[16,64,128]{2,1,0:T(8,128)(2,1)S(1)}, u32[]{:S(2)}, u32[]{:S(2)}) async-start(bf16[16,64,128]{2,1,0:T(8,128)(2,1)} %broadcast_in_dim.24), calls=%async_computation.2 | async-start | bytes 524288 | tf_op jit(solution)/shard_map/all_to_all | solution.py:85
  133.7 19.0 %all-to-all-start.4 = ((f32[32,1,128]{2,1,0:T(1,128)}), f32[32,1,128]{2,1,0:T(1,128)S(1)}, u32[]{:S(2)}, u32[]{:S(2)}) async-start(f32[32,1,128]{2,1,0:T(1,128)} %bitcast.14), calls=%async_computation.4 | async-start | bytes 32768 | tf_op jit(solution)/shard_map/all_to_all | solution.py:85

commit v9 on v8

--- a/solution.py
+++ b/solution.py
@@ -11,6 +11,7 @@
 QBLOCK = 128
 LANES = 128
 VMEM_LIMIT = 8 << 20
+WHOLE = pl.BlockSpec(memory_space=pltpu.VMEM)
 
 
 outer_decay = 0.9
@@ -113,6 +114,68 @@
     return spread(own_next, REPLICA).reshape(-1), new_momentum.reshape(-1)
 
 
+def in_vmem(shape, dtype):
+    return pltpu.VMEM(shape, dtype)
+
+
+def product_kernel(scaled_ref, *refs):
+    *weight_refs, partial_ref = refs
+    group = weight_refs[0].shape[0]
+    partial_ref[...] = total(
+        [
+            jnp.dot(
+                scaled_ref[:, k * group : (k + 1) * group],
+                ref[...],
+                preferred_element_type=jnp.float32,
+            )
+            for k, ref in enumerate(weight_refs)
+        ]
+    )
+
+
+def product(scaled, weights):
+    return pl.pallas_call(
+        product_kernel,
+        out_shape=in_vmem((scaled.shape[0], weights[0].shape[1]), jnp.float32),
+        in_specs=[WHOLE] * (1 + len(weights)),
+        out_specs=WHOLE,
+        compiler_params=pltpu.CompilerParams(vmem_limit_bytes=2 * VMEM_LIMIT),
+        name="product",
+    )(scaled, *weights)
+
+
+def gradient_kernel(scaled_ref, mine_ref, theirs_ref, *refs):
+    *target_refs, first, second, third, fourth, residual_ref = refs
+    tokens = target_refs[0].shape[0]
+    for half, target_ref in enumerate(target_refs):
+        here = slice(half * tokens, (half + 1) * tokens)
+        there = slice((1 - half) * tokens, (2 - half) * tokens)
+        residual_ref[here, :] = (
+            mine_ref[here, :] + theirs_ref[there, :] - target_ref[...].astype(jnp.float32)
+        ).astype(jnp.bfloat16)
+    group = first.shape[0]
+    for k, ref in enumerate((first, second, third, fourth)):
+        ref[...] = lax.dot_general(
+            scaled_ref[:, k * group : (k + 1) * group],
+            residual_ref[...],
+            (((0,), (0,)), ((), ())),
+            preferred_element_type=jnp.float32,
+        ).astype(jnp.bfloat16)
+
+
+def gradient_blocks(scaled, mine, theirs, targets):
+    block = (scaled.shape[1] // AXES["x"], mine.shape[1])
+    return pl.pallas_call(
+        gradient_kernel,
+        out_shape=(in_vmem(block, jnp.bfloat16),) * AXES["x"],
+        in_specs=[WHOLE] * 5,
+        out_specs=(WHOLE,) * AXES["x"],
+        scratch_shapes=[pltpu.VMEM(mine.shape, jnp.bfloat16)],
+        compiler_params=pltpu.CompilerParams(vmem_limit_bytes=3 * VMEM_LIMIT),
+        name="gradient",
+    )(scaled, mine, theirs, *targets)
+
+
 def collect_kernel(arrived_ref, gradient_ref, squares_ref):
     gradient = total([arrived_ref[k] for k in range(arrived_ref.shape[0])])
     gradient_ref[...] = gradient
@@ -123,15 +186,14 @@
 
 
 def collect(arrived):
-    in_vmem = pl.BlockSpec(memory_space=pltpu.VMEM)
     return pl.pallas_call(
         collect_kernel,
         out_shape=(
             jax.ShapeDtypeStruct(arrived.shape[1:], jnp.float32),
             jax.ShapeDtypeStruct((CHIPS * AXES["core"], LANES), jnp.float32),
         ),
-        in_specs=[in_vmem],
-        out_specs=(in_vmem, in_vmem),
+        in_specs=[WHOLE],
+        out_specs=(WHOLE, WHOLE),
         compiler_params=pltpu.CompilerParams(vmem_limit_bytes=VMEM_LIMIT),
         name="collect",
     )(arrived)
@@ -146,48 +208,33 @@
 
 
 def clip(squares, gradient, entries):
-    in_vmem = pl.BlockSpec(memory_space=pltpu.VMEM)
     return pl.pallas_call(
         functools.partial(clip_kernel, entries),
         out_shape=jax.ShapeDtypeStruct(gradient.shape, jnp.bfloat16),
-        in_specs=[in_vmem, in_vmem],
-        out_specs=in_vmem,
+        in_specs=[WHOLE, WHOLE],
+        out_specs=WHOLE,
         compiler_params=pltpu.CompilerParams(vmem_limit_bytes=VMEM_LIMIT),
         name="clip",
     )(squares, gradient)
 
 
 def shards(inputs, feature_gain, key_weight, teacher_keys, global_frag, local_frag, momentum):
-    tokens, features = inputs.shape[1:]
+    features = inputs.shape[2]
     rows, width = key_weight.shape[1:]
 
     column = spread(key_weight[0], "y_hi").reshape(AXES["y_hi"] * rows, width)
     raw = send(inputs[0], "core", 1)
     their_targets = send(teacher_keys[0], "core", 1)
-    targets = jnp.concatenate([teacher_keys[0], their_targets], axis=0)
+    targets = (teacher_keys[0], their_targets)
     scaled = arrange(inputs[0], raw, feature_gain)
     column, scaled, targets, global_frag, local_frag = tied(
         column, scaled, targets, global_frag, local_frag
     )
-    far = {k: send(column, "x", -k) for k in STEPS}
+    far = [column] + [send(column, "x", -k) for k in (1, 2, 3)]
     arrived = exchange(fragment_codes(global_frag, local_frag[0]), REPLICA)
-    group = scaled.shape[1] // AXES["x"]
-    blocks = [scaled[:, k * group : (k + 1) * group] for k in range(AXES["x"])]
-    partial = jnp.dot(blocks[0], column, preferred_element_type=jnp.float32)
-    last = STEPS[-1]
-    far[last], arrived = tied(far[last], arrived)
-    for k in STEPS:
-        partial += jnp.dot(blocks[k], far[k], preferred_element_type=jnp.float32)
-
-    theirs = send(partial, "core", 1)
-    projected = partial + jnp.concatenate([theirs[tokens:], theirs[:tokens]], axis=0)
-    residual = (projected - targets.astype(jnp.float32)).astype(jnp.bfloat16)
-    gradient = [
-        lax.dot_general(
-            block, residual, (((0,), (0,)), ((), ())), preferred_element_type=jnp.float32
-        ).astype(jnp.bfloat16)
-        for block in blocks
-    ]
+    far, arrived = tied(far, arrived)
+    partial = product(scaled, far)
+    gradient = list(gradient_blocks(scaled, partial, send(partial, "core", 1), targets))
     gradient[0], arrived = tied(gradient[0], arrived)
     new_global, new_momentum = fragment_update(arrived, global_frag, momentum)
     mine = total([gradient[0]] + [send(gradient[k], "x", k) for k in STEPS])

time: 155 us -> 150 us (0.968)
  blocking collectives: 17.7 us -> 35.6 us
  matrix products: 14.5 us -> 0 us
  starting transfers between devices: 64.6 us -> 51.6 us
  Pallas kernels: 3.49 us -> 12.6 us
  other arithmetic: 10.9 us -> 7.4 us
  waiting for transfers between devices: 31.8 us -> 29.4 us
    all_to_all x1 -> x2, blocking collectives: 17.7 us -> 35.6 us  [exchange(): return lax.all_to_all(parts, axis, split_axis=0, concat_axis=0, tiled=True)]
    dot_general x8 -> x0, matrix products: 14.5 us -> none  [the longest x3 6.03 us: shards(): partial += jnp.dot(blocks[k], far[k], preferred_element_type=jnp.float32)]
    all_to_all x4 -> x3, starting transfers between devices: 32.2 us -> 17.9 us  [exchange(): return lax.all_to_all(parts, axis, split_axis=0, concat_axis=0, tiled=True)]
    pallas_call x0 -> x2, Pallas kernels: none -> 9.11 us  [the longest x1 4.6 us: gradient_blocks(): pl.pallas_call(gradient_kernel, out_shape=(in_vmem(block, jnp.bfloat16),)...]
    ppermute x9, waiting for transfers between devices: 18.5 us -> 15.8 us  [send(): lax.ppermute(value, axis, [(i, (i + step) % size) for i in range(size)])]
    unnamed x19 -> x23, local copies, waits for them, and re-layouts: 6.16 us -> 8.66 us
    concatenate x1 -> x0, other arithmetic: 1.93 us -> none  [shards(): targets = jnp.concatenate([teacher_keys[0], their_targets], axis=0)]
    convert_element_type x1 -> x0, other arithmetic: 1.87 us -> none  [shards(): residual = (projected - targets.astype(jnp.float32)).astype(jnp.bfloat16)]
  transfers between devices with their start and end apart: 13 -> 12, of which waited for: 7 -> 5; matrix products, arithmetic and copies ran while one was open for 10% -> 7% of each run, Pallas kernels for 1% -> 1%
where the time goes in v9:
time: 150 us; the launch traced here: 149 us
  starting transfers between devices  51.6 us (34%)
  blocking collectives  35.6 us (24%)
  waiting for transfers between devices  29.4 us (20%)
  Pallas kernels  12.6 us (8%)
  local copies, waits for them, and re-layouts  11.2 us (7%)
  other arithmetic  7.4 us (5%)
    all_to_all x2, blocking collectives, exchange(): return lax.all_to_all(parts, axis, split_axis=0, concat_axis=0, tiled=True)  35.6 us
    ppermute x9, starting transfers between devices, send(): lax.ppermute(value, axis, [(i, (i + step) % size) for i in range(size)])  33.6 us
    all_to_all x3, starting transfers between devices, exchange(): return lax.all_to_all(parts, axis, split_axis=0, concat_axis=0, tiled=True)  17.9 us
    ppermute x9, waiting for transfers between devices, send(): lax.ppermute(value, axis, [(i, (i + step) % size) for i in range(size)])  15.8 us
    all_to_all x3, waiting for transfers between devices, exchange(): return lax.all_to_all(parts, axis, split_axis=0, concat_axis=0, tiled=True)  13.6 us
    unnamed x23, local copies, waits for them, and re-layouts  8.66 us
    pallas_call x1, Pallas kernels, gradient_blocks(): pl.pallas_call(gradient_kernel, out_shape=(in_vmem(block, jnp.bfloat16),)...  4.6 us
    pallas_call x1, Pallas kernels, product(): pl.pallas_call(product_kernel, out_shape=in_vmem((scaled.shape[0], weight...  4.51 us
  transfers between devices with their start and end apart: 12, of which 5 were waited for; matrix products, arithmetic and copies ran while one was open for 7% of the time, Pallas kernels for 1%

profile of v9, /device:TPU:1, one launch (start us, length us, event | category | flops | bytes accessed | tf_op | source)
XLA Modules:
  0.0 148.7 jit_solution(4399597319060119134)
XLA Ops:
  0.6 8.8 %collective-permute-start = (bf16[384,4096]{1,0:T(8,128)(2,1)}, bf16[384,4096]{1,0:T(8,128)(2,1)S(1)}, u32[]{:S(2)}, u32[]{:S(2)}) collective-permute-start(bf16[384,4096]{1,0:T(8,128)(2,1)} %bitcast.34), channel_id=1, source_target_pairs={{0,1},{1,0},{2,3},{3,2},{4,5},{5,4},{6,7},{7,6},{8,9},{9,8},{10,11... | collective-permute-start | bytes 9437192 | tf_op jit(solution)/shard_map/ppermute | solution.py:42
  9.4 1.7 %broadcast_in_dim.22 = bf16[4,128,512]{2,1,0:T(8,128)(2,1)} broadcast(bf16[128,512]{1,0:T(8,128)(2,1)} %bitcast.44), dimensions={1,2} | broadcast | bytes 655360 | tf_op jit(solution)/shard_map/broadcast_in_dim | solution.py:90
  11.2 4.1 %all-to-all-start = ((bf16[4,128,512]{2,1,0:T(8,128)(2,1)}), bf16[4,128,512]{2,1,0:T(8,128)(2,1)}, u32[]{:S(2)}, u32[]{:S(2)}) async-start(bf16[4,128,512]{2,1,0:T(8,128)(2,1)} %broadcast_in_dim.22), calls=%async_computation | async-start | bytes 1048576 | tf_op jit(solution)/shard_map/all_to_all | solution.py:86
  15.3 1.9 %collective-permute-start.1 = (bf16[384,512]{1,0:T(8,128)(2,1)}, bf16[384,512]{1,0:T(8,128)(2,1)S(1)}, u32[]{:S(2)}, u32[]{:S(2)}) collective-permute-start(bf16[384,512]{1,0:T(8,128)(2,1)} %bitcast.36), channel_id=1, source_target_pairs={{0,1},{1,0},{2,3},{3,2},{4,5},{5,4},{6,7},{7,6},{8,9},{9,8},{10,11... | collective-permute-start | bytes 1179656 | tf_op jit(solution)/shard_map/ppermute | solution.py:42
  17.3 0.0 collective-permute-done.theirs_ref
  17.3 0.0 copy-start.1
  17.3 1.6 %copy-done.1 = bf16[384,4096]{1,0:T(8,128)(2,1)} copy-done((bf16[384,4096]{1,0:T(8,128)(2,1)}, bf16[384,4096]{1,0:T(8,128)(2,1)S(1)}, u32[]{:S(2)}) %copy-start.1) | copy-done | bytes 3145752
  18.9 0.0 copy-start
  18.9 1.9 %copy-done = bf16[1,384,4096]{2,1,0:T(8,128)(2,1)S(1)} copy-done((bf16[1,384,4096]{2,1,0:T(8,128)(2,1)S(1)}, bf16[1,384,4096]{2,1,0:T(8,128)(2,1)}, u32[]{:S(2)}) %copy-start) | copy-done | bytes 3145752
  20.8 0.0 copy-start.2
  20.8 1.9 %copy-done.2 = bf16[384,4096]{1,0:T(8,128)(2,1)S(1)} copy-done((bf16[384,4096]{1,0:T(8,128)(2,1)S(1)}, bf16[384,4096]{1,0:T(8,128)(2,1)}, u32[]{:S(2)}) %copy-start.2) | copy-done | bytes 3145752
  22.7 0.0 copy-start.7
  22.7 0.7 copy-done.7
  23.4 2.0 %arrange.1 = bf16[2,384,2048]{2,1,0:T(8,128)(2,1)S(1)} custom-call(s32[16]{0:T(128)S(1)} %fusion.10.order_ref, bf16[384,4096]{1,0:T(8,128)(2,1)S(1)} %bitcast.35, bf16[384,4096]{1,0:T(8,128)(2,1)S(1)} %copy-done.2, f32[1,4096]{1,0:T(1,128)S(1)} %bitcast.39), custom_call_target="tpu_custom_call" | custom-call | tf_op jit(solution)/shard_map/arrange/pallas_call | solution.py:68
  25.4 0.0 collective-permute-done.1.refs_1_
  25.4 0.0 copy-start.5
  25.4 4.8 %all-to-all-done = bf16[4,128,512]{2,1,0:T(8,128)(2,1)} async-done(((bf16[4,128,512]{2,1,0:T(8,128)(2,1)}), bf16[4,128,512]{2,1,0:T(8,128)(2,1)}, u32[]{:S(2)}, u32[]{:S(2)}) %all-to-all-start) | async-done | bytes 524320 | tf_op jit(solution)/shard_map/all_to_all | solution.py:86
  30.2 1.9 %collective-permute-start.4 = (bf16[512,512]{1,0:T(8,128)(2,1)}, bf16[512,512]{1,0:T(8,128)(2,1)}, u32[]{:S(2)}, u32[]{:S(2)}) collective-permute-start(bf16[512,512]{1,0:T(8,128)(2,1)} %bitcast.1.refs_0_), channel_id=1, source_target_pairs={{0,2},{2,4},{4,6},{6,0},{1,3},{3,5},{5,7},{7,1},{8,10},{10,12},{12... | collective-permute-start | bytes 1572872 | tf_op jit(solution)/shard_map/ppermute | solution.py:42
  32.1 2.2 %collective-permute-start.3 = (bf16[512,512]{1,0:T(8,128)(2,1)}, bf16[512,512]{1,0:T(8,128)(2,1)}, u32[]{:S(2)}, u32[]{:S(2)}) collective-permute-start(bf16[512,512]{1,0:T(8,128)(2,1)} %bitcast.1.refs_0_), channel_id=1, source_target_pairs={{0,4},{2,6},{4,0},{6,2},{1,5},{3,7},{5,1},{7,3},{8,12},{10,14},{12... | collective-permute-start | bytes 1572872 | tf_op jit(solution)/shard_map/ppermute | solution.py:42
  34.4 4.2 %collective-permute-start.2 = (bf16[512,512]{1,0:T(8,128)(2,1)}, bf16[512,512]{1,0:T(8,128)(2,1)}, u32[]{:S(2)}, u32[]{:S(2)}) collective-permute-start(bf16[512,512]{1,0:T(8,128)(2,1)} %bitcast.1.refs_0_), channel_id=1, source_target_pairs={{0,6},{2,0},{4,2},{6,4},{1,7},{3,1},{5,3},{7,5},{8,14},{10,8},{12,... | collective-permute-start | bytes 1572872 | tf_op jit(solution)/shard_map/ppermute | solution.py:42
  38.6 1.6 %convert_element_type.85 = f32[1,131072]{1,0:T(1,128)S(1)} convert(bf16[1,131072]{1,0:T(2,128)(2,1)} %param.12) | non-fusion elementwise | flops 131072 | bytes 786432 | tf_op jit(solution)/shard_map/convert_element_type | solution.py:98
  40.2 1.8 %bitcast_reduce_fusion = (f32[1024]{0:T(1024)S(1)}, f32[131072]{0:T(1024)}) fusion(f32[131072]{0:T(1024)S(1)} %bitcast.42, bf16[131072]{0:T(1024)(128)(2,1)} %param.11), kind=kLoop, calls=%fused_computation.1 | loop fusion | flops 523264 | bytes 1314816 | tf_op jit(solution)/shard_map/reduce_sum | solution.py:31
  42.1 0.1 reshape.90
  42.1 1.3 multiply_convert_fusion
  43.4 0.0 copy-done.5
  43.4 18.5 %all_to_all.31 = bf16[16,64,128]{2,1,0:T(8,128)(2,1)} all-to-all(bf16[16,64,128]{2,1,0:T(8,128)(2,1)S(1)} %multiply_convert_fusion), channel_id=1, replica_groups=mesh['z'=8,'y_lo'=2,'y_hi'=4,'x'=4,'core'=2] {'z','y_lo'}, dimensions={0} | all-to-all | bytes 524288 | tf_op jit(solution)/shard_map/all_to_all | solution.py:86
  61.9 0.0 copy-start.4
  61.9 0.0 collective-permute-done.4.refs_3_
  61.9 0.0 collective-permute-done.3.refs_2_
  61.9 0.0 collective-permute-done.2.refs_1_
  61.9 4.5 %product.1.mine_ref = f32[768,512]{1,0:T(8,128)} custom-call(bf16[768,2048]{1,0:T(8,128)(2,1)S(1)} %bitcast.32, bf16[512,512]{1,0:T(8,128)(2,1)} %bitcast.1.refs_0_, bf16[512,512]{1,0:T(8,128)(2,1)} %collective-permute-done.2.refs_1_, bf16[512,512]{1,0:T(8,128)(2,1)} %collective-permute-done.3.refs_2_, bf16[512,512]{1,0:T(8,128)(2,1)} %collective-permute-done.4.refs_3_), custom_call_target="tpu_custom_call" | custom-call | tf_op jit(solution)/shard_map/product/pallas_call | solution.py:137
  66.4 5.8 %collective-permute-start.5 = (f32[768,512]{1,0:T(8,128)}, f32[768,512]{1,0:T(8,128)}, u32[]{:S(2)}, u32[]{:S(2)}) collective-permute-start(f32[768,512]{1,0:T(8,128)} %product.1.mine_ref), channel_id=1, source_target_pairs={{0,1},{1,0},{2,3},{3,2},{4,5},{5,4},{6,7},{7,6},{8,9},{9,8},{10,11... | collective-permute-start | bytes 4718600 | tf_op jit(solution)/shard_map/ppermute | solution.py:42
  72.2 3.4 %collective-permute-done.5.theirs_ref = f32[768,512]{1,0:T(8,128)} collective-permute-done((f32[768,512]{1,0:T(8,128)}, f32[768,512]{1,0:T(8,128)}, u32[]{:S(2)}, u32[]{:S(2)}) %collective-permute-start.5) | collective-permute-done | bytes 1572896 | tf_op jit(solution)/shard_map/ppermute | solution.py:42
  75.6 0.0 copy-done.4
  75.6 0.0 copy-start.6
  75.6 1.0 copy-done.6
  76.6 0.0 copy-start.8
  76.6 0.0 copy-start.9
  76.6 4.6 %gradient.1 = (bf16[512,512]{1,0:T(8,128)(2,1)S(1)}, bf16[512,512]{1,0:T(8,128)(2,1)}, bf16[512,512]{1,0:T(8,128)(2,1)}, bf16[512,512]{1,0:T(8,128)(2,1)}) custom-call(bf16[768,2048]{1,0:T(8,128)(2,1)S(1)} %bitcast.33, f32[768,512]{1,0:T(8,128)} %product.1.mine_ref, f32[768,512]{1,0:T(8,128)} %collective-permute-done.5.theirs_ref, ...), custom_call_target="tpu_custom_call" | custom-call | tf_op jit(solution)/shard_map/gradient/pallas_call | solution.py:168
  81.2 0.0 copy-start.3
  81.2 0.8 copy-done.3
  82.0 0.0 copy-start.10
  82.0 2.3 %collective-permute-start.6 = (bf16[512,512]{1,0:T(8,128)(2,1)}, bf16[512,512]{1,0:T(8,128)(2,1)S(1)}, u32[]{:S(2)}, u32[]{:S(2)}) collective-permute-start(bf16[512,512]{1,0:T(8,128)(2,1)} %get-tuple-element.37), channel_id=1, source_target_pairs={{0,4},{2,6},{4,0},{6,2},{1,5},{3,7},{5,1},{7,3},{8,12},{10,14},{12... | collective-permute-start | bytes 1572872 | tf_op jit(solution)/shard_map/ppermute | solution.py:42
  84.2 2.0 %collective-permute-start.7 = (bf16[512,512]{1,0:T(8,128)(2,1)}, bf16[512,512]{1,0:T(8,128)(2,1)S(1)}, u32[]{:S(2)}, u32[]{:S(2)}) collective-permute-start(bf16[512,512]{1,0:T(8,128)(2,1)} %get-tuple-element.38), channel_id=1, source_target_pairs={{0,2},{2,4},{4,6},{6,0},{1,3},{3,5},{5,7},{7,1},{8,10},{10,12},{12... | collective-permute-start | bytes 1572872 | tf_op jit(solution)/shard_map/ppermute | solution.py:42
  86.2 4.5 %collective-permute-start.8 = (bf16[512,512]{1,0:T(8,128)(2,1)}, bf16[512,512]{1,0:T(8,128)(2,1)S(1)}, u32[]{:S(2)}, u32[]{:S(2)}) collective-permute-start(bf16[512,512]{1,0:T(8,128)(2,1)} %get-tuple-element.39), channel_id=1, source_target_pairs={{0,6},{2,0},{4,2},{6,4},{1,7},{3,1},{5,3},{7,5},{8,14},{10,8},{12,... | collective-permute-start | bytes 1572872 | tf_op jit(solution)/shard_map/ppermute | solution.py:42
  90.7 0.0 copy-done.8
  90.8 0.0 copy-done.9
  90.8 0.7 fusion
  91.5 0.8 broadcast_in_dim.24
  92.3 6.0 %all-to-all-start.2 = ((bf16[16,64,128]{2,1,0:T(8,128)(2,1)}), bf16[16,64,128]{2,1,0:T(8,128)(2,1)S(1)}, u32[]{:S(2)}, u32[]{:S(2)}) async-start(bf16[16,64,128]{2,1,0:T(8,128)(2,1)} %broadcast_in_dim.24), calls=%async_computation.2 | async-start | bytes 524288 | tf_op jit(solution)/shard_map/all_to_all | solution.py:86
  98.3 0.6 collective-permute-done.6
  98.9 11.9 %collective-permute-done.7 = bf16[512,512]{1,0:T(8,128)(2,1)S(1)} collective-permute-done((bf16[512,512]{1,0:T(8,128)(2,1)}, bf16[512,512]{1,0:T(8,128)(2,1)S(1)}, u32[]{:S(2)}, u32[]{:S(2)}) %collective-permute-start.7) | collective-permute-done | bytes 524320 | tf_op jit(solution)/shard_map/ppermute | solution.py:42
  110.8 0.0 collective-permute-done.8
  110.8 1.3 add_convert_fusion
  112.1 0.0 all-to-all-done.2
  112.1 17.2 %all_to_all.32.arrived_ref = bf16[4,128,512]{2,1,0:T(8,128)(2,1)S(1)} all-to-all(bf16[4,128,512]{2,1,0:T(8,128)(2,1)S(1)} %bitcast.40), channel_id=1, replica_groups=mesh['z'=8,'y_lo'=2,'y_hi'=4,'x'=4,'core'=2] {'y_hi'}, dimensions={0} | all-to-all | bytes 1048576 | tf_op jit(solution)/shard_map/all_to_all | solution.py:86
  129.3 0.8 collect.1
  130.1 7.8 %all-to-all-start.4 = ((f32[32,1,128]{2,1,0:T(1,128)}), f32[32,1,128]{2,1,0:T(1,128)S(1)}, u32[]{:S(2)}, u32[]{:S(2)}) async-start(f32[32,1,128]{2,1,0:T(1,128)} %bitcast.14), calls=%async_computation.4 | async-start | bytes 32768 | tf_op jit(solution)/shard_map/all_to_all | solution.py:86
  137.9 0.0 copy-done.10
  137.9 0.6 bitcast_add_fusion
  138.5 8.8 %all-to-all-done.4 = f32[32,1,128]{2,1,0:T(1,128)S(1)} async-done(((f32[32,1,128]{2,1,0:T(1,128)}), f32[32,1,128]{2,1,0:T(1,128)S(1)}, u32[]{:S(2)}, u32[]{:S(2)}) %all-to-all-start.4) | async-done | bytes 16416 | tf_op jit(solution)/shard_map/all_to_all | solution.py:86
  147.3 0.7 clip.1
  148.0 0.7 copy.13
  (3 shorter events, 0.1 us)
Async XLA Ops:
  0.6 16.6 %collective-permute-start = (bf16[384,4096]{1,0:T(8,128)(2,1)}, bf16[384,4096]{1,0:T(8,128)(2,1)S(1)}, u32[]{:S(2)}, u32[]{:S(2)}) collective-permute-start(bf16[384,4096]{1,0:T(8,128)(2,1)} %bitcast.34), channel_id=1, source_target_pairs={{0,1},{1,0},{2,3},{3,2},{4,5},{5,4},{6,7},{7,6},{8,9},{9,8},{10,11... | collective-permute-start | bytes 9437192 | tf_op jit(solution)/shard_map/ppermute | solution.py:42
  11.2 19.0 %all-to-all-start = ((bf16[4,128,512]{2,1,0:T(8,128)(2,1)}), bf16[4,128,512]{2,1,0:T(8,128)(2,1)}, u32[]{:S(2)}, u32[]{:S(2)}) async-start(bf16[4,128,512]{2,1,0:T(8,128)(2,1)} %broadcast_in_dim.22), calls=%async_computation | async-start | bytes 1048576 | tf_op jit(solution)/shard_map/all_to_all | solution.py:86
  15.3 10.1 %collective-permute-start.1 = (bf16[384,512]{1,0:T(8,128)(2,1)}, bf16[384,512]{1,0:T(8,128)(2,1)S(1)}, u32[]{:S(2)}, u32[]{:S(2)}) collective-permute-start(bf16[384,512]{1,0:T(8,128)(2,1)} %bitcast.36), channel_id=1, source_target_pairs={{0,1},{1,0},{2,3},{3,2},{4,5},{5,4},{6,7},{7,6},{8,9},{9,8},{10,11... | collective-permute-start | bytes 1179656 | tf_op jit(solution)/shard_map/ppermute | solution.py:42
  17.3 1.6 %copy-start.1 = (bf16[384,4096]{1,0:T(8,128)(2,1)}, bf16[384,4096]{1,0:T(8,128)(2,1)S(1)}, u32[]{:S(2)}) copy-start(bf16[384,4096]{1,0:T(8,128)(2,1)S(1)} %collective-permute-done.theirs_ref) | copy-start | bytes 9437188
  18.9 1.9 %copy-start = (bf16[1,384,4096]{2,1,0:T(8,128)(2,1)S(1)}, bf16[1,384,4096]{2,1,0:T(8,128)(2,1)}, u32[]{:S(2)}) copy-start(bf16[1,384,4096]{2,1,0:T(8,128)(2,1)} %param.7) | copy-start | bytes 9437188
  20.8 1.9 %copy-start.2 = (bf16[384,4096]{1,0:T(8,128)(2,1)S(1)}, bf16[384,4096]{1,0:T(8,128)(2,1)}, u32[]{:S(2)}) copy-start(bf16[384,4096]{1,0:T(8,128)(2,1)} %copy-done.1) | copy-start | bytes 9437188
  22.7 0.7 copy-start.7
  25.4 18.0 %copy-start.5 = (bf16[384,512]{1,0:T(8,128)(2,1)}, bf16[384,512]{1,0:T(8,128)(2,1)S(1)}, u32[]{:S(2)}) copy-start(bf16[384,512]{1,0:T(8,128)(2,1)S(1)} %collective-permute-done.1.refs_1_) | copy-start | bytes 1179652
  30.2 31.7 %collective-permute-start.4 = (bf16[512,512]{1,0:T(8,128)(2,1)}, bf16[512,512]{1,0:T(8,128)(2,1)}, u32[]{:S(2)}, u32[]{:S(2)}) collective-permute-start(bf16[512,512]{1,0:T(8,128)(2,1)} %bitcast.1.refs_0_), channel_id=1, source_target_pairs={{0,2},{2,4},{4,6},{6,0},{1,3},{3,5},{5,7},{7,1},{8,10},{10,12},{12... | collective-permute-start | bytes 1572872 | tf_op jit(solution)/shard_map/ppermute | solution.py:42
  32.1 29.7 %collective-permute-start.3 = (bf16[512,512]{1,0:T(8,128)(2,1)}, bf16[512,512]{1,0:T(8,128)(2,1)}, u32[]{:S(2)}, u32[]{:S(2)}) collective-permute-start(bf16[512,512]{1,0:T(8,128)(2,1)} %bitcast.1.refs_0_), channel_id=1, source_target_pairs={{0,4},{2,6},{4,0},{6,2},{1,5},{3,7},{5,1},{7,3},{8,12},{10,14},{12... | collective-permute-start | bytes 1572872 | tf_op jit(solution)/shard_map/ppermute | solution.py:42
  34.4 27.5 %collective-permute-start.2 = (bf16[512,512]{1,0:T(8,128)(2,1)}, bf16[512,512]{1,0:T(8,128)(2,1)}, u32[]{:S(2)}, u32[]{:S(2)}) collective-permute-start(bf16[512,512]{1,0:T(8,128)(2,1)} %bitcast.1.refs_0_), channel_id=1, source_target_pairs={{0,6},{2,0},{4,2},{6,4},{1,7},{3,1},{5,3},{7,5},{8,14},{10,8},{12,... | collective-permute-start | bytes 1572872 | tf_op jit(solution)/shard_map/ppermute | solution.py:42
  61.9 13.7 %copy-start.4 = (bf16[1,384,512]{2,1,0:T(8,128)(2,1)S(1)}, bf16[1,384,512]{2,1,0:T(8,128)(2,1)}, u32[]{:S(2)}) copy-start(bf16[1,384,512]{2,1,0:T(8,128)(2,1)} %param.10) | copy-start | bytes 1179652
  66.4 9.2 %collective-permute-start.5 = (f32[768,512]{1,0:T(8,128)}, f32[768,512]{1,0:T(8,128)}, u32[]{:S(2)}, u32[]{:S(2)}) collective-permute-start(f32[768,512]{1,0:T(8,128)} %product.1.mine_ref), channel_id=1, source_target_pairs={{0,1},{1,0},{2,3},{3,2},{4,5},{5,4},{6,7},{7,6},{8,9},{9,8},{10,11... | collective-permute-start | bytes 4718600 | tf_op jit(solution)/shard_map/ppermute | solution.py:42
  75.6 1.0 copy-start.6
  76.6 14.2 %copy-start.8 = (bf16[16,64,128]{2,1,0:T(8,128)(2,1)S(1)}, bf16[16,64,128]{2,1,0:T(8,128)(2,1)}, u32[]{:S(2)}) copy-start(bf16[16,64,128]{2,1,0:T(8,128)(2,1)} %all_to_all.31) | copy-start | bytes 786436
  76.6 14.2 %copy-start.9 = (f32[8192]{0:T(1024)S(1)}, f32[8192]{0:T(1024)}, u32[]{:S(2)}) copy-start(f32[8192]{0:T(1024)} %param.13) | copy-start | bytes 98308
  81.2 0.8 copy-start.3
  82.0 55.9 %copy-start.10 = (f32[8192]{0:T(1024)S(1)}, f32[8192]{0:T(1024)}, u32[]{:S(2)}) copy-start(f32[8192]{0:T(1024)} %param.13) | copy-start | bytes 98308
  82.0 16.9 %collective-permute-start.6 = (bf16[512,512]{1,0:T(8,128)(2,1)}, bf16[512,512]{1,0:T(8,128)(2,1)S(1)}, u32[]{:S(2)}, u32[]{:S(2)}) collective-permute-start(bf16[512,512]{1,0:T(8,128)(2,1)} %get-tuple-element.37), channel_id=1, source_target_pairs={{0,4},{2,6},{4,0},{6,2},{1,5},{3,7},{5,1},{7,3},{8,12},{10,14},{12... | collective-permute-start | bytes 1572872 | tf_op jit(solution)/shard_map/ppermute | solution.py:42
  84.2 26.5 %collective-permute-start.7 = (bf16[512,512]{1,0:T(8,128)(2,1)}, bf16[512,512]{1,0:T(8,128)(2,1)S(1)}, u32[]{:S(2)}, u32[]{:S(2)}) collective-permute-start(bf16[512,512]{1,0:T(8,128)(2,1)} %get-tuple-element.38), channel_id=1, source_target_pairs={{0,2},{2,4},{4,6},{6,0},{1,3},{3,5},{5,7},{7,1},{8,10},{10,12},{12... | collective-permute-start | bytes 1572872 | tf_op jit(solution)/shard_map/ppermute | solution.py:42
  86.2 24.5 %collective-permute-start.8 = (bf16[512,512]{1,0:T(8,128)(2,1)}, bf16[512,512]{1,0:T(8,128)(2,1)S(1)}, u32[]{:S(2)}, u32[]{:S(2)}) collective-permute-start(bf16[512,512]{1,0:T(8,128)(2,1)} %get-tuple-element.39), channel_id=1, source_target_pairs={{0,6},{2,0},{4,2},{6,4},{1,7},{3,1},{5,3},{7,5},{8,14},{10,8},{12,... | collective-permute-start | bytes 1572872 | tf_op jit(solution)/shard_map/ppermute | solution.py:42
  92.3 19.8 %all-to-all-start.2 = ((bf16[16,64,128]{2,1,0:T(8,128)(2,1)}), bf16[16,64,128]{2,1,0:T(8,128)(2,1)S(1)}, u32[]{:S(2)}, u32[]{:S(2)}) async-start(bf16[16,64,128]{2,1,0:T(8,128)(2,1)} %broadcast_in_dim.24), calls=%async_computation.2 | async-start | bytes 524288 | tf_op jit(solution)/shard_map/all_to_all | solution.py:86
  130.1 17.2 %all-to-all-start.4 = ((f32[32,1,128]{2,1,0:T(1,128)}), f32[32,1,128]{2,1,0:T(1,128)S(1)}, u32[]{:S(2)}, u32[]{:S(2)}) async-start(f32[32,1,128]{2,1,0:T(1,128)} %bitcast.14), calls=%async_computation.4 | async-start | bytes 32768 | tf_op jit(solution)/shard_map/all_to_all | solution.py:86

commit v10 on v9

--- a/solution.py
+++ b/solution.py
@@ -24,17 +24,6 @@
 FSDP = ("y_hi", "x", "core")
 CHIPS = AXES["x"] * AXES["y_hi"]
 STEPS = (2, 1, 3)
-
-
-def encode(difference):
-    blocks = difference.reshape(-1, QBLOCK)
-    scales = (clip_ratio * jnp.sqrt(jnp.mean(blocks * blocks, axis=-1) + epsilon)).astype(
-        jnp.bfloat16
-    )
-    block_codes = jnp.clip(blocks / scales.astype(jnp.float32)[:, None], -1.0, 1.0).astype(
-        jnp.bfloat16
-    )
-    return (block_codes, scales)
 
 
 def send(value, axis, step):
@@ -57,12 +46,15 @@
             ).astype(jnp.bfloat16)
 
 
-def arrange(inputs, theirs, feature_gain):
-    tokens, features = inputs.shape
+def feature_order():
     x, core = lax.axis_index("x"), lax.axis_index("core")
     rx, y = jnp.arange(CHIPS) // AXES["y_hi"], jnp.arange(CHIPS) % AXES["y_hi"]
     chip = y * AXES["x"] + (x + rx) % AXES["x"]
-    order = (chip * 2 + core).astype(jnp.int32)
+    return (chip * 2 + core).astype(jnp.int32)
+
+
+def arrange(order, inputs, theirs, feature_gain):
+    tokens, features = inputs.shape
     step = 32
     block = pl.BlockSpec((step, features), lambda i: (i, 0))
     scaled = pl.pallas_call(
@@ -76,7 +68,7 @@
             pl.BlockSpec((1, features), lambda i: (0, 0)),
         ],
         out_specs=pl.BlockSpec((2, step, features // 2), lambda i: (0, i, 0)),
-        compiler_params=pltpu.CompilerParams(vmem_limit_bytes=VMEM_LIMIT),
+        compiler_params=pltpu.CompilerParams(vmem_limit_bytes=6 * VMEM_LIMIT),
         name="arrange",
     )(order, inputs, theirs, feature_gain[None, :])
     return scaled.reshape(2 * tokens, features // 2)
@@ -86,32 +78,72 @@
     return lax.all_to_all(parts, axis, split_axis=0, concat_axis=0, tiled=True)
 
 
-def spread(value, axis):
-    return exchange(jnp.broadcast_to(value[None], (lax.axis_size(axis), *value.shape)), axis)
+def copies_of(value, axis):
+    return jnp.broadcast_to(value[None], (lax.axis_size(axis), *value.shape))
 
 
 def total(values):
     return functools.reduce(jnp.add, [value.astype(jnp.float32) for value in values])
 
 
+def codes_kernel(global_ref, local_ref, decoded_ref):
+    difference = global_ref[...].astype(jnp.float32) - local_ref[...].astype(jnp.float32)
+    mean = jnp.mean(difference * difference, axis=-1, keepdims=True)
+    scales = (clip_ratio * jnp.sqrt(mean + epsilon)).astype(jnp.bfloat16).astype(jnp.float32)
+    codes = jnp.clip(difference / scales, -1.0, 1.0).astype(jnp.bfloat16)
+    decoded_ref[...] = (codes.astype(jnp.float32) * scales).astype(jnp.bfloat16)
+
+
 def fragment_codes(global_frag, local_frag):
-    difference = global_frag.astype(jnp.float32) - local_frag.astype(jnp.float32)
-    block_codes, scales = encode(difference)
-    decoded = block_codes.astype(jnp.float32) * scales.astype(jnp.float32)[:, None]
-    return decoded.astype(jnp.bfloat16).reshape(lax.axis_size(REPLICA), -1, QBLOCK)
-
-
-def fragment_update(arrived, global_frag, momentum):
+    step = min(256, global_frag.shape[0])
+    block = pl.BlockSpec((step, QBLOCK), lambda i: (i, 0))
+    return pl.pallas_call(
+        codes_kernel,
+        grid=(global_frag.shape[0] // step,),
+        out_shape=jax.ShapeDtypeStruct(global_frag.shape, jnp.bfloat16),
+        in_specs=[block, block],
+        out_specs=block,
+        compiler_params=pltpu.CompilerParams(vmem_limit_bytes=VMEM_LIMIT),
+        name="codes",
+    )(global_frag, local_frag)
+
+
+def update_kernel(replica_ref, arrived_ref, momentum_ref, global_ref, momentum_out, copies_ref):
+    replicas = arrived_ref.shape[0]
+    pseudo = total([arrived_ref[i] for i in range(replicas)]) / replicas
+    new_momentum = outer_decay * momentum_ref[...] + pseudo
+    momentum_out[...] = new_momentum
+    own_next = (
+        global_ref[...].astype(jnp.float32)
+        - outer_rate * (pseudo + outer_decay * new_momentum)
+    ).astype(jnp.bfloat16)
+    for i in range(replicas):
+        copies_ref[i] = own_next
+
+
+def fragment_update(replica, arrived, global_frag, momentum):
     replicas, rows = arrived.shape[:2]
-    share = rows * QBLOCK
-    pseudo = jnp.sum(arrived.astype(jnp.float32), axis=0) / replicas
-    new_momentum = outer_decay * momentum.reshape(rows, QBLOCK) + pseudo
-    offset = lax.axis_index(REPLICA) * share
-    own_global = lax.dynamic_slice_in_dim(global_frag, offset, share).reshape(rows, QBLOCK)
-    own_next = (
-        own_global.astype(jnp.float32) - outer_rate * (pseudo + outer_decay * new_momentum)
-    ).astype(jnp.bfloat16)
-    return spread(own_next, REPLICA).reshape(-1), new_momentum.reshape(-1)
+    shares = pl.BlockSpec((replicas, rows, QBLOCK), lambda i, replica: (0, 0, 0))
+    share = pl.BlockSpec((rows, QBLOCK), lambda i, replica: (0, 0))
+    return pl.pallas_call(
+        update_kernel,
+        grid_spec=pltpu.PrefetchScalarGridSpec(
+            num_scalar_prefetch=1,
+            grid=(1,),
+            in_specs=[
+                shares,
+                share,
+                pl.BlockSpec((rows, QBLOCK), lambda i, replica: (replica[0], 0)),
+            ],
+            out_specs=(share, shares),
+        ),
+        out_shape=(
+            jax.ShapeDtypeStruct((rows, QBLOCK), jnp.float32),
+            jax.ShapeDtypeStruct(arrived.shape, jnp.bfloat16),
+        ),
+        compiler_params=pltpu.CompilerParams(vmem_limit_bytes=VMEM_LIMIT),
+        name="update",
+    )(replica, arrived, momentum, global_frag)
 
 
 def in_vmem(shape, dtype):
@@ -221,28 +253,36 @@
 def shards(inputs, feature_gain, key_weight, teacher_keys, global_frag, local_frag, momentum):
     features = inputs.shape[2]
     rows, width = key_weight.shape[1:]
-
-    column = spread(key_weight[0], "y_hi").reshape(AXES["y_hi"] * rows, width)
+    replicas = lax.axis_size(REPLICA)
+    replica = lax.axis_index(REPLICA).astype(jnp.int32)[None]
+    global_frag = global_frag.reshape(-1, QBLOCK)
+    local_frag = local_frag[0].reshape(-1, QBLOCK)
+    momentum = momentum.reshape(-1, QBLOCK)
+    key_weight, order, replica = tied(key_weight, feature_order(), replica)
+
+    own, inputs, teacher_keys = tied(copies_of(key_weight[0], "y_hi"), inputs, teacher_keys)
+    column = exchange(own, "y_hi").reshape(AXES["y_hi"] * rows, width)
     raw = send(inputs[0], "core", 1)
-    their_targets = send(teacher_keys[0], "core", 1)
-    targets = (teacher_keys[0], their_targets)
-    scaled = arrange(inputs[0], raw, feature_gain)
-    column, scaled, targets, global_frag, local_frag = tied(
-        column, scaled, targets, global_frag, local_frag
+    targets = (teacher_keys[0], send(teacher_keys[0], "core", 1))
+    scaled = arrange(order, inputs[0], raw, feature_gain)
+    column, scaled, targets, global_frag, local_frag, replica = tied(
+        column, scaled, targets, global_frag, local_frag, replica
     )
     far = [column] + [send(column, "x", -k) for k in (1, 2, 3)]
-    arrived = exchange(fragment_codes(global_frag, local_frag[0]), REPLICA)
+    decoded = fragment_codes(global_frag, local_frag)
+    arrived = exchange(decoded.reshape(replicas, -1, QBLOCK), REPLICA)
     far, arrived = tied(far, arrived)
     partial = product(scaled, far)
     gradient = list(gradient_blocks(scaled, partial, send(partial, "core", 1), targets))
     gradient[0], arrived = tied(gradient[0], arrived)
-    new_global, new_momentum = fragment_update(arrived, global_frag, momentum)
+    new_momentum, copies = fragment_update(replica, arrived, global_frag, momentum)
+    new_global = exchange(copies, REPLICA)
     mine = total([gradient[0]] + [send(gradient[k], "x", k) for k in STEPS])
     mine, new_global = tied(mine.astype(jnp.bfloat16), new_global)
     gradient, squares = collect(exchange(mine.reshape(AXES["y_hi"], rows, width), "y_hi"))
 
     clipped_grad = clip(exchange(squares, FSDP), gradient, features * width)[None]
-    return (clipped_grad, new_global, new_momentum)
+    return (clipped_grad, new_global.reshape(-1), new_momentum.reshape(-1))
 
 
 def solution(mesh):

time: 150 us -> 144 us (0.960)
  waiting for transfers between devices: 29.4 us -> 23.4 us
  local copies, waits for them, and re-layouts: 11.2 us -> 5.79 us
  Pallas kernels: 12.6 us -> 16.8 us
  blocking collectives: 35.6 us -> 39.4 us
  other arithmetic: 7.4 us -> 4.52 us
    pallas_call x1, Pallas kernels: 1.99 us -> 7.29 us  [arrange(): pl.pallas_call(arrange_kernel, grid=(tokens // step,), out_shape=jax.Shap...]
    unnamed x23 -> x15, local copies, waits for them, and re-layouts: 8.66 us -> 4.04 us
    all_to_all x3, waiting for transfers between devices: 13.6 us -> 9.42 us  [exchange(): return lax.all_to_all(parts, axis, split_axis=0, concat_axis=0, tiled=True)]
    all_to_all x2, blocking collectives: 35.6 us -> 39.4 us  [exchange(): return lax.all_to_all(parts, axis, split_axis=0, concat_axis=0, tiled=True)]
    convert_element_type x4 -> x0, other arithmetic: 3.58 us -> none  [the longest x1 1.58 us: fragment_codes(): local_frag.astype(jnp.float32)]
    unnamed x0 -> x1, other arithmetic: none -> 3.19 us
    all_to_all x3, starting transfers between devices: 17.9 us -> 21.1 us  [exchange(): return lax.all_to_all(parts, axis, split_axis=0, concat_axis=0, tiled=True)]
    ppermute x9, starting transfers between devices: 33.6 us -> 31.6 us  [send(): lax.ppermute(value, axis, [(i, (i + step) % size) for i in range(size)])]
  transfers between devices with their start and end apart: 12 -> 12, of which waited for: 5 -> 5; matrix products, arithmetic and copies ran while one was open for 7% -> 3% of each run, Pallas kernels for 1% -> 6%
where the time goes in v10:
time: 144 us; the launch traced here: 143 us
  starting transfers between devices  52.6 us (37%)
  blocking collectives  39.4 us (27%)
  waiting for transfers between devices  23.4 us (16%)
  Pallas kernels  16.8 us (12%)
  local copies, waits for them, and re-layouts  5.79 us (4%)
  other arithmetic  4.52 us (3%)
    all_to_all x2, blocking collectives, exchange(): return lax.all_to_all(parts, axis, split_axis=0, concat_axis=0, tiled=True)  39.4 us
    ppermute x9, starting transfers between devices, send(): lax.ppermute(value, axis, [(i, (i + step) % size) for i in range(size)])  31.6 us
    all_to_all x3, starting transfers between devices, exchange(): return lax.all_to_all(parts, axis, split_axis=0, concat_axis=0, tiled=True)  21.1 us
    ppermute x9, waiting for transfers between devices, send(): lax.ppermute(value, axis, [(i, (i + step) % size) for i in range(size)])  14 us
    all_to_all x3, waiting for transfers between devices, exchange(): return lax.all_to_all(parts, axis, split_axis=0, concat_axis=0, tiled=True)  9.42 us
    pallas_call x1, Pallas kernels, arrange(): pl.pallas_call(arrange_kernel, grid=(tokens // step,), out_shape=jax.Shap...  7.29 us
    unnamed x15, local copies, waits for them, and re-layouts  4.04 us
    pallas_call x1, Pallas kernels, gradient_blocks(): pl.pallas_call(gradient_kernel, out_shape=(in_vmem(block, jnp.bfloat16),)...  3.67 us
  transfers between devices with their start and end apart: 12, of which 5 were waited for; matrix products, arithmetic and copies ran while one was open for 3% of the time, Pallas kernels for 6%

profile of v10, /device:TPU:1, one launch (start us, length us, event | category | flops | bytes accessed | tf_op | source)
XLA Modules:
  0.0 143.3 jit_solution(412591363968080317)
XLA Ops:
  0.7 1.7 %broadcast_in_dim.18 = bf16[4,128,512]{2,1,0:T(8,128)(2,1)} broadcast(bf16[128,512]{1,0:T(8,128)(2,1)} %bitcast.34), dimensions={1,2} | broadcast | bytes 655360 | tf_op jit(solution)/shard_map/broadcast_in_dim | solution.py:82
  2.4 8.8 %collective-permute-start = (bf16[384,4096]{1,0:T(8,128)(2,1)}, bf16[384,4096]{1,0:T(8,128)(2,1)S(1)}, u32[]{:S(2)}, u32[]{:S(2)}) collective-permute-start(bf16[384,4096]{1,0:T(8,128)(2,1)} %bitcast.30), channel_id=1, source_target_pairs={{0,1},{1,0},{2,3},{3,2},{4,5},{5,4},{6,7},{7,6},{8,9},{9,8},{10,11... | collective-permute-start | bytes 9437192 | tf_op jit(solution)/shard_map/ppermute | solution.py:31
  11.2 4.1 %all-to-all-start = ((bf16[4,128,512]{2,1,0:T(8,128)(2,1)}), bf16[4,128,512]{2,1,0:T(8,128)(2,1)}, u32[]{:S(2)}, u32[]{:S(2)}) async-start(bf16[4,128,512]{2,1,0:T(8,128)(2,1)} %broadcast_in_dim.18), calls=%async_computation | async-start | bytes 1048576 | tf_op jit(solution)/shard_map/all_to_all | solution.py:78
  15.3 1.9 %collective-permute-start.1 = (bf16[384,512]{1,0:T(8,128)(2,1)}, bf16[384,512]{1,0:T(8,128)(2,1)}, u32[]{:S(2)}, u32[]{:S(2)}) collective-permute-start(bf16[384,512]{1,0:T(8,128)(2,1)} %bitcast.25), channel_id=1, source_target_pairs={{0,1},{1,0},{2,3},{3,2},{4,5},{5,4},{6,7},{7,6},{8,9},{9,8},{10,11... | collective-permute-start | bytes 1179656 | tf_op jit(solution)/shard_map/ppermute | solution.py:31
  17.3 3.2 %reduce = bf16[131072]{0:T(1024)(128)(2,1)} reduce(bf16[1,131072]{1,0:T(2,128)(2,1)} %param.12, bf16[]{:T(256)} %constant.61), dimensions={0}, to_apply=%param.12.reduce_sub_computation | reduce | bytes 524290 | tf_op args[5]
  20.5 0.0 collective-permute-done.theirs_ref
  20.5 0.0 copy-start.6
  20.5 1.6 %copy-done.6 = bf16[384,4096]{1,0:T(8,128)(2,1)} copy-done((bf16[384,4096]{1,0:T(8,128)(2,1)}, bf16[384,4096]{1,0:T(8,128)(2,1)S(1)}, u32[]{:S(2)}) %copy-start.6) | copy-done | bytes 3145752
  22.1 0.0 copy-start.5
  22.1 0.7 copy-done.5
  22.8 0.0 copy-start
  22.8 7.3 %arrange.1 = bf16[2,384,2048]{2,1,0:T(8,128)(2,1)S(1)} custom-call(s32[16]{0:T(128)S(1)} %fusion.5.order_ref, bf16[384,4096]{1,0:T(8,128)(2,1)} %bitcast.31, bf16[384,4096]{1,0:T(8,128)(2,1)} %copy-done.6, f32[1,4096]{1,0:T(1,128)S(1)} %bitcast.29), custom_call_target="tpu_custom_call" | custom-call | tf_op jit(solution)/shard_map/arrange/pallas_call | solution.py:60
  30.1 0.0 collective-permute-done.1.refs_1_
  30.1 0.1 all-to-all-done
  30.2 1.9 %collective-permute-start.4 = (bf16[512,512]{1,0:T(8,128)(2,1)}, bf16[512,512]{1,0:T(8,128)(2,1)S(1)}, u32[]{:S(2)}, u32[]{:S(2)}) collective-permute-start(bf16[512,512]{1,0:T(8,128)(2,1)} %bitcast.2.refs_0_), channel_id=1, source_target_pairs={{0,2},{2,4},{4,6},{6,0},{1,3},{3,5},{5,7},{7,1},{8,10},{10,12},{12... | collective-permute-start | bytes 1572872 | tf_op jit(solution)/shard_map/ppermute | solution.py:31
  32.2 3.0 %collective-permute-start.3 = (bf16[512,512]{1,0:T(8,128)(2,1)}, bf16[512,512]{1,0:T(8,128)(2,1)S(1)}, u32[]{:S(2)}, u32[]{:S(2)}) collective-permute-start(bf16[512,512]{1,0:T(8,128)(2,1)} %bitcast.2.refs_0_), channel_id=1, source_target_pairs={{0,4},{2,6},{4,0},{6,2},{1,5},{3,7},{5,1},{7,3},{8,12},{10,14},{12... | collective-permute-start | bytes 1572872 | tf_op jit(solution)/shard_map/ppermute | solution.py:31
  35.2 3.5 %collective-permute-start.2 = (bf16[512,512]{1,0:T(8,128)(2,1)}, bf16[512,512]{1,0:T(8,128)(2,1)S(1)}, u32[]{:S(2)}, u32[]{:S(2)}) collective-permute-start(bf16[512,512]{1,0:T(8,128)(2,1)} %bitcast.2.refs_0_), channel_id=1, source_target_pairs={{0,6},{2,0},{4,2},{6,4},{1,7},{3,1},{5,3},{7,5},{8,14},{10,8},{12,... | collective-permute-start | bytes 1572872 | tf_op jit(solution)/shard_map/ppermute | solution.py:31
  38.7 0.0 copy-done
  38.7 0.0 copy-start.1
  38.7 0.9 copy-done.1
  39.6 0.7 codes.1
  40.3 18.5 %all_to_all.31.arrived_ref = bf16[16,64,128]{2,1,0:T(8,128)(2,1)S(1)} all-to-all(bf16[16,64,128]{2,1,0:T(8,128)(2,1)S(1)} %bitcast.23), channel_id=1, replica_groups=mesh['z'=8,'y_lo'=2,'y_hi'=4,'x'=4,'core'=2] {'z','y_lo'}, dimensions={0} | all-to-all | bytes 524288 | tf_op jit(solution)/shard_map/all_to_all | solution.py:78
  58.8 0.0 copy-start.3
  58.8 0.0 collective-permute-done.4.refs_3_
  58.8 0.0 collective-permute-done.3.refs_2_
  58.8 1.4 collective-permute-done.2.refs_1_
  60.2 2.8 %product.1.mine_ref = f32[768,512]{1,0:T(8,128)S(1)} custom-call(bf16[768,2048]{1,0:T(8,128)(2,1)S(1)} %bitcast.19, bf16[512,512]{1,0:T(8,128)(2,1)} %bitcast.2.refs_0_, bf16[512,512]{1,0:T(8,128)(2,1)S(1)} %collective-permute-done.2.refs_1_, bf16[512,512]{1,0:T(8,128)(2,1)S(1)} %collective-permute-done.3.refs_2_, ...), custom_call_target="tpu_custom_call" | custom-call | tf_op jit(solution)/shard_map/product/pallas_call | solution.py:169
  63.0 0.0 copy-start.4
  63.0 3.9 %collective-permute-start.5 = (f32[768,512]{1,0:T(8,128)S(1)}, f32[768,512]{1,0:T(8,128)S(1)}, u32[]{:S(2)}, u32[]{:S(2)}) collective-permute-start(f32[768,512]{1,0:T(8,128)S(1)} %product.1.mine_ref), channel_id=1, source_target_pairs={{0,1},{1,0},{2,3},{3,2},{4,5},{5,4},{6,7},{7,6},{8,9},{9,8},{10,11... | collective-permute-start | bytes 4718600 | tf_op jit(solution)/shard_map/ppermute | solution.py:31
  66.9 3.0 %collective-permute-done.5.theirs_ref = f32[768,512]{1,0:T(8,128)S(1)} collective-permute-done((f32[768,512]{1,0:T(8,128)S(1)}, f32[768,512]{1,0:T(8,128)S(1)}, u32[]{:S(2)}, u32[]{:S(2)}) %collective-permute-start.5) | collective-permute-done | bytes 1572896 | tf_op jit(solution)/shard_map/ppermute | solution.py:31
  70.0 0.0 copy-done.3
  70.0 3.7 %gradient.1 = (bf16[512,512]{1,0:T(8,128)(2,1)S(1)}, bf16[512,512]{1,0:T(8,128)(2,1)}, bf16[512,512]{1,0:T(8,128)(2,1)}, bf16[512,512]{1,0:T(8,128)(2,1)}) custom-call(bf16[768,2048]{1,0:T(8,128)(2,1)S(1)} %bitcast.20, f32[768,512]{1,0:T(8,128)S(1)} %product.1.mine_ref, f32[768,512]{1,0:T(8,128)S(1)} %collective-permute-done.5.theirs_ref, ...), custom_call_target="tpu_custom_call" | custom-call | tf_op jit(solution)/shard_map/gradient/pallas_call | solution.py:200
  73.6 0.0 copy-start.2
  73.6 2.1 %collective-permute-start.6 = (bf16[512,512]{1,0:T(8,128)(2,1)}, bf16[512,512]{1,0:T(8,128)(2,1)S(1)}, u32[]{:S(2)}, u32[]{:S(2)}) collective-permute-start(bf16[512,512]{1,0:T(8,128)(2,1)} %get-tuple-element.52), channel_id=1, source_target_pairs={{0,4},{2,6},{4,0},{6,2},{1,5},{3,7},{5,1},{7,3},{8,12},{10,14},{12... | collective-permute-start | bytes 1572872 | tf_op jit(solution)/shard_map/ppermute | solution.py:31
  75.8 4.1 %collective-permute-start.7 = (bf16[512,512]{1,0:T(8,128)(2,1)}, bf16[512,512]{1,0:T(8,128)(2,1)S(1)}, u32[]{:S(2)}, u32[]{:S(2)}) collective-permute-start(bf16[512,512]{1,0:T(8,128)(2,1)} %get-tuple-element.53), channel_id=1, source_target_pairs={{0,2},{2,4},{4,6},{6,0},{1,3},{3,5},{5,7},{7,1},{8,10},{10,12},{12... | collective-permute-start | bytes 1572872 | tf_op jit(solution)/shard_map/ppermute | solution.py:31
  79.9 2.4 %collective-permute-start.8 = (bf16[512,512]{1,0:T(8,128)(2,1)}, bf16[512,512]{1,0:T(8,128)(2,1)S(1)}, u32[]{:S(2)}, u32[]{:S(2)}) collective-permute-start(bf16[512,512]{1,0:T(8,128)(2,1)} %get-tuple-element.54), channel_id=1, source_target_pairs={{0,6},{2,0},{4,2},{6,4},{1,7},{3,1},{5,3},{7,5},{8,14},{10,8},{12,... | collective-permute-start | bytes 1572872 | tf_op jit(solution)/shard_map/ppermute | solution.py:31
  82.3 0.0 copy-done.4
  82.3 0.8 update.1
  83.1 0.0 copy-done.2
  83.1 9.7 %all-to-all-start.2 = ((bf16[16,64,128]{2,1,0:T(8,128)(2,1)}), bf16[16,64,128]{2,1,0:T(8,128)(2,1)S(1)}, u32[]{:S(2)}, u32[]{:S(2)}) async-start(bf16[16,64,128]{2,1,0:T(8,128)(2,1)} %get-tuple-element.57), calls=%async_computation.2 | async-start | bytes 524288 | tf_op jit(solution)/shard_map/all_to_all | solution.py:78
  92.8 0.0 collective-permute-done.6
  92.8 9.5 %collective-permute-done.7 = bf16[512,512]{1,0:T(8,128)(2,1)S(1)} collective-permute-done((bf16[512,512]{1,0:T(8,128)(2,1)}, bf16[512,512]{1,0:T(8,128)(2,1)S(1)}, u32[]{:S(2)}, u32[]{:S(2)}) %collective-permute-start.7) | collective-permute-done | bytes 524320 | tf_op jit(solution)/shard_map/ppermute | solution.py:31
  102.3 0.0 collective-permute-done.8
  102.3 1.3 add_convert_fusion
  103.6 0.0 all-to-all-done.2
  103.6 21.0 %all_to_all.32.arrived_ref = bf16[4,128,512]{2,1,0:T(8,128)(2,1)S(1)} all-to-all(bf16[4,128,512]{2,1,0:T(8,128)(2,1)S(1)} %bitcast.32), channel_id=1, replica_groups=mesh['z'=8,'y_lo'=2,'y_hi'=4,'x'=4,'core'=2] {'y_hi'}, dimensions={0} | all-to-all | bytes 1048576 | tf_op jit(solution)/shard_map/all_to_all | solution.py:78
  124.6 0.8 collect.1
  125.4 7.2 %all-to-all-start.4 = ((f32[32,1,128]{2,1,0:T(1,128)}), f32[32,1,128]{2,1,0:T(1,128)S(1)}, u32[]{:S(2)}, u32[]{:S(2)}) async-start(f32[32,1,128]{2,1,0:T(1,128)} %bitcast.12), calls=%async_computation.4 | async-start | bytes 32768 | tf_op jit(solution)/shard_map/all_to_all | solution.py:78
  132.6 9.3 %all-to-all-done.4 = f32[32,1,128]{2,1,0:T(1,128)S(1)} async-done(((f32[32,1,128]{2,1,0:T(1,128)}), f32[32,1,128]{2,1,0:T(1,128)S(1)}, u32[]{:S(2)}, u32[]{:S(2)}) %all-to-all-start.4) | async-done | bytes 16416 | tf_op jit(solution)/shard_map/all_to_all | solution.py:78
  141.9 0.7 clip.1
  142.6 0.7 copy.12
  (1 shorter events, 0.0 us)
Async XLA Ops:
  2.4 18.1 %collective-permute-start = (bf16[384,4096]{1,0:T(8,128)(2,1)}, bf16[384,4096]{1,0:T(8,128)(2,1)S(1)}, u32[]{:S(2)}, u32[]{:S(2)}) collective-permute-start(bf16[384,4096]{1,0:T(8,128)(2,1)} %bitcast.30), channel_id=1, source_target_pairs={{0,1},{1,0},{2,3},{3,2},{4,5},{5,4},{6,7},{7,6},{8,9},{9,8},{10,11... | collective-permute-start | bytes 9437192 | tf_op jit(solution)/shard_map/ppermute | solution.py:31
  11.2 19.1 %all-to-all-start = ((bf16[4,128,512]{2,1,0:T(8,128)(2,1)}), bf16[4,128,512]{2,1,0:T(8,128)(2,1)}, u32[]{:S(2)}, u32[]{:S(2)}) async-start(bf16[4,128,512]{2,1,0:T(8,128)(2,1)} %broadcast_in_dim.18), calls=%async_computation | async-start | bytes 1048576 | tf_op jit(solution)/shard_map/all_to_all | solution.py:78
  15.3 14.8 %collective-permute-start.1 = (bf16[384,512]{1,0:T(8,128)(2,1)}, bf16[384,512]{1,0:T(8,128)(2,1)}, u32[]{:S(2)}, u32[]{:S(2)}) collective-permute-start(bf16[384,512]{1,0:T(8,128)(2,1)} %bitcast.25), channel_id=1, source_target_pairs={{0,1},{1,0},{2,3},{3,2},{4,5},{5,4},{6,7},{7,6},{8,9},{9,8},{10,11... | collective-permute-start | bytes 1179656 | tf_op jit(solution)/shard_map/ppermute | solution.py:31
  20.5 1.6 %copy-start.6 = (bf16[384,4096]{1,0:T(8,128)(2,1)}, bf16[384,4096]{1,0:T(8,128)(2,1)S(1)}, u32[]{:S(2)}) copy-start(bf16[384,4096]{1,0:T(8,128)(2,1)S(1)} %collective-permute-done.theirs_ref) | copy-start | bytes 9437188
  22.1 0.7 copy-start.5
  22.8 15.8 %copy-start = (bf16[131072]{0:T(1024)(128)(2,1)S(1)}, bf16[131072]{0:T(1024)(128)(2,1)}, u32[]{:S(2)}) copy-start(bf16[131072]{0:T(1024)(128)(2,1)} %param.11) | copy-start | bytes 786436
  30.2 28.6 %collective-permute-start.4 = (bf16[512,512]{1,0:T(8,128)(2,1)}, bf16[512,512]{1,0:T(8,128)(2,1)S(1)}, u32[]{:S(2)}, u32[]{:S(2)}) collective-permute-start(bf16[512,512]{1,0:T(8,128)(2,1)} %bitcast.2.refs_0_), channel_id=1, source_target_pairs={{0,2},{2,4},{4,6},{6,0},{1,3},{3,5},{5,7},{7,1},{8,10},{10,12},{12... | collective-permute-start | bytes 1572872 | tf_op jit(solution)/shard_map/ppermute | solution.py:31
  32.2 26.6 %collective-permute-start.3 = (bf16[512,512]{1,0:T(8,128)(2,1)}, bf16[512,512]{1,0:T(8,128)(2,1)S(1)}, u32[]{:S(2)}, u32[]{:S(2)}) collective-permute-start(bf16[512,512]{1,0:T(8,128)(2,1)} %bitcast.2.refs_0_), channel_id=1, source_target_pairs={{0,4},{2,6},{4,0},{6,2},{1,5},{3,7},{5,1},{7,3},{8,12},{10,14},{12... | collective-permute-start | bytes 1572872 | tf_op jit(solution)/shard_map/ppermute | solution.py:31
  35.2 25.0 %collective-permute-start.2 = (bf16[512,512]{1,0:T(8,128)(2,1)}, bf16[512,512]{1,0:T(8,128)(2,1)S(1)}, u32[]{:S(2)}, u32[]{:S(2)}) collective-permute-start(bf16[512,512]{1,0:T(8,128)(2,1)} %bitcast.2.refs_0_), channel_id=1, source_target_pairs={{0,6},{2,0},{4,2},{6,4},{1,7},{3,1},{5,3},{7,5},{8,14},{10,8},{12,... | collective-permute-start | bytes 1572872 | tf_op jit(solution)/shard_map/ppermute | solution.py:31
  38.7 1.0 copy-start.1
  58.8 11.2 %copy-start.3 = (bf16[1,384,512]{2,1,0:T(8,128)(2,1)S(1)}, bf16[1,384,512]{2,1,0:T(8,128)(2,1)}, u32[]{:S(2)}) copy-start(bf16[1,384,512]{2,1,0:T(8,128)(2,1)} %param.10) | copy-start | bytes 1179652
  63.0 19.2 %copy-start.4 = (f32[8192]{0:T(1024)S(1)}, f32[8192]{0:T(1024)}, u32[]{:S(2)}) copy-start(f32[8192]{0:T(1024)} %param.13) | copy-start | bytes 98308
  63.0 6.9 %collective-permute-start.5 = (f32[768,512]{1,0:T(8,128)S(1)}, f32[768,512]{1,0:T(8,128)S(1)}, u32[]{:S(2)}, u32[]{:S(2)}) collective-permute-start(f32[768,512]{1,0:T(8,128)S(1)} %product.1.mine_ref), channel_id=1, source_target_pairs={{0,1},{1,0},{2,3},{3,2},{4,5},{5,4},{6,7},{7,6},{8,9},{9,8},{10,11... | collective-permute-start | bytes 4718600 | tf_op jit(solution)/shard_map/ppermute | solution.py:31
  73.6 9.4 %copy-start.2 = (bf16[512,512]{1,0:T(8,128)(2,1)}, bf16[512,512]{1,0:T(8,128)(2,1)S(1)}, u32[]{:S(2)}) copy-start(bf16[512,512]{1,0:T(8,128)(2,1)S(1)} %get-tuple-element.51) | copy-start | bytes 1572868
  73.6 19.1 %collective-permute-start.6 = (bf16[512,512]{1,0:T(8,128)(2,1)}, bf16[512,512]{1,0:T(8,128)(2,1)S(1)}, u32[]{:S(2)}, u32[]{:S(2)}) collective-permute-start(bf16[512,512]{1,0:T(8,128)(2,1)} %get-tuple-element.52), channel_id=1, source_target_pairs={{0,4},{2,6},{4,0},{6,2},{1,5},{3,7},{5,1},{7,3},{8,12},{10,14},{12... | collective-permute-start | bytes 1572872 | tf_op jit(solution)/shard_map/ppermute | solution.py:31
  75.8 26.6 %collective-permute-start.7 = (bf16[512,512]{1,0:T(8,128)(2,1)}, bf16[512,512]{1,0:T(8,128)(2,1)S(1)}, u32[]{:S(2)}, u32[]{:S(2)}) collective-permute-start(bf16[512,512]{1,0:T(8,128)(2,1)} %get-tuple-element.53), channel_id=1, source_target_pairs={{0,2},{2,4},{4,6},{6,0},{1,3},{3,5},{5,7},{7,1},{8,10},{10,12},{12... | collective-permute-start | bytes 1572872 | tf_op jit(solution)/shard_map/ppermute | solution.py:31
  79.9 22.5 %collective-permute-start.8 = (bf16[512,512]{1,0:T(8,128)(2,1)}, bf16[512,512]{1,0:T(8,128)(2,1)S(1)}, u32[]{:S(2)}, u32[]{:S(2)}) collective-permute-start(bf16[512,512]{1,0:T(8,128)(2,1)} %get-tuple-element.54), channel_id=1, source_target_pairs={{0,6},{2,0},{4,2},{6,4},{1,7},{3,1},{5,3},{7,5},{8,14},{10,8},{12,... | collective-permute-start | bytes 1572872 | tf_op jit(solution)/shard_map/ppermute | solution.py:31
  83.1 20.6 %all-to-all-start.2 = ((bf16[16,64,128]{2,1,0:T(8,128)(2,1)}), bf16[16,64,128]{2,1,0:T(8,128)(2,1)S(1)}, u32[]{:S(2)}, u32[]{:S(2)}) async-start(bf16[16,64,128]{2,1,0:T(8,128)(2,1)} %get-tuple-element.57), calls=%async_computation.2 | async-start | bytes 524288 | tf_op jit(solution)/shard_map/all_to_all | solution.py:78
  125.4 16.5 %all-to-all-start.4 = ((f32[32,1,128]{2,1,0:T(1,128)}), f32[32,1,128]{2,1,0:T(1,128)S(1)}, u32[]{:S(2)}, u32[]{:S(2)}) async-start(f32[32,1,128]{2,1,0:T(1,128)} %bitcast.12), calls=%async_computation.4 | async-start | bytes 32768 | tf_op jit(solution)/shard_map/all_to_all | solution.py:78

commit v11 on v10

--- a/solution.py
+++ b/solution.py
@@ -26,9 +26,22 @@
 STEPS = (2, 1, 3)
 
 
-def send(value, axis, step):
-    size = AXES[axis]
-    return lax.ppermute(value, axis, [(i, (i + step) % size) for i in range(size)])
+def swap(value):
+    return lax.ppermute(value, "core", [(0, 1), (1, 0)])
+
+
+def send(value, wide, step):
+    pairs = []
+    for y in range(AXES["y_hi"]):
+        for x in range(AXES["x"]):
+            for core in range(AXES["core"]):
+                to_y, to_x = y, x
+                if (core == 0) == wide:
+                    to_x = (x + step) % AXES["x"]
+                else:
+                    to_y = (y + step) % AXES["y_hi"]
+                pairs.append(((y * AXES["x"] + x) * 2 + core, (to_y * AXES["x"] + to_x) * 2 + core))
+    return lax.ppermute(value, FSDP, pairs)
 
 
 def tied(*values):
@@ -47,15 +60,16 @@
 
 
 def feature_order():
-    x, core = lax.axis_index("x"), lax.axis_index("core")
-    rx, y = jnp.arange(CHIPS) // AXES["y_hi"], jnp.arange(CHIPS) % AXES["y_hi"]
-    chip = y * AXES["x"] + (x + rx) % AXES["x"]
-    return (chip * 2 + core).astype(jnp.int32)
+    y, x, core = (lax.axis_index(name) for name in FSDP)
+    wide, narrow = jnp.arange(CHIPS) // 4, jnp.arange(CHIPS) % 4
+    to_y = (y + jnp.where(core == 0, narrow, wide)) % AXES["y_hi"]
+    to_x = (x + jnp.where(core == 0, wide, narrow)) % AXES["x"]
+    return ((to_y * AXES["x"] + to_x) * 2 + core).astype(jnp.int32)
 
 
 def arrange(order, inputs, theirs, feature_gain):
     tokens, features = inputs.shape
-    step = 32
+    step = 96
     block = pl.BlockSpec((step, features), lambda i: (i, 0))
     scaled = pl.pallas_call(
         arrange_kernel,
@@ -68,7 +82,7 @@
             pl.BlockSpec((1, features), lambda i: (0, 0)),
         ],
         out_specs=pl.BlockSpec((2, step, features // 2), lambda i: (0, i, 0)),
-        compiler_params=pltpu.CompilerParams(vmem_limit_bytes=6 * VMEM_LIMIT),
+        compiler_params=pltpu.CompilerParams(vmem_limit_bytes=3 * VMEM_LIMIT),
         name="arrange",
     )(order, inputs, theirs, feature_gain[None, :])
     return scaled.reshape(2 * tokens, features // 2)
@@ -76,10 +90,6 @@
 
 def exchange(parts, axis):
     return lax.all_to_all(parts, axis, split_axis=0, concat_axis=0, tiled=True)
-
-
-def copies_of(value, axis):
-    return jnp.broadcast_to(value[None], (lax.axis_size(axis), *value.shape))
 
 
 def total(values):
@@ -208,8 +218,46 @@
     )(scaled, mine, theirs, *targets)
 
 
-def collect_kernel(arrived_ref, gradient_ref, squares_ref):
-    gradient = total([arrived_ref[k] for k in range(arrived_ref.shape[0])])
+def join_kernel(*refs):
+    *part_refs, joined_ref = refs
+    rows = part_refs[0].shape[0]
+    for k, ref in enumerate(part_refs):
+        joined_ref[k * rows : (k + 1) * rows, :] = ref[...]
+
+
+def join(parts):
+    rows, width = parts[0].shape
+    return pl.pallas_call(
+        join_kernel,
+        out_shape=in_vmem((len(parts) * rows, width), parts[0].dtype),
+        in_specs=[WHOLE] * len(parts),
+        out_specs=WHOLE,
+        compiler_params=pltpu.CompilerParams(vmem_limit_bytes=VMEM_LIMIT),
+        name="join",
+    )(*parts)
+
+
+def add_kernel(first, second, third, fourth, *out_refs):
+    rows = out_refs[0].shape[0]
+    for k, ref in enumerate(out_refs):
+        here = slice(k * rows, (k + 1) * rows)
+        ref[...] = total([r[here, :] for r in (first, second, third, fourth)]).astype(jnp.bfloat16)
+
+
+def add(blocks):
+    rows, width = blocks[0].shape
+    return pl.pallas_call(
+        add_kernel,
+        out_shape=(in_vmem((rows // 4, width), jnp.bfloat16),) * 4,
+        in_specs=[WHOLE] * 4,
+        out_specs=(WHOLE,) * 4,
+        compiler_params=pltpu.CompilerParams(vmem_limit_bytes=VMEM_LIMIT),
+        name="add",
+    )(*blocks)
+
+
+def collect_kernel(first, second, third, fourth, gradient_ref, squares_ref):
+    gradient = total([ref[...] for ref in (first, second, third, fourth)])
     gradient_ref[...] = gradient
     squares = jnp.sum(gradient * gradient, axis=0, keepdims=True)
     squares_ref[...] = jnp.broadcast_to(
@@ -217,18 +265,18 @@
     )
 
 
-def collect(arrived):
+def collect(blocks):
     return pl.pallas_call(
         collect_kernel,
         out_shape=(
-            jax.ShapeDtypeStruct(arrived.shape[1:], jnp.float32),
+            jax.ShapeDtypeStruct(blocks[0].shape, jnp.float32),
             jax.ShapeDtypeStruct((CHIPS * AXES["core"], LANES), jnp.float32),
         ),
-        in_specs=[WHOLE],
+        in_specs=[WHOLE] * 4,
         out_specs=(WHOLE, WHOLE),
         compiler_params=pltpu.CompilerParams(vmem_limit_bytes=VMEM_LIMIT),
         name="collect",
-    )(arrived)
+    )(*blocks)
 
 
 def clip_kernel(entries, squares_ref, gradient_ref, clipped_ref):
@@ -260,26 +308,27 @@
     momentum = momentum.reshape(-1, QBLOCK)
     key_weight, order, replica = tied(key_weight, feature_order(), replica)
 
-    own, inputs, teacher_keys = tied(copies_of(key_weight[0], "y_hi"), inputs, teacher_keys)
-    column = exchange(own, "y_hi").reshape(AXES["y_hi"] * rows, width)
-    raw = send(inputs[0], "core", 1)
-    targets = (teacher_keys[0], send(teacher_keys[0], "core", 1))
+    weight = key_weight[0]
+    column = join([weight] + [send(weight, False, -k) for k in (1, 2, 3)])
+    raw = swap(inputs[0])
+    targets = (teacher_keys[0], swap(teacher_keys[0]))
+    column, targets, global_frag, local_frag, replica = tied(
+        column, targets, global_frag, local_frag, replica
+    )
+    far = [column] + [send(column, True, -k) for k in (1, 2, 3)]
+    decoded = fragment_codes(global_frag, local_frag)
     scaled = arrange(order, inputs[0], raw, feature_gain)
-    column, scaled, targets, global_frag, local_frag, replica = tied(
-        column, scaled, targets, global_frag, local_frag, replica
-    )
-    far = [column] + [send(column, "x", -k) for k in (1, 2, 3)]
-    decoded = fragment_codes(global_frag, local_frag)
+    decoded, scaled = tied(decoded, scaled)
     arrived = exchange(decoded.reshape(replicas, -1, QBLOCK), REPLICA)
     far, arrived = tied(far, arrived)
     partial = product(scaled, far)
-    gradient = list(gradient_blocks(scaled, partial, send(partial, "core", 1), targets))
+    gradient = list(gradient_blocks(scaled, partial, swap(partial), targets))
     gradient[0], arrived = tied(gradient[0], arrived)
     new_momentum, copies = fragment_update(replica, arrived, global_frag, momentum)
     new_global = exchange(copies, REPLICA)
-    mine = total([gradient[0]] + [send(gradient[k], "x", k) for k in STEPS])
-    mine, new_global = tied(mine.astype(jnp.bfloat16), new_global)
-    gradient, squares = collect(exchange(mine.reshape(AXES["y_hi"], rows, width), "y_hi"))
+    mine = add([gradient[0]] + [send(gradient[k], True, k) for k in STEPS])
+    mine, new_global = tied(mine, new_global)
+    gradient, squares = collect([mine[0]] + [send(mine[k], False, k) for k in STEPS])
 
     clipped_grad = clip(exchange(squares, FSDP), gradient, features * width)[None]
     return (clipped_grad, new_global.reshape(-1), new_momentum.reshape(-1))

time: 144 us -> 151 us (1.049)
  blocking collectives: 39.4 us -> 0 us
  starting transfers between devices: 52.6 us -> 78.4 us
  waiting for transfers between devices: 23.4 us -> 43.1 us
  local copies, waits for them, and re-layouts: 5.79 us -> 9.76 us
  other arithmetic: 4.52 us -> 2.51 us
  Pallas kernels: 16.8 us -> 14.9 us
    all_to_all x2 -> x0, blocking collectives: 39.4 us -> none  [exchange(): return lax.all_to_all(parts, axis, split_axis=0, concat_axis=0, tiled=True)]
    ppermute x9 -> x15, starting transfers between devices: 31.6 us -> 58.1 us  [the longest x12 39.3 us: send(): return lax.ppermute(value, FSDP, pairs)]
    all_to_all x3, waiting for transfers between devices: 9.42 us -> 19.3 us  [exchange(): return lax.all_to_all(parts, axis, split_axis=0, concat_axis=0, tiled=True)]
    ppermute x9 -> x15, waiting for transfers between devices: 14 us -> 23.8 us  [the longest x12 20.8 us: send(): return lax.ppermute(value, FSDP, pairs)]
    unnamed x15 -> x23, local copies, waits for them, and re-layouts: 4.04 us -> 9.76 us
    pallas_call x1, Pallas kernels: 7.29 us -> 1.74 us  [arrange(): pl.pallas_call(arrange_kernel, grid=(tokens // step,), out_shape=jax.Shap...]
    pallas_call x1 -> x3, Pallas kernels: 0.8 us -> 2.86 us  [the longest x1 1.8 us: join(): pl.pallas_call(join_kernel, out_shape=in_vmem((len(parts) * rows, width),...]
    broadcast_in_dim x1 -> x0, local copies, waits for them, and re-layouts: 1.74 us -> none  [copies_of(): return jnp.broadcast_to(value[None], (lax.axis_size(axis), *value.shape))]
  transfers between devices with their start and end apart: 12 -> 18, of which waited for: 5 -> 10; matrix products, arithmetic and copies ran while one was open for 3% -> 2% of each run, Pallas kernels for 6% -> 4%
where the time goes in v11:
time: 151 us; the launch traced here: 150 us
  starting transfers between devices  78.4 us (52%)
  waiting for transfers between devices  43.1 us (29%)
  Pallas kernels  14.9 us (10%)
  local copies, waits for them, and re-layouts  9.76 us (6%)
  other arithmetic  2.51 us (2%)
    ppermute x12, starting transfers between devices, send(): return lax.ppermute(value, FSDP, pairs)  39.3 us
    ppermute x12, waiting for transfers between devices, send(): return lax.ppermute(value, FSDP, pairs)  20.8 us
    all_to_all x3, starting transfers between devices, exchange(): return lax.all_to_all(parts, axis, split_axis=0, concat_axis=0, tiled=True)  20.3 us
    all_to_all x3, waiting for transfers between devices, exchange(): return lax.all_to_all(parts, axis, split_axis=0, concat_axis=0, tiled=True)  19.3 us
    ppermute x3, starting transfers between devices, swap(): return lax.ppermute(value, 'core', [(0, 1), (1, 0)])  18.8 us
    unnamed x23, local copies, waits for them, and re-layouts  9.76 us
    pallas_call x1, Pallas kernels, gradient_blocks(): pl.pallas_call(gradient_kernel, out_shape=(in_vmem(block, jnp.bfloat16),)...  3.67 us
    pallas_call x1, Pallas kernels, product(): pl.pallas_call(product_kernel, out_shape=in_vmem((scaled.shape[0], weight...  3.35 us
  transfers between devices with their start and end apart: 18, of which 10 were waited for; matrix products, arithmetic and copies ran while one was open for 2% of the time, Pallas kernels for 4%

profile of v11, /device:TPU:1, one launch (start us, length us, event | category | flops | bytes accessed | tf_op | source)
XLA Modules:
  0.0 149.6 jit_solution(5401129286834410542)
XLA Ops:
  0.6 8.8 %collective-permute-start.4 = (bf16[384,4096]{1,0:T(8,128)(2,1)}, bf16[384,4096]{1,0:T(8,128)(2,1)S(1)}, u32[]{:S(2)}, u32[]{:S(2)}) collective-permute-start(bf16[384,4096]{1,0:T(8,128)(2,1)} %bitcast.19), channel_id=1, source_target_pairs={{0,1},{1,0},{2,3},{3,2},{4,5},{5,4},{6,7},{7,6},{8,9},{9,8},{10,11... | collective-permute-start | bytes 9437192 | tf_op jit(solution)/shard_map/ppermute | solution.py:30
  9.4 1.9 %collective-permute-start.3 = (bf16[384,512]{1,0:T(8,128)(2,1)}, bf16[384,512]{1,0:T(8,128)(2,1)}, u32[]{:S(2)}, u32[]{:S(2)}) collective-permute-start(bf16[384,512]{1,0:T(8,128)(2,1)} %bitcast.24), channel_id=1, source_target_pairs={{0,1},{1,0},{2,3},{3,2},{4,5},{5,4},{6,7},{7,6},{8,9},{9,8},{10,11... | collective-permute-start | bytes 1179656 | tf_op jit(solution)/shard_map/ppermute | solution.py:30
  11.4 1.9 %collective-permute-start = (bf16[128,512]{1,0:T(8,128)(2,1)}, bf16[128,512]{1,0:T(8,128)(2,1)S(1)}, u32[]{:S(2)}, u32[]{:S(2)}) collective-permute-start(bf16[128,512]{1,0:T(8,128)(2,1)} %bitcast.26), channel_id=1, source_target_pairs={{0,24},{1,7},{2,26},{3,1},{4,28},{5,3},{6,30},{7,5},{8,0},{9,15},{... | collective-permute-start | bytes 393224 | tf_op jit(solution)/shard_map/ppermute | solution.py:44
  13.3 1.9 %collective-permute-start.1 = (bf16[128,512]{1,0:T(8,128)(2,1)}, bf16[128,512]{1,0:T(8,128)(2,1)}, u32[]{:S(2)}, u32[]{:S(2)}) collective-permute-start(bf16[128,512]{1,0:T(8,128)(2,1)} %bitcast.27), channel_id=1, source_target_pairs={{0,16},{1,5},{2,18},{3,7},{4,20},{5,1},{6,22},{7,3},{8,24},{9,13},... | collective-permute-start | bytes 393224 | tf_op jit(solution)/shard_map/ppermute | solution.py:44
  15.3 3.4 %collective-permute-start.2 = (bf16[128,512]{1,0:T(8,128)(2,1)}, bf16[128,512]{1,0:T(8,128)(2,1)}, u32[]{:S(2)}, u32[]{:S(2)}) collective-permute-start(bf16[128,512]{1,0:T(8,128)(2,1)} %bitcast.28), channel_id=1, source_target_pairs={{0,8},{1,3},{2,10},{3,5},{4,12},{5,7},{6,14},{7,1},{8,16},{9,11},{... | collective-permute-start | bytes 393224 | tf_op jit(solution)/shard_map/ppermute | solution.py:44
  18.6 2.5 %reduce = bf16[131072]{0:T(1024)(128)(2,1)S(1)} reduce(bf16[1,131072]{1,0:T(2,128)(2,1)} %param.12, bf16[]{:T(256)} %constant.69), dimensions={0}, to_apply=%param.12.reduce_sub_computation | reduce | bytes 524290 | tf_op args[5]
  21.1 0.0 collective-permute-done.refs_1_
  21.1 0.0 collective-permute-done.1.refs_2_
  21.1 2.8 %collective-permute-done.2.refs_3_ = bf16[128,512]{1,0:T(8,128)(2,1)} collective-permute-done((bf16[128,512]{1,0:T(8,128)(2,1)}, bf16[128,512]{1,0:T(8,128)(2,1)}, u32[]{:S(2)}, u32[]{:S(2)}) %collective-permute-start.2) | collective-permute-done | bytes 131104 | tf_op jit(solution)/shard_map/ppermute | solution.py:44
  24.0 0.0 copy-start.8
  24.0 0.9 copy-done.8
  24.9 1.8 %join.1.refs_0_ = bf16[512,512]{1,0:T(8,128)(2,1)} custom-call(bf16[128,512]{1,0:T(8,128)(2,1)S(1)} %bitcast.29, bf16[128,512]{1,0:T(8,128)(2,1)S(1)} %collective-permute-done.refs_1_, bf16[128,512]{1,0:T(8,128)(2,1)} %collective-permute-done.1.refs_2_, bf16[128,512]{1,0:T(8,128)(2,1)} %collective-permute-done.2.refs_3_), custom_call_target="tpu_custom_call" | custom-call | tf_op jit(solution)/shard_map/join/pallas_call | solution.py:230
  26.7 0.0 collective-permute-done.3.refs_1_
  26.7 2.3 %collective-permute-start.5 = (bf16[512,512]{1,0:T(8,128)(2,1)}, bf16[512,512]{1,0:T(8,128)(2,1)}, u32[]{:S(2)}, u32[]{:S(2)}) collective-permute-start(bf16[512,512]{1,0:T(8,128)(2,1)} %join.1.refs_0_), channel_id=1, source_target_pairs={{0,6},{1,25},{2,0},{3,27},{4,2},{5,29},{6,4},{7,31},{8,14},{9,1},{... | collective-permute-start | bytes 1572872 | tf_op jit(solution)/shard_map/ppermute | solution.py:44
  29.0 3.2 %collective-permute-start.6 = (bf16[512,512]{1,0:T(8,128)(2,1)}, bf16[512,512]{1,0:T(8,128)(2,1)}, u32[]{:S(2)}, u32[]{:S(2)}) collective-permute-start(bf16[512,512]{1,0:T(8,128)(2,1)} %join.1.refs_0_), channel_id=1, source_target_pairs={{0,4},{1,17},{2,6},{3,19},{4,0},{5,21},{6,2},{7,23},{8,12},{9,25},... | collective-permute-start | bytes 1572872 | tf_op jit(solution)/shard_map/ppermute | solution.py:44
  32.2 4.2 %collective-permute-start.7 = (bf16[512,512]{1,0:T(8,128)(2,1)}, bf16[512,512]{1,0:T(8,128)(2,1)}, u32[]{:S(2)}, u32[]{:S(2)}) collective-permute-start(bf16[512,512]{1,0:T(8,128)(2,1)} %join.1.refs_0_), channel_id=1, source_target_pairs={{0,2},{1,9},{2,4},{3,11},{4,6},{5,13},{6,0},{7,15},{8,10},{9,17},{... | collective-permute-start | bytes 1572872 | tf_op jit(solution)/shard_map/ppermute | solution.py:44
  36.5 0.0 copy-start.3
  36.5 0.9 copy-done.3
  37.4 1.8 %codes.1 = bf16[1024,128]{1,0:T(8,128)(2,1)} custom-call(bf16[1024,128]{1,0:T(8,128)(2,1)S(1)} %bitcast.21, bf16[1024,128]{1,0:T(8,128)(2,1)S(1)} %bitcast.23), custom_call_target="tpu_custom_call" | custom-call | tf_op jit(solution)/shard_map/codes/pallas_call | solution.py:110
  39.2 0.0 collective-permute-done.4.theirs_ref
  39.2 0.0 copy-start.1
  39.2 1.6 %copy-done.1 = bf16[384,4096]{1,0:T(8,128)(2,1)} copy-done((bf16[384,4096]{1,0:T(8,128)(2,1)}, bf16[384,4096]{1,0:T(8,128)(2,1)S(1)}, u32[]{:S(2)}) %copy-start.1) | copy-done | bytes 3145752
  40.8 1.9 %copy-done = bf16[1,384,4096]{2,1,0:T(8,128)(2,1)S(1)} copy-done((bf16[1,384,4096]{2,1,0:T(8,128)(2,1)S(1)}, bf16[1,384,4096]{2,1,0:T(8,128)(2,1)}, u32[]{:S(2)}) %copy-start) | copy-done | bytes 3145752
  42.7 1.9 %copy-done.2 = bf16[384,4096]{1,0:T(8,128)(2,1)S(1)} copy-done((bf16[384,4096]{1,0:T(8,128)(2,1)S(1)}, bf16[384,4096]{1,0:T(8,128)(2,1)}, u32[]{:S(2)}) %copy-start.2) | copy-done | bytes 3145752
  44.6 0.7 copy-done.10
  45.3 1.7 %arrange.1 = bf16[2,384,2048]{2,1,0:T(8,128)(2,1)S(1)} custom-call(s32[16]{0:T(128)S(1)} %multiply_add_fusion.order_ref, bf16[384,4096]{1,0:T(8,128)(2,1)S(1)} %bitcast.20, bf16[384,4096]{1,0:T(8,128)(2,1)S(1)} %copy-done.2, f32[1,4096]{1,0:T(1,128)S(1)} %bitcast.32), custom_call_target="tpu_custom_call" | custom-call | tf_op jit(solution)/shard_map/arrange/pallas_call | solution.py:74
  47.1 10.6 %all-to-all-start = ((bf16[16,64,128]{2,1,0:T(8,128)(2,1)}), bf16[16,64,128]{2,1,0:T(8,128)(2,1)S(1)}, u32[]{:S(2)}, u32[]{:S(2)}) async-start(bf16[16,64,128]{2,1,0:T(8,128)(2,1)} %bitcast.7), calls=%async_computation | async-start | bytes 524288 | tf_op jit(solution)/shard_map/all_to_all | solution.py:92
  57.6 0.0 collective-permute-done.5.refs_1_
  57.6 0.0 collective-permute-done.6.refs_2_
  57.7 0.0 collective-permute-done.7.refs_3_
  57.7 8.5 %all-to-all-done.arrived_ref = bf16[16,64,128]{2,1,0:T(8,128)(2,1)S(1)} async-done(((bf16[16,64,128]{2,1,0:T(8,128)(2,1)}), bf16[16,64,128]{2,1,0:T(8,128)(2,1)S(1)}, u32[]{:S(2)}, u32[]{:S(2)}) %all-to-all-start) | async-done | bytes 262176 | tf_op jit(solution)/shard_map/all_to_all | solution.py:92
  66.2 0.0 copy-start.7
  66.2 3.3 %product.1.mine_ref = f32[768,512]{1,0:T(8,128)S(1)} custom-call(bf16[768,2048]{1,0:T(8,128)(2,1)S(1)} %bitcast.17, bf16[512,512]{1,0:T(8,128)(2,1)} %join.1.refs_0_, bf16[512,512]{1,0:T(8,128)(2,1)} %collective-permute-done.5.refs_1_, bf16[512,512]{1,0:T(8,128)(2,1)} %collective-permute-done.6.refs_2_, bf16[512,512]{1,0:T(8,128)(2,1)} %collective-permute-done.7.refs_3_), custom_call_target="tpu_custom_call" | custom-call | tf_op jit(solution)/shard_map/product/pallas_call | solution.py:179
  69.6 0.0 copy-start.4
  69.6 0.0 copy-start.9
  69.6 8.1 %collective-permute-start.8 = (f32[768,512]{1,0:T(8,128)S(1)}, f32[768,512]{1,0:T(8,128)S(1)}, u32[]{:S(2)}, u32[]{:S(2)}) collective-permute-start(f32[768,512]{1,0:T(8,128)S(1)} %product.1.mine_ref), channel_id=1, source_target_pairs={{0,1},{1,0},{2,3},{3,2},{4,5},{5,4},{6,7},{7,6},{8,9},{9,8},{10,11... | collective-permute-start | bytes 4718600 | tf_op jit(solution)/shard_map/ppermute | solution.py:30
  77.7 3.0 %collective-permute-done.8.theirs_ref = f32[768,512]{1,0:T(8,128)S(1)} collective-permute-done((f32[768,512]{1,0:T(8,128)S(1)}, f32[768,512]{1,0:T(8,128)S(1)}, u32[]{:S(2)}, u32[]{:S(2)}) %collective-permute-start.8) | collective-permute-done | bytes 1572896 | tf_op jit(solution)/shard_map/ppermute | solution.py:30
  80.7 0.0 copy-done.7
  80.7 3.7 %gradient.1 = (bf16[512,512]{1,0:T(8,128)(2,1)S(1)}, bf16[512,512]{1,0:T(8,128)(2,1)}, bf16[512,512]{1,0:T(8,128)(2,1)}, bf16[512,512]{1,0:T(8,128)(2,1)}) custom-call(bf16[768,2048]{1,0:T(8,128)(2,1)S(1)} %bitcast.18, f32[768,512]{1,0:T(8,128)S(1)} %product.1.mine_ref, f32[768,512]{1,0:T(8,128)S(1)} %collective-permute-done.8.theirs_ref, ...), custom_call_target="tpu_custom_call" | custom-call | tf_op jit(solution)/shard_map/gradient/pallas_call | solution.py:210
  84.4 2.3 %collective-permute-start.10 = (bf16[512,512]{1,0:T(8,128)(2,1)}, bf16[512,512]{1,0:T(8,128)(2,1)S(1)}, u32[]{:S(2)}, u32[]{:S(2)}) collective-permute-start(bf16[512,512]{1,0:T(8,128)(2,1)} %get-tuple-element.56), channel_id=1, source_target_pairs={{0,2},{1,9},{2,4},{3,11},{4,6},{5,13},{6,0},{7,15},{8,10},{9,17},{... | collective-permute-start | bytes 1572872 | tf_op jit(solution)/shard_map/ppermute | solution.py:44
  86.7 5.1 %collective-permute-start.11 = (bf16[512,512]{1,0:T(8,128)(2,1)}, bf16[512,512]{1,0:T(8,128)(2,1)S(1)}, u32[]{:S(2)}, u32[]{:S(2)}) collective-permute-start(bf16[512,512]{1,0:T(8,128)(2,1)} %get-tuple-element.57), channel_id=1, source_target_pairs={{0,6},{1,25},{2,0},{3,27},{4,2},{5,29},{6,4},{7,31},{8,14},{9,1},{... | collective-permute-start | bytes 1572872 | tf_op jit(solution)/shard_map/ppermute | solution.py:44
  91.8 4.9 %collective-permute-start.9 = (bf16[512,512]{1,0:T(8,128)(2,1)}, bf16[512,512]{1,0:T(8,128)(2,1)S(1)}, u32[]{:S(2)}, u32[]{:S(2)}) collective-permute-start(bf16[512,512]{1,0:T(8,128)(2,1)} %get-tuple-element.55), channel_id=1, source_target_pairs={{0,4},{1,17},{2,6},{3,19},{4,0},{5,21},{6,2},{7,23},{8,12},{9,25},... | collective-permute-start | bytes 1572872 | tf_op jit(solution)/shard_map/ppermute | solution.py:44
  96.7 0.0 copy-done.4
  96.7 0.0 copy-done.9
  96.7 0.8 update.1
  97.5 0.0 copy-done.5
  97.5 3.6 %all-to-all-start.1 = ((bf16[16,64,128]{2,1,0:T(8,128)(2,1)}), bf16[16,64,128]{2,1,0:T(8,128)(2,1)S(1)}, u32[]{:S(2)}, u32[]{:S(2)}) async-start(bf16[16,64,128]{2,1,0:T(8,128)(2,1)} %get-tuple-element.64), calls=%async_computation.1 | async-start | bytes 524288 | tf_op jit(solution)/shard_map/all_to_all | solution.py:92
  101.0 2.0 %collective-permute-done.10.third = bf16[512,512]{1,0:T(8,128)(2,1)S(1)} collective-permute-done((bf16[512,512]{1,0:T(8,128)(2,1)}, bf16[512,512]{1,0:T(8,128)(2,1)S(1)}, u32[]{:S(2)}, u32[]{:S(2)}) %collective-permute-start.10) | collective-permute-done | bytes 524320 | tf_op jit(solution)/shard_map/ppermute | solution.py:44
  103.0 4.0 %collective-permute-done.11.fourth = bf16[512,512]{1,0:T(8,128)(2,1)S(1)} collective-permute-done((bf16[512,512]{1,0:T(8,128)(2,1)}, bf16[512,512]{1,0:T(8,128)(2,1)S(1)}, u32[]{:S(2)}, u32[]{:S(2)}) %collective-permute-start.11) | collective-permute-done | bytes 524320 | tf_op jit(solution)/shard_map/ppermute | solution.py:44
  107.1 9.5 %collective-permute-done.9.second = bf16[512,512]{1,0:T(8,128)(2,1)S(1)} collective-permute-done((bf16[512,512]{1,0:T(8,128)(2,1)}, bf16[512,512]{1,0:T(8,128)(2,1)S(1)}, u32[]{:S(2)}, u32[]{:S(2)}) %collective-permute-start.9) | collective-permute-done | bytes 524320 | tf_op jit(solution)/shard_map/ppermute | solution.py:44
  116.6 1.0 copy-done.6
  117.6 0.3 add.88
  117.9 1.5 all-to-all-done.1
  119.4 2.6 %collective-permute-start.12 = (bf16[128,512]{1,0:T(8,128)(2,1)S(1)}, bf16[128,512]{1,0:T(8,128)(2,1)S(1)}, u32[]{:S(2)}, u32[]{:S(2)}) collective-permute-start(bf16[128,512]{1,0:T(8,128)(2,1)S(1)} %get-tuple-element.66), channel_id=1, source_target_pairs={{0,16},{1,5},{2,18},{3,7},{4,20},{5,1},{6,22},{7,3},{8,24},{9,13},... | collective-permute-start | bytes 393224 | tf_op jit(solution)/shard_map/ppermute | solution.py:44
  122.0 4.1 %collective-permute-start.13 = (bf16[128,512]{1,0:T(8,128)(2,1)S(1)}, bf16[128,512]{1,0:T(8,128)(2,1)S(1)}, u32[]{:S(2)}, u32[]{:S(2)}) collective-permute-start(bf16[128,512]{1,0:T(8,128)(2,1)S(1)} %get-tuple-element.67), channel_id=1, source_target_pairs={{0,8},{1,3},{2,10},{3,5},{4,12},{5,7},{6,14},{7,1},{8,16},{9,11},{... | collective-permute-start | bytes 393224 | tf_op jit(solution)/shard_map/ppermute | solution.py:44
  126.1 3.3 %collective-permute-start.14 = (bf16[128,512]{1,0:T(8,128)(2,1)S(1)}, bf16[128,512]{1,0:T(8,128)(2,1)S(1)}, u32[]{:S(2)}, u32[]{:S(2)}) collective-permute-start(bf16[128,512]{1,0:T(8,128)(2,1)S(1)} %get-tuple-element.68), channel_id=1, source_target_pairs={{0,24},{1,7},{2,26},{3,1},{4,28},{5,3},{6,30},{7,5},{8,0},{9,15},{... | collective-permute-start | bytes 393224 | tf_op jit(solution)/shard_map/ppermute | solution.py:44
  129.4 0.0 collective-permute-done.12.second
  129.4 0.4 collective-permute-done.13.third
  129.8 2.0 %collective-permute-done.14.fourth = bf16[128,512]{1,0:T(8,128)(2,1)S(1)} collective-permute-done((bf16[128,512]{1,0:T(8,128)(2,1)S(1)}, bf16[128,512]{1,0:T(8,128)(2,1)S(1)}, u32[]{:S(2)}, u32[]{:S(2)}) %collective-permute-start.14) | collective-permute-done | bytes 131104 | tf_op jit(solution)/shard_map/ppermute | solution.py:44
  131.8 0.8 collect.1
  132.7 6.2 %all-to-all-start.2 = ((f32[32,1,128]{2,1,0:T(1,128)}), f32[32,1,128]{2,1,0:T(1,128)S(1)}, u32[]{:S(2)}, u32[]{:S(2)}) async-start(f32[32,1,128]{2,1,0:T(1,128)} %bitcast.10), calls=%async_computation.2 | async-start | bytes 32768 | tf_op jit(solution)/shard_map/all_to_all | solution.py:92
  138.9 9.3 %all-to-all-done.2 = f32[32,1,128]{2,1,0:T(1,128)S(1)} async-done(((f32[32,1,128]{2,1,0:T(1,128)}), f32[32,1,128]{2,1,0:T(1,128)S(1)}, u32[]{:S(2)}, u32[]{:S(2)}) %all-to-all-start.2) | async-done | bytes 16416 | tf_op jit(solution)/shard_map/all_to_all | solution.py:92
  148.2 0.7 clip.1
  148.9 0.7 copy.12
  (6 shorter events, 0.0 us)
Async XLA Ops:
  0.6 38.6 %collective-permute-start.4 = (bf16[384,4096]{1,0:T(8,128)(2,1)}, bf16[384,4096]{1,0:T(8,128)(2,1)S(1)}, u32[]{:S(2)}, u32[]{:S(2)}) collective-permute-start(bf16[384,4096]{1,0:T(8,128)(2,1)} %bitcast.19), channel_id=1, source_target_pairs={{0,1},{1,0},{2,3},{3,2},{4,5},{5,4},{6,7},{7,6},{8,9},{9,8},{10,11... | collective-permute-start | bytes 9437192 | tf_op jit(solution)/shard_map/ppermute | solution.py:30
  9.4 17.2 %collective-permute-start.3 = (bf16[384,512]{1,0:T(8,128)(2,1)}, bf16[384,512]{1,0:T(8,128)(2,1)}, u32[]{:S(2)}, u32[]{:S(2)}) collective-permute-start(bf16[384,512]{1,0:T(8,128)(2,1)} %bitcast.24), channel_id=1, source_target_pairs={{0,1},{1,0},{2,3},{3,2},{4,5},{5,4},{6,7},{7,6},{8,9},{9,8},{10,11... | collective-permute-start | bytes 1179656 | tf_op jit(solution)/shard_map/ppermute | solution.py:30
  11.4 9.7 %collective-permute-start = (bf16[128,512]{1,0:T(8,128)(2,1)}, bf16[128,512]{1,0:T(8,128)(2,1)S(1)}, u32[]{:S(2)}, u32[]{:S(2)}) collective-permute-start(bf16[128,512]{1,0:T(8,128)(2,1)} %bitcast.26), channel_id=1, source_target_pairs={{0,24},{1,7},{2,26},{3,1},{4,28},{5,3},{6,30},{7,5},{8,0},{9,15},{... | collective-permute-start | bytes 393224 | tf_op jit(solution)/shard_map/ppermute | solution.py:44
  13.3 7.8 %collective-permute-start.1 = (bf16[128,512]{1,0:T(8,128)(2,1)}, bf16[128,512]{1,0:T(8,128)(2,1)}, u32[]{:S(2)}, u32[]{:S(2)}) collective-permute-start(bf16[128,512]{1,0:T(8,128)(2,1)} %bitcast.27), channel_id=1, source_target_pairs={{0,16},{1,5},{2,18},{3,7},{4,20},{5,1},{6,22},{7,3},{8,24},{9,13},... | collective-permute-start | bytes 393224 | tf_op jit(solution)/shard_map/ppermute | solution.py:44
  15.3 8.7 %collective-permute-start.2 = (bf16[128,512]{1,0:T(8,128)(2,1)}, bf16[128,512]{1,0:T(8,128)(2,1)}, u32[]{:S(2)}, u32[]{:S(2)}) collective-permute-start(bf16[128,512]{1,0:T(8,128)(2,1)} %bitcast.28), channel_id=1, source_target_pairs={{0,8},{1,3},{2,10},{3,5},{4,12},{5,7},{6,14},{7,1},{8,16},{9,11},{... | collective-permute-start | bytes 393224 | tf_op jit(solution)/shard_map/ppermute | solution.py:44
  24.0 0.9 copy-start.8
  26.7 31.0 %collective-permute-start.5 = (bf16[512,512]{1,0:T(8,128)(2,1)}, bf16[512,512]{1,0:T(8,128)(2,1)}, u32[]{:S(2)}, u32[]{:S(2)}) collective-permute-start(bf16[512,512]{1,0:T(8,128)(2,1)} %join.1.refs_0_), channel_id=1, source_target_pairs={{0,6},{1,25},{2,0},{3,27},{4,2},{5,29},{6,4},{7,31},{8,14},{9,1},{... | collective-permute-start | bytes 1572872 | tf_op jit(solution)/shard_map/ppermute | solution.py:44
  29.0 28.7 %collective-permute-start.6 = (bf16[512,512]{1,0:T(8,128)(2,1)}, bf16[512,512]{1,0:T(8,128)(2,1)}, u32[]{:S(2)}, u32[]{:S(2)}) collective-permute-start(bf16[512,512]{1,0:T(8,128)(2,1)} %join.1.refs_0_), channel_id=1, source_target_pairs={{0,4},{1,17},{2,6},{3,19},{4,0},{5,21},{6,2},{7,23},{8,12},{9,25},... | collective-permute-start | bytes 1572872 | tf_op jit(solution)/shard_map/ppermute | solution.py:44
  32.2 25.4 %collective-permute-start.7 = (bf16[512,512]{1,0:T(8,128)(2,1)}, bf16[512,512]{1,0:T(8,128)(2,1)}, u32[]{:S(2)}, u32[]{:S(2)}) collective-permute-start(bf16[512,512]{1,0:T(8,128)(2,1)} %join.1.refs_0_), channel_id=1, source_target_pairs={{0,2},{1,9},{2,4},{3,11},{4,6},{5,13},{6,0},{7,15},{8,10},{9,17},{... | collective-permute-start | bytes 1572872 | tf_op jit(solution)/shard_map/ppermute | solution.py:44
  36.5 1.0 copy-start.3
  39.2 1.6 %copy-start.1 = (bf16[384,4096]{1,0:T(8,128)(2,1)}, bf16[384,4096]{1,0:T(8,128)(2,1)S(1)}, u32[]{:S(2)}) copy-start(bf16[384,4096]{1,0:T(8,128)(2,1)S(1)} %collective-permute-done.4.theirs_ref) | copy-start | bytes 9437188
  40.8 1.9 %copy-start = (bf16[1,384,4096]{2,1,0:T(8,128)(2,1)S(1)}, bf16[1,384,4096]{2,1,0:T(8,128)(2,1)}, u32[]{:S(2)}) copy-start(bf16[1,384,4096]{2,1,0:T(8,128)(2,1)} %param.7) | copy-start | bytes 9437188
  42.7 1.9 %copy-start.2 = (bf16[384,4096]{1,0:T(8,128)(2,1)S(1)}, bf16[384,4096]{1,0:T(8,128)(2,1)}, u32[]{:S(2)}) copy-start(bf16[384,4096]{1,0:T(8,128)(2,1)} %copy-done.1) | copy-start | bytes 9437188
  44.6 0.7 copy-start.10
  47.1 19.1 %all-to-all-start = ((bf16[16,64,128]{2,1,0:T(8,128)(2,1)}), bf16[16,64,128]{2,1,0:T(8,128)(2,1)S(1)}, u32[]{:S(2)}, u32[]{:S(2)}) async-start(bf16[16,64,128]{2,1,0:T(8,128)(2,1)} %bitcast.7), calls=%async_computation | async-start | bytes 524288 | tf_op jit(solution)/shard_map/all_to_all | solution.py:92
  66.2 14.5 %copy-start.7 = (bf16[1,384,512]{2,1,0:T(8,128)(2,1)S(1)}, bf16[1,384,512]{2,1,0:T(8,128)(2,1)}, u32[]{:S(2)}) copy-start(bf16[1,384,512]{2,1,0:T(8,128)(2,1)} %param.10) | copy-start | bytes 1179652
  69.6 27.1 %copy-start.4 = (bf16[131072]{0:T(1024)(128)(2,1)S(1)}, bf16[131072]{0:T(1024)(128)(2,1)}, u32[]{:S(2)}) copy-start(bf16[131072]{0:T(1024)(128)(2,1)} %param.11) | copy-start | bytes 786436
  69.6 27.1 %copy-start.9 = (f32[8192]{0:T(1024)S(1)}, f32[8192]{0:T(1024)}, u32[]{:S(2)}) copy-start(f32[8192]{0:T(1024)} %param.13) | copy-start | bytes 98308
  69.6 11.1 %collective-permute-start.8 = (f32[768,512]{1,0:T(8,128)S(1)}, f32[768,512]{1,0:T(8,128)S(1)}, u32[]{:S(2)}, u32[]{:S(2)}) collective-permute-start(f32[768,512]{1,0:T(8,128)S(1)} %product.1.mine_ref), channel_id=1, source_target_pairs={{0,1},{1,0},{2,3},{3,2},{4,5},{5,4},{6,7},{7,6},{8,9},{9,8},{10,11... | collective-permute-start | bytes 4718600 | tf_op jit(solution)/shard_map/ppermute | solution.py:30
  84.4 13.1 %copy-start.5 = (bf16[512,512]{1,0:T(8,128)(2,1)}, bf16[512,512]{1,0:T(8,128)(2,1)S(1)}, u32[]{:S(2)}) copy-start(bf16[512,512]{1,0:T(8,128)(2,1)S(1)} %get-tuple-element.54.first) | copy-start | bytes 1572868
  84.4 18.6 %collective-permute-start.10 = (bf16[512,512]{1,0:T(8,128)(2,1)}, bf16[512,512]{1,0:T(8,128)(2,1)S(1)}, u32[]{:S(2)}, u32[]{:S(2)}) collective-permute-start(bf16[512,512]{1,0:T(8,128)(2,1)} %get-tuple-element.56), channel_id=1, source_target_pairs={{0,2},{1,9},{2,4},{3,11},{4,6},{5,13},{6,0},{7,15},{8,10},{9,17},{... | collective-permute-start | bytes 1572872 | tf_op jit(solution)/shard_map/ppermute | solution.py:44
  86.7 20.4 %collective-permute-start.11 = (bf16[512,512]{1,0:T(8,128)(2,1)}, bf16[512,512]{1,0:T(8,128)(2,1)S(1)}, u32[]{:S(2)}, u32[]{:S(2)}) collective-permute-start(bf16[512,512]{1,0:T(8,128)(2,1)} %get-tuple-element.57), channel_id=1, source_target_pairs={{0,6},{1,25},{2,0},{3,27},{4,2},{5,29},{6,4},{7,31},{8,14},{9,1},{... | collective-permute-start | bytes 1572872 | tf_op jit(solution)/shard_map/ppermute | solution.py:44
  91.8 24.8 %collective-permute-start.9 = (bf16[512,512]{1,0:T(8,128)(2,1)}, bf16[512,512]{1,0:T(8,128)(2,1)S(1)}, u32[]{:S(2)}, u32[]{:S(2)}) collective-permute-start(bf16[512,512]{1,0:T(8,128)(2,1)} %get-tuple-element.55), channel_id=1, source_target_pairs={{0,4},{1,17},{2,6},{3,19},{4,0},{5,21},{6,2},{7,23},{8,12},{9,25},... | collective-permute-start | bytes 1572872 | tf_op jit(solution)/shard_map/ppermute | solution.py:44
  97.5 21.9 %all-to-all-start.1 = ((bf16[16,64,128]{2,1,0:T(8,128)(2,1)}), bf16[16,64,128]{2,1,0:T(8,128)(2,1)S(1)}, u32[]{:S(2)}, u32[]{:S(2)}) async-start(bf16[16,64,128]{2,1,0:T(8,128)(2,1)} %get-tuple-element.64), calls=%async_computation.1 | async-start | bytes 524288 | tf_op jit(solution)/shard_map/all_to_all | solution.py:92
  116.6 1.0 copy-start.6
  119.4 10.1 %collective-permute-start.12 = (bf16[128,512]{1,0:T(8,128)(2,1)S(1)}, bf16[128,512]{1,0:T(8,128)(2,1)S(1)}, u32[]{:S(2)}, u32[]{:S(2)}) collective-permute-start(bf16[128,512]{1,0:T(8,128)(2,1)S(1)} %get-tuple-element.66), channel_id=1, source_target_pairs={{0,16},{1,5},{2,18},{3,7},{4,20},{5,1},{6,22},{7,3},{8,24},{9,13},... | collective-permute-start | bytes 393224 | tf_op jit(solution)/shard_map/ppermute | solution.py:44
  122.0 7.8 %collective-permute-start.13 = (bf16[128,512]{1,0:T(8,128)(2,1)S(1)}, bf16[128,512]{1,0:T(8,128)(2,1)S(1)}, u32[]{:S(2)}, u32[]{:S(2)}) collective-permute-start(bf16[128,512]{1,0:T(8,128)(2,1)S(1)} %get-tuple-element.67), channel_id=1, source_target_pairs={{0,8},{1,3},{2,10},{3,5},{4,12},{5,7},{6,14},{7,1},{8,16},{9,11},{... | collective-permute-start | bytes 393224 | tf_op jit(solution)/shard_map/ppermute | solution.py:44
  126.1 5.7 %collective-permute-start.14 = (bf16[128,512]{1,0:T(8,128)(2,1)S(1)}, bf16[128,512]{1,0:T(8,128)(2,1)S(1)}, u32[]{:S(2)}, u32[]{:S(2)}) collective-permute-start(bf16[128,512]{1,0:T(8,128)(2,1)S(1)} %get-tuple-element.68), channel_id=1, source_target_pairs={{0,24},{1,7},{2,26},{3,1},{4,28},{5,3},{6,30},{7,5},{8,0},{9,15},{... | collective-permute-start | bytes 393224 | tf_op jit(solution)/shard_map/ppermute | solution.py:44
  132.7 15.5 %all-to-all-start.2 = ((f32[32,1,128]{2,1,0:T(1,128)}), f32[32,1,128]{2,1,0:T(1,128)S(1)}, u32[]{:S(2)}, u32[]{:S(2)}) async-start(f32[32,1,128]{2,1,0:T(1,128)} %bitcast.10), calls=%async_computation.2 | async-start | bytes 32768 | tf_op jit(solution)/shard_map/all_to_all | solution.py:92

commit v12 on v10

--- a/solution.py
+++ b/solution.py
@@ -29,6 +29,20 @@
 def send(value, axis, step):
     size = AXES[axis]
     return lax.ppermute(value, axis, [(i, (i + step) % size) for i in range(size)])
+
+
+def deliver(value, wide, step):
+    pairs = []
+    for y in range(AXES["y_hi"]):
+        for x in range(AXES["x"]):
+            for core in range(AXES["core"]):
+                to_y, to_x = y, x
+                if (core == 0) == wide:
+                    to_x = (x + step) % AXES["x"]
+                else:
+                    to_y = (y + step) % AXES["y_hi"]
+                pairs.append(((y * AXES["x"] + x) * 2 + core, (to_y * AXES["x"] + to_x) * 2 + core))
+    return lax.ppermute(value, FSDP, pairs)
 
 
 def tied(*values):
@@ -53,9 +67,17 @@
     return (chip * 2 + core).astype(jnp.int32)
 
 
+def block_order():
+    y, core = lax.axis_index("y_hi"), lax.axis_index("core")
+    wide, narrow = jnp.arange(CHIPS) // 4, jnp.arange(CHIPS) % 4
+    to_y = (y + jnp.where(core == 0, narrow, wide)) % AXES["y_hi"]
+    to_x = jnp.where(core == 0, wide, narrow)
+    return (to_x * AXES["y_hi"] + to_y).astype(jnp.int32)
+
+
 def arrange(order, inputs, theirs, feature_gain):
     tokens, features = inputs.shape
-    step = 32
+    step = 96
     block = pl.BlockSpec((step, features), lambda i: (i, 0))
     scaled = pl.pallas_call(
         arrange_kernel,
@@ -176,8 +198,8 @@
     )(scaled, *weights)
 
 
-def gradient_kernel(scaled_ref, mine_ref, theirs_ref, *refs):
-    *target_refs, first, second, third, fourth, residual_ref = refs
+def gradient_kernel(order_ref, scaled_ref, mine_ref, theirs_ref, *refs):
+    *target_refs, first, second, third, fourth, residual_ref, columns_ref = refs
     tokens = target_refs[0].shape[0]
     for half, target_ref in enumerate(target_refs):
         here = slice(half * tokens, (half + 1) * tokens)
@@ -185,31 +207,56 @@
         residual_ref[here, :] = (
             mine_ref[here, :] + theirs_ref[there, :] - target_ref[...].astype(jnp.float32)
         ).astype(jnp.bfloat16)
-    group = first.shape[0]
+    parts = first.shape[0] // LANES
     for k, ref in enumerate((first, second, third, fourth)):
+        for j in range(parts):
+            start = pl.multiple_of(order_ref[k * parts + j] * LANES, LANES)
+            columns_ref[:, j * LANES : (j + 1) * LANES] = scaled_ref[:, pl.ds(start, LANES)]
         ref[...] = lax.dot_general(
-            scaled_ref[:, k * group : (k + 1) * group],
+            columns_ref[...],
             residual_ref[...],
             (((0,), (0,)), ((), ())),
             preferred_element_type=jnp.float32,
         ).astype(jnp.bfloat16)
 
 
-def gradient_blocks(scaled, mine, theirs, targets):
+def gradient_blocks(order, scaled, mine, theirs, targets):
     block = (scaled.shape[1] // AXES["x"], mine.shape[1])
     return pl.pallas_call(
         gradient_kernel,
         out_shape=(in_vmem(block, jnp.bfloat16),) * AXES["x"],
-        in_specs=[WHOLE] * 5,
+        in_specs=[pl.BlockSpec(memory_space=pltpu.SMEM)] + [WHOLE] * 5,
         out_specs=(WHOLE,) * AXES["x"],
-        scratch_shapes=[pltpu.VMEM(mine.shape, jnp.bfloat16)],
+        scratch_shapes=[
+            pltpu.VMEM(mine.shape, jnp.bfloat16),
+            pltpu.VMEM((scaled.shape[0], block[0]), jnp.bfloat16),
+        ],
         compiler_params=pltpu.CompilerParams(vmem_limit_bytes=3 * VMEM_LIMIT),
         name="gradient",
-    )(scaled, mine, theirs, *targets)
-
-
-def collect_kernel(arrived_ref, gradient_ref, squares_ref):
-    gradient = total([arrived_ref[k] for k in range(arrived_ref.shape[0])])
+    )(order, scaled, mine, theirs, *targets)
+
+
+def add_kernel(first, second, third, fourth, *out_refs):
+    rows = out_refs[0].shape[0]
+    for k, ref in enumerate(out_refs):
+        here = slice(k * rows, (k + 1) * rows)
+        ref[...] = total([r[here, :] for r in (first, second, third, fourth)]).astype(jnp.bfloat16)
+
+
+def add(blocks):
+    rows, width = blocks[0].shape
+    return pl.pallas_call(
+        add_kernel,
+        out_shape=(in_vmem((rows // 4, width), jnp.bfloat16),) * 4,
+        in_specs=[WHOLE] * 4,
+        out_specs=(WHOLE,) * 4,
+        compiler_params=pltpu.CompilerParams(vmem_limit_bytes=VMEM_LIMIT),
+        name="add",
+    )(*blocks)
+
+
+def collect_kernel(first, second, third, fourth, gradient_ref, squares_ref):
+    gradient = total([ref[...] for ref in (first, second, third, fourth)])
     gradient_ref[...] = gradient
     squares = jnp.sum(gradient * gradient, axis=0, keepdims=True)
     squares_ref[...] = jnp.broadcast_to(
@@ -217,18 +264,18 @@
     )
 
 
-def collect(arrived):
+def collect(blocks):
     return pl.pallas_call(
         collect_kernel,
         out_shape=(
-            jax.ShapeDtypeStruct(arrived.shape[1:], jnp.float32),
+            jax.ShapeDtypeStruct(blocks[0].shape, jnp.float32),
             jax.ShapeDtypeStruct((CHIPS * AXES["core"], LANES), jnp.float32),
         ),
-        in_specs=[WHOLE],
+        in_specs=[WHOLE] * 4,
         out_specs=(WHOLE, WHOLE),
         compiler_params=pltpu.CompilerParams(vmem_limit_bytes=VMEM_LIMIT),
         name="collect",
-    )(arrived)
+    )(*blocks)
 
 
 def clip_kernel(entries, squares_ref, gradient_ref, clipped_ref):
@@ -258,28 +305,30 @@
     global_frag = global_frag.reshape(-1, QBLOCK)
     local_frag = local_frag[0].reshape(-1, QBLOCK)
     momentum = momentum.reshape(-1, QBLOCK)
-    key_weight, order, replica = tied(key_weight, feature_order(), replica)
+    key_weight, order, blocks, replica = tied(
+        key_weight, feature_order(), block_order(), replica
+    )
 
     own, inputs, teacher_keys = tied(copies_of(key_weight[0], "y_hi"), inputs, teacher_keys)
     column = exchange(own, "y_hi").reshape(AXES["y_hi"] * rows, width)
     raw = send(inputs[0], "core", 1)
     targets = (teacher_keys[0], send(teacher_keys[0], "core", 1))
     scaled = arrange(order, inputs[0], raw, feature_gain)
-    column, scaled, targets, global_frag, local_frag, replica = tied(
-        column, scaled, targets, global_frag, local_frag, replica
+    column, scaled, targets, global_frag, local_frag, replica, blocks = tied(
+        column, scaled, targets, global_frag, local_frag, replica, blocks
     )
     far = [column] + [send(column, "x", -k) for k in (1, 2, 3)]
     decoded = fragment_codes(global_frag, local_frag)
     arrived = exchange(decoded.reshape(replicas, -1, QBLOCK), REPLICA)
     far, arrived = tied(far, arrived)
     partial = product(scaled, far)
-    gradient = list(gradient_blocks(scaled, partial, send(partial, "core", 1), targets))
+    gradient = list(gradient_blocks(blocks, scaled, partial, send(partial, "core", 1), targets))
     gradient[0], arrived = tied(gradient[0], arrived)
     new_momentum, copies = fragment_update(replica, arrived, global_frag, momentum)
     new_global = exchange(copies, REPLICA)
-    mine = total([gradient[0]] + [send(gradient[k], "x", k) for k in STEPS])
-    mine, new_global = tied(mine.astype(jnp.bfloat16), new_global)
-    gradient, squares = collect(exchange(mine.reshape(AXES["y_hi"], rows, width), "y_hi"))
+    mine = add([gradient[0]] + [deliver(gradient[k], True, k) for k in STEPS])
+    mine, new_global = tied(mine, new_global)
+    gradient, squares = collect([mine[0]] + [deliver(mine[k], False, k) for k in STEPS])
 
     clipped_grad = clip(exchange(squares, FSDP), gradient, features * width)[None]
     return (clipped_grad, new_global.reshape(-1), new_momentum.reshape(-1))

time: 144 us -> 147 us (1.021)
  blocking collectives: 39.4 us -> 18.4 us
  starting transfers between devices: 52.6 us -> 68 us
  waiting for transfers between devices: 23.4 us -> 34 us
  Pallas kernels: 16.8 us -> 14.5 us
    ppermute x0 -> x6, starting transfers between devices: none -> 22.9 us  [deliver(): return lax.ppermute(value, FSDP, pairs)]
    all_to_all x2 -> x1, blocking collectives: 39.4 us -> 18.4 us  [exchange(): return lax.all_to_all(parts, axis, split_axis=0, concat_axis=0, tiled=True)]
    ppermute x0 -> x6, waiting for transfers between devices: none -> 14.6 us  [deliver(): return lax.ppermute(value, FSDP, pairs)]
    ppermute x9 -> x6, waiting for transfers between devices: 14 us -> 4.52 us  [send(): lax.ppermute(value, axis, [(i, (i + step) % size) for i in range(size)])]
    ppermute x9 -> x6, starting transfers between devices: 31.6 us -> 23.5 us  [send(): lax.ppermute(value, axis, [(i, (i + step) % size) for i in range(size)])]
    all_to_all x3, waiting for transfers between devices: 9.42 us -> 14.9 us  [exchange(): return lax.all_to_all(parts, axis, split_axis=0, concat_axis=0, tiled=True)]
    pallas_call x1, Pallas kernels: 7.29 us -> 3.99 us  [arrange(): pl.pallas_call(arrange_kernel, grid=(tokens // step,), out_shape=jax.Shap...]
    unnamed x15 -> x17, local copies, waits for them, and re-layouts: 4.04 us -> 5.08 us
  transfers between devices with their start and end apart: 12 -> 15, of which waited for: 5 -> 8; matrix products, arithmetic and copies ran while one was open for 3% -> 2% of each run, Pallas kernels for 6% -> 4%
where the time goes in v12:
time: 147 us; the launch traced here: 146 us
  starting transfers between devices  68 us (46%)
  waiting for transfers between devices  34 us (23%)
  blocking collectives  18.4 us (13%)
  Pallas kernels  14.5 us (10%)
  local copies, waits for them, and re-layouts  6.81 us (5%)
  other arithmetic  3.21 us (2%)
    ppermute x6, starting transfers between devices, send(): lax.ppermute(value, axis, [(i, (i + step) % size) for i in range(size)])  23.5 us
    ppermute x6, starting transfers between devices, deliver(): return lax.ppermute(value, FSDP, pairs)  22.9 us
    all_to_all x3, starting transfers between devices, exchange(): return lax.all_to_all(parts, axis, split_axis=0, concat_axis=0, tiled=True)  21.6 us
    all_to_all x1, blocking collectives, exchange(): return lax.all_to_all(parts, axis, split_axis=0, concat_axis=0, tiled=True)  18.4 us
    all_to_all x3, waiting for transfers between devices, exchange(): return lax.all_to_all(parts, axis, split_axis=0, concat_axis=0, tiled=True)  14.9 us
    ppermute x6, waiting for transfers between devices, deliver(): return lax.ppermute(value, FSDP, pairs)  14.6 us
    unnamed x17, local copies, waits for them, and re-layouts  5.08 us
    ppermute x6, waiting for transfers between devices, send(): lax.ppermute(value, axis, [(i, (i + step) % size) for i in range(size)])  4.52 us
  transfers between devices with their start and end apart: 15, of which 8 were waited for; matrix products, arithmetic and copies ran while one was open for 2% of the time, Pallas kernels for 4%

profile of v12, /device:TPU:1, one launch (start us, length us, event | category | flops | bytes accessed | tf_op | source)
XLA Modules:
  0.0 145.7 jit_solution(14419167311647675117)
XLA Ops:
  0.7 1.7 %broadcast_in_dim.18 = bf16[4,128,512]{2,1,0:T(8,128)(2,1)} broadcast(bf16[128,512]{1,0:T(8,128)(2,1)} %bitcast.32), dimensions={1,2} | broadcast | bytes 655360 | tf_op jit(solution)/shard_map/broadcast_in_dim | solution.py:104
  2.4 8.8 %collective-permute-start = (bf16[384,4096]{1,0:T(8,128)(2,1)}, bf16[384,4096]{1,0:T(8,128)(2,1)S(1)}, u32[]{:S(2)}, u32[]{:S(2)}) collective-permute-start(bf16[384,4096]{1,0:T(8,128)(2,1)} %bitcast.29), channel_id=1, source_target_pairs={{0,1},{1,0},{2,3},{3,2},{4,5},{5,4},{6,7},{7,6},{8,9},{9,8},{10,11... | collective-permute-start | bytes 9437192 | tf_op jit(solution)/shard_map/ppermute | solution.py:31
  11.2 4.1 %all-to-all-start = ((bf16[4,128,512]{2,1,0:T(8,128)(2,1)}), bf16[4,128,512]{2,1,0:T(8,128)(2,1)}, u32[]{:S(2)}, u32[]{:S(2)}) async-start(bf16[4,128,512]{2,1,0:T(8,128)(2,1)} %broadcast_in_dim.18), calls=%async_computation | async-start | bytes 1048576 | tf_op jit(solution)/shard_map/all_to_all | solution.py:100
  15.3 1.9 %collective-permute-start.1 = (bf16[384,512]{1,0:T(8,128)(2,1)}, bf16[384,512]{1,0:T(8,128)(2,1)}, u32[]{:S(2)}, u32[]{:S(2)}) collective-permute-start(bf16[384,512]{1,0:T(8,128)(2,1)} %bitcast.24), channel_id=1, source_target_pairs={{0,1},{1,0},{2,3},{3,2},{4,5},{5,4},{6,7},{7,6},{8,9},{9,8},{10,11... | collective-permute-start | bytes 1179656 | tf_op jit(solution)/shard_map/ppermute | solution.py:31
  17.3 3.2 %reduce = bf16[131072]{0:T(1024)(128)(2,1)} reduce(bf16[1,131072]{1,0:T(2,128)(2,1)} %param.12, bf16[]{:T(256)} %constant.74), dimensions={0}, to_apply=%param.12.reduce_sub_computation | reduce | bytes 524290 | tf_op args[5]
  20.5 0.0 collective-permute-done.theirs_ref
  20.5 0.0 copy-start.7
  20.5 1.6 %copy-done.7 = bf16[384,4096]{1,0:T(8,128)(2,1)} copy-done((bf16[384,4096]{1,0:T(8,128)(2,1)}, bf16[384,4096]{1,0:T(8,128)(2,1)S(1)}, u32[]{:S(2)}) %copy-start.7) | copy-done | bytes 3145752
  22.1 0.0 copy-start.6
  22.1 0.7 copy-done.6
  22.8 0.0 copy-start
  22.8 4.0 %arrange.1 = bf16[2,384,2048]{2,1,0:T(8,128)(2,1)S(1)} custom-call(s32[16]{0:T(128)S(1)} %get-tuple-element.44.order_ref, bf16[384,4096]{1,0:T(8,128)(2,1)} %bitcast.30, bf16[384,4096]{1,0:T(8,128)(2,1)} %copy-done.7, f32[1,4096]{1,0:T(1,128)S(1)} %bitcast.28), custom_call_target="tpu_custom_call" | custom-call | tf_op jit(solution)/shard_map/arrange/pallas_call | solution.py:82
  26.8 0.0 collective-permute-done.1.refs_1_
  26.8 3.4 %all-to-all-done = bf16[4,128,512]{2,1,0:T(8,128)(2,1)} async-done(((bf16[4,128,512]{2,1,0:T(8,128)(2,1)}), bf16[4,128,512]{2,1,0:T(8,128)(2,1)}, u32[]{:S(2)}, u32[]{:S(2)}) %all-to-all-start) | async-done | bytes 524320 | tf_op jit(solution)/shard_map/all_to_all | solution.py:100
  30.2 1.9 %collective-permute-start.4 = (bf16[512,512]{1,0:T(8,128)(2,1)}, bf16[512,512]{1,0:T(8,128)(2,1)S(1)}, u32[]{:S(2)}, u32[]{:S(2)}) collective-permute-start(bf16[512,512]{1,0:T(8,128)(2,1)} %bitcast.2.refs_0_), channel_id=1, source_target_pairs={{0,2},{2,4},{4,6},{6,0},{1,3},{3,5},{5,7},{7,1},{8,10},{10,12},{12... | collective-permute-start | bytes 1572872 | tf_op jit(solution)/shard_map/ppermute | solution.py:31
  32.2 2.2 %collective-permute-start.3 = (bf16[512,512]{1,0:T(8,128)(2,1)}, bf16[512,512]{1,0:T(8,128)(2,1)S(1)}, u32[]{:S(2)}, u32[]{:S(2)}) collective-permute-start(bf16[512,512]{1,0:T(8,128)(2,1)} %bitcast.2.refs_0_), channel_id=1, source_target_pairs={{0,4},{2,6},{4,0},{6,2},{1,5},{3,7},{5,1},{7,3},{8,12},{10,14},{12... | collective-permute-start | bytes 1572872 | tf_op jit(solution)/shard_map/ppermute | solution.py:31
  34.4 4.2 %collective-permute-start.2 = (bf16[512,512]{1,0:T(8,128)(2,1)}, bf16[512,512]{1,0:T(8,128)(2,1)S(1)}, u32[]{:S(2)}, u32[]{:S(2)}) collective-permute-start(bf16[512,512]{1,0:T(8,128)(2,1)} %bitcast.2.refs_0_), channel_id=1, source_target_pairs={{0,6},{2,0},{4,2},{6,4},{1,7},{3,1},{5,3},{7,5},{8,14},{10,8},{12,... | collective-permute-start | bytes 1572872 | tf_op jit(solution)/shard_map/ppermute | solution.py:31
  38.7 0.0 copy-done
  38.7 0.0 copy-start.1
  38.7 0.9 copy-done.1
  39.6 0.7 codes.1
  40.3 18.4 %all_to_all.26.arrived_ref = bf16[16,64,128]{2,1,0:T(8,128)(2,1)S(1)} all-to-all(bf16[16,64,128]{2,1,0:T(8,128)(2,1)S(1)} %bitcast.22), channel_id=1, replica_groups=mesh['z'=8,'y_lo'=2,'y_hi'=4,'x'=4,'core'=2] {'z','y_lo'}, dimensions={0} | all-to-all | bytes 524288 | tf_op jit(solution)/shard_map/all_to_all | solution.py:100
  58.7 0.0 copy-start.4
  58.7 0.0 collective-permute-done.4.refs_3_
  58.7 0.0 collective-permute-done.3.refs_2_
  58.7 1.5 %collective-permute-done.2.refs_1_ = bf16[512,512]{1,0:T(8,128)(2,1)S(1)} collective-permute-done((bf16[512,512]{1,0:T(8,128)(2,1)}, bf16[512,512]{1,0:T(8,128)(2,1)S(1)}, u32[]{:S(2)}, u32[]{:S(2)}) %collective-permute-start.2) | collective-permute-done | bytes 524320 | tf_op jit(solution)/shard_map/ppermute | solution.py:31
  60.2 2.8 %product.1.mine_ref = f32[768,512]{1,0:T(8,128)S(1)} custom-call(bf16[768,2048]{1,0:T(8,128)(2,1)S(1)} %bitcast.18, bf16[512,512]{1,0:T(8,128)(2,1)} %bitcast.2.refs_0_, bf16[512,512]{1,0:T(8,128)(2,1)S(1)} %collective-permute-done.2.refs_1_, bf16[512,512]{1,0:T(8,128)(2,1)S(1)} %collective-permute-done.3.refs_2_, ...), custom_call_target="tpu_custom_call" | custom-call | tf_op jit(solution)/shard_map/product/pallas_call | solution.py:191
  63.0 0.0 copy-start.5
  63.0 4.4 %collective-permute-start.5 = (f32[768,512]{1,0:T(8,128)S(1)}, f32[768,512]{1,0:T(8,128)S(1)}, u32[]{:S(2)}, u32[]{:S(2)}) collective-permute-start(f32[768,512]{1,0:T(8,128)S(1)} %product.1.mine_ref), channel_id=1, source_target_pairs={{0,1},{1,0},{2,3},{3,2},{4,5},{5,4},{6,7},{7,6},{8,9},{9,8},{10,11... | collective-permute-start | bytes 4718600 | tf_op jit(solution)/shard_map/ppermute | solution.py:31
  67.4 3.0 %collective-permute-done.5.theirs_ref = f32[768,512]{1,0:T(8,128)S(1)} collective-permute-done((f32[768,512]{1,0:T(8,128)S(1)}, f32[768,512]{1,0:T(8,128)S(1)}, u32[]{:S(2)}, u32[]{:S(2)}) %collective-permute-start.5) | collective-permute-done | bytes 1572896 | tf_op jit(solution)/shard_map/ppermute | solution.py:31
  70.4 0.0 copy-done.4
  70.4 4.4 %gradient.1 = (bf16[512,512]{1,0:T(8,128)(2,1)S(1)}, bf16[512,512]{1,0:T(8,128)(2,1)}, bf16[512,512]{1,0:T(8,128)(2,1)}, bf16[512,512]{1,0:T(8,128)(2,1)}) custom-call(s32[16]{0:T(128)S(1)} %get-tuple-element.49.order_ref, bf16[768,2048]{1,0:T(8,128)(2,1)S(1)} %bitcast.19, f32[768,512]{1,0:T(8,128)S(1)} %product.1.mine_ref, ...), custom_call_target="tpu_custom_call" | custom-call | tf_op jit(solution)/shard_map/gradient/pallas_call | solution.py:225
  74.8 0.0 copy-start.2
  74.8 4.2 %collective-permute-start.6 = (bf16[512,512]{1,0:T(8,128)(2,1)}, bf16[512,512]{1,0:T(8,128)(2,1)S(1)}, u32[]{:S(2)}, u32[]{:S(2)}) collective-permute-start(bf16[512,512]{1,0:T(8,128)(2,1)} %get-tuple-element.63), channel_id=1, source_target_pairs={{0,4},{1,17},{2,6},{3,19},{4,0},{5,21},{6,2},{7,23},{8,12},{9,25},... | collective-permute-start | bytes 1572872 | tf_op jit(solution)/shard_map/ppermute | solution.py:45
  79.0 4.2 %collective-permute-start.7 = (bf16[512,512]{1,0:T(8,128)(2,1)}, bf16[512,512]{1,0:T(8,128)(2,1)S(1)}, u32[]{:S(2)}, u32[]{:S(2)}) collective-permute-start(bf16[512,512]{1,0:T(8,128)(2,1)} %get-tuple-element.64), channel_id=1, source_target_pairs={{0,2},{1,9},{2,4},{3,11},{4,6},{5,13},{6,0},{7,15},{8,10},{9,17},{... | collective-permute-start | bytes 1572872 | tf_op jit(solution)/shard_map/ppermute | solution.py:45
  83.2 3.2 %collective-permute-start.8 = (bf16[512,512]{1,0:T(8,128)(2,1)}, bf16[512,512]{1,0:T(8,128)(2,1)S(1)}, u32[]{:S(2)}, u32[]{:S(2)}) collective-permute-start(bf16[512,512]{1,0:T(8,128)(2,1)} %get-tuple-element.65), channel_id=1, source_target_pairs={{0,6},{1,25},{2,0},{3,27},{4,2},{5,29},{6,4},{7,31},{8,14},{9,1},{... | collective-permute-start | bytes 1572872 | tf_op jit(solution)/shard_map/ppermute | solution.py:45
  86.4 0.0 copy-done.5
  86.4 0.8 update.1
  87.2 0.0 copy-done.2
  87.2 7.2 %all-to-all-start.2 = ((bf16[16,64,128]{2,1,0:T(8,128)(2,1)}), bf16[16,64,128]{2,1,0:T(8,128)(2,1)S(1)}, u32[]{:S(2)}, u32[]{:S(2)}) async-start(bf16[16,64,128]{2,1,0:T(8,128)(2,1)} %get-tuple-element.72), calls=%async_computation.2 | async-start | bytes 524288 | tf_op jit(solution)/shard_map/all_to_all | solution.py:100
  94.5 0.0 collective-permute-done.6.second
  94.5 12.7 %collective-permute-done.7.third = bf16[512,512]{1,0:T(8,128)(2,1)S(1)} collective-permute-done((bf16[512,512]{1,0:T(8,128)(2,1)}, bf16[512,512]{1,0:T(8,128)(2,1)S(1)}, u32[]{:S(2)}, u32[]{:S(2)}) %collective-permute-start.7) | collective-permute-done | bytes 524320 | tf_op jit(solution)/shard_map/ppermute | solution.py:45
  107.1 0.0 collective-permute-done.8.fourth
  107.1 0.0 copy-start.3
  107.1 1.0 copy-done.3
  108.2 0.3 add.89
  108.5 2.1 %all-to-all-done.2 = bf16[16,64,128]{2,1,0:T(8,128)(2,1)S(1)} async-done(((bf16[16,64,128]{2,1,0:T(8,128)(2,1)}), bf16[16,64,128]{2,1,0:T(8,128)(2,1)S(1)}, u32[]{:S(2)}, u32[]{:S(2)}) %all-to-all-start.2) | async-done | bytes 262176 | tf_op jit(solution)/shard_map/all_to_all | solution.py:100
  110.6 4.9 %collective-permute-start.9 = (bf16[128,512]{1,0:T(8,128)(2,1)S(1)}, bf16[128,512]{1,0:T(8,128)(2,1)S(1)}, u32[]{:S(2)}, u32[]{:S(2)}) collective-permute-start(bf16[128,512]{1,0:T(8,128)(2,1)S(1)} %get-tuple-element.74), channel_id=1, source_target_pairs={{0,16},{1,5},{2,18},{3,7},{4,20},{5,1},{6,22},{7,3},{8,24},{9,13},... | collective-permute-start | bytes 393224 | tf_op jit(solution)/shard_map/ppermute | solution.py:45
  115.5 2.1 %collective-permute-start.10 = (bf16[128,512]{1,0:T(8,128)(2,1)S(1)}, bf16[128,512]{1,0:T(8,128)(2,1)S(1)}, u32[]{:S(2)}, u32[]{:S(2)}) collective-permute-start(bf16[128,512]{1,0:T(8,128)(2,1)S(1)} %get-tuple-element.75), channel_id=1, source_target_pairs={{0,8},{1,3},{2,10},{3,5},{4,12},{5,7},{6,14},{7,1},{8,16},{9,11},{... | collective-permute-start | bytes 393224 | tf_op jit(solution)/shard_map/ppermute | solution.py:45
  117.6 4.4 %collective-permute-start.11 = (bf16[128,512]{1,0:T(8,128)(2,1)S(1)}, bf16[128,512]{1,0:T(8,128)(2,1)S(1)}, u32[]{:S(2)}, u32[]{:S(2)}) collective-permute-start(bf16[128,512]{1,0:T(8,128)(2,1)S(1)} %get-tuple-element.76), channel_id=1, source_target_pairs={{0,24},{1,7},{2,26},{3,1},{4,28},{5,3},{6,30},{7,5},{8,0},{9,15},{... | collective-permute-start | bytes 393224 | tf_op jit(solution)/shard_map/ppermute | solution.py:45
  122.0 0.0 collective-permute-done.9.second
  122.0 0.4 collective-permute-done.10.third
  122.4 1.5 %collective-permute-done.11.fourth = bf16[128,512]{1,0:T(8,128)(2,1)S(1)} collective-permute-done((bf16[128,512]{1,0:T(8,128)(2,1)S(1)}, bf16[128,512]{1,0:T(8,128)(2,1)S(1)}, u32[]{:S(2)}, u32[]{:S(2)}) %collective-permute-start.11) | collective-permute-done | bytes 131104 | tf_op jit(solution)/shard_map/ppermute | solution.py:45
  123.9 0.8 collect.1
  124.7 10.2 %all-to-all-start.3 = ((f32[32,1,128]{2,1,0:T(1,128)}), f32[32,1,128]{2,1,0:T(1,128)S(1)}, u32[]{:S(2)}, u32[]{:S(2)}) async-start(f32[32,1,128]{2,1,0:T(1,128)} %bitcast.11), calls=%async_computation.3 | async-start | bytes 32768 | tf_op jit(solution)/shard_map/all_to_all | solution.py:100
  134.9 9.3 %all-to-all-done.3 = f32[32,1,128]{2,1,0:T(1,128)S(1)} async-done(((f32[32,1,128]{2,1,0:T(1,128)}), f32[32,1,128]{2,1,0:T(1,128)S(1)}, u32[]{:S(2)}, u32[]{:S(2)}) %all-to-all-start.3) | async-done | bytes 16416 | tf_op jit(solution)/shard_map/all_to_all | solution.py:100
  144.2 0.7 clip.1
  144.9 0.7 copy.12
  (1 shorter events, 0.0 us)
Async XLA Ops:
  2.4 18.1 %collective-permute-start = (bf16[384,4096]{1,0:T(8,128)(2,1)}, bf16[384,4096]{1,0:T(8,128)(2,1)S(1)}, u32[]{:S(2)}, u32[]{:S(2)}) collective-permute-start(bf16[384,4096]{1,0:T(8,128)(2,1)} %bitcast.29), channel_id=1, source_target_pairs={{0,1},{1,0},{2,3},{3,2},{4,5},{5,4},{6,7},{7,6},{8,9},{9,8},{10,11... | collective-permute-start | bytes 9437192 | tf_op jit(solution)/shard_map/ppermute | solution.py:31
  11.2 19.1 %all-to-all-start = ((bf16[4,128,512]{2,1,0:T(8,128)(2,1)}), bf16[4,128,512]{2,1,0:T(8,128)(2,1)}, u32[]{:S(2)}, u32[]{:S(2)}) async-start(bf16[4,128,512]{2,1,0:T(8,128)(2,1)} %broadcast_in_dim.18), calls=%async_computation | async-start | bytes 1048576 | tf_op jit(solution)/shard_map/all_to_all | solution.py:100
  15.3 11.5 %collective-permute-start.1 = (bf16[384,512]{1,0:T(8,128)(2,1)}, bf16[384,512]{1,0:T(8,128)(2,1)}, u32[]{:S(2)}, u32[]{:S(2)}) collective-permute-start(bf16[384,512]{1,0:T(8,128)(2,1)} %bitcast.24), channel_id=1, source_target_pairs={{0,1},{1,0},{2,3},{3,2},{4,5},{5,4},{6,7},{7,6},{8,9},{9,8},{10,11... | collective-permute-start | bytes 1179656 | tf_op jit(solution)/shard_map/ppermute | solution.py:31
  20.5 1.6 %copy-start.7 = (bf16[384,4096]{1,0:T(8,128)(2,1)}, bf16[384,4096]{1,0:T(8,128)(2,1)S(1)}, u32[]{:S(2)}) copy-start(bf16[384,4096]{1,0:T(8,128)(2,1)S(1)} %collective-permute-done.theirs_ref) | copy-start | bytes 9437188
  22.1 0.7 copy-start.6
  22.8 15.9 %copy-start = (bf16[131072]{0:T(1024)(128)(2,1)S(1)}, bf16[131072]{0:T(1024)(128)(2,1)}, u32[]{:S(2)}) copy-start(bf16[131072]{0:T(1024)(128)(2,1)} %param.11) | copy-start | bytes 786436
  30.2 28.5 %collective-permute-start.4 = (bf16[512,512]{1,0:T(8,128)(2,1)}, bf16[512,512]{1,0:T(8,128)(2,1)S(1)}, u32[]{:S(2)}, u32[]{:S(2)}) collective-permute-start(bf16[512,512]{1,0:T(8,128)(2,1)} %bitcast.2.refs_0_), channel_id=1, source_target_pairs={{0,2},{2,4},{4,6},{6,0},{1,3},{3,5},{5,7},{7,1},{8,10},{10,12},{12... | collective-permute-start | bytes 1572872 | tf_op jit(solution)/shard_map/ppermute | solution.py:31
  32.2 26.5 %collective-permute-start.3 = (bf16[512,512]{1,0:T(8,128)(2,1)}, bf16[512,512]{1,0:T(8,128)(2,1)S(1)}, u32[]{:S(2)}, u32[]{:S(2)}) collective-permute-start(bf16[512,512]{1,0:T(8,128)(2,1)} %bitcast.2.refs_0_), channel_id=1, source_target_pairs={{0,4},{2,6},{4,0},{6,2},{1,5},{3,7},{5,1},{7,3},{8,12},{10,14},{12... | collective-permute-start | bytes 1572872 | tf_op jit(solution)/shard_map/ppermute | solution.py:31
  34.4 25.8 %collective-permute-start.2 = (bf16[512,512]{1,0:T(8,128)(2,1)}, bf16[512,512]{1,0:T(8,128)(2,1)S(1)}, u32[]{:S(2)}, u32[]{:S(2)}) collective-permute-start(bf16[512,512]{1,0:T(8,128)(2,1)} %bitcast.2.refs_0_), channel_id=1, source_target_pairs={{0,6},{2,0},{4,2},{6,4},{1,7},{3,1},{5,3},{7,5},{8,14},{10,8},{12,... | collective-permute-start | bytes 1572872 | tf_op jit(solution)/shard_map/ppermute | solution.py:31
  38.7 1.0 copy-start.1
  58.7 11.7 %copy-start.4 = (bf16[1,384,512]{2,1,0:T(8,128)(2,1)S(1)}, bf16[1,384,512]{2,1,0:T(8,128)(2,1)}, u32[]{:S(2)}) copy-start(bf16[1,384,512]{2,1,0:T(8,128)(2,1)} %param.10) | copy-start | bytes 1179652
  63.0 23.4 %copy-start.5 = (f32[8192]{0:T(1024)S(1)}, f32[8192]{0:T(1024)}, u32[]{:S(2)}) copy-start(f32[8192]{0:T(1024)} %param.13) | copy-start | bytes 98308
  63.0 7.4 %collective-permute-start.5 = (f32[768,512]{1,0:T(8,128)S(1)}, f32[768,512]{1,0:T(8,128)S(1)}, u32[]{:S(2)}, u32[]{:S(2)}) collective-permute-start(f32[768,512]{1,0:T(8,128)S(1)} %product.1.mine_ref), channel_id=1, source_target_pairs={{0,1},{1,0},{2,3},{3,2},{4,5},{5,4},{6,7},{7,6},{8,9},{9,8},{10,11... | collective-permute-start | bytes 4718600 | tf_op jit(solution)/shard_map/ppermute | solution.py:31
  74.8 12.4 %copy-start.2 = (bf16[512,512]{1,0:T(8,128)(2,1)}, bf16[512,512]{1,0:T(8,128)(2,1)S(1)}, u32[]{:S(2)}) copy-start(bf16[512,512]{1,0:T(8,128)(2,1)S(1)} %get-tuple-element.62.first) | copy-start | bytes 1572868
  74.8 19.6 %collective-permute-start.6 = (bf16[512,512]{1,0:T(8,128)(2,1)}, bf16[512,512]{1,0:T(8,128)(2,1)S(1)}, u32[]{:S(2)}, u32[]{:S(2)}) collective-permute-start(bf16[512,512]{1,0:T(8,128)(2,1)} %get-tuple-element.63), channel_id=1, source_target_pairs={{0,4},{1,17},{2,6},{3,19},{4,0},{5,21},{6,2},{7,23},{8,12},{9,25},... | collective-permute-start | bytes 1572872 | tf_op jit(solution)/shard_map/ppermute | solution.py:45
  79.0 28.1 %collective-permute-start.7 = (bf16[512,512]{1,0:T(8,128)(2,1)}, bf16[512,512]{1,0:T(8,128)(2,1)S(1)}, u32[]{:S(2)}, u32[]{:S(2)}) collective-permute-start(bf16[512,512]{1,0:T(8,128)(2,1)} %get-tuple-element.64), channel_id=1, source_target_pairs={{0,2},{1,9},{2,4},{3,11},{4,6},{5,13},{6,0},{7,15},{8,10},{9,17},{... | collective-permute-start | bytes 1572872 | tf_op jit(solution)/shard_map/ppermute | solution.py:45
  83.2 23.9 %collective-permute-start.8 = (bf16[512,512]{1,0:T(8,128)(2,1)}, bf16[512,512]{1,0:T(8,128)(2,1)S(1)}, u32[]{:S(2)}, u32[]{:S(2)}) collective-permute-start(bf16[512,512]{1,0:T(8,128)(2,1)} %get-tuple-element.65), channel_id=1, source_target_pairs={{0,6},{1,25},{2,0},{3,27},{4,2},{5,29},{6,4},{7,31},{8,14},{9,1},{... | collective-permute-start | bytes 1572872 | tf_op jit(solution)/shard_map/ppermute | solution.py:45
  87.2 23.4 %all-to-all-start.2 = ((bf16[16,64,128]{2,1,0:T(8,128)(2,1)}), bf16[16,64,128]{2,1,0:T(8,128)(2,1)S(1)}, u32[]{:S(2)}, u32[]{:S(2)}) async-start(bf16[16,64,128]{2,1,0:T(8,128)(2,1)} %get-tuple-element.72), calls=%async_computation.2 | async-start | bytes 524288 | tf_op jit(solution)/shard_map/all_to_all | solution.py:100
  107.1 1.0 copy-start.3
  110.6 11.4 %collective-permute-start.9 = (bf16[128,512]{1,0:T(8,128)(2,1)S(1)}, bf16[128,512]{1,0:T(8,128)(2,1)S(1)}, u32[]{:S(2)}, u32[]{:S(2)}) collective-permute-start(bf16[128,512]{1,0:T(8,128)(2,1)S(1)} %get-tuple-element.74), channel_id=1, source_target_pairs={{0,16},{1,5},{2,18},{3,7},{4,20},{5,1},{6,22},{7,3},{8,24},{9,13},... | collective-permute-start | bytes 393224 | tf_op jit(solution)/shard_map/ppermute | solution.py:45
  115.5 6.9 %collective-permute-start.10 = (bf16[128,512]{1,0:T(8,128)(2,1)S(1)}, bf16[128,512]{1,0:T(8,128)(2,1)S(1)}, u32[]{:S(2)}, u32[]{:S(2)}) collective-permute-start(bf16[128,512]{1,0:T(8,128)(2,1)S(1)} %get-tuple-element.75), channel_id=1, source_target_pairs={{0,8},{1,3},{2,10},{3,5},{4,12},{5,7},{6,14},{7,1},{8,16},{9,11},{... | collective-permute-start | bytes 393224 | tf_op jit(solution)/shard_map/ppermute | solution.py:45
  117.6 6.3 %collective-permute-start.11 = (bf16[128,512]{1,0:T(8,128)(2,1)S(1)}, bf16[128,512]{1,0:T(8,128)(2,1)S(1)}, u32[]{:S(2)}, u32[]{:S(2)}) collective-permute-start(bf16[128,512]{1,0:T(8,128)(2,1)S(1)} %get-tuple-element.76), channel_id=1, source_target_pairs={{0,24},{1,7},{2,26},{3,1},{4,28},{5,3},{6,30},{7,5},{8,0},{9,15},{... | collective-permute-start | bytes 393224 | tf_op jit(solution)/shard_map/ppermute | solution.py:45
  124.7 19.5 %all-to-all-start.3 = ((f32[32,1,128]{2,1,0:T(1,128)}), f32[32,1,128]{2,1,0:T(1,128)S(1)}, u32[]{:S(2)}, u32[]{:S(2)}) async-start(f32[32,1,128]{2,1,0:T(1,128)} %bitcast.11), calls=%async_computation.3 | async-start | bytes 32768 | tf_op jit(solution)/shard_map/all_to_all | solution.py:100

commit v13 on v10

--- a/solution.py
+++ b/solution.py
@@ -55,7 +55,7 @@
 
 def arrange(order, inputs, theirs, feature_gain):
     tokens, features = inputs.shape
-    step = 32
+    step = 96
     block = pl.BlockSpec((step, features), lambda i: (i, 0))
     scaled = pl.pallas_call(
         arrange_kernel,
@@ -199,13 +199,48 @@
     block = (scaled.shape[1] // AXES["x"], mine.shape[1])
     return pl.pallas_call(
         gradient_kernel,
-        out_shape=(in_vmem(block, jnp.bfloat16),) * AXES["x"],
+        out_shape=(jax.ShapeDtypeStruct(block, jnp.bfloat16),) * AXES["x"],
         in_specs=[WHOLE] * 5,
         out_specs=(WHOLE,) * AXES["x"],
         scratch_shapes=[pltpu.VMEM(mine.shape, jnp.bfloat16)],
         compiler_params=pltpu.CompilerParams(vmem_limit_bytes=3 * VMEM_LIMIT),
         name="gradient",
     )(scaled, mine, theirs, *targets)
+
+
+def add_kernel(first, second, third, fourth, sum_ref):
+    sum_ref[...] = total([ref[...] for ref in (first, second, third, fourth)]).astype(
+        jnp.bfloat16
+    )
+
+
+def add(blocks):
+    return pl.pallas_call(
+        add_kernel,
+        out_shape=jax.ShapeDtypeStruct(blocks[0].shape, jnp.bfloat16),
+        in_specs=[WHOLE] * 4,
+        out_specs=WHOLE,
+        compiler_params=pltpu.CompilerParams(vmem_limit_bytes=VMEM_LIMIT),
+        name="add",
+    )(*blocks)
+
+
+def place_kernel(value_ref, placed_ref):
+    placed_ref[...] = value_ref[...]
+
+
+def place(value):
+    step = value.shape[0] // 4
+    block = pl.BlockSpec((step, value.shape[1]), lambda i: (i, 0))
+    return pl.pallas_call(
+        place_kernel,
+        grid=(4,),
+        out_shape=jax.ShapeDtypeStruct(value.shape, value.dtype),
+        in_specs=[block],
+        out_specs=block,
+        compiler_params=pltpu.CompilerParams(vmem_limit_bytes=VMEM_LIMIT),
+        name="place",
+    )(value)
 
 
 def collect_kernel(arrived_ref, gradient_ref, squares_ref):
@@ -277,10 +312,12 @@
     gradient[0], arrived = tied(gradient[0], arrived)
     new_momentum, copies = fragment_update(replica, arrived, global_frag, momentum)
     new_global = exchange(copies, REPLICA)
-    mine = total([gradient[0]] + [send(gradient[k], "x", k) for k in STEPS])
-    mine, new_global = tied(mine.astype(jnp.bfloat16), new_global)
+    mine = add([gradient[0]] + [send(gradient[k], "x", k) for k in STEPS])
+    mine, new_global = tied(mine, new_global)
     gradient, squares = collect(exchange(mine.reshape(AXES["y_hi"], rows, width), "y_hi"))
 
+    squares, new_global = tied(squares, new_global)
+    new_global = place(new_global.reshape(-1, QBLOCK))
     clipped_grad = clip(exchange(squares, FSDP), gradient, features * width)[None]
     return (clipped_grad, new_global.reshape(-1), new_momentum.reshape(-1))
 

time: 144 us -> 141 us (0.979)
  blocking collectives: 39.4 us -> 33.9 us
  waiting for transfers between devices: 23.4 us -> 26.1 us
  starting transfers between devices: 52.6 us -> 55 us
  Pallas kernels: 16.8 us -> 15 us
    all_to_all x2, blocking collectives: 39.4 us -> 33.9 us  [exchange(): return lax.all_to_all(parts, axis, split_axis=0, concat_axis=0, tiled=True)]
    pallas_call x1, Pallas kernels: 7.29 us -> 3.99 us  [arrange(): pl.pallas_call(arrange_kernel, grid=(tokens // step,), out_shape=jax.Shap...]
    all_to_all x3, waiting for transfers between devices: 9.42 us -> 11.5 us  [exchange(): return lax.all_to_all(parts, axis, split_axis=0, concat_axis=0, tiled=True)]
    all_to_all x3, starting transfers between devices: 21.1 us -> 22.9 us  [exchange(): return lax.all_to_all(parts, axis, split_axis=0, concat_axis=0, tiled=True)]
    pallas_call x1 -> x3, Pallas kernels: 3.67 us -> 5.24 us  [the longest x1 3.67 us: gradient_blocks(): pl.pallas_call(gradient_kernel, out_shape=(jax.ShapeDtypeStruct(block, jn...]
    unnamed x15 -> x16, local copies, waits for them, and re-layouts: 4.04 us -> 4.36 us
  transfers between devices with their start and end apart: 12 -> 12, of which waited for: 5 -> 5; matrix products, arithmetic and copies ran while one was open for 3% -> 2% of each run, Pallas kernels for 6% -> 5%
where the time goes in v13:
time: 141 us; the launch traced here: 140 us
  starting transfers between devices  55 us (39%)
  blocking collectives  33.9 us (24%)
  waiting for transfers between devices  26.1 us (19%)
  Pallas kernels  15 us (11%)
  local copies, waits for them, and re-layouts  6.1 us (4%)
  other arithmetic  3.21 us (2%)
    all_to_all x2, blocking collectives, exchange(): return lax.all_to_all(parts, axis, split_axis=0, concat_axis=0, tiled=True)  33.9 us
    ppermute x9, starting transfers between devices, send(): lax.ppermute(value, axis, [(i, (i + step) % size) for i in range(size)])  32.1 us
    all_to_all x3, starting transfers between devices, exchange(): return lax.all_to_all(parts, axis, split_axis=0, concat_axis=0, tiled=True)  22.9 us
    ppermute x9, waiting for transfers between devices, send(): lax.ppermute(value, axis, [(i, (i + step) % size) for i in range(size)])  14.6 us
    all_to_all x3, waiting for transfers between devices, exchange(): return lax.all_to_all(parts, axis, split_axis=0, concat_axis=0, tiled=True)  11.5 us
    unnamed x16, local copies, waits for them, and re-layouts  4.36 us
    pallas_call x1, Pallas kernels, arrange(): pl.pallas_call(arrange_kernel, grid=(tokens // step,), out_shape=jax.Shap...  3.99 us
    pallas_call x1, Pallas kernels, gradient_blocks(): pl.pallas_call(gradient_kernel, out_shape=(jax.ShapeDtypeStruct(block, jn...  3.67 us
  transfers between devices with their start and end apart: 12, of which 5 were waited for; matrix products, arithmetic and copies ran while one was open for 2% of the time, Pallas kernels for 5%

profile of v13, /device:TPU:1, one launch (start us, length us, event | category | flops | bytes accessed | tf_op | source)
XLA Modules:
  0.0 140.1 jit_solution(5712557995655228474)
XLA Ops:
  0.7 1.7 %broadcast_in_dim.18 = bf16[4,128,512]{2,1,0:T(8,128)(2,1)} broadcast(bf16[128,512]{1,0:T(8,128)(2,1)} %bitcast.36), dimensions={1,2} | broadcast | bytes 655360 | tf_op jit(solution)/shard_map/broadcast_in_dim | solution.py:82
  2.4 8.8 %collective-permute-start = (bf16[384,4096]{1,0:T(8,128)(2,1)}, bf16[384,4096]{1,0:T(8,128)(2,1)S(1)}, u32[]{:S(2)}, u32[]{:S(2)}) collective-permute-start(bf16[384,4096]{1,0:T(8,128)(2,1)} %bitcast.33), channel_id=1, source_target_pairs={{0,1},{1,0},{2,3},{3,2},{4,5},{5,4},{6,7},{7,6},{8,9},{9,8},{10,11... | collective-permute-start | bytes 9437192 | tf_op jit(solution)/shard_map/ppermute | solution.py:31
  11.2 4.1 %all-to-all-start = ((bf16[4,128,512]{2,1,0:T(8,128)(2,1)}), bf16[4,128,512]{2,1,0:T(8,128)(2,1)}, u32[]{:S(2)}, u32[]{:S(2)}) async-start(bf16[4,128,512]{2,1,0:T(8,128)(2,1)} %broadcast_in_dim.18), calls=%async_computation | async-start | bytes 1048576 | tf_op jit(solution)/shard_map/all_to_all | solution.py:78
  15.3 1.9 %collective-permute-start.1 = (bf16[384,512]{1,0:T(8,128)(2,1)}, bf16[384,512]{1,0:T(8,128)(2,1)}, u32[]{:S(2)}, u32[]{:S(2)}) collective-permute-start(bf16[384,512]{1,0:T(8,128)(2,1)} %bitcast.28), channel_id=1, source_target_pairs={{0,1},{1,0},{2,3},{3,2},{4,5},{5,4},{6,7},{7,6},{8,9},{9,8},{10,11... | collective-permute-start | bytes 1179656 | tf_op jit(solution)/shard_map/ppermute | solution.py:31
  17.3 3.2 %reduce = bf16[131072]{0:T(1024)(128)(2,1)} reduce(bf16[1,131072]{1,0:T(2,128)(2,1)} %param.12, bf16[]{:T(256)} %constant.61), dimensions={0}, to_apply=%param.12.reduce_sub_computation | reduce | bytes 524290 | tf_op args[5]
  20.5 0.0 collective-permute-done.theirs_ref
  20.5 0.0 copy-start.7
  20.5 1.6 %copy-done.7 = bf16[384,4096]{1,0:T(8,128)(2,1)} copy-done((bf16[384,4096]{1,0:T(8,128)(2,1)}, bf16[384,4096]{1,0:T(8,128)(2,1)S(1)}, u32[]{:S(2)}) %copy-start.7) | copy-done | bytes 3145752
  22.1 0.0 copy-start.6
  22.1 0.7 copy-done.6
  22.8 0.0 copy-start
  22.8 4.0 %arrange.1 = bf16[2,384,2048]{2,1,0:T(8,128)(2,1)S(1)} custom-call(s32[16]{0:T(128)S(1)} %fusion.5.order_ref, bf16[384,4096]{1,0:T(8,128)(2,1)} %bitcast.34, bf16[384,4096]{1,0:T(8,128)(2,1)} %copy-done.7, f32[1,4096]{1,0:T(1,128)S(1)} %bitcast.32), custom_call_target="tpu_custom_call" | custom-call | tf_op jit(solution)/shard_map/arrange/pallas_call | solution.py:60
  26.8 0.0 collective-permute-done.1.refs_1_
  26.8 3.4 %all-to-all-done = bf16[4,128,512]{2,1,0:T(8,128)(2,1)} async-done(((bf16[4,128,512]{2,1,0:T(8,128)(2,1)}), bf16[4,128,512]{2,1,0:T(8,128)(2,1)}, u32[]{:S(2)}, u32[]{:S(2)}) %all-to-all-start) | async-done | bytes 524320 | tf_op jit(solution)/shard_map/all_to_all | solution.py:78
  30.2 1.9 %collective-permute-start.4 = (bf16[512,512]{1,0:T(8,128)(2,1)}, bf16[512,512]{1,0:T(8,128)(2,1)S(1)}, u32[]{:S(2)}, u32[]{:S(2)}) collective-permute-start(bf16[512,512]{1,0:T(8,128)(2,1)} %bitcast.2.refs_0_), channel_id=1, source_target_pairs={{0,2},{2,4},{4,6},{6,0},{1,3},{3,5},{5,7},{7,1},{8,10},{10,12},{12... | collective-permute-start | bytes 1572872 | tf_op jit(solution)/shard_map/ppermute | solution.py:31
  32.2 2.2 %collective-permute-start.3 = (bf16[512,512]{1,0:T(8,128)(2,1)}, bf16[512,512]{1,0:T(8,128)(2,1)S(1)}, u32[]{:S(2)}, u32[]{:S(2)}) collective-permute-start(bf16[512,512]{1,0:T(8,128)(2,1)} %bitcast.2.refs_0_), channel_id=1, source_target_pairs={{0,4},{2,6},{4,0},{6,2},{1,5},{3,7},{5,1},{7,3},{8,12},{10,14},{12... | collective-permute-start | bytes 1572872 | tf_op jit(solution)/shard_map/ppermute | solution.py:31
  34.4 4.2 %collective-permute-start.2 = (bf16[512,512]{1,0:T(8,128)(2,1)}, bf16[512,512]{1,0:T(8,128)(2,1)S(1)}, u32[]{:S(2)}, u32[]{:S(2)}) collective-permute-start(bf16[512,512]{1,0:T(8,128)(2,1)} %bitcast.2.refs_0_), channel_id=1, source_target_pairs={{0,6},{2,0},{4,2},{6,4},{1,7},{3,1},{5,3},{7,5},{8,14},{10,8},{12,... | collective-permute-start | bytes 1572872 | tf_op jit(solution)/shard_map/ppermute | solution.py:31
  38.7 0.0 copy-done
  38.7 0.0 copy-start.1
  38.7 0.9 copy-done.1
  39.6 0.7 codes.1
  40.3 18.4 %all_to_all.31.arrived_ref = bf16[16,64,128]{2,1,0:T(8,128)(2,1)S(1)} all-to-all(bf16[16,64,128]{2,1,0:T(8,128)(2,1)S(1)} %bitcast.25), channel_id=1, replica_groups=mesh['z'=8,'y_lo'=2,'y_hi'=4,'x'=4,'core'=2] {'z','y_lo'}, dimensions={0} | all-to-all | bytes 524288 | tf_op jit(solution)/shard_map/all_to_all | solution.py:78
  58.7 0.0 copy-start.4
  58.7 0.0 collective-permute-done.4.refs_3_
  58.7 0.0 collective-permute-done.3.refs_2_
  58.7 1.5 %collective-permute-done.2.refs_1_ = bf16[512,512]{1,0:T(8,128)(2,1)S(1)} collective-permute-done((bf16[512,512]{1,0:T(8,128)(2,1)}, bf16[512,512]{1,0:T(8,128)(2,1)S(1)}, u32[]{:S(2)}, u32[]{:S(2)}) %collective-permute-start.2) | collective-permute-done | bytes 524320 | tf_op jit(solution)/shard_map/ppermute | solution.py:31
  60.2 2.8 %product.1.mine_ref = f32[768,512]{1,0:T(8,128)S(1)} custom-call(bf16[768,2048]{1,0:T(8,128)(2,1)S(1)} %bitcast.20, bf16[512,512]{1,0:T(8,128)(2,1)} %bitcast.2.refs_0_, bf16[512,512]{1,0:T(8,128)(2,1)S(1)} %collective-permute-done.2.refs_1_, bf16[512,512]{1,0:T(8,128)(2,1)S(1)} %collective-permute-done.3.refs_2_, ...), custom_call_target="tpu_custom_call" | custom-call | tf_op jit(solution)/shard_map/product/pallas_call | solution.py:169
  63.0 0.0 copy-start.5
  63.0 4.4 %collective-permute-start.5 = (f32[768,512]{1,0:T(8,128)S(1)}, f32[768,512]{1,0:T(8,128)S(1)}, u32[]{:S(2)}, u32[]{:S(2)}) collective-permute-start(f32[768,512]{1,0:T(8,128)S(1)} %product.1.mine_ref), channel_id=1, source_target_pairs={{0,1},{1,0},{2,3},{3,2},{4,5},{5,4},{6,7},{7,6},{8,9},{9,8},{10,11... | collective-permute-start | bytes 4718600 | tf_op jit(solution)/shard_map/ppermute | solution.py:31
  67.4 3.0 %collective-permute-done.5.theirs_ref = f32[768,512]{1,0:T(8,128)S(1)} collective-permute-done((f32[768,512]{1,0:T(8,128)S(1)}, f32[768,512]{1,0:T(8,128)S(1)}, u32[]{:S(2)}, u32[]{:S(2)}) %collective-permute-start.5) | collective-permute-done | bytes 1572896 | tf_op jit(solution)/shard_map/ppermute | solution.py:31
  70.4 0.0 copy-done.4
  70.4 3.7 %gradient.1 = (bf16[512,512]{1,0:T(8,128)(2,1)S(1)}, bf16[512,512]{1,0:T(8,128)(2,1)}, bf16[512,512]{1,0:T(8,128)(2,1)}, bf16[512,512]{1,0:T(8,128)(2,1)}) custom-call(bf16[768,2048]{1,0:T(8,128)(2,1)S(1)} %bitcast.21, f32[768,512]{1,0:T(8,128)S(1)} %product.1.mine_ref, f32[768,512]{1,0:T(8,128)S(1)} %collective-permute-done.5.theirs_ref, ...), custom_call_target="tpu_custom_call" | custom-call | tf_op jit(solution)/shard_map/gradient/pallas_call | solution.py:200
  74.1 0.0 copy-start.2
  74.1 2.1 %collective-permute-start.6 = (bf16[512,512]{1,0:T(8,128)(2,1)}, bf16[512,512]{1,0:T(8,128)(2,1)S(1)}, u32[]{:S(2)}, u32[]{:S(2)}) collective-permute-start(bf16[512,512]{1,0:T(8,128)(2,1)} %get-tuple-element.54), channel_id=1, source_target_pairs={{0,4},{2,6},{4,0},{6,2},{1,5},{3,7},{5,1},{7,3},{8,12},{10,14},{12... | collective-permute-start | bytes 1572872 | tf_op jit(solution)/shard_map/ppermute | solution.py:31
  76.2 3.6 %collective-permute-start.7 = (bf16[512,512]{1,0:T(8,128)(2,1)}, bf16[512,512]{1,0:T(8,128)(2,1)S(1)}, u32[]{:S(2)}, u32[]{:S(2)}) collective-permute-start(bf16[512,512]{1,0:T(8,128)(2,1)} %get-tuple-element.55), channel_id=1, source_target_pairs={{0,2},{2,4},{4,6},{6,0},{1,3},{3,5},{5,7},{7,1},{8,10},{10,12},{12... | collective-permute-start | bytes 1572872 | tf_op jit(solution)/shard_map/ppermute | solution.py:31
  79.9 2.9 %collective-permute-start.8 = (bf16[512,512]{1,0:T(8,128)(2,1)}, bf16[512,512]{1,0:T(8,128)(2,1)S(1)}, u32[]{:S(2)}, u32[]{:S(2)}) collective-permute-start(bf16[512,512]{1,0:T(8,128)(2,1)} %get-tuple-element.56), channel_id=1, source_target_pairs={{0,6},{2,0},{4,2},{6,4},{1,7},{3,1},{5,3},{7,5},{8,14},{10,8},{12,... | collective-permute-start | bytes 1572872 | tf_op jit(solution)/shard_map/ppermute | solution.py:31
  82.7 0.0 copy-done.5
  82.8 0.8 update.1
  83.5 0.0 copy-done.2
  83.5 9.1 %all-to-all-start.2 = ((bf16[16,64,128]{2,1,0:T(8,128)(2,1)}), bf16[16,64,128]{2,1,0:T(8,128)(2,1)S(1)}, u32[]{:S(2)}, u32[]{:S(2)}) async-start(bf16[16,64,128]{2,1,0:T(8,128)(2,1)} %get-tuple-element.59), calls=%async_computation.2 | async-start | bytes 524288 | tf_op jit(solution)/shard_map/all_to_all | solution.py:78
  92.6 0.0 collective-permute-done.6.second
  92.7 10.1 %collective-permute-done.7.third = bf16[512,512]{1,0:T(8,128)(2,1)S(1)} collective-permute-done((bf16[512,512]{1,0:T(8,128)(2,1)}, bf16[512,512]{1,0:T(8,128)(2,1)S(1)}, u32[]{:S(2)}, u32[]{:S(2)}) %collective-permute-start.7) | collective-permute-done | bytes 524320 | tf_op jit(solution)/shard_map/ppermute | solution.py:31
  102.8 0.0 collective-permute-done.8.fourth
  102.8 0.0 copy-start.3
  102.8 1.0 copy-done.3
  103.8 0.3 add.70
  104.1 0.0 all-to-all-done.2
  104.1 15.5 %all_to_all.32.arrived_ref = bf16[4,128,512]{2,1,0:T(8,128)(2,1)S(1)} all-to-all(bf16[4,128,512]{2,1,0:T(8,128)(2,1)S(1)} %bitcast.22), channel_id=1, replica_groups=mesh['z'=8,'y_lo'=2,'y_hi'=4,'x'=4,'core'=2] {'y_hi'}, dimensions={0} | all-to-all | bytes 1048576 | tf_op jit(solution)/shard_map/all_to_all | solution.py:78
  119.6 0.8 collect.1
  120.4 9.6 %all-to-all-start.4 = ((f32[32,1,128]{2,1,0:T(1,128)}), f32[32,1,128]{2,1,0:T(1,128)S(1)}, u32[]{:S(2)}, u32[]{:S(2)}) async-start(f32[32,1,128]{2,1,0:T(1,128)} %bitcast.12), calls=%async_computation.4 | async-start | bytes 32768 | tf_op jit(solution)/shard_map/all_to_all | solution.py:78
  130.0 1.3 place.1
  131.4 8.1 %all-to-all-done.4 = f32[32,1,128]{2,1,0:T(1,128)S(1)} async-done(((f32[32,1,128]{2,1,0:T(1,128)}), f32[32,1,128]{2,1,0:T(1,128)S(1)}, u32[]{:S(2)}, u32[]{:S(2)}) %all-to-all-start.4) | async-done | bytes 16416 | tf_op jit(solution)/shard_map/all_to_all | solution.py:78
  139.4 0.7 clip.1
  (1 shorter events, 0.0 us)
Async XLA Ops:
  2.4 18.1 %collective-permute-start = (bf16[384,4096]{1,0:T(8,128)(2,1)}, bf16[384,4096]{1,0:T(8,128)(2,1)S(1)}, u32[]{:S(2)}, u32[]{:S(2)}) collective-permute-start(bf16[384,4096]{1,0:T(8,128)(2,1)} %bitcast.33), channel_id=1, source_target_pairs={{0,1},{1,0},{2,3},{3,2},{4,5},{5,4},{6,7},{7,6},{8,9},{9,8},{10,11... | collective-permute-start | bytes 9437192 | tf_op jit(solution)/shard_map/ppermute | solution.py:31
  11.2 19.1 %all-to-all-start = ((bf16[4,128,512]{2,1,0:T(8,128)(2,1)}), bf16[4,128,512]{2,1,0:T(8,128)(2,1)}, u32[]{:S(2)}, u32[]{:S(2)}) async-start(bf16[4,128,512]{2,1,0:T(8,128)(2,1)} %broadcast_in_dim.18), calls=%async_computation | async-start | bytes 1048576 | tf_op jit(solution)/shard_map/all_to_all | solution.py:78
  15.3 11.5 %collective-permute-start.1 = (bf16[384,512]{1,0:T(8,128)(2,1)}, bf16[384,512]{1,0:T(8,128)(2,1)}, u32[]{:S(2)}, u32[]{:S(2)}) collective-permute-start(bf16[384,512]{1,0:T(8,128)(2,1)} %bitcast.28), channel_id=1, source_target_pairs={{0,1},{1,0},{2,3},{3,2},{4,5},{5,4},{6,7},{7,6},{8,9},{9,8},{10,11... | collective-permute-start | bytes 1179656 | tf_op jit(solution)/shard_map/ppermute | solution.py:31
  20.5 1.6 %copy-start.7 = (bf16[384,4096]{1,0:T(8,128)(2,1)}, bf16[384,4096]{1,0:T(8,128)(2,1)S(1)}, u32[]{:S(2)}) copy-start(bf16[384,4096]{1,0:T(8,128)(2,1)S(1)} %collective-permute-done.theirs_ref) | copy-start | bytes 9437188
  22.1 0.7 copy-start.6
  22.8 15.8 %copy-start = (bf16[131072]{0:T(1024)(128)(2,1)S(1)}, bf16[131072]{0:T(1024)(128)(2,1)}, u32[]{:S(2)}) copy-start(bf16[131072]{0:T(1024)(128)(2,1)} %param.11) | copy-start | bytes 786436
  30.2 28.5 %collective-permute-start.4 = (bf16[512,512]{1,0:T(8,128)(2,1)}, bf16[512,512]{1,0:T(8,128)(2,1)S(1)}, u32[]{:S(2)}, u32[]{:S(2)}) collective-permute-start(bf16[512,512]{1,0:T(8,128)(2,1)} %bitcast.2.refs_0_), channel_id=1, source_target_pairs={{0,2},{2,4},{4,6},{6,0},{1,3},{3,5},{5,7},{7,1},{8,10},{10,12},{12... | collective-permute-start | bytes 1572872 | tf_op jit(solution)/shard_map/ppermute | solution.py:31
  32.2 26.5 %collective-permute-start.3 = (bf16[512,512]{1,0:T(8,128)(2,1)}, bf16[512,512]{1,0:T(8,128)(2,1)S(1)}, u32[]{:S(2)}, u32[]{:S(2)}) collective-permute-start(bf16[512,512]{1,0:T(8,128)(2,1)} %bitcast.2.refs_0_), channel_id=1, source_target_pairs={{0,4},{2,6},{4,0},{6,2},{1,5},{3,7},{5,1},{7,3},{8,12},{10,14},{12... | collective-permute-start | bytes 1572872 | tf_op jit(solution)/shard_map/ppermute | solution.py:31
  34.4 25.8 %collective-permute-start.2 = (bf16[512,512]{1,0:T(8,128)(2,1)}, bf16[512,512]{1,0:T(8,128)(2,1)S(1)}, u32[]{:S(2)}, u32[]{:S(2)}) collective-permute-start(bf16[512,512]{1,0:T(8,128)(2,1)} %bitcast.2.refs_0_), channel_id=1, source_target_pairs={{0,6},{2,0},{4,2},{6,4},{1,7},{3,1},{5,3},{7,5},{8,14},{10,8},{12,... | collective-permute-start | bytes 1572872 | tf_op jit(solution)/shard_map/ppermute | solution.py:31
  38.7 1.0 copy-start.1
  58.7 11.7 %copy-start.4 = (bf16[1,384,512]{2,1,0:T(8,128)(2,1)S(1)}, bf16[1,384,512]{2,1,0:T(8,128)(2,1)}, u32[]{:S(2)}) copy-start(bf16[1,384,512]{2,1,0:T(8,128)(2,1)} %param.10) | copy-start | bytes 1179652
  63.0 19.7 %copy-start.5 = (f32[8192]{0:T(1024)S(1)}, f32[8192]{0:T(1024)}, u32[]{:S(2)}) copy-start(f32[8192]{0:T(1024)} %param.13) | copy-start | bytes 98308
  63.0 7.4 %collective-permute-start.5 = (f32[768,512]{1,0:T(8,128)S(1)}, f32[768,512]{1,0:T(8,128)S(1)}, u32[]{:S(2)}, u32[]{:S(2)}) collective-permute-start(f32[768,512]{1,0:T(8,128)S(1)} %product.1.mine_ref), channel_id=1, source_target_pairs={{0,1},{1,0},{2,3},{3,2},{4,5},{5,4},{6,7},{7,6},{8,9},{9,8},{10,11... | collective-permute-start | bytes 4718600 | tf_op jit(solution)/shard_map/ppermute | solution.py:31
  74.1 9.4 %copy-start.2 = (bf16[512,512]{1,0:T(8,128)(2,1)}, bf16[512,512]{1,0:T(8,128)(2,1)S(1)}, u32[]{:S(2)}) copy-start(bf16[512,512]{1,0:T(8,128)(2,1)S(1)} %get-tuple-element.53.first) | copy-start | bytes 1572868
  74.1 18.5 %collective-permute-start.6 = (bf16[512,512]{1,0:T(8,128)(2,1)}, bf16[512,512]{1,0:T(8,128)(2,1)S(1)}, u32[]{:S(2)}, u32[]{:S(2)}) collective-permute-start(bf16[512,512]{1,0:T(8,128)(2,1)} %get-tuple-element.54), channel_id=1, source_target_pairs={{0,4},{2,6},{4,0},{6,2},{1,5},{3,7},{5,1},{7,3},{8,12},{10,14},{12... | collective-permute-start | bytes 1572872 | tf_op jit(solution)/shard_map/ppermute | solution.py:31
  76.2 26.5 %collective-permute-start.7 = (bf16[512,512]{1,0:T(8,128)(2,1)}, bf16[512,512]{1,0:T(8,128)(2,1)S(1)}, u32[]{:S(2)}, u32[]{:S(2)}) collective-permute-start(bf16[512,512]{1,0:T(8,128)(2,1)} %get-tuple-element.55), channel_id=1, source_target_pairs={{0,2},{2,4},{4,6},{6,0},{1,3},{3,5},{5,7},{7,1},{8,10},{10,12},{12... | collective-permute-start | bytes 1572872 | tf_op jit(solution)/shard_map/ppermute | solution.py:31
  79.9 22.9 %collective-permute-start.8 = (bf16[512,512]{1,0:T(8,128)(2,1)}, bf16[512,512]{1,0:T(8,128)(2,1)S(1)}, u32[]{:S(2)}, u32[]{:S(2)}) collective-permute-start(bf16[512,512]{1,0:T(8,128)(2,1)} %get-tuple-element.56), channel_id=1, source_target_pairs={{0,6},{2,0},{4,2},{6,4},{1,7},{3,1},{5,3},{7,5},{8,14},{10,8},{12,... | collective-permute-start | bytes 1572872 | tf_op jit(solution)/shard_map/ppermute | solution.py:31
  83.5 20.5 %all-to-all-start.2 = ((bf16[16,64,128]{2,1,0:T(8,128)(2,1)}), bf16[16,64,128]{2,1,0:T(8,128)(2,1)S(1)}, u32[]{:S(2)}, u32[]{:S(2)}) async-start(bf16[16,64,128]{2,1,0:T(8,128)(2,1)} %get-tuple-element.59), calls=%async_computation.2 | async-start | bytes 524288 | tf_op jit(solution)/shard_map/all_to_all | solution.py:78
  102.8 1.0 copy-start.3
  120.4 19.0 %all-to-all-start.4 = ((f32[32,1,128]{2,1,0:T(1,128)}), f32[32,1,128]{2,1,0:T(1,128)S(1)}, u32[]{:S(2)}, u32[]{:S(2)}) async-start(f32[32,1,128]{2,1,0:T(1,128)} %bitcast.12), calls=%async_computation.4 | async-start | bytes 32768 | tf_op jit(solution)/shard_map/all_to_all | solution.py:78

commit v14 on v13

--- a/solution.py
+++ b/solution.py
@@ -300,11 +300,9 @@
     raw = send(inputs[0], "core", 1)
     targets = (teacher_keys[0], send(teacher_keys[0], "core", 1))
     scaled = arrange(order, inputs[0], raw, feature_gain)
-    column, scaled, targets, global_frag, local_frag, replica = tied(
-        column, scaled, targets, global_frag, local_frag, replica
-    )
+    decoded = fragment_codes(global_frag, local_frag)
+    column, scaled, targets, decoded, replica = tied(column, scaled, targets, decoded, replica)
     far = [column] + [send(column, "x", -k) for k in (1, 2, 3)]
-    decoded = fragment_codes(global_frag, local_frag)
     arrived = exchange(decoded.reshape(replicas, -1, QBLOCK), REPLICA)
     far, arrived = tied(far, arrived)
     partial = product(scaled, far)

time: 141 us -> 141 us (level)
  local copies, waits for them, and re-layouts: 6.1 us -> 3.75 us
  waiting for transfers between devices: 26.1 us -> 28.2 us
    unnamed x16 -> x14, local copies, waits for them, and re-layouts: 4.36 us -> 2.01 us
  transfers between devices with their start and end apart: 12 -> 12, of which waited for: 5 -> 6; matrix products, arithmetic and copies ran while one was open for 2% -> 2% of each run, Pallas kernels for 5% -> 5%
where the time goes in v14:
time: 141 us; the launch traced here: 140 us
  starting transfers between devices  55.8 us (40%)
  blocking collectives  34.1 us (24%)
  waiting for transfers between devices  28.2 us (20%)
  Pallas kernels  15 us (11%)
  local copies, waits for them, and re-layouts  3.75 us (3%)
  other arithmetic  2.51 us (2%)
    all_to_all x2, blocking collectives, exchange(): return lax.all_to_all(parts, axis, split_axis=0, concat_axis=0, tiled=True)  34.1 us
    ppermute x9, starting transfers between devices, send(): lax.ppermute(value, axis, [(i, (i + step) % size) for i in range(size)])  31.6 us
    all_to_all x3, starting transfers between devices, exchange(): return lax.all_to_all(parts, axis, split_axis=0, concat_axis=0, tiled=True)  24.2 us
    ppermute x9, waiting for transfers between devices, send(): lax.ppermute(value, axis, [(i, (i + step) % size) for i in range(size)])  15.4 us
    all_to_all x3, waiting for transfers between devices, exchange(): return lax.all_to_all(parts, axis, split_axis=0, concat_axis=0, tiled=True)  12.8 us
    pallas_call x1, Pallas kernels, arrange(): pl.pallas_call(arrange_kernel, grid=(tokens // step,), out_shape=jax.Shap...  3.96 us
    pallas_call x1, Pallas kernels, gradient_blocks(): pl.pallas_call(gradient_kernel, out_shape=(jax.ShapeDtypeStruct(block, jn...  3.67 us
    pallas_call x1, Pallas kernels, product(): pl.pallas_call(product_kernel, out_shape=in_vmem((scaled.shape[0], weight...  2.82 us
  transfers between devices with their start and end apart: 12, of which 6 were waited for; matrix products, arithmetic and copies ran while one was open for 2% of the time, Pallas kernels for 5%

profile of v14, /device:TPU:1, one launch (start us, length us, event | category | flops | bytes accessed | tf_op | source)
XLA Modules:
  0.0 140.2 jit_solution(8009855889283398135)
XLA Ops:
  0.6 0.0 copy-start.6
  0.7 1.7 %broadcast_in_dim.18 = bf16[4,128,512]{2,1,0:T(8,128)(2,1)} broadcast(bf16[128,512]{1,0:T(8,128)(2,1)} %bitcast.36), dimensions={1,2} | broadcast | bytes 655360 | tf_op jit(solution)/shard_map/broadcast_in_dim | solution.py:82
  2.4 8.8 %collective-permute-start = (bf16[384,4096]{1,0:T(8,128)(2,1)}, bf16[384,4096]{1,0:T(8,128)(2,1)}, u32[]{:S(2)}, u32[]{:S(2)}) collective-permute-start(bf16[384,4096]{1,0:T(8,128)(2,1)} %bitcast.33), channel_id=1, source_target_pairs={{0,1},{1,0},{2,3},{3,2},{4,5},{5,4},{6,7},{7,6},{8,9},{9,8},{10,11... | collective-permute-start | bytes 9437192 | tf_op jit(solution)/shard_map/ppermute | solution.py:31
  11.2 4.2 %all-to-all-start = ((bf16[4,128,512]{2,1,0:T(8,128)(2,1)}), bf16[4,128,512]{2,1,0:T(8,128)(2,1)}, u32[]{:S(2)}, u32[]{:S(2)}) async-start(bf16[4,128,512]{2,1,0:T(8,128)(2,1)} %broadcast_in_dim.18), calls=%async_computation | async-start | bytes 1048576 | tf_op jit(solution)/shard_map/all_to_all | solution.py:78
  15.4 1.9 %collective-permute-start.1 = (bf16[384,512]{1,0:T(8,128)(2,1)}, bf16[384,512]{1,0:T(8,128)(2,1)}, u32[]{:S(2)}, u32[]{:S(2)}) collective-permute-start(bf16[384,512]{1,0:T(8,128)(2,1)} %bitcast.28), channel_id=1, source_target_pairs={{0,1},{1,0},{2,3},{3,2},{4,5},{5,4},{6,7},{7,6},{8,9},{9,8},{10,11... | collective-permute-start | bytes 1179656 | tf_op jit(solution)/shard_map/ppermute | solution.py:31
  17.3 2.5 %reduce = bf16[131072]{0:T(1024)(128)(2,1)S(1)} reduce(bf16[1,131072]{1,0:T(2,128)(2,1)} %param.12, bf16[]{:T(256)} %constant.61), dimensions={0}, to_apply=%param.12.reduce_sub_computation | reduce | bytes 524290 | tf_op args[5]
  19.8 0.0 copy-start
  19.8 0.9 copy-done
  20.7 0.7 codes.1
  21.5 0.0 collective-permute-done.theirs_ref
  21.5 0.0 copy-done.6
  21.5 4.0 %arrange.1 = bf16[2,384,2048]{2,1,0:T(8,128)(2,1)S(1)} custom-call(s32[16]{0:T(128)S(1)} %fusion.5.order_ref, bf16[384,4096]{1,0:T(8,128)(2,1)} %bitcast.34, bf16[384,4096]{1,0:T(8,128)(2,1)} %collective-permute-done.theirs_ref, f32[1,4096]{1,0:T(1,128)S(1)} %bitcast.32), custom_call_target="tpu_custom_call" | custom-call | tf_op jit(solution)/shard_map/arrange/pallas_call | solution.py:60
  25.4 0.0 collective-permute-done.1.refs_1_
  25.5 4.8 %all-to-all-done = bf16[4,128,512]{2,1,0:T(8,128)(2,1)} async-done(((bf16[4,128,512]{2,1,0:T(8,128)(2,1)}), bf16[4,128,512]{2,1,0:T(8,128)(2,1)}, u32[]{:S(2)}, u32[]{:S(2)}) %all-to-all-start) | async-done | bytes 524320 | tf_op jit(solution)/shard_map/all_to_all | solution.py:78
  30.3 1.9 %collective-permute-start.4 = (bf16[512,512]{1,0:T(8,128)(2,1)}, bf16[512,512]{1,0:T(8,128)(2,1)S(1)}, u32[]{:S(2)}, u32[]{:S(2)}) collective-permute-start(bf16[512,512]{1,0:T(8,128)(2,1)} %bitcast.2.refs_0_), channel_id=1, source_target_pairs={{0,2},{2,4},{4,6},{6,0},{1,3},{3,5},{5,7},{7,1},{8,10},{10,12},{12... | collective-permute-start | bytes 1572872 | tf_op jit(solution)/shard_map/ppermute | solution.py:31
  32.2 2.2 %collective-permute-start.3 = (bf16[512,512]{1,0:T(8,128)(2,1)}, bf16[512,512]{1,0:T(8,128)(2,1)S(1)}, u32[]{:S(2)}, u32[]{:S(2)}) collective-permute-start(bf16[512,512]{1,0:T(8,128)(2,1)} %bitcast.2.refs_0_), channel_id=1, source_target_pairs={{0,4},{2,6},{4,0},{6,2},{1,5},{3,7},{5,1},{7,3},{8,12},{10,14},{12... | collective-permute-start | bytes 1572872 | tf_op jit(solution)/shard_map/ppermute | solution.py:31
  34.4 4.3 %collective-permute-start.2 = (bf16[512,512]{1,0:T(8,128)(2,1)}, bf16[512,512]{1,0:T(8,128)(2,1)S(1)}, u32[]{:S(2)}, u32[]{:S(2)}) collective-permute-start(bf16[512,512]{1,0:T(8,128)(2,1)} %bitcast.2.refs_0_), channel_id=1, source_target_pairs={{0,6},{2,0},{4,2},{6,4},{1,7},{3,1},{5,3},{7,5},{8,14},{10,8},{12,... | collective-permute-start | bytes 1572872 | tf_op jit(solution)/shard_map/ppermute | solution.py:31
  38.7 18.3 %all_to_all.31.arrived_ref = bf16[16,64,128]{2,1,0:T(8,128)(2,1)S(1)} all-to-all(bf16[16,64,128]{2,1,0:T(8,128)(2,1)S(1)} %bitcast.25), channel_id=1, replica_groups=mesh['z'=8,'y_lo'=2,'y_hi'=4,'x'=4,'core'=2] {'z','y_lo'}, dimensions={0} | all-to-all | bytes 524288 | tf_op jit(solution)/shard_map/all_to_all | solution.py:78
  57.0 0.0 copy-start.4
  57.0 0.4 collective-permute-done.4.refs_3_
  57.5 0.0 collective-permute-done.3.refs_2_
  57.5 2.8 %collective-permute-done.2.refs_1_ = bf16[512,512]{1,0:T(8,128)(2,1)S(1)} collective-permute-done((bf16[512,512]{1,0:T(8,128)(2,1)}, bf16[512,512]{1,0:T(8,128)(2,1)S(1)}, u32[]{:S(2)}, u32[]{:S(2)}) %collective-permute-start.2) | collective-permute-done | bytes 524320 | tf_op jit(solution)/shard_map/ppermute | solution.py:31
  60.2 2.8 %product.1.mine_ref = f32[768,512]{1,0:T(8,128)S(1)} custom-call(bf16[768,2048]{1,0:T(8,128)(2,1)S(1)} %bitcast.20, bf16[512,512]{1,0:T(8,128)(2,1)} %bitcast.2.refs_0_, bf16[512,512]{1,0:T(8,128)(2,1)S(1)} %collective-permute-done.2.refs_1_, bf16[512,512]{1,0:T(8,128)(2,1)S(1)} %collective-permute-done.3.refs_2_, ...), custom_call_target="tpu_custom_call" | custom-call | tf_op jit(solution)/shard_map/product/pallas_call | solution.py:169
  63.1 0.0 copy-start.1
  63.1 0.0 copy-start.5
  63.1 3.5 %collective-permute-start.5 = (f32[768,512]{1,0:T(8,128)S(1)}, f32[768,512]{1,0:T(8,128)S(1)}, u32[]{:S(2)}, u32[]{:S(2)}) collective-permute-start(f32[768,512]{1,0:T(8,128)S(1)} %product.1.mine_ref), channel_id=1, source_target_pairs={{0,1},{1,0},{2,3},{3,2},{4,5},{5,4},{6,7},{7,6},{8,9},{9,8},{10,11... | collective-permute-start | bytes 4718600 | tf_op jit(solution)/shard_map/ppermute | solution.py:31
  66.6 3.0 %collective-permute-done.5.theirs_ref = f32[768,512]{1,0:T(8,128)S(1)} collective-permute-done((f32[768,512]{1,0:T(8,128)S(1)}, f32[768,512]{1,0:T(8,128)S(1)}, u32[]{:S(2)}, u32[]{:S(2)}) %collective-permute-start.5) | collective-permute-done | bytes 1572896 | tf_op jit(solution)/shard_map/ppermute | solution.py:31
  69.6 0.0 copy-done.4
  69.6 3.7 %gradient.1 = (bf16[512,512]{1,0:T(8,128)(2,1)S(1)}, bf16[512,512]{1,0:T(8,128)(2,1)}, bf16[512,512]{1,0:T(8,128)(2,1)}, bf16[512,512]{1,0:T(8,128)(2,1)}) custom-call(bf16[768,2048]{1,0:T(8,128)(2,1)S(1)} %bitcast.21, f32[768,512]{1,0:T(8,128)S(1)} %product.1.mine_ref, f32[768,512]{1,0:T(8,128)S(1)} %collective-permute-done.5.theirs_ref, ...), custom_call_target="tpu_custom_call" | custom-call | tf_op jit(solution)/shard_map/gradient/pallas_call | solution.py:200
  73.3 0.0 copy-start.2
  73.3 2.5 %collective-permute-start.6 = (bf16[512,512]{1,0:T(8,128)(2,1)}, bf16[512,512]{1,0:T(8,128)(2,1)S(1)}, u32[]{:S(2)}, u32[]{:S(2)}) collective-permute-start(bf16[512,512]{1,0:T(8,128)(2,1)} %get-tuple-element.52), channel_id=1, source_target_pairs={{0,4},{2,6},{4,0},{6,2},{1,5},{3,7},{5,1},{7,3},{8,12},{10,14},{12... | collective-permute-start | bytes 1572872 | tf_op jit(solution)/shard_map/ppermute | solution.py:31
  75.8 4.2 %collective-permute-start.7 = (bf16[512,512]{1,0:T(8,128)(2,1)}, bf16[512,512]{1,0:T(8,128)(2,1)S(1)}, u32[]{:S(2)}, u32[]{:S(2)}) collective-permute-start(bf16[512,512]{1,0:T(8,128)(2,1)} %get-tuple-element.53), channel_id=1, source_target_pairs={{0,2},{2,4},{4,6},{6,0},{1,3},{3,5},{5,7},{7,1},{8,10},{10,12},{12... | collective-permute-start | bytes 1572872 | tf_op jit(solution)/shard_map/ppermute | solution.py:31
  80.0 2.3 %collective-permute-start.8 = (bf16[512,512]{1,0:T(8,128)(2,1)}, bf16[512,512]{1,0:T(8,128)(2,1)S(1)}, u32[]{:S(2)}, u32[]{:S(2)}) collective-permute-start(bf16[512,512]{1,0:T(8,128)(2,1)} %get-tuple-element.54), channel_id=1, source_target_pairs={{0,6},{2,0},{4,2},{6,4},{1,7},{3,1},{5,3},{7,5},{8,14},{10,8},{12,... | collective-permute-start | bytes 1572872 | tf_op jit(solution)/shard_map/ppermute | solution.py:31
  82.3 0.0 copy-done.1
  82.3 0.0 copy-done.5
  82.3 0.8 update.1
  83.1 0.0 copy-done.2
  83.1 9.7 %all-to-all-start.2 = ((bf16[16,64,128]{2,1,0:T(8,128)(2,1)}), bf16[16,64,128]{2,1,0:T(8,128)(2,1)S(1)}, u32[]{:S(2)}, u32[]{:S(2)}) async-start(bf16[16,64,128]{2,1,0:T(8,128)(2,1)} %get-tuple-element.57), calls=%async_computation.2 | async-start | bytes 524288 | tf_op jit(solution)/shard_map/all_to_all | solution.py:78
  92.8 0.0 collective-permute-done.6.second
  92.8 9.1 %collective-permute-done.7.third = bf16[512,512]{1,0:T(8,128)(2,1)S(1)} collective-permute-done((bf16[512,512]{1,0:T(8,128)(2,1)}, bf16[512,512]{1,0:T(8,128)(2,1)S(1)}, u32[]{:S(2)}, u32[]{:S(2)}) %collective-permute-start.7) | collective-permute-done | bytes 524320 | tf_op jit(solution)/shard_map/ppermute | solution.py:31
  102.0 0.0 collective-permute-done.8.fourth
  102.0 0.0 copy-start.3
  102.0 1.0 copy-done.3
  103.0 0.3 add.70
  103.3 0.0 all-to-all-done.2
  103.3 15.8 %all_to_all.32.arrived_ref = bf16[4,128,512]{2,1,0:T(8,128)(2,1)S(1)} all-to-all(bf16[4,128,512]{2,1,0:T(8,128)(2,1)S(1)} %bitcast.22), channel_id=1, replica_groups=mesh['z'=8,'y_lo'=2,'y_hi'=4,'x'=4,'core'=2] {'y_hi'}, dimensions={0} | all-to-all | bytes 1048576 | tf_op jit(solution)/shard_map/all_to_all | solution.py:78
  119.1 0.8 collect.1
  119.9 10.3 %all-to-all-start.4 = ((f32[32,1,128]{2,1,0:T(1,128)}), f32[32,1,128]{2,1,0:T(1,128)S(1)}, u32[]{:S(2)}, u32[]{:S(2)}) async-start(f32[32,1,128]{2,1,0:T(1,128)} %bitcast.12), calls=%async_computation.4 | async-start | bytes 32768 | tf_op jit(solution)/shard_map/all_to_all | solution.py:78
  130.2 1.3 place.1
  131.5 8.0 %all-to-all-done.4 = f32[32,1,128]{2,1,0:T(1,128)S(1)} async-done(((f32[32,1,128]{2,1,0:T(1,128)}), f32[32,1,128]{2,1,0:T(1,128)S(1)}, u32[]{:S(2)}, u32[]{:S(2)}) %all-to-all-start.4) | async-done | bytes 16416 | tf_op jit(solution)/shard_map/all_to_all | solution.py:78
  139.5 0.7 clip.1
  (1 shorter events, 0.0 us)
Async XLA Ops:
  0.6 20.8 %copy-start.6 = (f32[4096]{0:T(1024)S(1)}, f32[4096]{0:T(1024)}, u32[]{:S(2)}) copy-start(f32[4096]{0:T(1024)} %param.8) | copy-start | bytes 49156
  2.4 19.1 %collective-permute-start = (bf16[384,4096]{1,0:T(8,128)(2,1)}, bf16[384,4096]{1,0:T(8,128)(2,1)}, u32[]{:S(2)}, u32[]{:S(2)}) collective-permute-start(bf16[384,4096]{1,0:T(8,128)(2,1)} %bitcast.33), channel_id=1, source_target_pairs={{0,1},{1,0},{2,3},{3,2},{4,5},{5,4},{6,7},{7,6},{8,9},{9,8},{10,11... | collective-permute-start | bytes 9437192 | tf_op jit(solution)/shard_map/ppermute | solution.py:31
  11.2 19.1 %all-to-all-start = ((bf16[4,128,512]{2,1,0:T(8,128)(2,1)}), bf16[4,128,512]{2,1,0:T(8,128)(2,1)}, u32[]{:S(2)}, u32[]{:S(2)}) async-start(bf16[4,128,512]{2,1,0:T(8,128)(2,1)} %broadcast_in_dim.18), calls=%async_computation | async-start | bytes 1048576 | tf_op jit(solution)/shard_map/all_to_all | solution.py:78
  15.4 10.1 %collective-permute-start.1 = (bf16[384,512]{1,0:T(8,128)(2,1)}, bf16[384,512]{1,0:T(8,128)(2,1)}, u32[]{:S(2)}, u32[]{:S(2)}) collective-permute-start(bf16[384,512]{1,0:T(8,128)(2,1)} %bitcast.28), channel_id=1, source_target_pairs={{0,1},{1,0},{2,3},{3,2},{4,5},{5,4},{6,7},{7,6},{8,9},{9,8},{10,11... | collective-permute-start | bytes 1179656 | tf_op jit(solution)/shard_map/ppermute | solution.py:31
  19.8 1.0 copy-start
  30.3 27.2 %collective-permute-start.4 = (bf16[512,512]{1,0:T(8,128)(2,1)}, bf16[512,512]{1,0:T(8,128)(2,1)S(1)}, u32[]{:S(2)}, u32[]{:S(2)}) collective-permute-start(bf16[512,512]{1,0:T(8,128)(2,1)} %bitcast.2.refs_0_), channel_id=1, source_target_pairs={{0,2},{2,4},{4,6},{6,0},{1,3},{3,5},{5,7},{7,1},{8,10},{10,12},{12... | collective-permute-start | bytes 1572872 | tf_op jit(solution)/shard_map/ppermute | solution.py:31
  32.2 25.3 %collective-permute-start.3 = (bf16[512,512]{1,0:T(8,128)(2,1)}, bf16[512,512]{1,0:T(8,128)(2,1)S(1)}, u32[]{:S(2)}, u32[]{:S(2)}) collective-permute-start(bf16[512,512]{1,0:T(8,128)(2,1)} %bitcast.2.refs_0_), channel_id=1, source_target_pairs={{0,4},{2,6},{4,0},{6,2},{1,5},{3,7},{5,1},{7,3},{8,12},{10,14},{12... | collective-permute-start | bytes 1572872 | tf_op jit(solution)/shard_map/ppermute | solution.py:31
  34.4 25.8 %collective-permute-start.2 = (bf16[512,512]{1,0:T(8,128)(2,1)}, bf16[512,512]{1,0:T(8,128)(2,1)S(1)}, u32[]{:S(2)}, u32[]{:S(2)}) collective-permute-start(bf16[512,512]{1,0:T(8,128)(2,1)} %bitcast.2.refs_0_), channel_id=1, source_target_pairs={{0,6},{2,0},{4,2},{6,4},{1,7},{3,1},{5,3},{7,5},{8,14},{10,8},{12,... | collective-permute-start | bytes 1572872 | tf_op jit(solution)/shard_map/ppermute | solution.py:31
  57.0 12.6 %copy-start.4 = (bf16[1,384,512]{2,1,0:T(8,128)(2,1)S(1)}, bf16[1,384,512]{2,1,0:T(8,128)(2,1)}, u32[]{:S(2)}) copy-start(bf16[1,384,512]{2,1,0:T(8,128)(2,1)} %param.10) | copy-start | bytes 1179652
  63.1 19.2 %copy-start.1 = (bf16[131072]{0:T(1024)(128)(2,1)S(1)}, bf16[131072]{0:T(1024)(128)(2,1)}, u32[]{:S(2)}) copy-start(bf16[131072]{0:T(1024)(128)(2,1)} %param.11) | copy-start | bytes 786436
  63.1 19.2 %copy-start.5 = (f32[8192]{0:T(1024)S(1)}, f32[8192]{0:T(1024)}, u32[]{:S(2)}) copy-start(f32[8192]{0:T(1024)} %param.13) | copy-start | bytes 98308
  63.1 6.5 %collective-permute-start.5 = (f32[768,512]{1,0:T(8,128)S(1)}, f32[768,512]{1,0:T(8,128)S(1)}, u32[]{:S(2)}, u32[]{:S(2)}) collective-permute-start(f32[768,512]{1,0:T(8,128)S(1)} %product.1.mine_ref), channel_id=1, source_target_pairs={{0,1},{1,0},{2,3},{3,2},{4,5},{5,4},{6,7},{7,6},{8,9},{9,8},{10,11... | collective-permute-start | bytes 4718600 | tf_op jit(solution)/shard_map/ppermute | solution.py:31
  73.3 9.8 %copy-start.2 = (bf16[512,512]{1,0:T(8,128)(2,1)}, bf16[512,512]{1,0:T(8,128)(2,1)S(1)}, u32[]{:S(2)}) copy-start(bf16[512,512]{1,0:T(8,128)(2,1)S(1)} %get-tuple-element.51.first) | copy-start | bytes 1572868
  73.3 19.5 %collective-permute-start.6 = (bf16[512,512]{1,0:T(8,128)(2,1)}, bf16[512,512]{1,0:T(8,128)(2,1)S(1)}, u32[]{:S(2)}, u32[]{:S(2)}) collective-permute-start(bf16[512,512]{1,0:T(8,128)(2,1)} %get-tuple-element.52), channel_id=1, source_target_pairs={{0,4},{2,6},{4,0},{6,2},{1,5},{3,7},{5,1},{7,3},{8,12},{10,14},{12... | collective-permute-start | bytes 1572872 | tf_op jit(solution)/shard_map/ppermute | solution.py:31
  75.8 26.2 %collective-permute-start.7 = (bf16[512,512]{1,0:T(8,128)(2,1)}, bf16[512,512]{1,0:T(8,128)(2,1)S(1)}, u32[]{:S(2)}, u32[]{:S(2)}) collective-permute-start(bf16[512,512]{1,0:T(8,128)(2,1)} %get-tuple-element.53), channel_id=1, source_target_pairs={{0,2},{2,4},{4,6},{6,0},{1,3},{3,5},{5,7},{7,1},{8,10},{10,12},{12... | collective-permute-start | bytes 1572872 | tf_op jit(solution)/shard_map/ppermute | solution.py:31
  80.0 21.9 %collective-permute-start.8 = (bf16[512,512]{1,0:T(8,128)(2,1)}, bf16[512,512]{1,0:T(8,128)(2,1)S(1)}, u32[]{:S(2)}, u32[]{:S(2)}) collective-permute-start(bf16[512,512]{1,0:T(8,128)(2,1)} %get-tuple-element.54), channel_id=1, source_target_pairs={{0,6},{2,0},{4,2},{6,4},{1,7},{3,1},{5,3},{7,5},{8,14},{10,8},{12,... | collective-permute-start | bytes 1572872 | tf_op jit(solution)/shard_map/ppermute | solution.py:31
  83.1 20.2 %all-to-all-start.2 = ((bf16[16,64,128]{2,1,0:T(8,128)(2,1)}), bf16[16,64,128]{2,1,0:T(8,128)(2,1)S(1)}, u32[]{:S(2)}, u32[]{:S(2)}) async-start(bf16[16,64,128]{2,1,0:T(8,128)(2,1)} %get-tuple-element.57), calls=%async_computation.2 | async-start | bytes 524288 | tf_op jit(solution)/shard_map/all_to_all | solution.py:78
  102.0 1.0 copy-start.3
  119.9 19.6 %all-to-all-start.4 = ((f32[32,1,128]{2,1,0:T(1,128)}), f32[32,1,128]{2,1,0:T(1,128)S(1)}, u32[]{:S(2)}, u32[]{:S(2)}) async-start(f32[32,1,128]{2,1,0:T(1,128)} %bitcast.12), calls=%async_computation.4 | async-start | bytes 32768 | tf_op jit(solution)/shard_map/all_to_all | solution.py:78
